TPU v7x, 32 devices: a whole 2x2x4 slice. The times are simulated.
32 devices in a mesh: groups: 2 (over y), grid: 4 (over z), dp: 4 (over x, core).
Axes of the slice: x: 2, y: 2, z: 4, core: 2. Of those that a mesh axis runs over, the one named last changes fastest.
Arguments:
- tokens: bfloat16 [128, 4096], P(('groups', 'grid'), 'dp'), parts along dimension 0, may hold values from -6 to 6
- w_gate: bfloat16 [4096, 16384], P('dp', 'grid'), may hold values from -0.09375 to 0.09375
- w_up: bfloat16 [4096, 16384], P('dp', 'grid'), may hold values from -0.09375 to 0.09375
- w_down: bfloat16 [16384, 4096], P('grid', 'dp'), may hold values from -0.046875 to 0.046875
- mask_gate: int32 [64, 128], P(('groups', 'dp'), 'grid'), parts along dimension 0, may hold values from 0 to 1, as said below
- mask_up: int32 [64, 128], P(('groups', 'dp'), 'grid'), parts along dimension 0, may hold values from 0 to 1, as said below
- mask_down: int32 [256, 32], P(('groups', 'grid'), 'dp'), parts along dimension 0, may hold values from 0 to 1, as said below
- grad_out: bfloat16 [128, 4096], P(('groups', 'grid'), 'dp'), parts along dimension 0, may hold values from -6 to 6
Outputs:
- output: bfloat16 [128, 4096], P(('groups', 'grid'), 'dp'), parts along dimension 0
- grad_tokens: bfloat16 [128, 4096], P(('groups', 'grid'), 'dp'), parts along dimension 0
- grad_gate: float32 [8192, 16384], P(('groups', 'dp'), 'grid'), parts along dimension 0
- grad_up: float32 [8192, 16384], P(('groups', 'dp'), 'grid'), parts along dimension 0
- grad_down: float32 [32768, 4096], P(('groups', 'grid'), 'dp'), parts along dimension 0
There are 2 independent parts, one for each index of `groups`. A program takes and returns all parts, laid end to end along the dimension named above; an argument that names none is the same for every part. Nothing has to cross between parts.
Inputs may be any that keep to these rules, and one draw needn't show every extreme that they name: `mask_gate`: 1 keeps the weight block, 0 drops it; the share kept differs between bands of 4 x 4 blocks. `mask_up`: as for mask_gate, drawn independently. `mask_down`: as for mask_gate, drawn independently.
All inputs are finite; a program needn't handle non-finite values.
Results may differ from a plain program's by a relative error of at most 0.005.
Values may be sent and summed in bfloat16 or wider, within the bound.
No kernel may reach another device: no remote copies, remote signals or barrier semaphores. Data moves between devices by JAX's collectives and lax.ppermute only.
A program may use at most 320 MiB of HBM per device.

v0:
```python
import jax
import jax.numpy as jnp
from jax import lax
from jax.sharding import PartitionSpec as P


def blocked(weight, mask):
    rows, cols = weight.shape
    mask_rows, mask_cols = mask.shape
    shaped = weight.reshape(mask_rows, rows // mask_rows, mask_cols, cols // mask_cols)
    return (shaped * mask.astype(weight.dtype)[:, None, :, None]).reshape(rows, cols)


def swiglu_parts(gate):
    sigmoid_gate = jax.nn.sigmoid(gate)
    silu_gate = gate * sigmoid_gate
    slope = sigmoid_gate * (1.0 + gate * (1.0 - sigmoid_gate))
    return (silu_gate, slope)


def contract_rows(left, right):
    return lax.dot_general(
        left, right, (((0,), (0,)), ((), ())), preferred_element_type=jnp.float32
    )


def contract_cols(left, right):
    return lax.dot_general(
        left, right, (((1,), (1,)), ((), ())), preferred_element_type=jnp.float32
    )


def shards(tokens, w_gate, w_up, w_down, mask_gate, mask_up, mask_down, grad_out):
    width = w_gate.shape[1]
    both_eff = jnp.concatenate([blocked(w_gate, mask_gate), blocked(w_up, mask_up)], axis=1)
    down_eff = blocked(w_down, mask_down)
    whole_tokens = lax.all_gather(tokens, "grid", axis=0, tiled=True)
    partial_value = jnp.dot(whole_tokens, both_eff, preferred_element_type=jnp.float32)
    summed = lax.psum(partial_value, "dp")
    gate = summed[:, :width]
    up_val = summed[:, width:]
    silu_gate, slope = swiglu_parts(gate)
    hidden = (silu_gate * up_val).astype(jnp.bfloat16)
    rows = hidden
    output = lax.psum_scatter(
        jnp.dot(rows, down_eff, preferred_element_type=jnp.float32),
        "grid",
        scatter_dimension=0,
        tiled=True,
    ).astype(jnp.bfloat16)
    whole_cotangent = lax.all_gather(grad_out, "grid", axis=0, tiled=True)
    grad_down = blocked(contract_rows(hidden, whole_cotangent), mask_down)
    hidden_partial = contract_cols(whole_cotangent, down_eff)
    hidden_grad = lax.psum(hidden_partial, "dp")
    stacked = jnp.concatenate(
        [
            (hidden_grad * up_val * slope).astype(jnp.bfloat16),
            (hidden_grad * silu_gate).astype(jnp.bfloat16),
        ],
        axis=1,
    )
    grad_both = contract_rows(whole_tokens, stacked)
    grad_gate = blocked(grad_both[:, :width], mask_gate)
    grad_up = blocked(grad_both[:, width:], mask_up)
    rows = stacked
    grad_tokens = lax.psum_scatter(
        contract_cols(rows, both_eff), "grid", scatter_dimension=0, tiled=True
    ).astype(jnp.bfloat16)
    return (output, grad_tokens, grad_gate, grad_up, grad_down)


def solution(mesh):
    in_specs = (
        P(("groups", "grid"), "dp"),
        P("dp", "grid"),
        P("dp", "grid"),
        P("grid", "dp"),
        P(("groups", "dp"), "grid"),
        P(("groups", "dp"), "grid"),
        P(("groups", "grid"), "dp"),
        P(("groups", "grid"), "dp"),
    )
    out_specs = (
        P(("groups", "grid"), "dp"),
        P(("groups", "grid"), "dp"),
        P(("groups", "dp"), "grid"),
        P(("groups", "dp"), "grid"),
        P(("groups", "grid"), "dp"),
    )
    return jax.shard_map(shards, mesh=mesh, in_specs=in_specs, out_specs=out_specs, check_vma=False)
```

profile of v0, /device:TPU:0, one launch (start us, length us, event | category | flops | bytes accessed | tf_op | source)
XLA Modules:
  0.0 282.8 jit_solution(6269946465491274139)
XLA Ops:
  7.2 0.0 all-reduce.3.cloned.1.call-start
  7.2 15.3 %all_gather.6 = bf16[64,1024]{1,0:T(8,128)(2,1)S(1)} all-gather(bf16[16,1024]{1,0:T(8,128)(2,1)} %param.8), channel_id=1, replica_groups=mesh['groups'=2,'grid'=4,'dp'=4] {'grid'}, dimensions={0}, use_global_device_ids=true | all-gather | bytes 163840 | tf_op jit(solution)/shard_map/all_gather | solution.py:37
  22.5 0.8 fusion.9
  23.3 0.8 fusion.10
  24.0 13.7 %all_gather.7 = bf16[64,1024]{1,0:T(8,128)(2,1)S(1)} all-gather(bf16[16,1024]{1,0:T(8,128)(2,1)} %param.15), channel_id=1, replica_groups=mesh['groups'=2,'grid'=4,'dp'=4] {'grid'}, dimensions={0}, use_global_device_ids=true | all-gather | bytes 163840 | tf_op jit(solution)/shard_map/all_gather | solution.py:51
  37.7 0.8 fusion.8
  38.5 0.1 copy.13
  38.6 1.1 mul.90
  39.7 1.1 mul.87
  40.9 14.4 %bitcast_multiply_fusion.4 = (bf16[1024,4096]{1,0:T(8,128)(2,1)}, bf16[1024,4096]{1,0:T(8,128)(2,1)}) fusion(bf16[1024,4096]{1,0:T(8,128)(2,1)} %param.10, bf16[128,8,32,128]{3,2,1,0:T(8,128)(2,1)S(1)} %bitcast.45, bf16[1024,4096]{1,0:T(8,128)(2,1)} %param.9, bf16[128,8,32,128]{3,2,1,0:T(8,128)(2,1)S(1)} %bitcast.46), kind=kLoop, calls=%fused_computation.9 | loop fusion | flops 8388608 | bytes 50331648 | tf_op jit(solution)/shard_map/mul | solution.py:11
  55.3 8.7 %fusion.2 = f32[64,8192]{1,0:T(8,128)} fusion(bf16[64,1024]{1,0:T(8,128)(2,1)S(1)} %all_gather.6, bf16[1024,4096]{1,0:T(8,128)(2,1)} %get-tuple-element.23, bf16[1024,4096]{1,0:T(8,128)(2,1)} %get-tuple-element.24), kind=kOutput, calls=%fused_computation.7 | convolution fusion | flops 1107296256 | bytes 19005440 | tf_op jit(solution)/shard_map/dot_general | solution.py:38
  64.0 1.1 mul.95
  65.2 0.0 copy-start
  65.2 3.4 %copy-done = bf16[32,128,8,128]{3,2,1,0:T(8,128)(2,1)} copy-done((bf16[32,128,8,128]{3,2,1,0:T(8,128)(2,1)}, bf16[32,128,8,128]{3,2,1,0:T(8,128)(2,1)S(1)}, u32[]{:S(2)}) %copy-start) | copy-done | bytes 8388632
  68.6 7.0 %convolution_bitcast_fusion.1 = f32[64,4096]{1,0:T(8,128)} fusion(bf16[64,1024]{1,0:T(8,128)(2,1)S(1)} %all_gather.7, bf16[4096,1024]{1,0:T(8,128)(2,1)} %param.11, bf16[512,8,8,128]{3,2,1,0:T(8,128)(2,1)S(1)} %bitcast.47), kind=kOutput, calls=%fused_computation.11 | convolution fusion | flops 541065216 | bytes 17956864 | tf_op jit(solution)/shard_map/dot_general | solution.py:28
  75.6 0.0 all-reduce.3.cloned.1.call-update
  75.6 0.0 reduce-scatter.3.cloned.1.call-start
  75.7 0.1 copy.15
  75.8 0.1 copy.14
  75.8 0.1 copy.16
  75.9 69.7 %all-reduce.3.cloned.1.call-done = (f32[64,8192]{1,0:T(8,128)}, f32[64,4096]{1,0:T(8,128)}) async-done(((f32[64,8192]{1,0:T(8,128)}, f32[64,4096]{1,0:T(8,128)}), (f32[64,8192]{1,0:T(8,128)}, f32[64,4096]{1,0:T(8,128)})) %all-reduce.3.cloned.1.call-update) | async-done | bytes 3145744 | tf_op jit(solution)/shard_map/psum | solution.py:39
  145.6 2.4 multiply_convert_fusion.1
  148.1 8.0 %fusion.3 = f32[64,1024]{1,0:T(8,128)} fusion(bf16[64,4096]{1,0:T(8,128)(2,1)S(1)} %get-tuple-element.16, bf16[4096,1024]{1,0:T(8,128)(2,1)} %param.11, bf16[512,8,8,128]{3,2,1,0:T(8,128)(2,1)} %bitcast.48), kind=kOutput, calls=%fused_computation.12 | convolution fusion | flops 541065216 | bytes 17563648 | tf_op jit(solution)/shard_map/dot_general | solution.py:46
  156.0 0.0 reduce-scatter.3.cloned.1.call-update
  156.1 0.2 reduce-scatter.5.cloned.1.call-start
  156.3 13.2 %convolution_bitcast_fusion = f32[1024,8192]{0,1:T(8,128)} fusion(bf16[64,1024]{1,0:T(8,128)(2,1)S(1)} %all_gather.6, bf16[64,4096]{1,0:T(8,128)(2,1)S(1)} %get-tuple-element.15, bf16[64,4096]{1,0:T(8,128)(2,1)S(1)} %get-tuple-element.14), kind=kOutput, calls=%fused_computation | convolution fusion | flops 1075838976 | bytes 34734080 | tf_op jit(solution)/shard_map/dot_general | solution.py:22
  169.5 9.5 %fusion = f32[64,1024]{1,0:T(8,128)} fusion(bf16[1024,4096]{1,0:T(8,128)(2,1)} %get-tuple-element.23, bf16[1024,4096]{1,0:T(8,128)(2,1)} %get-tuple-element.24, bf16[64,4096]{1,0:T(8,128)(2,1)S(1)} %get-tuple-element.15, bf16[64,4096]{1,0:T(8,128)(2,1)S(1)} %get-tuple-element.14), kind=kOutput, calls=%fused_computation.5 | convolution fusion | flops 1109393408 | bytes 18087936 | tf_op jit(solution)/shard_map/dot_general | solution.py:28
  179.0 0.0 reduce-scatter.5.cloned.1.call-update
  179.0 7.3 %mul.106 = f32[8,128,32,128]{1,0,3,2:T(8,128)} broadcast(f32[8,32]{0,1:T(8,128)S(1)} %copy.15), dimensions={0,2} | broadcast | bytes 16778240 | tf_op jit(solution)/shard_map/mul | solution.py:11
  186.4 7.3 %mul.103 = f32[8,128,32,128]{1,0,3,2:T(8,128)} broadcast(f32[8,32]{0,1:T(8,128)S(1)} %copy.14), dimensions={0,2} | broadcast | bytes 16778240 | tf_op jit(solution)/shard_map/mul | solution.py:11
  193.7 33.9 %bitcast_multiply_fusion.1 = (f32[1024,4096]{0,1:T(8,128)}, f32[1024,4096]{0,1:T(8,128)}) fusion(f32[512,8,8,128]{3,2,1,0:T(8,128)} %bitcast.43, f32[1024,8192]{0,1:T(8,128)} %convolution_bitcast_fusion, f32[512,8,8,128]{3,2,1,0:T(8,128)} %bitcast.44), kind=kLoop, calls=%fused_computation.2 | loop fusion | flops 8388608 | bytes 100663296 | tf_op jit(solution)/shard_map/mul | solution.py:11
  227.6 1.1 mul.109
  228.7 9.7 %bitcast_multiply_fusion = f32[4096,1024]{1,0:T(8,128)} fusion(f32[512,8,8,128]{3,2,1,0:T(8,128)S(1)} %bitcast.42, bf16[64,4096]{1,0:T(8,128)(2,1)S(1)} %get-tuple-element.16, bf16[64,1024]{1,0:T(8,128)(2,1)S(1)} %all_gather.7), kind=kOutput, calls=%fused_computation.1 | convolution fusion | flops 541065216 | bytes 34209792 | tf_op jit(solution)/shard_map/dot_general | solution.py:22
  238.4 17.4 %copy.17 = f32[1024,4096]{1,0:T(8,128)} copy(f32[1024,4096]{0,1:T(8,128)} %get-tuple-element.13) | data formatting | bytes 33554432
  255.9 17.4 %copy.18 = f32[1024,4096]{1,0:T(8,128)} copy(f32[1024,4096]{0,1:T(8,128)} %get-tuple-element.12) | data formatting | bytes 33554432
  273.3 0.0 reduce-scatter.3.cloned.1.call-done
  273.3 1.5 convert_element_type.37
  274.8 0.0 reduce-scatter.5.cloned.1.call-done
  274.8 1.5 convert_element_type.40
Async XLA Ops:
  7.2 138.5 %all-reduce.3.cloned.1.call-start = ((), (), s32[]{:S(2)}) async-start(), calls=%async_computation.4 | async-start | bytes 6291456 | tf_op jit(solution)/shard_map/psum | solution.py:39
  65.2 3.4 %copy-start = (bf16[32,128,8,128]{3,2,1,0:T(8,128)(2,1)}, bf16[32,128,8,128]{3,2,1,0:T(8,128)(2,1)S(1)}, u32[]{:S(2)}) copy-start(bf16[32,128,8,128]{3,2,1,0:T(8,128)(2,1)S(1)} %mul.95) | copy-start | bytes 25165828
  75.6 197.7 %reduce-scatter.3.cloned.1.call-start = ((), (), s32[]{:S(2)}) async-start(), calls=%async_computation.2 | async-start | bytes 327680 | tf_op jit(solution)/shard_map/reduce_scatter | solution.py:45
  156.1 118.7 %reduce-scatter.5.cloned.1.call-start = ((), (), s32[]{:S(2)}) async-start(), calls=%async_computation.3 | async-start | bytes 327680 | tf_op jit(solution)/shard_map/reduce_scatter | solution.py:66
Sparse Core Ops, SparseCore 0:
  75.8 69.8 all-reduce.2
  156.2 19.7 reduce-scatter.2
  179.2 19.7 reduce-scatter.4
where the time goes:
time: 284 us; the launch traced here: 283 us
  waiting for transfers between devices  69.8 us (25%)
  local copies, waits for them, and re-layouts  57.8 us (20%)
  matrix products  56.2 us (20%)
  other arithmetic  55.9 us (20%)
  blocking collectives  29 us (10%)
  between operations  13.8 us (5%)
    psum x1, waiting for transfers between devices, shards(): summed = lax.psum(partial_value, 'dp')  69.7 us
    mul x2, other arithmetic, blocked(): shaped * mask.astype(weight.dtype)[:, None, :, None]  48.3 us
    unnamed x4, local copies, waits for them, and re-layouts  38.3 us
    dot_general x2, matrix products, contract_rows(): lax.dot_general(left, right, (((0,), (0,)), ((), ())), preferred_element_...  23 us
    mul x6, local copies, waits for them, and re-layouts, blocked(): shaped * mask.astype(weight.dtype)[:, None, :, None]  19.2 us
    dot_general x2, matrix products, contract_cols(): lax.dot_general(left, right, (((1,), (1,)), ((), ())), preferred_element_...  16.5 us
    all_gather x1, blocking collectives, shards(): whole_tokens = lax.all_gather(tokens, 'grid', axis=0, tiled=True)  15.3 us
    all_gather x1, blocking collectives, shards(): whole_cotangent = lax.all_gather(grad_out, 'grid', axis=0, tiled=True)  13.7 us
  transfers between devices with their start and end apart: 3, of which 1 were waited for; matrix products, arithmetic and copies ran while one was open for 42% of the time, Pallas kernels for 0%

commit v1 on v0

v1 whole, which is shorter than its diff:
```python
import functools

import jax
import jax.numpy as jnp
from jax import lax
from jax.experimental import pallas as pl
from jax.experimental.pallas import tpu as pltpu
from jax.sharding import PartitionSpec as P

BLK = 128
MIB = 1024 * 1024
F32 = jnp.float32
BF16 = jnp.bfloat16


def dot(left, right, dims=(1, 0)):
    return lax.dot_general(
        left, right, (((dims[0],), (dims[1],)), ((), ())), preferred_element_type=F32
    )


def masked_rows(w_ref, row_of):
    bands = [
        w_ref[b * BLK : (b + 1) * BLK, :] * row_of(b).astype(BF16)
        for b in range(w_ref.shape[0] // BLK)
    ]
    return bands[0] if len(bands) == 1 else jnp.concatenate(bands, axis=0)


def call(kernel, scalars, grid, ins, outs, scratch=(), aliases=None, cost=None, name=None):
    return pl.pallas_call(
        kernel,
        out_shape=[shape for shape, _ in outs],
        grid_spec=pltpu.PrefetchScalarGridSpec(
            num_scalar_prefetch=1,
            grid=grid,
            in_specs=[spec for _, spec in ins],
            out_specs=[spec for _, spec in outs],
            scratch_shapes=list(scratch),
        ),
        input_output_aliases=aliases or {},
        compiler_params=pltpu.CompilerParams(vmem_limit_bytes=32 * MIB),
        cost_estimate=cost,
        name=name,
    )(scalars, *[array for array, _ in ins])


def whole(array):
    return pl.BlockSpec(array.shape, lambda *_: (0,) * len(array.shape))


def partial_kernel(add, idx, tok, cot, wg, wu, wd, mg, mu, md, *rest):
    gate = dot(tok[...], masked_rows(wg, lambda b: mg[b : b + 1, :]))
    up = dot(tok[...], masked_rows(wu, lambda b: mu[b : b + 1, :]))
    back = dot(cot[...], masked_rows(wd, lambda b: md[b]), (1, 1))
    if add:
        received, own, send = rest
        for k, value in enumerate((gate, up, back)):
            total = value + received[k].astype(F32)
            own[k] = total
            send[k] = total.astype(BF16)
    else:
        (send,) = rest
        for k, value in enumerate((gate, up, back)):
            send[k] = value.astype(BF16)


def act_kernel(idx, own, *rest):
    act = rest[-1]
    gate, up, back = (
        sum((r[k].astype(F32) for r in rest[:-1]), own[k]) for k in range(3)
    )
    sigma = 1.0 / (1.0 + jnp.exp(-gate))
    silu = gate * sigma
    slope = sigma * (1.0 + gate * (1.0 - sigma))
    act[0] = (silu * up).astype(BF16)
    act[1] = (back * up * slope).astype(BF16)
    act[2] = (back * silu).astype(BF16)


def rows_kernel(first, last, tiles, idx, own, other, wg, wu, wd, mg, mu, md, *rest):
    if first:
        carried, rest = None, rest
    else:
        carried, rest = rest[0], rest[1:]
    outs, acc = rest[:-1], rest[-1]
    step = pl.program_id(0)

    @pl.when(step == 0)
    def _():
        if first:
            acc[...] = jnp.zeros_like(acc)
        else:
            acc[...] = carried[...]

    def add(act):
        down = masked_rows(wd, lambda b: md[b])
        acc[0] += dot(act[0], down)
        gate = masked_rows(wg, lambda b: mg[b : b + 1, :])
        up = masked_rows(wu, lambda b: mu[b : b + 1, :])
        acc[1] += dot(act[1], gate, (1, 1)) + dot(act[2], up, (1, 1))

    @pl.when(step < tiles)
    def _():
        add(own)

    @pl.when(step >= tiles)
    def _():
        add(other)

    @pl.when(step == 2 * tiles - 1)
    def _():
        if last:
            rows = outs[0].shape[1]
            for k, out in enumerate(outs):
                out[...] = acc[:, k * rows : (k + 1) * rows, :].astype(out.dtype)
        else:
            outs[0][...] = acc[...]


def grads_kernel(carried, idx, act, tok_t, cot, mg, mu, md, *rest):
    gg, gu, gd = rest[-3:]
    for out, k, mask in ((gg, 1, mg), (gu, 2, mu)):
        for b in range(gg.shape[0] // BLK):
            band = slice(b * BLK, (b + 1) * BLK)
            out[band, :] = dot(tok_t[band, :], act[k]) * mask[b : b + 1, :]
    hidden_t = act[0].T
    for b in range(gd.shape[0] // BLK):
        band = slice(b * BLK, (b + 1) * BLK)
        gd[band, :] = dot(hidden_t[band, :], cot[...]) * md[b]


def shards(sizes, tokens, w_gate, w_up, w_down, mask_gate, mask_up, mask_down, grad_out):
    n_grid, n_dp = sizes
    width, units = w_gate.shape
    pairs = n_dp // 2
    half = units // 2
    pieces = 2 if half % (2 * BLK) == 0 else 1
    piece = half // pieces
    tile = 256 if piece % 256 == 0 else BLK
    tiles = piece // tile

    core = lax.axis_index("dp") % 2
    scalars = jnp.stack([core, 1 - core]).astype(jnp.int32)

    def gather(block):
        if n_grid > 4:
            return lax.all_gather(block, "grid", axis=0, tiled=True)
        blocks = [block]
        for s in range(1, n_grid):
            blocks.append(
                lax.ppermute(block, "grid", [(i, (i + s) % n_grid) for i in range(n_grid)])
            )
        return jnp.concatenate(blocks, axis=0)

    def swap(array):
        return lax.ppermute(array, "dp", [(i, i ^ 1) for i in range(n_dp)])

    def across(array):
        return [
            lax.ppermute(
                array,
                "dp",
                [(i, ((i // 2 + s) % pairs) * 2 + i % 2) for i in range(n_dp)],
            )
            for s in range(1, pairs)
        ]

    tok = gather(tokens)
    cot = gather(grad_out)
    rows = tok.shape[0]
    tok_t = tok.T

    mg = jnp.repeat(mask_gate.astype(F32), BLK, axis=1)
    mu = jnp.repeat(mask_up.astype(F32), BLK, axis=1)
    md = jnp.repeat(mask_down.astype(F32), BLK, axis=1)[:, None, :]

    def place(which, p):
        def at(step, idx):
            return idx[which] * (half // tile) + p * tiles + step

        return at

    def cols(at, height):
        return pl.BlockSpec((height, tile), lambda i, idx: (0, at(i, idx)))

    def bands(at):
        return pl.BlockSpec((tile // BLK, 1, width), lambda i, idx: (at(i, idx), 0, 0))

    def downs(at):
        return pl.BlockSpec((tile, width), lambda i, idx: (at(i, idx), 0))

    def weights(at):
        return [
            (w_gate, cols(at, width)),
            (w_up, cols(at, width)),
            (w_down, downs(at)),
            (mg, cols(at, width // BLK)),
            (mu, cols(at, width // BLK)),
            (md, bands(at)),
        ]

    trio = pl.BlockSpec((3, rows, tile), lambda i, idx: (0, 0, i))
    trio_bf16 = (jax.ShapeDtypeStruct((3, rows, piece), BF16), trio)
    trio_f32 = (jax.ShapeDtypeStruct((3, rows, piece), F32), trio)
    macs = 3 * rows * width * piece
    weight_bytes = 3 * width * piece * 2

    def partials(which, p, received=None):
        ins = [(tok, whole(tok)), (cot, whole(cot))] + weights(place(which, p))
        outs = [trio_bf16]
        if received is not None:
            ins.append((received, trio))
            outs = [trio_f32, trio_bf16]
        return call(
            functools.partial(partial_kernel, received is not None),
            scalars,
            (tiles,),
            ins,
            outs,
            cost=pl.CostEstimate(flops=2 * macs, bytes_accessed=weight_bytes, transcendentals=0),
            name="partials",
        )

    def activate(own, others):
        ins = [(a, whole(a)) for a in (own, *others)]
        shape = jax.ShapeDtypeStruct(own.shape, BF16)
        return call(
            act_kernel,
            scalars,
            (1,),
            ins,
            [(shape, whole(shape))],
            cost=pl.CostEstimate(
                flops=20 * rows * piece, bytes_accessed=12 * rows * piece, transcendentals=rows * piece
            ),
            name="activate",
        )[0]

    n_out = n_grid if n_grid <= 4 else 1

    def sum_rows(p, own, other, carried):
        first, last = carried is None, p == pieces - 1

        def at(step, idx):
            which = step // tiles
            return (idx[0] * (1 - which) + idx[1] * which) * (half // tile) + p * tiles + step % tiles

        acts = [
            (own, pl.BlockSpec((3, rows, tile), lambda i, idx: (0, 0, jnp.minimum(i, tiles - 1)))),
            (other, pl.BlockSpec((3, rows, tile), lambda i, idx: (0, 0, jnp.maximum(i - tiles, 0)))),
        ]
        ins = acts + weights(at)
        if not first:
            ins.append((carried, whole(carried)))
        if last:
            kind = BF16 if n_out > 1 else F32
            shape = jax.ShapeDtypeStruct((2, rows // n_out, width), kind)
            outs = [(shape, whole(shape))] * n_out
        else:
            shape = jax.ShapeDtypeStruct((2, rows, width), F32)
            outs = [(shape, whole(shape))]
        return call(
            functools.partial(rows_kernel, first, last, tiles),
            scalars,
            (2 * tiles,),
            ins,
            outs,
            scratch=[pltpu.VMEM((2, rows, width), F32)],
            cost=pl.CostEstimate(flops=4 * macs, bytes_accessed=2 * weight_bytes, transcendentals=0),
            name="sum_rows",
        )

    def weight_grads(which, p, act, carried):
        at = place(which, p)
        ins = [(act, trio), (tok_t, whole(tok_t)), (cot, whole(cot))] + weights(at)[3:]
        shapes = [
            jax.ShapeDtypeStruct((width, units), F32),
            jax.ShapeDtypeStruct((width, units), F32),
            jax.ShapeDtypeStruct((units, width), F32),
        ]
        specs = [cols(at, width), cols(at, width), downs(at)]
        aliases = {}
        if carried is not None:
            aliases = {1 + len(ins) + k: k for k in range(3)}
            ins = ins + [(c, pl.BlockSpec(memory_space=pl.ANY)) for c in carried]
        return call(
            functools.partial(grads_kernel, carried is not None),
            scalars,
            (tiles,),
            ins,
            list(zip(shapes, specs)),
            aliases=aliases,
            cost=pl.CostEstimate(flops=2 * macs, bytes_accessed=2 * weight_bytes, transcendentals=0),
            name="weight_grads",
        )

    sent = [swap(partials(1, p)[0]) for p in range(pieces)]
    sums, theirs = [], []
    for p in range(pieces):
        own, send = partials(0, p, sent[p])
        sums.append(own)
        theirs.append(across(send))

    grads, carried = None, None
    for p in range(pieces):
        act = activate(sums[p], theirs[p])
        act_other = swap(act)
        carried = sum_rows(p, act, act_other, carried)
        if p < pieces - 1:
            carried = carried[0]
        grads = weight_grads(0, p, act, grads)
        grads = weight_grads(1, p, act_other, grads)

    if n_out == 1:
        both = lax.psum_scatter(carried[0], "grid", scatter_dimension=1, tiled=True)
    else:
        both = carried[0].astype(F32)
        for s in range(1, n_grid):
            both += lax.ppermute(
                carried[s], "grid", [(i, (i - s) % n_grid) for i in range(n_grid)]
            ).astype(F32)
    both = both.astype(BF16)
    return (both[0], both[1], *grads)


def solution(mesh):
    in_specs = (
        P(("groups", "grid"), "dp"),
        P("dp", "grid"),
        P("dp", "grid"),
        P("grid", "dp"),
        P(("groups", "dp"), "grid"),
        P(("groups", "dp"), "grid"),
        P(("groups", "grid"), "dp"),
        P(("groups", "grid"), "dp"),
    )
    out_specs = (
        P(("groups", "grid"), "dp"),
        P(("groups", "grid"), "dp"),
        P(("groups", "dp"), "grid"),
        P(("groups", "dp"), "grid"),
        P(("groups", "grid"), "dp"),
    )
    sizes = (mesh.shape["grid"], mesh.shape["dp"])
    return jax.shard_map(
        functools.partial(shards, sizes),
        mesh=mesh,
        in_specs=in_specs,
        out_specs=out_specs,
        check_vma=False,
    )
```

time: 284 us -> 125 us (0.44)
  Pallas kernels: 0 us -> 60.7 us
  matrix products: 56.2 us -> 0 us
  other arithmetic: 55.9 us -> 2.54 us
  local copies, waits for them, and re-layouts: 57.8 us -> 13 us
  waiting for transfers between devices: 69.8 us -> 25.8 us
  blocking collectives: 29 us -> 0 us
  starting transfers between devices: 0.3 us -> 20.7 us
  between operations: 13.8 us -> 0.87 us
    psum x1 -> x0, waiting for transfers between devices: 69.7 us -> none  [shards(): summed = lax.psum(partial_value, 'dp')]
    pallas_call x0 -> x12, Pallas kernels: none -> 60.7 us  [call(): pl.pallas_call(kernel, out_shape=[shape for shape, _ in outs], grid_spec=...]
    dot_general x6 -> x0, matrix products: 56.2 us -> none  [the longest x2 23 us: contract_rows(): lax.dot_general(left, right, (((0,), (0,)), ((), ())), preferred_element_...]
    mul x2 -> x0, other arithmetic: 48.3 us -> none  [blocked(): shaped * mask.astype(weight.dtype)[:, None, :, None]]
    all_gather x2 -> x0, blocking collectives: 29 us -> none  [the longest x1 15.3 us: shards(): whole_tokens = lax.all_gather(tokens, 'grid', axis=0, tiled=True)]
    unnamed x4 -> x14, local copies, waits for them, and re-layouts: 38.3 us -> 11.8 us
    ppermute x0 -> x15, waiting for transfers between devices: none -> 25.8 us  [the longest x6 14.6 us: gather(): lax.ppermute(block, 'grid', [(i, (i + s) % n_grid) for i in range(n_grid)])]
    ppermute x0 -> x15, starting transfers between devices: none -> 20.7 us  [the longest x6 13 us: gather(): lax.ppermute(block, 'grid', [(i, (i + s) % n_grid) for i in range(n_grid)])]
  transfers between devices with their start and end apart: 3 -> 15, of which waited for: 1 -> 4; matrix products, arithmetic and copies ran while one was open for 42% -> 4% of each run, Pallas kernels for 0% -> 38%
where the time goes in v1:
time: 125 us; the launch traced here: 124 us
  Pallas kernels  60.7 us (49%)
  waiting for transfers between devices  25.8 us (21%)
  starting transfers between devices  20.7 us (17%)
  local copies, waits for them, and re-layouts  13 us (10%)
  other arithmetic  2.54 us (2%)
    pallas_call x12, Pallas kernels, call(): pl.pallas_call(kernel, out_shape=[shape for shape, _ in outs], grid_spec=...  60.7 us
    ppermute x6, waiting for transfers between devices, gather(): lax.ppermute(block, 'grid', [(i, (i + s) % n_grid) for i in range(n_grid)])  14.6 us
    ppermute x6, starting transfers between devices, gather(): lax.ppermute(block, 'grid', [(i, (i + s) % n_grid) for i in range(n_grid)])  13 us
    unnamed x14, local copies, waits for them, and re-layouts  11.8 us
    ppermute x2, waiting for transfers between devices, across(): lax.ppermute(array, 'dp', [(i, (i // 2 + s) % pairs * 2 + i % 2) for i in...  11.2 us
    ppermute x3, starting transfers between devices, shards(): lax.ppermute(carried[s], 'grid', [(i, (i - s) % n_grid) for i in range(n_...  4.37 us
    ppermute x2, starting transfers between devices, across(): lax.ppermute(array, 'dp', [(i, (i // 2 + s) % pairs * 2 + i % 2) for i in...  2.62 us
  transfers between devices with their start and end apart: 15, of which 4 were waited for; matrix products, arithmetic and copies ran while one was open for 4% of the time, Pallas kernels for 38%

profile of v1, /device:TPU:0, one launch (start us, length us, event | category | flops | bytes accessed | tf_op | source)
XLA Modules:
  0.0 123.7 jit_solution(5047335210681743656)
XLA Ops:
  0.6 4.1 %collective-permute-start.4 = (bf16[16,1024]{1,0:T(8,128)(2,1)}, bf16[16,1024]{1,0:T(8,128)(2,1)S(1)}, u32[]{:S(2)}, u32[]{:S(2)}) collective-permute-start(bf16[16,1024]{1,0:T(8,128)(2,1)} %param.15), channel_id=1, source_target_pairs={{0,8},{4,12},{8,0},{12,4},{1,9},{5,13},{9,1},{13,5},{2,10},{6,14},... | collective-permute-start | bytes 98312 | tf_op jit(solution)/shard_map/ppermute | solution.py:152
  4.7 1.6 %collective-permute-start.3 = (bf16[16,1024]{1,0:T(8,128)(2,1)}, bf16[16,1024]{1,0:T(8,128)(2,1)S(1)}, u32[]{:S(2)}, u32[]{:S(2)}) collective-permute-start(bf16[16,1024]{1,0:T(8,128)(2,1)} %param.15), channel_id=1, source_target_pairs={{0,4},{4,8},{8,12},{12,0},{1,5},{5,9},{9,13},{13,1},{2,6},{6,10},{... | collective-permute-start | bytes 98312 | tf_op jit(solution)/shard_map/ppermute | solution.py:152
  6.3 0.9 copy.25
  7.2 2.3 %collective-permute-start.2 = (bf16[16,1024]{0,1:T(8,128)(2,1)S(1)}, bf16[16,1024]{0,1:T(8,128)(2,1)S(1)}, u32[]{:S(2)}, u32[]{:S(2)}) collective-permute-start(bf16[16,1024]{0,1:T(8,128)(2,1)S(1)} %copy.25), channel_id=1, source_target_pairs={{0,12},{4,0},{8,4},{12,8},{1,13},{5,1},{9,5},{13,9},{2,14},{6,2},{... | collective-permute-start | bytes 98312 | tf_op jit(solution)/shard_map/ppermute | solution.py:152
  9.5 0.0 collective-permute-start.1
  9.5 0.6 collective-permute-start
  10.2 0.8 constant_dynamic-update-slice_fusion.3
  10.9 0.7 convert_element_type.24
  11.6 0.7 convert_element_type.25
  12.3 0.1 copy.27
  12.4 0.1 copy.26
  12.5 0.1 broadcast_bitcast_fusion
  12.6 0.1 pad_add_fusion.idx
  12.7 0.7 convert_element_type.26
  13.4 0.1 copy.28
  13.5 2.9 %collective-permute-done.2 = bf16[16,1024]{0,1:T(8,128)(2,1)S(1)} collective-permute-done((bf16[16,1024]{0,1:T(8,128)(2,1)S(1)}, bf16[16,1024]{0,1:T(8,128)(2,1)S(1)}, u32[]{:S(2)}, u32[]{:S(2)}) %collective-permute-start.2) | collective-permute-done | bytes 32800 | tf_op jit(solution)/shard_map/ppermute | solution.py:152
  16.3 4.3 %collective-permute-start.5 = (bf16[16,1024]{1,0:T(8,128)(2,1)}, bf16[16,1024]{1,0:T(8,128)(2,1)S(1)}, u32[]{:S(2)}, u32[]{:S(2)}) collective-permute-start(bf16[16,1024]{1,0:T(8,128)(2,1)} %param.15), channel_id=1, source_target_pairs={{0,12},{4,0},{8,4},{12,8},{1,13},{5,1},{9,5},{13,9},{2,14},{6,2},{... | collective-permute-start | bytes 98312 | tf_op jit(solution)/shard_map/ppermute | solution.py:152
  20.7 11.7 %collective-permute-done.1 = bf16[16,1024]{0,1:T(8,128)(2,1)S(1)} collective-permute-done((bf16[16,1024]{0,1:T(8,128)(2,1)S(1)}, bf16[16,1024]{0,1:T(8,128)(2,1)S(1)}, u32[]{:S(2)}, u32[]{:S(2)}) %collective-permute-start.1) | collective-permute-done | bytes 32800 | tf_op jit(solution)/shard_map/ppermute | solution.py:152
  32.4 0.0 collective-permute-done
  32.4 0.4 pad_maximum_fusion
  32.8 0.0 collective-permute-done.3
  32.8 0.0 collective-permute-done.4
  32.8 0.1 copy.30.tok
  32.9 0.0 collective-permute-done.5
  33.0 0.1 broadcast_in_dim.11
  33.1 0.0 copy-start
  33.1 3.4 %copy-done = bf16[1024,4096]{1,0:T(8,128)(2,1)S(1)} copy-done((bf16[1024,4096]{1,0:T(8,128)(2,1)S(1)}, bf16[1024,4096]{1,0:T(8,128)(2,1)}, u32[]{:S(2)}) %copy-start) | copy-done | bytes 8388632
  36.5 3.4 %copy-done.1 = bf16[1024,4096]{1,0:T(8,128)(2,1)S(1)} copy-done((bf16[1024,4096]{1,0:T(8,128)(2,1)S(1)}, bf16[1024,4096]{1,0:T(8,128)(2,1)}, u32[]{:S(2)}) %copy-start.1) | copy-done | bytes 8388632
  39.8 4.6 %partials.6 = bf16[3,64,1024]{2,1,0:T(8,128)(2,1)S(1)} custom-call(s32[2]{0:T(128)S(1)} %pad_add_fusion.idx, bf16[64,1024]{1,0:T(8,128)(2,1)S(1)} %copy.30.tok, bf16[64,1024]{1,0:T(8,128)(2,1)S(1)} %constant_dynamic-update-slice_fusion.cot, bf16[1024,4096]{1,0:T(8,128)(2,1)S(1)} %copy-done, bf16[1024,4096]{1,0:T(8,128)(2,1)S(1)} %copy-done.1, ...), custom_call_target="tpu_custom_call" | custom-call | flops 402653184 | bytes 6291456 | tf_op jit(solution)/shard_map/partials/pallas_call | solution.py:31
  44.5 0.1 collective-permute-start.9
  44.6 4.7 %partials.4 = bf16[3,64,1024]{2,1,0:T(8,128)(2,1)S(1)} custom-call(s32[2]{0:T(128)S(1)} %pad_add_fusion.idx, bf16[64,1024]{1,0:T(8,128)(2,1)S(1)} %copy.30.tok, bf16[64,1024]{1,0:T(8,128)(2,1)S(1)} %constant_dynamic-update-slice_fusion.cot, bf16[1024,4096]{1,0:T(8,128)(2,1)S(1)} %copy-done, bf16[1024,4096]{1,0:T(8,128)(2,1)S(1)} %copy-done.1, ...), custom_call_target="tpu_custom_call" | custom-call | flops 402653184 | bytes 6291456 | tf_op jit(solution)/shard_map/partials/pallas_call | solution.py:31
  49.2 0.6 collective-permute-start.6
  49.8 0.0 collective-permute-done.9.rest_0_
  49.8 4.7 %partials.7 = (f32[3,64,1024]{2,1,0:T(8,128)S(1)}, bf16[3,64,1024]{2,1,0:T(8,128)(2,1)S(1)}) custom-call(s32[2]{0:T(128)S(1)} %pad_add_fusion.idx, bf16[64,1024]{1,0:T(8,128)(2,1)S(1)} %copy.30.tok, bf16[64,1024]{1,0:T(8,128)(2,1)S(1)} %constant_dynamic-update-slice_fusion.cot, bf16[1024,4096]{1,0:T(8,128)(2,1)S(1)} %copy-done, ...), custom_call_target="tpu_custom_call" | custom-call | flops 402653184 | bytes 6291456 | tf_op jit(solution)/shard_map/partials/pallas_call | solution.py:31
  54.5 0.0 slice-start
  54.5 0.0 slice-start.1
  54.6 1.6 %collective-permute-start.10 = (bf16[3,64,1024]{2,1,0:T(8,128)(2,1)S(1)}, bf16[3,64,1024]{2,1,0:T(8,128)(2,1)S(1)}, u32[]{:S(2)}, u32[]{:S(2)}) collective-permute-start(bf16[3,64,1024]{2,1,0:T(8,128)(2,1)S(1)} %get-tuple-element.28), channel_id=1, source_target_pairs={{0,2},{1,3},{2,0},{3,1},{4,6},{5,7},{6,4},{7,5},{8,10},{9,11},{10,... | collective-permute-start | bytes 1179656 | tf_op jit(solution)/shard_map/ppermute | solution.py:161
  56.1 0.0 collective-permute-done.6.rest_0_
  56.1 4.9 %partials.5 = (f32[3,64,1024]{2,1,0:T(8,128)S(1)}, bf16[3,64,1024]{2,1,0:T(8,128)(2,1)S(1)}) custom-call(s32[2]{0:T(128)S(1)} %pad_add_fusion.idx, bf16[64,1024]{1,0:T(8,128)(2,1)S(1)} %copy.30.tok, bf16[64,1024]{1,0:T(8,128)(2,1)S(1)} %constant_dynamic-update-slice_fusion.cot, bf16[1024,4096]{1,0:T(8,128)(2,1)S(1)} %copy-done, ...), custom_call_target="tpu_custom_call" | custom-call | flops 402653184 | bytes 6291456 | tf_op jit(solution)/shard_map/partials/pallas_call | solution.py:31
  61.0 1.1 collective-permute-start.7
  62.1 4.5 %collective-permute-done.10.rest_0_ = bf16[3,64,1024]{2,1,0:T(8,128)(2,1)S(1)} collective-permute-done((bf16[3,64,1024]{2,1,0:T(8,128)(2,1)S(1)}, bf16[3,64,1024]{2,1,0:T(8,128)(2,1)S(1)}, u32[]{:S(2)}, u32[]{:S(2)}) %collective-permute-start.10) | collective-permute-done | bytes 393248 | tf_op jit(solution)/shard_map/ppermute | solution.py:161
  66.6 0.7 activate.3.own.act
  67.3 0.1 collective-permute-start.11
  67.4 6.7 %collective-permute-done.7.rest_0_ = bf16[3,64,1024]{2,1,0:T(8,128)(2,1)S(1)} collective-permute-done((bf16[3,64,1024]{2,1,0:T(8,128)(2,1)S(1)}, bf16[3,64,1024]{2,1,0:T(8,128)(2,1)S(1)}, u32[]{:S(2)}, u32[]{:S(2)}) %collective-permute-start.7) | collective-permute-done | bytes 393248 | tf_op jit(solution)/shard_map/ppermute | solution.py:161
  74.1 0.7 activate.2.own.act
  74.8 0.1 collective-permute-start.8
  74.9 5.7 %weight_grads.4 = (f32[1024,4096]{1,0:T(8,128)}, f32[1024,4096]{1,0:T(8,128)}, f32[4096,1024]{1,0:T(8,128)}) custom-call(s32[2]{0:T(128)S(1)} %pad_add_fusion.idx, bf16[3,64,1024]{2,1,0:T(8,128)(2,1)S(1)} %activate.3.own.act, bf16[1024,64]{1,0:T(8,128)(2,1)S(1)} %bitcast.24, bf16[64,1024]{1,0:T(8,128)(2,1)S(1)} %constant_dynamic-update-slice_fusion.cot, ...), custom_call_target="tpu_custom_call" | custom-call | flops 402653184 | bytes 12582912 | tf_op jit(solution)/shard_map/weight_grads/pallas_call | solution.py:31
  80.6 0.0 collective-permute-done.11.other.act
  80.6 0.0 slice-done.1
  80.6 0.0 copy-start.2
  80.6 3.4 %copy-done.2 = bf16[1024,4096]{1,0:T(8,128)(2,1)S(1)} copy-done((bf16[1024,4096]{1,0:T(8,128)(2,1)S(1)}, bf16[1024,4096]{1,0:T(8,128)(2,1)}, u32[]{:S(2)}) %copy-start.2) | copy-done | bytes 8388632
  84.0 8.8 %sum_rows.2.rest_0_ = f32[2,64,1024]{2,1,0:T(8,128)S(1)} custom-call(s32[2]{0:T(128)S(1)} %pad_add_fusion.idx, bf16[3,64,1024]{2,1,0:T(8,128)(2,1)S(1)} %activate.3.own.act, bf16[3,64,1024]{2,1,0:T(8,128)(2,1)S(1)} %collective-permute-done.11.other.act, bf16[1024,4096]{1,0:T(8,128)(2,1)S(1)} %bitcast.13, bf16[1024,4096]{1,0:T(8,128)(2,1)S(1)} %copy-done.2, ...), custom_call_target="tpu_custom_call" | custom-call | flops 805306368 | bytes 12582912 | tf_op jit(solution)/shard_map/sum_rows/pallas_call | solution.py:31
  92.8 0.0 collective-permute-done.8.other.act
  92.8 8.8 %sum_rows.3 = (bf16[2,16,1024]{2,1,0:T(8,128)(2,1)S(1)}, bf16[2,16,1024]{2,1,0:T(8,128)(2,1)S(1)}, bf16[2,16,1024]{2,1,0:T(8,128)(2,1)S(1)}, bf16[2,16,1024]{2,1,0:T(8,128)(2,1)S(1)}) custom-call(s32[2]{0:T(128)S(1)} %pad_add_fusion.idx, bf16[3,64,1024]{2,1,0:T(8,128)(2,1)S(1)} %activate.2.own.act, ...), custom_call_target="tpu_custom_call" | custom-call | flops 805306368 | bytes 12582912 | tf_op jit(solution)/shard_map/sum_rows/pallas_call | solution.py:31
  101.7 0.1 collective-permute-start.12
  101.7 2.4 %collective-permute-start.13 = (bf16[2,16,1024]{2,1,0:T(8,128)(2,1)S(1)}, bf16[2,16,1024]{2,1,0:T(8,128)(2,1)S(1)}, u32[]{:S(2)}, u32[]{:S(2)}) collective-permute-start(bf16[2,16,1024]{2,1,0:T(8,128)(2,1)S(1)} %get-tuple-element.31), channel_id=1, source_target_pairs={{0,8},{4,12},{8,0},{12,4},{1,9},{5,13},{9,1},{13,5},{2,10},{6,14},... | collective-permute-start | bytes 196616 | tf_op jit(solution)/shard_map/ppermute | solution.py:320
  104.1 1.9 %collective-permute-start.14 = (bf16[2,16,1024]{2,1,0:T(8,128)(2,1)S(1)}, bf16[2,16,1024]{2,1,0:T(8,128)(2,1)S(1)}, u32[]{:S(2)}, u32[]{:S(2)}) collective-permute-start(bf16[2,16,1024]{2,1,0:T(8,128)(2,1)S(1)} %get-tuple-element.32), channel_id=1, source_target_pairs={{0,4},{4,8},{8,12},{12,0},{1,5},{5,9},{9,13},{13,1},{2,6},{6,10},{... | collective-permute-start | bytes 196616 | tf_op jit(solution)/shard_map/ppermute | solution.py:320
  106.0 5.6 %weight_grads.5 = (f32[1024,4096]{1,0:T(8,128)}, f32[1024,4096]{1,0:T(8,128)}, f32[4096,1024]{1,0:T(8,128)}) custom-call(s32[2]{0:T(128)S(1)} %pad_add_fusion.idx, bf16[3,64,1024]{2,1,0:T(8,128)(2,1)S(1)} %collective-permute-done.11.other.act, bf16[1024,64]{1,0:T(8,128)(2,1)S(1)} %bitcast.25, ...), custom_call_target="tpu_custom_call", output_to_operand_aliasing={{0}: (7, {}), {1}: (8, {}), {2}: (9, {})} | custom-call | flops 402653184 | bytes 12582912 | tf_op jit(solution)/shard_map/weight_grads/pallas_call | solution.py:31
  111.7 5.7 %weight_grads.6 = (f32[1024,4096]{1,0:T(8,128)}, f32[1024,4096]{1,0:T(8,128)}, f32[4096,1024]{1,0:T(8,128)}) custom-call(s32[2]{0:T(128)S(1)} %pad_add_fusion.idx, bf16[3,64,1024]{2,1,0:T(8,128)(2,1)S(1)} %activate.2.own.act, bf16[1024,64]{1,0:T(8,128)(2,1)S(1)} %bitcast.26, ...), custom_call_target="tpu_custom_call", output_to_operand_aliasing={{0}: (7, {}), {1}: (8, {}), {2}: (9, {})} | custom-call | flops 402653184 | bytes 12582912 | tf_op jit(solution)/shard_map/weight_grads/pallas_call | solution.py:31
  117.3 5.7 %weight_grads.7 = (f32[1024,4096]{1,0:T(8,128)}, f32[1024,4096]{1,0:T(8,128)}, f32[4096,1024]{1,0:T(8,128)}) custom-call(s32[2]{0:T(128)S(1)} %pad_add_fusion.idx, bf16[3,64,1024]{2,1,0:T(8,128)(2,1)S(1)} %collective-permute-done.8.other.act, bf16[1024,64]{1,0:T(8,128)(2,1)S(1)} %bitcast.27, ...), custom_call_target="tpu_custom_call", output_to_operand_aliasing={{0}: (7, {}), {1}: (8, {}), {2}: (9, {})} | custom-call | flops 402653184 | bytes 12582912 | tf_op jit(solution)/shard_map/weight_grads/pallas_call | solution.py:31
  123.0 0.0 collective-permute-done.12
  123.0 0.0 collective-permute-done.13
  123.0 0.0 collective-permute-done.14
  123.1 0.6 slice_bitcast_fusion
  (7 shorter events, 0.1 us)
Async XLA Ops:
  0.6 32.2 %collective-permute-start.4 = (bf16[16,1024]{1,0:T(8,128)(2,1)}, bf16[16,1024]{1,0:T(8,128)(2,1)S(1)}, u32[]{:S(2)}, u32[]{:S(2)}) collective-permute-start(bf16[16,1024]{1,0:T(8,128)(2,1)} %param.15), channel_id=1, source_target_pairs={{0,8},{4,12},{8,0},{12,4},{1,9},{5,13},{9,1},{13,5},{2,10},{6,14},... | collective-permute-start | bytes 98312 | tf_op jit(solution)/shard_map/ppermute | solution.py:152
  4.7 28.0 %collective-permute-start.3 = (bf16[16,1024]{1,0:T(8,128)(2,1)}, bf16[16,1024]{1,0:T(8,128)(2,1)S(1)}, u32[]{:S(2)}, u32[]{:S(2)}) collective-permute-start(bf16[16,1024]{1,0:T(8,128)(2,1)} %param.15), channel_id=1, source_target_pairs={{0,4},{4,8},{8,12},{12,0},{1,5},{5,9},{9,13},{13,1},{2,6},{6,10},{... | collective-permute-start | bytes 98312 | tf_op jit(solution)/shard_map/ppermute | solution.py:152
  7.2 9.1 %collective-permute-start.2 = (bf16[16,1024]{0,1:T(8,128)(2,1)S(1)}, bf16[16,1024]{0,1:T(8,128)(2,1)S(1)}, u32[]{:S(2)}, u32[]{:S(2)}) collective-permute-start(bf16[16,1024]{0,1:T(8,128)(2,1)S(1)} %copy.25), channel_id=1, source_target_pairs={{0,12},{4,0},{8,4},{12,8},{1,13},{5,1},{9,5},{13,9},{2,14},{6,2},{... | collective-permute-start | bytes 98312 | tf_op jit(solution)/shard_map/ppermute | solution.py:152
  9.5 22.9 %collective-permute-start.1 = (bf16[16,1024]{0,1:T(8,128)(2,1)S(1)}, bf16[16,1024]{0,1:T(8,128)(2,1)S(1)}, u32[]{:S(2)}, u32[]{:S(2)}) collective-permute-start(bf16[16,1024]{0,1:T(8,128)(2,1)S(1)} %copy.25), channel_id=1, source_target_pairs={{0,8},{4,12},{8,0},{12,4},{1,9},{5,13},{9,1},{13,5},{2,10},{6,14},... | collective-permute-start | bytes 98312 | tf_op jit(solution)/shard_map/ppermute | solution.py:152
  9.5 22.9 %collective-permute-start = (bf16[16,1024]{0,1:T(8,128)(2,1)S(1)}, bf16[16,1024]{0,1:T(8,128)(2,1)S(1)}, u32[]{:S(2)}, u32[]{:S(2)}) collective-permute-start(bf16[16,1024]{0,1:T(8,128)(2,1)S(1)} %copy.25), channel_id=1, source_target_pairs={{0,4},{4,8},{8,12},{12,0},{1,5},{5,9},{9,13},{13,1},{2,6},{6,10},{... | collective-permute-start | bytes 98312 | tf_op jit(solution)/shard_map/ppermute | solution.py:152
  16.3 16.6 %collective-permute-start.5 = (bf16[16,1024]{1,0:T(8,128)(2,1)}, bf16[16,1024]{1,0:T(8,128)(2,1)S(1)}, u32[]{:S(2)}, u32[]{:S(2)}) collective-permute-start(bf16[16,1024]{1,0:T(8,128)(2,1)} %param.15), channel_id=1, source_target_pairs={{0,12},{4,0},{8,4},{12,8},{1,13},{5,1},{9,5},{13,9},{2,14},{6,2},{... | collective-permute-start | bytes 98312 | tf_op jit(solution)/shard_map/ppermute | solution.py:152
  33.1 3.4 %copy-start = (bf16[1024,4096]{1,0:T(8,128)(2,1)S(1)}, bf16[1024,4096]{1,0:T(8,128)(2,1)}, u32[]{:S(2)}) copy-start(bf16[1024,4096]{1,0:T(8,128)(2,1)} %wg.11) | copy-start | bytes 25165828
  36.5 3.4 %copy-start.1 = (bf16[1024,4096]{1,0:T(8,128)(2,1)S(1)}, bf16[1024,4096]{1,0:T(8,128)(2,1)}, u32[]{:S(2)}) copy-start(bf16[1024,4096]{1,0:T(8,128)(2,1)} %wu.11) | copy-start | bytes 25165828
  44.5 5.3 %collective-permute-start.9 = (bf16[3,64,1024]{2,1,0:T(8,128)(2,1)S(1)}, bf16[3,64,1024]{2,1,0:T(8,128)(2,1)S(1)}, u32[]{:S(2)}, u32[]{:S(2)}) collective-permute-start(bf16[3,64,1024]{2,1,0:T(8,128)(2,1)S(1)} %partials.6), channel_id=1, source_target_pairs={{0,1},{1,0},{2,3},{3,2},{4,5},{5,4},{6,7},{7,6},{8,9},{9,8},{10,11... | collective-permute-start | bytes 1179656 | tf_op jit(solution)/shard_map/ppermute | solution.py:157
  49.2 6.9 %collective-permute-start.6 = (bf16[3,64,1024]{2,1,0:T(8,128)(2,1)S(1)}, bf16[3,64,1024]{2,1,0:T(8,128)(2,1)S(1)}, u32[]{:S(2)}, u32[]{:S(2)}) collective-permute-start(bf16[3,64,1024]{2,1,0:T(8,128)(2,1)S(1)} %partials.4), channel_id=1, source_target_pairs={{0,1},{1,0},{2,3},{3,2},{4,5},{5,4},{6,7},{7,6},{8,9},{9,8},{10,11... | collective-permute-start | bytes 1179656 | tf_op jit(solution)/shard_map/ppermute | solution.py:157
  54.5 26.1 %slice-start = ((s8[8388608]{0:T(1024)(128)(4,1)}), s8[4194304]{0:T(1024)(128)(4,1)S(1)}, s32[]{:S(2)}) async-start(s8[8388608]{0:T(1024)(128)(4,1)} %bitcast.12), calls=%async_computation | async-start | bytes 8388608
  54.5 26.1 %slice-start.1 = ((s8[8388608]{0:T(1024)(128)(4,1)}), s8[4194304]{0:T(1024)(128)(4,1)S(1)}, s32[]{:S(2)}) async-start(s8[8388608]{0:T(1024)(128)(4,1)} %bitcast.12), calls=%async_computation.1 | async-start | bytes 8388608
  54.6 12.0 %collective-permute-start.10 = (bf16[3,64,1024]{2,1,0:T(8,128)(2,1)S(1)}, bf16[3,64,1024]{2,1,0:T(8,128)(2,1)S(1)}, u32[]{:S(2)}, u32[]{:S(2)}) collective-permute-start(bf16[3,64,1024]{2,1,0:T(8,128)(2,1)S(1)} %get-tuple-element.28), channel_id=1, source_target_pairs={{0,2},{1,3},{2,0},{3,1},{4,6},{5,7},{6,4},{7,5},{8,10},{9,11},{10,... | collective-permute-start | bytes 1179656 | tf_op jit(solution)/shard_map/ppermute | solution.py:161
  61.0 13.1 %collective-permute-start.7 = (bf16[3,64,1024]{2,1,0:T(8,128)(2,1)S(1)}, bf16[3,64,1024]{2,1,0:T(8,128)(2,1)S(1)}, u32[]{:S(2)}, u32[]{:S(2)}) collective-permute-start(bf16[3,64,1024]{2,1,0:T(8,128)(2,1)S(1)} %get-tuple-element.26), channel_id=1, source_target_pairs={{0,2},{1,3},{2,0},{3,1},{4,6},{5,7},{6,4},{7,5},{8,10},{9,11},{10,... | collective-permute-start | bytes 1179656 | tf_op jit(solution)/shard_map/ppermute | solution.py:161
  67.3 13.3 %collective-permute-start.11 = (bf16[3,64,1024]{2,1,0:T(8,128)(2,1)S(1)}, bf16[3,64,1024]{2,1,0:T(8,128)(2,1)S(1)}, u32[]{:S(2)}, u32[]{:S(2)}) collective-permute-start(bf16[3,64,1024]{2,1,0:T(8,128)(2,1)S(1)} %activate.3.own.act), channel_id=1, source_target_pairs={{0,1},{1,0},{2,3},{3,2},{4,5},{5,4},{6,7},{7,6},{8,9},{9,8},{10,11... | collective-permute-start | bytes 1179656 | tf_op jit(solution)/shard_map/ppermute | solution.py:157
  74.8 18.0 %collective-permute-start.8 = (bf16[3,64,1024]{2,1,0:T(8,128)(2,1)S(1)}, bf16[3,64,1024]{2,1,0:T(8,128)(2,1)S(1)}, u32[]{:S(2)}, u32[]{:S(2)}) collective-permute-start(bf16[3,64,1024]{2,1,0:T(8,128)(2,1)S(1)} %activate.2.own.act), channel_id=1, source_target_pairs={{0,1},{1,0},{2,3},{3,2},{4,5},{5,4},{6,7},{7,6},{8,9},{9,8},{10,11... | collective-permute-start | bytes 1179656 | tf_op jit(solution)/shard_map/ppermute | solution.py:157
  80.6 3.4 %copy-start.2 = (bf16[1024,4096]{1,0:T(8,128)(2,1)S(1)}, bf16[1024,4096]{1,0:T(8,128)(2,1)}, u32[]{:S(2)}) copy-start(bf16[1024,4096]{1,0:T(8,128)(2,1)} %wu.11) | copy-start | bytes 25165828
  101.7 21.3 %collective-permute-start.12 = (bf16[2,16,1024]{2,1,0:T(8,128)(2,1)S(1)}, bf16[2,16,1024]{2,1,0:T(8,128)(2,1)S(1)}, u32[]{:S(2)}, u32[]{:S(2)}) collective-permute-start(bf16[2,16,1024]{2,1,0:T(8,128)(2,1)S(1)} %get-tuple-element.30), channel_id=1, source_target_pairs={{0,12},{4,0},{8,4},{12,8},{1,13},{5,1},{9,5},{13,9},{2,14},{6,2},{... | collective-permute-start | bytes 196616 | tf_op jit(solution)/shard_map/ppermute | solution.py:320
  101.7 21.3 %collective-permute-start.13 = (bf16[2,16,1024]{2,1,0:T(8,128)(2,1)S(1)}, bf16[2,16,1024]{2,1,0:T(8,128)(2,1)S(1)}, u32[]{:S(2)}, u32[]{:S(2)}) collective-permute-start(bf16[2,16,1024]{2,1,0:T(8,128)(2,1)S(1)} %get-tuple-element.31), channel_id=1, source_target_pairs={{0,8},{4,12},{8,0},{12,4},{1,9},{5,13},{9,1},{13,5},{2,10},{6,14},... | collective-permute-start | bytes 196616 | tf_op jit(solution)/shard_map/ppermute | solution.py:320
  104.1 18.9 %collective-permute-start.14 = (bf16[2,16,1024]{2,1,0:T(8,128)(2,1)S(1)}, bf16[2,16,1024]{2,1,0:T(8,128)(2,1)S(1)}, u32[]{:S(2)}, u32[]{:S(2)}) collective-permute-start(bf16[2,16,1024]{2,1,0:T(8,128)(2,1)S(1)} %get-tuple-element.32), channel_id=1, source_target_pairs={{0,4},{4,8},{8,12},{12,0},{1,5},{5,9},{9,13},{13,1},{2,6},{6,10},{... | collective-permute-start | bytes 196616 | tf_op jit(solution)/shard_map/ppermute | solution.py:320

commit v2 on v0

v2 whole, which is shorter than its diff:
```python
import functools
import types

import jax
import jax.numpy as jnp
from jax import lax
from jax.experimental import pallas as pl
from jax.experimental.pallas import tpu as pltpu
from jax.sharding import PartitionSpec as P

BLK = 128
PIECES = [3, 3, 2]
MIB = 1024 * 1024
F32 = jnp.float32
BF16 = jnp.bfloat16


def dot(left, right, dims=(1, 0)):
    return lax.dot_general(
        left, right, (((dims[0],), (dims[1],)), ((), ())), preferred_element_type=F32
    )


def masked_rows(w_ref, row_of):
    bands = [
        w_ref[b * BLK : (b + 1) * BLK, :] * row_of(b).astype(BF16)
        for b in range(w_ref.shape[0] // BLK)
    ]
    return bands[0] if len(bands) == 1 else jnp.concatenate(bands, axis=0)


def call(kernel, name, scalars, grid, ins, outs, scratch=None, aliases=None, cost=None):
    scratch = scratch or {}
    names = [*ins, *outs, *scratch]
    in_names, out_names = list(ins), list(outs)

    def body(_, *refs):
        kernel(types.SimpleNamespace(**dict(zip(names, refs))))

    results = pl.pallas_call(
        body,
        out_shape=[shape for shape, _ in outs.values()],
        grid_spec=pltpu.PrefetchScalarGridSpec(
            num_scalar_prefetch=1,
            grid=grid,
            in_specs=[spec for _, spec in ins.values()],
            out_specs=[spec for _, spec in outs.values()],
            scratch_shapes=list(scratch.values()),
        ),
        input_output_aliases={
            1 + in_names.index(i): out_names.index(o) for i, o in (aliases or {}).items()
        },
        compiler_params=pltpu.CompilerParams(vmem_limit_bytes=40 * MIB),
        cost_estimate=cost,
        name=name,
    )(scalars, *[array for array, _ in ins.values()])
    return dict(zip(out_names, results))


def whole(array):
    return pl.BlockSpec(array.shape, lambda *_: (0,) * len(array.shape))


def assemble_kernel(r):
    blocks = [ref for name, ref in vars(r).items() if name.startswith("block")]
    rows = blocks[0].shape[1]
    for k, block in enumerate(blocks):
        r.tok[k * rows : (k + 1) * rows, :] = block[0]
        r.cot[k * rows : (k + 1) * rows, :] = block[1]
    r.tok_t[...] = r.tok[...].T


def partial_kernel(r):
    gate = dot(r.tok[...], masked_rows(r.wg, lambda b: r.mg[b : b + 1, :]))
    up = dot(r.tok[...], masked_rows(r.wu, lambda b: r.mu[b : b + 1, :]))
    back = dot(masked_rows(r.wd, lambda b: r.md[b]), r.cot[...], (1, 1)).T
    for k, value in enumerate((gate, up, back)):
        if hasattr(r, "received"):
            value = value + r.received[k]
            r.own[k] = value
        r.send[k] = value.astype(r.send.dtype)


def act_kernel(r):
    others = [ref for name, ref in vars(r).items() if name.startswith("other")]
    gate, up, back = (
        sum((other[k].astype(F32) for other in others), r.own[k]) for k in range(3)
    )
    sigma = 1.0 / (1.0 + jnp.exp(-gate))
    silu = gate * sigma
    slope = sigma * (1.0 + gate * (1.0 - sigma))
    r.act[0] = (silu * up).astype(BF16)
    r.act[1] = (back * up * slope).astype(BF16)
    r.act[2] = (back * silu).astype(BF16)


def add_rows(r, tiles):
    step = pl.program_id(0)

    @pl.when(step == 0)
    def _():
        for acc, carried in ((r.acc_out, "sum_out"), (r.acc_tok, "sum_tok")):
            acc[...] = getattr(r, carried)[...] if hasattr(r, carried) else jnp.zeros_like(acc)

    r.acc_out[...] += dot(r.act[0], masked_rows(r.wd, lambda b: r.md[b]))
    r.acc_tok[...] += dot(
        masked_rows(r.wg, lambda b: r.mg[b : b + 1, :]), r.act[1], (1, 1)
    ) + dot(masked_rows(r.wu, lambda b: r.mu[b : b + 1, :]), r.act[2], (1, 1))

    @pl.when(step == tiles - 1)
    def _():
        if hasattr(r, "new_out"):
            r.new_out[...] = r.acc_out[...]
            r.new_tok[...] = r.acc_tok[...]
        else:
            outs = [ref for name, ref in vars(r).items() if name.startswith("rows")]
            grad_tok = r.acc_tok[...].T
            rows = outs[0].shape[1]
            for k, out in enumerate(outs):
                band = slice(k * rows, (k + 1) * rows)
                out[0] = r.acc_out[band, :].astype(out.dtype)
                out[1] = grad_tok[band, :].astype(out.dtype)


def weight_grads(r):
    for out, k, mask in ((r.gg, 1, r.mg), (r.gu, 2, r.mu)):
        for b in range(out.shape[0] // BLK):
            band = slice(b * BLK, (b + 1) * BLK)
            out[band, :] = dot(r.tok_t[band, :], r.act[k]) * mask[b : b + 1, :]
    hidden_t = r.act[0].T
    for b in range(r.gd.shape[0] // BLK):
        band = slice(b * BLK, (b + 1) * BLK)
        r.gd[band, :] = dot(hidden_t[band, :], r.cot[...]) * r.md[b]


def back_kernel(do_rows, do_grads, tiles, r):
    if do_rows:
        add_rows(r, tiles)
    if do_grads:
        weight_grads(r)


def shards(sizes, tokens, w_gate, w_up, w_down, mask_gate, mask_up, mask_down, grad_out):
    n_grid, n_dp = sizes
    width, units = w_gate.shape
    pairs = n_dp // 2
    half = units // 2
    tile = 256 if half % 256 == 0 and half >= 1024 else BLK
    split = PIECES if sum(PIECES) * tile == half else [half // tile]
    starts = [sum(split[:p]) for p in range(len(split))]
    direct = n_grid == 4

    core = lax.axis_index("dp") % 2
    scalars = jnp.stack([core, 1 - core]).astype(jnp.int32)
    w_gate, w_up, w_down = (
        pltpu.with_memory_space_constraint(w, pltpu.HBM) for w in (w_gate, w_up, w_down)
    )

    def trade(array, s):
        return lax.ppermute(array, "grid", [(i, i ^ s) for i in range(n_grid)])

    def swap(array):
        return lax.ppermute(array, "dp", [(i, i ^ 1) for i in range(n_dp)])

    def across(array):
        return [
            lax.ppermute(
                array,
                "dp",
                [(i, ((i // 2 + s) % pairs) * 2 + i % 2) for i in range(n_dp)],
            )
            for s in range(1, pairs)
        ]

    mg = jnp.repeat(mask_gate.astype(F32), BLK, axis=1)
    mu = jnp.repeat(mask_up.astype(F32), BLK, axis=1)
    md = jnp.repeat(mask_down.astype(F32), BLK, axis=1)[:, None, :]

    block = jnp.stack([tokens, grad_out])
    if direct:
        blocks = [block] + [trade(block, s) for s in range(1, n_grid)]
    else:
        blocks = [lax.all_gather(block, "grid", axis=1, tiled=True)]
    rows = sum(b.shape[1] for b in blocks)
    row_shape = jax.ShapeDtypeStruct((rows, width), BF16)
    col_shape = jax.ShapeDtypeStruct((width, rows), BF16)
    gathered = call(
        assemble_kernel,
        "assemble",
        scalars,
        (1,),
        {f"block{k}": (b, whole(b)) for k, b in enumerate(blocks)},
        {
            "tok": (row_shape, whole(row_shape)),
            "cot": (row_shape, whole(row_shape)),
            "tok_t": (col_shape, whole(col_shape)),
        },
    )
    tok, cot, tok_t = gathered["tok"], gathered["cot"], gathered["tok_t"]

    def place(which, p):
        return lambda step, idx: idx[which] * (half // tile) + starts[p] + step

    def cols(at, height):
        return pl.BlockSpec((height, tile), lambda i, idx: (0, at(i, idx)))

    def downs(at):
        return pl.BlockSpec((tile, width), lambda i, idx: (at(i, idx), 0))

    def masks(at):
        bands = pl.BlockSpec((tile // BLK, 1, width), lambda i, idx: (at(i, idx), 0, 0))
        return {
            "mg": (mg, cols(at, width // BLK)),
            "mu": (mu, cols(at, width // BLK)),
            "md": (md, bands),
        }

    def weights(at):
        return {
            "wg": (w_gate, cols(at, width)),
            "wu": (w_up, cols(at, width)),
            "wd": (w_down, downs(at)),
        }

    trio = pl.BlockSpec((3, rows, tile), lambda i, idx: (0, 0, i))

    def trio_of(p, kind):
        return (jax.ShapeDtypeStruct((3, rows, split[p] * tile), kind), trio)

    def cost(p, matmuls, mats):
        step = width * split[p] * tile
        return pl.CostEstimate(
            flops=2 * matmuls * rows * step, bytes_accessed=2 * mats * step, transcendentals=0
        )

    def partials(which, p, after=None, received=None):
        at = place(which, p)
        ins = {"tok": (tok, whole(tok)), "cot": (cot, whole(cot)), **weights(at), **masks(at)}
        outs = {"send": trio_of(p, F32)}
        if after is not None:
            ins["after"] = (after, pl.BlockSpec(memory_space=pl.ANY))
        if received is not None:
            ins["received"] = (received, trio)
            outs = {"own": trio_of(p, F32), "send": trio_of(p, BF16)}
        return call(
            partial_kernel, "partials", scalars, (split[p],), ins, outs, cost=cost(p, 3, 3)
        )

    def activate(own, others, after):
        ins = {"own": (own, whole(own)), "after": (after, pl.BlockSpec(memory_space=pl.ANY))}
        ins.update({f"other{k}": (a, whole(a)) for k, a in enumerate(others)})
        shape = jax.ShapeDtypeStruct(own.shape, BF16)
        return call(act_kernel, "activate", scalars, (1,), ins, {"act": (shape, whole(shape))})["act"]

    def back(which, p, act, do_rows, do_grads, state, last=False):
        at = place(which, p)
        ins = {"act": (act, trio), **masks(at)}
        outs, aliases, scratch = {}, {}, {}
        if do_rows:
            ins.update(weights(at))
            sums = {
                "out": jax.ShapeDtypeStruct((rows, width), F32),
                "tok": jax.ShapeDtypeStruct((width, rows), F32),
            }
            for k, shape in sums.items():
                if "sum_" + k in state:
                    ins["sum_" + k] = (state["sum_" + k], whole(shape))
                scratch["acc_" + k] = pltpu.VMEM(shape.shape, F32)
            if last:
                n_out = n_grid if direct else 1
                shape = jax.ShapeDtypeStruct((2, rows // n_out, width), BF16 if direct else F32)
                outs.update({f"rows{k}": (shape, whole(shape)) for k in range(n_out)})
            else:
                outs.update({"new_" + k: (shape, whole(shape)) for k, shape in sums.items()})
        if do_grads:
            ins.update(tok_t=(tok_t, whole(tok_t)), cot=(cot, whole(cot)))
            by_cols = jax.ShapeDtypeStruct((width, units), F32)
            by_rows = jax.ShapeDtypeStruct((units, width), F32)
            outs["gg"] = (by_cols, cols(at, width))
            outs["gu"] = (by_cols, cols(at, width))
            outs["gd"] = (by_rows, downs(at))
            for k in ("gg", "gu", "gd"):
                if k in state:
                    ins["old_" + k] = (state[k], pl.BlockSpec(memory_space=pl.ANY))
                    aliases["old_" + k] = k
            if "rows0" in state:
                ins["after"] = (state["rows0"], pl.BlockSpec(memory_space=pl.ANY))
        got = call(
            functools.partial(back_kernel, do_rows, do_grads, split[p]),
            "_".join(["back"] + ["rows"] * do_rows + ["grads"] * do_grads),
            scalars,
            (split[p],),
            ins,
            outs,
            scratch=scratch,
            aliases=aliases,
            cost=cost(p, 3 * do_rows + 3 * do_grads, 3 * do_rows + 6 * do_grads),
        )
        renamed = {k.replace("new_", "sum_"): v for k, v in got.items()}
        return {**state, **renamed}

    n = len(split)
    sent, sums, theirs, after = [], [], [], None
    for p in range(n + 1):
        if p < n:
            after = partials(1, p, after)["send"]
            sent.append(swap(after))
        if p > 0:
            got = partials(0, p - 1, after, sent[p - 1])
            after = got["own"]
            sums.append(after)
            theirs.append(across(got["send"]))

    state = {}
    for p in range(n):
        last = p == n - 1
        act = activate(sums[p], theirs[p], state.get("sum_out", after))
        act_other = swap(act)
        state = back(0, p, act, True, not last, state)
        state = back(1, p, act_other, True, not last, state, last)
        if last:
            state = back(0, p, act, False, True, state)
            state = back(1, p, act_other, False, True, state)

    if direct:
        both = state["rows0"].astype(F32)
        for s in range(1, n_grid):
            both += trade(state[f"rows{s}"], s).astype(F32)
    else:
        both = lax.psum_scatter(state["rows0"], "grid", scatter_dimension=1, tiled=True)
    both = both.astype(BF16)
    return (both[0], both[1], state["gg"], state["gu"], state["gd"])


def solution(mesh):
    in_specs = (
        P(("groups", "grid"), "dp"),
        P("dp", "grid"),
        P("dp", "grid"),
        P("grid", "dp"),
        P(("groups", "dp"), "grid"),
        P(("groups", "dp"), "grid"),
        P(("groups", "grid"), "dp"),
        P(("groups", "grid"), "dp"),
    )
    out_specs = (
        P(("groups", "grid"), "dp"),
        P(("groups", "grid"), "dp"),
        P(("groups", "dp"), "grid"),
        P(("groups", "dp"), "grid"),
        P(("groups", "grid"), "dp"),
    )
    sizes = (mesh.shape["grid"], mesh.shape["dp"])
    return jax.shard_map(
        functools.partial(shards, sizes),
        mesh=mesh,
        in_specs=in_specs,
        out_specs=out_specs,
        check_vma=False,
    )
```

time: 284 us -> 97 us (0.34)
  Pallas kernels: 0 us -> 73.7 us
  waiting for transfers between devices: 69.8 us -> 2.85 us
  local copies, waits for them, and re-layouts: 57.8 us -> 1.07 us
  matrix products: 56.2 us -> 0 us
  other arithmetic: 55.9 us -> 2.97 us
  blocking collectives: 29 us -> 0 us
  starting transfers between devices: 0.3 us -> 14.9 us
  between operations: 13.8 us -> 0.79 us
    pallas_call x0 -> x18, Pallas kernels: none -> 73.7 us  [call(): pl.pallas_call(body, out_shape=[shape for shape, _ in outs.values()], gri...]
    psum x1 -> x0, waiting for transfers between devices: 69.7 us -> none  [shards(): summed = lax.psum(partial_value, 'dp')]
    dot_general x6 -> x0, matrix products: 56.2 us -> none  [the longest x2 23 us: contract_rows(): lax.dot_general(left, right, (((0,), (0,)), ((), ())), preferred_element_...]
    mul x2 -> x0, other arithmetic: 48.3 us -> none  [blocked(): shaped * mask.astype(weight.dtype)[:, None, :, None]]
    unnamed x4 -> x0, local copies, waits for them, and re-layouts: 38.3 us -> none
    all_gather x2 -> x0, blocking collectives: 29 us -> none  [the longest x1 15.3 us: shards(): whole_tokens = lax.all_gather(tokens, 'grid', axis=0, tiled=True)]
    mul x6 -> x0, local copies, waits for them, and re-layouts: 19.2 us -> none  [blocked(): shaped * mask.astype(weight.dtype)[:, None, :, None]]
    ppermute x0 -> x15, starting transfers between devices: none -> 14.9 us  [the longest x6 10.2 us: trade(): return lax.ppermute(array, 'grid', [(i, i ^ s) for i in range(n_grid)])]
  transfers between devices with their start and end apart: 3 -> 15, of which waited for: 1 -> 2; matrix products, arithmetic and copies ran while one was open for 42% -> 3% of each run, Pallas kernels for 0% -> 66%
where the time goes in v2:
time: 97 us; the launch traced here: 96.3 us
  Pallas kernels  73.7 us (76%)
  starting transfers between devices  14.9 us (15%)
  other arithmetic  2.97 us (3%)
  waiting for transfers between devices  2.85 us (3%)
  local copies, waits for them, and re-layouts  1.07 us (1%)
    pallas_call x18, Pallas kernels, call(): pl.pallas_call(body, out_shape=[shape for shape, _ in outs.values()], gri...  73.7 us
    ppermute x6, starting transfers between devices, trade(): return lax.ppermute(array, 'grid', [(i, i ^ s) for i in range(n_grid)])  10.2 us
    ppermute x3, starting transfers between devices, across(): lax.ppermute(array, 'dp', [(i, (i // 2 + s) % pairs * 2 + i % 2) for i in...  3.59 us
    ppermute x6, waiting for transfers between devices, trade(): return lax.ppermute(array, 'grid', [(i, i ^ s) for i in range(n_grid)])  2.47 us
  transfers between devices with their start and end apart: 15, of which 2 were waited for; matrix products, arithmetic and copies ran while one was open for 3% of the time, Pallas kernels for 66%

profile of v2, /device:TPU:0, one launch (start us, length us, event | category | flops | bytes accessed | tf_op | source)
XLA Modules:
  0.0 96.3 jit_solution(16978759270200596660)
XLA Ops:
  0.6 0.8 pad_maximum_fusion.refs_0_
  1.4 5.1 %collective-permute-start.2 = (bf16[2,16,1024]{2,1,0:T(8,128)(2,1)S(1)}, bf16[2,16,1024]{2,1,0:T(8,128)(2,1)S(1)}, u32[]{:S(2)}, u32[]{:S(2)}) collective-permute-start(bf16[2,16,1024]{2,1,0:T(8,128)(2,1)S(1)} %pad_maximum_fusion.refs_0_), channel_id=1, source_target_pairs={{0,12},{4,8},{8,4},{12,0},{1,13},{5,9},{9,5},{13,1},{2,14},{6,10},... | collective-permute-start | bytes 196616 | tf_op jit(solution)/shard_map/ppermute | solution.py:160
  6.5 0.0 collective-permute-start.1
  6.5 0.6 collective-permute-start
  7.2 0.7 convert_element_type.24
  7.8 0.7 convert_element_type.25
  8.5 0.7 convert_element_type.26
  9.2 0.1 copy.30
  9.3 0.1 copy.29
  9.4 0.1 copy.28
  9.5 0.1 broadcast_bitcast_fusion
  9.6 0.1 pad_add_fusion._
  9.7 0.0 collective-permute-done.2.refs_3_
  9.7 2.5 %collective-permute-done.1.refs_2_ = bf16[2,16,1024]{2,1,0:T(8,128)(2,1)S(1)} collective-permute-done((bf16[2,16,1024]{2,1,0:T(8,128)(2,1)S(1)}, bf16[2,16,1024]{2,1,0:T(8,128)(2,1)S(1)}, u32[]{:S(2)}, u32[]{:S(2)}) %collective-permute-start.1) | collective-permute-done | bytes 65568 | tf_op jit(solution)/shard_map/ppermute | solution.py:160
  12.1 0.0 collective-permute-done.refs_1_
  12.1 0.7 assemble.1
  12.8 0.1 broadcast_in_dim.11
  12.9 4.4 %partials.6.refs_8_ = f32[3,64,768]{2,1,0:T(8,128)S(1)} custom-call(s32[2]{0:T(128)S(1)} %pad_add_fusion._, bf16[64,1024]{1,0:T(8,128)(2,1)S(1)} %get-tuple-element.46.refs_0_, bf16[64,1024]{1,0:T(8,128)(2,1)S(1)} %get-tuple-element.47.refs_1_.refs_8_.refs_10_.refs_5_, bf16[1024,4096]{1,0:T(8,128)(2,1)} %refs_4_.23, bf16[1024,4096]{1,0:T(8,128)(2,1)} %refs_5_.11, ...), custom_call_target="tpu_custom_call" | custom-call | flops 301989888 | bytes 4718592 | tf_op jit(solution)/shard_map/partials/pallas_call | solution.py:40
  17.3 0.1 collective-permute-start.3
  17.4 4.4 %partials.7.refs_8_ = f32[3,64,768]{2,1,0:T(8,128)S(1)} custom-call(s32[2]{0:T(128)S(1)} %pad_add_fusion._, bf16[64,1024]{1,0:T(8,128)(2,1)S(1)} %get-tuple-element.46.refs_0_, bf16[64,1024]{1,0:T(8,128)(2,1)S(1)} %get-tuple-element.47.refs_1_.refs_8_.refs_10_.refs_5_, bf16[1024,4096]{1,0:T(8,128)(2,1)} %refs_4_.23, bf16[1024,4096]{1,0:T(8,128)(2,1)} %refs_5_.11, ...), custom_call_target="tpu_custom_call" | custom-call | flops 301989888 | bytes 4718592 | tf_op jit(solution)/shard_map/partials/pallas_call | solution.py:40
  21.8 0.6 collective-permute-start.4
  22.4 0.0 collective-permute-done.3.refs_9_
  22.4 4.4 %partials.8 = (f32[3,64,768]{2,1,0:T(8,128)S(1)}, bf16[3,64,768]{2,1,0:T(8,128)(2,1)S(1)}) custom-call(s32[2]{0:T(128)S(1)} %pad_add_fusion._, bf16[64,1024]{1,0:T(8,128)(2,1)S(1)} %get-tuple-element.46.refs_0_, bf16[64,1024]{1,0:T(8,128)(2,1)S(1)} %get-tuple-element.47.refs_1_.refs_8_.refs_10_.refs_5_, bf16[1024,4096]{1,0:T(8,128)(2,1)} %refs_4_.23, ...), custom_call_target="tpu_custom_call" | custom-call | flops 301989888 | bytes 4718592 | tf_op jit(solution)/shard_map/partials/pallas_call | solution.py:40
  26.8 3.1 %partials.9.refs_8_ = f32[3,64,512]{2,1,0:T(8,128)S(1)} custom-call(s32[2]{0:T(128)S(1)} %pad_add_fusion._, bf16[64,1024]{1,0:T(8,128)(2,1)S(1)} %get-tuple-element.46.refs_0_, bf16[64,1024]{1,0:T(8,128)(2,1)S(1)} %get-tuple-element.47.refs_1_.refs_8_.refs_10_.refs_5_, bf16[1024,4096]{1,0:T(8,128)(2,1)} %refs_4_.23, bf16[1024,4096]{1,0:T(8,128)(2,1)} %refs_5_.11, ...), custom_call_target="tpu_custom_call" | custom-call | flops 201326592 | bytes 3145728 | tf_op jit(solution)/shard_map/partials/pallas_call | solution.py:40
  29.9 0.1 collective-permute-start.5
  30.0 1.5 %collective-permute-start.6 = (bf16[3,64,768]{2,1,0:T(8,128)(2,1)S(1)}, bf16[3,64,768]{2,1,0:T(8,128)(2,1)S(1)}, u32[]{:S(2)}, u32[]{:S(2)}) collective-permute-start(bf16[3,64,768]{2,1,0:T(8,128)(2,1)S(1)} %get-tuple-element.51), channel_id=1, source_target_pairs={{0,2},{1,3},{2,0},{3,1},{4,6},{5,7},{6,4},{7,5},{8,10},{9,11},{10,... | collective-permute-start | bytes 884744 | tf_op jit(solution)/shard_map/ppermute | solution.py:167
  31.5 0.0 collective-permute-done.4.refs_9_
  31.5 4.4 %partials.10 = (f32[3,64,768]{2,1,0:T(8,128)S(1)}, bf16[3,64,768]{2,1,0:T(8,128)(2,1)S(1)}) custom-call(s32[2]{0:T(128)S(1)} %pad_add_fusion._, bf16[64,1024]{1,0:T(8,128)(2,1)S(1)} %get-tuple-element.46.refs_0_, bf16[64,1024]{1,0:T(8,128)(2,1)S(1)} %get-tuple-element.47.refs_1_.refs_8_.refs_10_.refs_5_, bf16[1024,4096]{1,0:T(8,128)(2,1)} %refs_4_.23, ...), custom_call_target="tpu_custom_call" | custom-call | flops 301989888 | bytes 4718592 | tf_op jit(solution)/shard_map/partials/pallas_call | solution.py:40
  35.9 0.0 collective-permute-done.5.refs_9_
  36.0 3.1 %partials.11 = (f32[3,64,512]{2,1,0:T(8,128)S(1)}, bf16[3,64,512]{2,1,0:T(8,128)(2,1)S(1)}) custom-call(s32[2]{0:T(128)S(1)} %pad_add_fusion._, bf16[64,1024]{1,0:T(8,128)(2,1)S(1)} %get-tuple-element.46.refs_0_, bf16[64,1024]{1,0:T(8,128)(2,1)S(1)} %get-tuple-element.47.refs_1_.refs_8_.refs_10_.refs_5_, bf16[1024,4096]{1,0:T(8,128)(2,1)} %refs_4_.23, ...), custom_call_target="tpu_custom_call" | custom-call | flops 201326592 | bytes 3145728 | tf_op jit(solution)/shard_map/partials/pallas_call | solution.py:40
  39.0 0.4 collective-permute-done.6.refs_2_
  39.4 0.7 activate.3.refs_0_
  40.1 0.1 collective-permute-start.7
  40.2 1.5 %collective-permute-start.8 = (bf16[3,64,768]{2,1,0:T(8,128)(2,1)S(1)}, bf16[3,64,768]{2,1,0:T(8,128)(2,1)S(1)}, u32[]{:S(2)}, u32[]{:S(2)}) collective-permute-start(bf16[3,64,768]{2,1,0:T(8,128)(2,1)S(1)} %get-tuple-element.59), channel_id=1, source_target_pairs={{0,2},{1,3},{2,0},{3,1},{4,6},{5,7},{6,4},{7,5},{8,10},{9,11},{10,... | collective-permute-start | bytes 884744 | tf_op jit(solution)/shard_map/ppermute | solution.py:167
  41.7 8.4 %back_rows_grads.4 = (f32[64,1024]{1,0:T(8,128)S(1)}, f32[1024,64]{1,0:T(8,128)S(1)}, f32[1024,4096]{1,0:T(8,128)}, f32[1024,4096]{1,0:T(8,128)}, f32[4096,1024]{1,0:T(8,128)}) custom-call(s32[2]{0:T(128)S(1)} %pad_add_fusion._, bf16[3,64,768]{2,1,0:T(8,128)(2,1)S(1)} %activate.3.refs_0_, f32[8,4096]{1,0:T(8,128)S(1)} %get-tuple-element.90.refs_5_.refs_1_, ...), custom_call_target="tpu_custom_call" | custom-call | flops 603979776 | bytes 14155776 | tf_op jit(solution)/shard_map/back_rows_grads/pallas_call | solution.py:40
  50.1 0.0 collective-permute-done.7.refs_0_
  50.1 8.4 %back_rows_grads.5 = (f32[64,1024]{1,0:T(8,128)S(1)}, f32[1024,64]{1,0:T(8,128)S(1)}, f32[1024,4096]{1,0:T(8,128)}, f32[1024,4096]{1,0:T(8,128)}, f32[4096,1024]{1,0:T(8,128)}) custom-call(s32[2]{0:T(128)S(1)} %pad_add_fusion._, ...), custom_call_target="tpu_custom_call", output_to_operand_aliasing={{2}: (12, {}), {3}: (13, {}), {4}: (14, {})} | custom-call | flops 603979776 | bytes 14155776 | tf_op jit(solution)/shard_map/back_rows_grads/pallas_call | solution.py:40
  58.4 0.0 collective-permute-done.8.refs_2_
  58.4 0.7 activate.4.refs_0_
  59.1 0.2 collective-permute-start.9
  59.4 0.6 collective-permute-start.10
  59.9 8.4 %back_rows_grads.6 = (f32[64,1024]{1,0:T(8,128)S(1)}, f32[1024,64]{1,0:T(8,128)S(1)}, f32[1024,4096]{1,0:T(8,128)}, f32[1024,4096]{1,0:T(8,128)}, f32[4096,1024]{1,0:T(8,128)}) custom-call(s32[2]{0:T(128)S(1)} %pad_add_fusion._, bf16[3,64,768]{2,1,0:T(8,128)(2,1)S(1)} %activate.4.refs_0_, ...), custom_call_target="tpu_custom_call", output_to_operand_aliasing={{2}: (12, {}), {3}: (13, {}), {4}: (14, {})} | custom-call | flops 603979776 | bytes 14155776 | tf_op jit(solution)/shard_map/back_rows_grads/pallas_call | solution.py:40
  68.3 0.0 collective-permute-done.9.refs_0_
  68.3 8.4 %back_rows_grads.7 = (f32[64,1024]{1,0:T(8,128)S(1)}, f32[1024,64]{1,0:T(8,128)S(1)}, f32[1024,4096]{1,0:T(8,128)}, f32[1024,4096]{1,0:T(8,128)}, f32[4096,1024]{1,0:T(8,128)}) custom-call(s32[2]{0:T(128)S(1)} %pad_add_fusion._, ...), custom_call_target="tpu_custom_call", output_to_operand_aliasing={{2}: (12, {}), {3}: (13, {}), {4}: (14, {})} | custom-call | flops 603979776 | bytes 14155776 | tf_op jit(solution)/shard_map/back_rows_grads/pallas_call | solution.py:40
  76.7 0.0 collective-permute-done.10.refs_2_
  76.7 0.6 activate.5.refs_0_
  77.3 0.1 collective-permute-start.11
  77.4 3.1 %back_rows.2 = (f32[64,1024]{1,0:T(8,128)S(1)}, f32[1024,64]{1,0:T(8,128)S(1)}) custom-call(s32[2]{0:T(128)S(1)} %pad_add_fusion._, bf16[3,64,512]{2,1,0:T(8,128)(2,1)S(1)} %activate.5.refs_0_, f32[8,4096]{1,0:T(8,128)S(1)} %get-tuple-element.90.refs_5_.refs_1_, f32[8,4096]{1,0:T(8,128)S(1)} %get-tuple-element.89.refs_6_.refs_2_, ...), custom_call_target="tpu_custom_call" | custom-call | flops 201326592 | bytes 3145728 | tf_op jit(solution)/shard_map/back_rows/pallas_call | solution.py:40
  80.6 0.0 collective-permute-done.11.refs_0_
  80.6 3.2 %back_rows.3 = (bf16[2,16,1024]{2,1,0:T(8,128)(2,1)S(1)}, bf16[2,16,1024]{2,1,0:T(8,128)(2,1)S(1)}, bf16[2,16,1024]{2,1,0:T(8,128)(2,1)S(1)}, bf16[2,16,1024]{2,1,0:T(8,128)(2,1)S(1)}) custom-call(s32[2]{0:T(128)S(1)} %pad_add_fusion._, bf16[3,64,512]{2,1,0:T(8,128)(2,1)S(1)} %collective-permute-done.11.refs_0_, ...), custom_call_target="tpu_custom_call" | custom-call | flops 201326592 | bytes 3145728 | tf_op jit(solution)/shard_map/back_rows/pallas_call | solution.py:40
  83.8 1.1 %collective-permute-start.12 = (bf16[2,16,1024]{2,1,0:T(8,128)(2,1)S(1)}, bf16[2,16,1024]{2,1,0:T(8,128)(2,1)S(1)}, u32[]{:S(2)}, u32[]{:S(2)}) collective-permute-start(bf16[2,16,1024]{2,1,0:T(8,128)(2,1)S(1)} %get-tuple-element.75), channel_id=1, source_target_pairs={{0,4},{4,0},{8,12},{12,8},{1,5},{5,1},{9,13},{13,9},{2,6},{6,2},{1... | collective-permute-start | bytes 196616 | tf_op jit(solution)/shard_map/ppermute | solution.py:160
  85.0 2.2 %collective-permute-start.13 = (bf16[2,16,1024]{2,1,0:T(8,128)(2,1)S(1)}, bf16[2,16,1024]{2,1,0:T(8,128)(2,1)S(1)}, u32[]{:S(2)}, u32[]{:S(2)}) collective-permute-start(bf16[2,16,1024]{2,1,0:T(8,128)(2,1)S(1)} %get-tuple-element.76), channel_id=1, source_target_pairs={{0,8},{4,12},{8,0},{12,4},{1,9},{5,13},{9,1},{13,5},{2,10},{6,14},... | collective-permute-start | bytes 196616 | tf_op jit(solution)/shard_map/ppermute | solution.py:160
  87.2 1.1 %collective-permute-start.14 = (bf16[2,16,1024]{2,1,0:T(8,128)(2,1)S(1)}, bf16[2,16,1024]{2,1,0:T(8,128)(2,1)S(1)}, u32[]{:S(2)}, u32[]{:S(2)}) collective-permute-start(bf16[2,16,1024]{2,1,0:T(8,128)(2,1)S(1)} %get-tuple-element.77), channel_id=1, source_target_pairs={{0,12},{4,8},{8,4},{12,0},{1,13},{5,9},{9,5},{13,1},{2,14},{6,10},... | collective-permute-start | bytes 196616 | tf_op jit(solution)/shard_map/ppermute | solution.py:160
  88.3 3.7 %back_grads.2 = (f32[1024,4096]{1,0:T(8,128)}, f32[1024,4096]{1,0:T(8,128)}, f32[4096,1024]{1,0:T(8,128)}) custom-call(s32[2]{0:T(128)S(1)} %pad_add_fusion._, bf16[3,64,512]{2,1,0:T(8,128)(2,1)S(1)} %activate.5.refs_0_, f32[8,4096]{1,0:T(8,128)S(1)} %get-tuple-element.90.refs_5_.refs_1_, ...), custom_call_target="tpu_custom_call", output_to_operand_aliasing={{0}: (7, {}), {1}: (8, {}), {2}: (9, {})} | custom-call | flops 201326592 | bytes 6291456 | tf_op jit(solution)/shard_map/back_grads/pallas_call | solution.py:40
  92.0 3.7 %back_grads.3 = (f32[1024,4096]{1,0:T(8,128)}, f32[1024,4096]{1,0:T(8,128)}, f32[4096,1024]{1,0:T(8,128)}) custom-call(s32[2]{0:T(128)S(1)} %pad_add_fusion._, bf16[3,64,512]{2,1,0:T(8,128)(2,1)S(1)} %collective-permute-done.11.refs_0_, f32[8,4096]{1,0:T(8,128)S(1)} %get-tuple-element.90.refs_5_.refs_1_, ...), custom_call_target="tpu_custom_call", output_to_operand_aliasing={{0}: (7, {}), {1}: (8, {}), {2}: (9, {})} | custom-call | flops 201326592 | bytes 6291456 | tf_op jit(solution)/shard_map/back_grads/pallas_call | solution.py:40
  95.6 0.0 collective-permute-done.12
  95.6 0.0 collective-permute-done.13
  95.6 0.0 collective-permute-done.14
  95.7 0.6 slice_bitcast_fusion
  (1 shorter events, 0.0 us)
Async XLA Ops:
  1.4 8.3 %collective-permute-start.2 = (bf16[2,16,1024]{2,1,0:T(8,128)(2,1)S(1)}, bf16[2,16,1024]{2,1,0:T(8,128)(2,1)S(1)}, u32[]{:S(2)}, u32[]{:S(2)}) collective-permute-start(bf16[2,16,1024]{2,1,0:T(8,128)(2,1)S(1)} %pad_maximum_fusion.refs_0_), channel_id=1, source_target_pairs={{0,12},{4,8},{8,4},{12,0},{1,13},{5,9},{9,5},{13,1},{2,14},{6,10},... | collective-permute-start | bytes 196616 | tf_op jit(solution)/shard_map/ppermute | solution.py:160
  6.5 5.6 %collective-permute-start.1 = (bf16[2,16,1024]{2,1,0:T(8,128)(2,1)S(1)}, bf16[2,16,1024]{2,1,0:T(8,128)(2,1)S(1)}, u32[]{:S(2)}, u32[]{:S(2)}) collective-permute-start(bf16[2,16,1024]{2,1,0:T(8,128)(2,1)S(1)} %pad_maximum_fusion.refs_0_), channel_id=1, source_target_pairs={{0,8},{4,12},{8,0},{12,4},{1,9},{5,13},{9,1},{13,5},{2,10},{6,14},... | collective-permute-start | bytes 196616 | tf_op jit(solution)/shard_map/ppermute | solution.py:160
  6.5 5.6 %collective-permute-start = (bf16[2,16,1024]{2,1,0:T(8,128)(2,1)S(1)}, bf16[2,16,1024]{2,1,0:T(8,128)(2,1)S(1)}, u32[]{:S(2)}, u32[]{:S(2)}) collective-permute-start(bf16[2,16,1024]{2,1,0:T(8,128)(2,1)S(1)} %pad_maximum_fusion.refs_0_), channel_id=1, source_target_pairs={{0,4},{4,0},{8,12},{12,8},{1,5},{5,1},{9,13},{13,9},{2,6},{6,2},{1... | collective-permute-start | bytes 196616 | tf_op jit(solution)/shard_map/ppermute | solution.py:160
  17.3 5.1 %collective-permute-start.3 = (f32[3,64,768]{2,1,0:T(8,128)S(1)}, f32[3,64,768]{2,1,0:T(8,128)S(1)}, u32[]{:S(2)}, u32[]{:S(2)}) collective-permute-start(f32[3,64,768]{2,1,0:T(8,128)S(1)} %partials.6.refs_8_), channel_id=1, source_target_pairs={{0,1},{1,0},{2,3},{3,2},{4,5},{5,4},{6,7},{7,6},{8,9},{9,8},{10,11... | collective-permute-start | bytes 1769480 | tf_op jit(solution)/shard_map/ppermute | solution.py:163
  21.8 9.7 %collective-permute-start.4 = (f32[3,64,768]{2,1,0:T(8,128)S(1)}, f32[3,64,768]{2,1,0:T(8,128)S(1)}, u32[]{:S(2)}, u32[]{:S(2)}) collective-permute-start(f32[3,64,768]{2,1,0:T(8,128)S(1)} %partials.7.refs_8_), channel_id=1, source_target_pairs={{0,1},{1,0},{2,3},{3,2},{4,5},{5,4},{6,7},{7,6},{8,9},{9,8},{10,11... | collective-permute-start | bytes 1769480 | tf_op jit(solution)/shard_map/ppermute | solution.py:163
  29.9 6.0 %collective-permute-start.5 = (f32[3,64,512]{2,1,0:T(8,128)S(1)}, f32[3,64,512]{2,1,0:T(8,128)S(1)}, u32[]{:S(2)}, u32[]{:S(2)}) collective-permute-start(f32[3,64,512]{2,1,0:T(8,128)S(1)} %partials.9.refs_8_), channel_id=1, source_target_pairs={{0,1},{1,0},{2,3},{3,2},{4,5},{5,4},{6,7},{7,6},{8,9},{9,8},{10,11... | collective-permute-start | bytes 1179656 | tf_op jit(solution)/shard_map/ppermute | solution.py:163
  30.0 9.4 %collective-permute-start.6 = (bf16[3,64,768]{2,1,0:T(8,128)(2,1)S(1)}, bf16[3,64,768]{2,1,0:T(8,128)(2,1)S(1)}, u32[]{:S(2)}, u32[]{:S(2)}) collective-permute-start(bf16[3,64,768]{2,1,0:T(8,128)(2,1)S(1)} %get-tuple-element.51), channel_id=1, source_target_pairs={{0,2},{1,3},{2,0},{3,1},{4,6},{5,7},{6,4},{7,5},{8,10},{9,11},{10,... | collective-permute-start | bytes 884744 | tf_op jit(solution)/shard_map/ppermute | solution.py:167
  40.1 10.0 %collective-permute-start.7 = (bf16[3,64,768]{2,1,0:T(8,128)(2,1)S(1)}, bf16[3,64,768]{2,1,0:T(8,128)(2,1)S(1)}, u32[]{:S(2)}, u32[]{:S(2)}) collective-permute-start(bf16[3,64,768]{2,1,0:T(8,128)(2,1)S(1)} %activate.3.refs_0_), channel_id=1, source_target_pairs={{0,1},{1,0},{2,3},{3,2},{4,5},{5,4},{6,7},{7,6},{8,9},{9,8},{10,11... | collective-permute-start | bytes 884744 | tf_op jit(solution)/shard_map/ppermute | solution.py:163
  40.2 18.3 %collective-permute-start.8 = (bf16[3,64,768]{2,1,0:T(8,128)(2,1)S(1)}, bf16[3,64,768]{2,1,0:T(8,128)(2,1)S(1)}, u32[]{:S(2)}, u32[]{:S(2)}) collective-permute-start(bf16[3,64,768]{2,1,0:T(8,128)(2,1)S(1)} %get-tuple-element.59), channel_id=1, source_target_pairs={{0,2},{1,3},{2,0},{3,1},{4,6},{5,7},{6,4},{7,5},{8,10},{9,11},{10,... | collective-permute-start | bytes 884744 | tf_op jit(solution)/shard_map/ppermute | solution.py:167
  59.1 9.2 %collective-permute-start.9 = (bf16[3,64,768]{2,1,0:T(8,128)(2,1)S(1)}, bf16[3,64,768]{2,1,0:T(8,128)(2,1)S(1)}, u32[]{:S(2)}, u32[]{:S(2)}) collective-permute-start(bf16[3,64,768]{2,1,0:T(8,128)(2,1)S(1)} %activate.4.refs_0_), channel_id=1, source_target_pairs={{0,1},{1,0},{2,3},{3,2},{4,5},{5,4},{6,7},{7,6},{8,9},{9,8},{10,11... | collective-permute-start | bytes 884744 | tf_op jit(solution)/shard_map/ppermute | solution.py:163
  59.4 17.3 %collective-permute-start.10 = (bf16[3,64,512]{2,1,0:T(8,128)(2,1)S(1)}, bf16[3,64,512]{2,1,0:T(8,128)(2,1)S(1)}, u32[]{:S(2)}, u32[]{:S(2)}) collective-permute-start(bf16[3,64,512]{2,1,0:T(8,128)(2,1)S(1)} %get-tuple-element.70), channel_id=1, source_target_pairs={{0,2},{1,3},{2,0},{3,1},{4,6},{5,7},{6,4},{7,5},{8,10},{9,11},{10,... | collective-permute-start | bytes 589832 | tf_op jit(solution)/shard_map/ppermute | solution.py:167
  77.3 3.3 %collective-permute-start.11 = (bf16[3,64,512]{2,1,0:T(8,128)(2,1)S(1)}, bf16[3,64,512]{2,1,0:T(8,128)(2,1)S(1)}, u32[]{:S(2)}, u32[]{:S(2)}) collective-permute-start(bf16[3,64,512]{2,1,0:T(8,128)(2,1)S(1)} %activate.5.refs_0_), channel_id=1, source_target_pairs={{0,1},{1,0},{2,3},{3,2},{4,5},{5,4},{6,7},{7,6},{8,9},{9,8},{10,11... | collective-permute-start | bytes 589832 | tf_op jit(solution)/shard_map/ppermute | solution.py:163
  83.8 11.8 %collective-permute-start.12 = (bf16[2,16,1024]{2,1,0:T(8,128)(2,1)S(1)}, bf16[2,16,1024]{2,1,0:T(8,128)(2,1)S(1)}, u32[]{:S(2)}, u32[]{:S(2)}) collective-permute-start(bf16[2,16,1024]{2,1,0:T(8,128)(2,1)S(1)} %get-tuple-element.75), channel_id=1, source_target_pairs={{0,4},{4,0},{8,12},{12,8},{1,5},{5,1},{9,13},{13,9},{2,6},{6,2},{1... | collective-permute-start | bytes 196616 | tf_op jit(solution)/shard_map/ppermute | solution.py:160
  85.0 10.7 %collective-permute-start.13 = (bf16[2,16,1024]{2,1,0:T(8,128)(2,1)S(1)}, bf16[2,16,1024]{2,1,0:T(8,128)(2,1)S(1)}, u32[]{:S(2)}, u32[]{:S(2)}) collective-permute-start(bf16[2,16,1024]{2,1,0:T(8,128)(2,1)S(1)} %get-tuple-element.76), channel_id=1, source_target_pairs={{0,8},{4,12},{8,0},{12,4},{1,9},{5,13},{9,1},{13,5},{2,10},{6,14},... | collective-permute-start | bytes 196616 | tf_op jit(solution)/shard_map/ppermute | solution.py:160
  87.2 8.5 %collective-permute-start.14 = (bf16[2,16,1024]{2,1,0:T(8,128)(2,1)S(1)}, bf16[2,16,1024]{2,1,0:T(8,128)(2,1)S(1)}, u32[]{:S(2)}, u32[]{:S(2)}) collective-permute-start(bf16[2,16,1024]{2,1,0:T(8,128)(2,1)S(1)} %get-tuple-element.77), channel_id=1, source_target_pairs={{0,12},{4,8},{8,4},{12,0},{1,13},{5,9},{9,5},{13,1},{2,14},{6,10},... | collective-permute-start | bytes 196616 | tf_op jit(solution)/shard_map/ppermute | solution.py:160

commit v3 on v2

v3 whole, which is shorter than its diff:
```python
import functools
import types

import jax
import jax.numpy as jnp
from jax import lax
from jax.experimental import pallas as pl
from jax.experimental.pallas import tpu as pltpu
from jax.sharding import PartitionSpec as P

BLK = 128
PIECES = [3, 3, 2]
MIB = 1024 * 1024
F32 = jnp.float32
BF16 = jnp.bfloat16


def dot(left, right, dims=(1, 0)):
    return lax.dot_general(
        left, right, (((dims[0],), (dims[1],)), ((), ())), preferred_element_type=F32
    )


def pinned(array):
    spec = pl.BlockSpec(memory_space=pltpu.VMEM)
    if isinstance(array, jax.ShapeDtypeStruct):
        return (pltpu.VMEM(array.shape, array.dtype), spec)
    return (pltpu.with_memory_space_constraint(array, pltpu.VMEM), spec)


def call(kernel, name, scalars, grid, ins, outs, scratch=None, aliases=None, cost=None):
    scratch = scratch or {}
    names = ["place", *ins, *outs, *scratch]
    in_names, out_names = list(ins), list(outs)

    def body(*refs):
        kernel(types.SimpleNamespace(**dict(zip(names, refs))))

    results = pl.pallas_call(
        body,
        out_shape=[shape for shape, _ in outs.values()],
        grid_spec=pltpu.PrefetchScalarGridSpec(
            num_scalar_prefetch=1,
            grid=grid,
            in_specs=[spec for _, spec in ins.values()],
            out_specs=[spec for _, spec in outs.values()],
            scratch_shapes=list(scratch.values()),
        ),
        input_output_aliases={
            1 + in_names.index(i): out_names.index(o) for i, o in (aliases or {}).items()
        },
        compiler_params=pltpu.CompilerParams(vmem_limit_bytes=11 * MIB),
        cost_estimate=cost,
        name=name,
    )(scalars, *[array for array, _ in ins.values()])
    return dict(zip(out_names, results))


def hbm(array):
    return pltpu.with_memory_space_constraint(array, pltpu.HBM)


def whole(array):
    return pl.BlockSpec(array.shape, lambda *_: (0,) * len(array.shape))


def assemble_kernel(r):
    blocks = [ref for name, ref in vars(r).items() if name.startswith("block")]
    rows = blocks[0].shape[1]
    for k, block in enumerate(blocks):
        r.tok[k * rows : (k + 1) * rows, :] = block[0]
        r.cot[k * rows : (k + 1) * rows, :] = block[1]
    r.tok_t[...] = r.tok[...].T


def mask_kernel(r):
    step = pl.program_id(0)

    @pl.when(step == 0)
    def _():
        for mask, out in ((r.mask_gate, r.mg), (r.mask_up, r.mu), (r.mask_down, r.md)):
            blocks, lanes = mask.shape[1], mask.shape[1] * BLK
            at = lax.broadcasted_iota(jnp.int32, (blocks, lanes), 0)
            column = lax.broadcasted_iota(jnp.int32, (blocks, lanes), 1)
            first = at * BLK
            spread = ((column >= first) & (column < first + BLK)).astype(F32).astype(BF16)
            wide = dot(mask[...].astype(F32).astype(BF16), spread)
            for b in range(mask.shape[0]):
                out[b] = wide[b : b + 1, :]

    for w, mask, out in ((r.w_gate, r.mg, r.wg), (r.w_up, r.mu, r.wu), (r.w_down, r.md, r.wd)):
        rows = w.shape[0]
        for b in range(rows // BLK):
            keep = mask[step * (rows // BLK) + b].astype(BF16)
            band = pl.ds(pl.multiple_of(step * rows + b * BLK, BLK), BLK)
            out[band, :] = w[b * BLK : (b + 1) * BLK, :] * keep


def tile_at(r, tile):
    return pl.ds(pl.multiple_of((r.place[0] + pl.program_id(0)) * tile, tile), tile)


def partial_kernel(r):
    at = tile_at(r, r.send.shape[2])
    gate = dot(r.tok[...], r.wg[:, at])
    up = dot(r.tok[...], r.wu[:, at])
    back = dot(r.cot[...], r.wd[at, :], (1, 1))
    for k, value in enumerate((gate, up, back)):
        if hasattr(r, "received"):
            value = value + r.received[k]
            r.own[k] = value
        r.send[k] = value.astype(r.send.dtype)


def act_kernel(r):
    others = [ref for name, ref in vars(r).items() if name.startswith("other")]
    gate, up, back = (
        sum((other[k].astype(F32) for other in others), r.own[k]) for k in range(3)
    )
    sigma = 1.0 / (1.0 + jnp.exp(-gate))
    silu = gate * sigma
    slope = sigma * (1.0 + gate * (1.0 - sigma))
    r.act[0] = (silu * up).astype(BF16)
    r.act[1] = (back * up * slope).astype(BF16)
    r.act[2] = (back * silu).astype(BF16)


def add_rows(r, tiles):
    step = pl.program_id(0)
    at = tile_at(r, r.act.shape[2])

    @pl.when(step == 0)
    def _():
        r.acc[...] = r.sums[...] if hasattr(r, "sums") else jnp.zeros_like(r.acc)

    r.acc[0] += dot(r.act[0], r.wd[at, :])
    r.acc[1] += dot(r.act[1], r.wg[:, at], (1, 1)) + dot(r.act[2], r.wu[:, at], (1, 1))

    @pl.when(step == tiles - 1)
    def _():
        if hasattr(r, "new_sums"):
            r.new_sums[...] = r.acc[...]
        else:
            outs = [ref for name, ref in vars(r).items() if name.startswith("rows")]
            rows = outs[0].shape[1]
            for k, out in enumerate(outs):
                out[...] = r.acc[:, k * rows : (k + 1) * rows, :].astype(out.dtype)


def weight_grads(r):
    tile = r.act.shape[2]
    at = tile_at(r, tile)
    for out, k, mask in ((r.gg, 1, r.mg), (r.gu, 2, r.mu)):
        value = dot(r.tok_t[...], r.act[k])
        for b in range(out.shape[0] // BLK):
            band = slice(b * BLK, (b + 1) * BLK)
            out[band, :] = value[band, :] * mask[b, :, at]
    value = dot(r.act[0].T, r.cot[...])
    for b in range(tile // BLK):
        band = slice(b * BLK, (b + 1) * BLK)
        row = (r.place[0] + pl.program_id(0)) * (tile // BLK) + b
        r.gd[band, :] = value[band, :] * r.md[row]


def back_kernel(do_rows, do_grads, tiles, r):
    if do_rows:
        add_rows(r, tiles)
    if do_grads:
        weight_grads(r)


def shards(sizes, tokens, w_gate, w_up, w_down, mask_gate, mask_up, mask_down, grad_out):
    n_grid, n_dp = sizes
    width, units = w_gate.shape
    pairs = n_dp // 2
    half = units // 2
    tile = 256 if half % 256 == 0 and half >= 1024 else BLK
    split = PIECES if sum(PIECES) * tile == half else [half // tile]
    starts = [sum(split[:p]) for p in range(len(split))]
    direct = n_grid == 4

    core = lax.axis_index("dp") % 2
    firsts = [
        jnp.stack([(half // tile) * h + start]).astype(jnp.int32)
        for h in (core, 1 - core)
        for start in starts
    ]
    place = lambda which, p: firsts[which * len(split) + p]
    none = jnp.zeros((1,), jnp.int32)

    def trade(array, s):
        return lax.ppermute(array, "grid", [(i, i ^ s) for i in range(n_grid)])

    def swap(array):
        return lax.ppermute(array, "dp", [(i, i ^ 1) for i in range(n_dp)])

    def across(array):
        return [
            lax.ppermute(
                array,
                "dp",
                [(i, ((i // 2 + s) % pairs) * 2 + i % 2) for i in range(n_dp)],
            )
            for s in range(1, pairs)
        ]

    block = jnp.stack([tokens, grad_out])
    if direct:
        blocks = [block] + [trade(block, s) for s in range(1, n_grid)]
    else:
        blocks = [lax.all_gather(block, "grid", axis=1, tiled=True)]
    rows = sum(b.shape[1] for b in blocks)
    row_shape = jax.ShapeDtypeStruct((rows, width), BF16)
    col_shape = jax.ShapeDtypeStruct((width, rows), BF16)
    bands = width // BLK
    by_cols = pl.BlockSpec((BLK, units), lambda i, _: (i, 0))
    by_rows = pl.BlockSpec((units // bands, width), lambda i, _: (i, 0))

    def spread(mask):
        return pinned(jax.ShapeDtypeStruct((mask.shape[0], 1, mask.shape[1] * BLK), F32))

    kept = call(
        mask_kernel,
        "mask",
        none,
        (bands,),
        {
            "mask_gate": (mask_gate, whole(mask_gate)),
            "mask_up": (mask_up, whole(mask_up)),
            "mask_down": (mask_down, whole(mask_down)),
            "w_gate": (hbm(w_gate), by_cols),
            "w_up": (hbm(w_up), by_cols),
            "w_down": (hbm(w_down), by_rows),
        },
        {
            "mg": spread(mask_gate),
            "mu": spread(mask_up),
            "md": spread(mask_down),
            "wg": pinned(jax.ShapeDtypeStruct(w_gate.shape, BF16)),
            "wu": pinned(jax.ShapeDtypeStruct(w_up.shape, BF16)),
            "wd": pinned(jax.ShapeDtypeStruct(w_down.shape, BF16)),
        },
        cost=pl.CostEstimate(flops=0, bytes_accessed=6 * width * units, transcendentals=0),
    )
    gathered = call(
        assemble_kernel,
        "assemble",
        none,
        (1,),
        {
            "after": (kept["mg"], pl.BlockSpec(memory_space=pl.ANY)),
            **{f"block{k}": (b, whole(b)) for k, b in enumerate(blocks)},
        },
        {"tok": pinned(row_shape), "cot": pinned(row_shape), "tok_t": pinned(col_shape)},
    )

    def held(*names):
        return {k: pinned(kept[k] if k in kept else gathered[k]) for k in names}

    trio = pl.BlockSpec((3, rows, tile), lambda i, idx: (0, 0, i))

    def trio_of(p, kind):
        return (jax.ShapeDtypeStruct((3, rows, split[p] * tile), kind), trio)

    def cost(p, matmuls, mats):
        step = width * split[p] * tile
        return pl.CostEstimate(
            flops=2 * matmuls * rows * step, bytes_accessed=2 * mats * step, transcendentals=0
        )

    def partials(which, p, after=None, received=None):
        ins = held("tok", "cot", "wg", "wu", "wd")
        outs = {"send": trio_of(p, F32)}
        if after is not None:
            ins["after"] = (after, pl.BlockSpec(memory_space=pl.ANY))
        if received is not None:
            ins["received"] = (received, trio)
            outs = {"own": trio_of(p, F32), "send": trio_of(p, BF16)}
        return call(
            partial_kernel, "partials", place(which, p), (split[p],), ins, outs, cost=cost(p, 3, 0)
        )

    def activate(own, others, after):
        ins = {"own": (own, whole(own)), "after": (after, pl.BlockSpec(memory_space=pl.ANY))}
        ins.update({f"other{k}": (a, whole(a)) for k, a in enumerate(others)})
        shape = jax.ShapeDtypeStruct(own.shape, BF16)
        return call(act_kernel, "activate", none, (1,), ins, {"act": (shape, whole(shape))})["act"]

    def back(which, p, act, do_rows, do_grads, state, last=False):
        ins = {"act": (act, trio)}
        outs, aliases, scratch = {}, {}, {}
        if do_rows:
            ins.update(held("wg", "wu", "wd"))
            shape = jax.ShapeDtypeStruct((2, rows, width), F32)
            scratch["acc"] = pltpu.VMEM(shape.shape, F32)
            if "sums" in state:
                ins["sums"] = pinned(state["sums"])
            if last:
                n_out = n_grid if direct else 1
                shape = jax.ShapeDtypeStruct((2, rows // n_out, width), BF16 if direct else F32)
                outs.update({f"rows{k}": (shape, whole(shape)) for k in range(n_out)})
            else:
                outs["new_sums"] = pinned(shape)
        if do_grads:
            ins.update(held("tok_t", "cot", "mg", "mu", "md"))
            cols = pl.BlockSpec((width, tile), lambda i, first: (0, first[0] + i))
            downs = pl.BlockSpec((tile, width), lambda i, first: (first[0] + i, 0))
            outs["gg"] = (jax.ShapeDtypeStruct((width, units), F32), cols)
            outs["gu"] = (jax.ShapeDtypeStruct((width, units), F32), cols)
            outs["gd"] = (jax.ShapeDtypeStruct((units, width), F32), downs)
            for k in ("gg", "gu", "gd"):
                if k in state:
                    ins["old_" + k] = (state[k], pl.BlockSpec(memory_space=pl.ANY))
                    aliases["old_" + k] = k
            if "rows0" in state:
                ins["after"] = (state["rows0"], pl.BlockSpec(memory_space=pl.ANY))
        got = call(
            functools.partial(back_kernel, do_rows, do_grads, split[p]),
            "_".join(["back"] + ["rows"] * do_rows + ["grads"] * do_grads),
            place(which, p),
            (split[p],),
            ins,
            outs,
            scratch=scratch,
            aliases=aliases,
            cost=cost(p, 3 * do_rows + 3 * do_grads, 6 * do_grads),
        )
        return {**state, **{k.replace("new_", ""): v for k, v in got.items()}}

    n = len(split)
    sent, sums, theirs, after = [], [], [], None
    for p in range(n + 1):
        if p < n:
            after = partials(1, p, after)["send"]
            sent.append(swap(after))
        if p > 0:
            got = partials(0, p - 1, after, sent[p - 1])
            after = got["own"]
            sums.append(after)
            theirs.append(across(got["send"]))

    state = {}
    for p in range(n):
        last = p == n - 1
        act = activate(sums[p], theirs[p], state.get("sums", after))
        act_other = swap(act)
        state = back(0, p, act, True, not last, state)
        state = back(1, p, act_other, True, not last, state, last)
        if last:
            state = back(0, p, act, False, True, state)
            state = back(1, p, act_other, False, True, state)

    if direct:
        both = state["rows0"].astype(F32)
        for s in range(1, n_grid):
            both += trade(state[f"rows{s}"], s).astype(F32)
    else:
        both = lax.psum_scatter(state["rows0"], "grid", scatter_dimension=1, tiled=True)
    both = both.astype(BF16)
    return (both[0], both[1], state["gg"], state["gu"], state["gd"])


def solution(mesh):
    in_specs = (
        P(("groups", "grid"), "dp"),
        P("dp", "grid"),
        P("dp", "grid"),
        P("grid", "dp"),
        P(("groups", "dp"), "grid"),
        P(("groups", "dp"), "grid"),
        P(("groups", "grid"), "dp"),
        P(("groups", "grid"), "dp"),
    )
    out_specs = (
        P(("groups", "grid"), "dp"),
        P(("groups", "grid"), "dp"),
        P(("groups", "dp"), "grid"),
        P(("groups", "dp"), "grid"),
        P(("groups", "grid"), "dp"),
    )
    sizes = (mesh.shape["grid"], mesh.shape["dp"])
    return jax.shard_map(
        functools.partial(shards, sizes),
        mesh=mesh,
        in_specs=in_specs,
        out_specs=out_specs,
        check_vma=False,
    )
```

time: 97 us -> 111 us (1.14)
  local copies, waits for them, and re-layouts: 1.07 us -> 41.2 us
  Pallas kernels: 73.7 us -> 52.3 us
  waiting for transfers between devices: 2.85 us -> 0.12 us
  other arithmetic: 2.97 us -> 0.82 us
    unnamed x0 -> x33, local copies, waits for them, and re-layouts: none -> 40.6 us
    pallas_call x18 -> x19, Pallas kernels: 73.7 us -> 52.3 us  [call(): pl.pallas_call(body, out_shape=[shape for shape, _ in outs.values()], gri...]
    ppermute x6, waiting for transfers between devices: 2.47 us -> 0.02 us  [trade(): return lax.ppermute(array, 'grid', [(i, i ^ s) for i in range(n_grid)])]
    convert_element_type x3 -> x0, other arithmetic: 2.07 us -> none  [the longest x1 0.69 us: shards(): mg = jnp.repeat(mask_gate.astype(F32), BLK, axis=1)]
  transfers between devices with their start and end apart: 15 -> 15, of which waited for: 2 -> 1; matrix products, arithmetic and copies ran while one was open for 3% -> 1% of each run, Pallas kernels for 66% -> 43%
where the time goes in v3:
time: 111 us; the launch traced here: 110 us
  Pallas kernels  52.3 us (47%)
  local copies, waits for them, and re-layouts  41.2 us (37%)
  starting transfers between devices  15.1 us (14%)
    pallas_call x19, Pallas kernels, call(): pl.pallas_call(body, out_shape=[shape for shape, _ in outs.values()], gri...  52.3 us
    unnamed x33, local copies, waits for them, and re-layouts  40.6 us
    ppermute x6, starting transfers between devices, trade(): return lax.ppermute(array, 'grid', [(i, i ^ s) for i in range(n_grid)])  10.2 us
    ppermute x3, starting transfers between devices, across(): lax.ppermute(array, 'dp', [(i, (i // 2 + s) % pairs * 2 + i % 2) for i in...  3.51 us
  transfers between devices with their start and end apart: 15, of which 1 were waited for; matrix products, arithmetic and copies ran while one was open for 1% of the time, Pallas kernels for 43%

profile of v3, /device:TPU:0, one launch (start us, length us, event | category | flops | bytes accessed | tf_op | source)
XLA Modules:
  0.0 110.4 jit_solution(6505597083375611144)
XLA Ops:
  0.6 0.8 pad_maximum_fusion.refs_2_
  1.4 5.1 %collective-permute-start.2 = (bf16[2,16,1024]{2,1,0:T(8,128)(2,1)S(1)}, bf16[2,16,1024]{2,1,0:T(8,128)(2,1)S(1)}, u32[]{:S(2)}, u32[]{:S(2)}) collective-permute-start(bf16[2,16,1024]{2,1,0:T(8,128)(2,1)S(1)} %pad_maximum_fusion.refs_2_), channel_id=1, source_target_pairs={{0,12},{4,8},{8,4},{12,0},{1,13},{5,9},{9,5},{13,1},{2,14},{6,10},... | collective-permute-start | bytes 196616 | tf_op jit(solution)/shard_map/ppermute | solution.py:192
  6.5 0.0 collective-permute-start.1
  6.5 0.6 collective-permute-start
  7.2 0.8 copy.28.refs_3_
  7.9 0.7 copy-done.12
  8.6 0.7 copy-done.13
  9.3 10.4 %mask.1 = (f32[8,1,4096]{2,1,0:T(1,128)S(1)}, f32[8,1,4096]{2,1,0:T(1,128)S(1)}, f32[32,1,1024]{2,1,0:T(1,128)S(1)}, bf16[1024,4096]{1,0:T(8,128)(2,1)S(1)}, bf1...) custom-call(s32[1]{0:T(128)} %constant.24.clone.1.refs_0_, s32[8,32]{1,0:T(8,128)S(1)} %copy-done.12, ...), custom_call_target="tpu_custom_call" | custom-call | bytes 25165824 | tf_op jit(solution)/shard_map/mask/pallas_call | solution.py:39
  19.7 0.0 copy-start.4
  19.7 0.0 copy-start.8
  19.7 0.0 collective-permute-done.2.refs_5_
  19.7 0.0 collective-permute-done.refs_3_
  19.8 0.1 assemble.1
  19.9 1.5 %partials.6.refs_6_ = f32[3,64,768]{2,1,0:T(8,128)S(1)} custom-call(s32[1]{0:T(128)} %bitcast.7.refs_0_, bf16[64,1024]{1,0:T(8,128)(2,1)S(1)} %get-tuple-element.47.refs_1_, bf16[64,1024]{1,0:T(8,128)(2,1)S(1)} %get-tuple-element.48.refs_2_.refs_6_.refs_7_.refs_3_, bf16[1024,4096]{1,0:T(8,128)(2,1)S(1)} %get-tuple-element.49.refs_3_.refs_2_, ...), custom_call_target="tpu_custom_call" | custom-call | flops 301989888 | tf_op jit(solution)/shard_map/partials/pallas_call | solution.py:39
  21.4 1.7 %copy-done.4 = bf16[1024,4096]{1,0:T(8,128)(2,1)} copy-done((bf16[1024,4096]{1,0:T(8,128)(2,1)}, bf16[1024,4096]{1,0:T(8,128)(2,1)S(1)}, u32[]{:S(2)}) %copy-start.4) | copy-done | bytes 8388632
  23.1 2.8 %copy-done.8 = bf16[4096,1024]{1,0:T(8,128)(2,1)} copy-done((bf16[4096,1024]{1,0:T(8,128)(2,1)}, bf16[4096,1024]{1,0:T(8,128)(2,1)S(1)}, u32[]{:S(2)}) %copy-start.8) | copy-done | bytes 8388632
  25.9 3.4 %copy-done = bf16[1024,4096]{1,0:T(8,128)(2,1)} copy-done((bf16[1024,4096]{1,0:T(8,128)(2,1)}, bf16[1024,4096]{1,0:T(8,128)(2,1)S(1)}, u32[]{:S(2)}) %copy-start) | copy-done | bytes 8388632
  29.3 0.0 collective-permute-start.3
  29.3 3.4 %copy-done.1 = bf16[1024,4096]{1,0:T(8,128)(2,1)S(1)} copy-done((bf16[1024,4096]{1,0:T(8,128)(2,1)S(1)}, bf16[1024,4096]{1,0:T(8,128)(2,1)}, u32[]{:S(2)}) %copy-start.1) | copy-done | bytes 8388632
  32.6 3.4 %copy-done.5 = bf16[1024,4096]{1,0:T(8,128)(2,1)S(1)} copy-done((bf16[1024,4096]{1,0:T(8,128)(2,1)S(1)}, bf16[1024,4096]{1,0:T(8,128)(2,1)}, u32[]{:S(2)}) %copy-start.5) | copy-done | bytes 8388632
  36.0 3.4 %copy-done.9 = bf16[4096,1024]{1,0:T(8,128)(2,1)S(1)} copy-done((bf16[4096,1024]{1,0:T(8,128)(2,1)S(1)}, bf16[4096,1024]{1,0:T(8,128)(2,1)}, u32[]{:S(2)}) %copy-start.9) | copy-done | bytes 8388632
  39.4 1.5 %partials.7.refs_6_ = f32[3,64,768]{2,1,0:T(8,128)S(1)} custom-call(s32[1]{0:T(128)} %bitcast.6.refs_0_, bf16[64,1024]{1,0:T(8,128)(2,1)S(1)} %get-tuple-element.47.refs_1_, bf16[64,1024]{1,0:T(8,128)(2,1)S(1)} %get-tuple-element.48.refs_2_.refs_6_.refs_7_.refs_3_, bf16[1024,4096]{1,0:T(8,128)(2,1)S(1)} %copy-done.1, bf16[1024,4096]{1,0:T(8,128)(2,1)S(1)} %copy-done.5, ...), custom_call_target="tpu_custom_call" | custom-call | flops 301989888 | tf_op jit(solution)/shard_map/partials/pallas_call | solution.py:39
  40.9 0.6 collective-permute-start.4
  41.5 3.4 %copy-done.2 = bf16[1024,4096]{1,0:T(8,128)(2,1)S(1)} copy-done((bf16[1024,4096]{1,0:T(8,128)(2,1)S(1)}, bf16[1024,4096]{1,0:T(8,128)(2,1)}, u32[]{:S(2)}) %copy-start.2) | copy-done | bytes 8388632
  44.8 3.4 %copy-done.6 = bf16[1024,4096]{1,0:T(8,128)(2,1)S(1)} copy-done((bf16[1024,4096]{1,0:T(8,128)(2,1)S(1)}, bf16[1024,4096]{1,0:T(8,128)(2,1)}, u32[]{:S(2)}) %copy-start.6) | copy-done | bytes 8388632
  48.2 3.4 %copy-done.10 = bf16[4096,1024]{1,0:T(8,128)(2,1)S(1)} copy-done((bf16[4096,1024]{1,0:T(8,128)(2,1)S(1)}, bf16[4096,1024]{1,0:T(8,128)(2,1)}, u32[]{:S(2)}) %copy-start.10) | copy-done | bytes 8388632
  51.6 3.6 %partials.8 = (f32[3,64,768]{2,1,0:T(8,128)S(1)}, bf16[3,64,768]{2,1,0:T(8,128)(2,1)}) custom-call(s32[1]{0:T(128)} %bitcast.5.refs_0_, bf16[64,1024]{1,0:T(8,128)(2,1)S(1)} %get-tuple-element.47.refs_1_, bf16[64,1024]{1,0:T(8,128)(2,1)S(1)} %get-tuple-element.48.refs_2_.refs_6_.refs_7_.refs_3_, bf16[1024,4096]{1,0:T(8,128)(2,1)S(1)} %copy-done.2, ...), custom_call_target="tpu_custom_call" | custom-call | flops 301989888 | tf_op jit(solution)/shard_map/partials/pallas_call | solution.py:39
  55.2 1.0 partials.9.refs_6_
  56.2 0.1 collective-permute-start.5
  56.3 1.7 %collective-permute-start.6 = (bf16[3,64,768]{2,1,0:T(8,128)(2,1)}, bf16[3,64,768]{2,1,0:T(8,128)(2,1)}, u32[]{:S(2)}, u32[]{:S(2)}) collective-permute-start(bf16[3,64,768]{2,1,0:T(8,128)(2,1)} %get-tuple-element.55), channel_id=1, source_target_pairs={{0,2},{1,3},{2,0},{3,1},{4,6},{5,7},{6,4},{7,5},{8,10},{9,11},{10,... | collective-permute-start | bytes 884744 | tf_op jit(solution)/shard_map/ppermute | solution.py:199
  57.9 3.4 %copy-done.3 = bf16[1024,4096]{1,0:T(8,128)(2,1)S(1)} copy-done((bf16[1024,4096]{1,0:T(8,128)(2,1)S(1)}, bf16[1024,4096]{1,0:T(8,128)(2,1)}, u32[]{:S(2)}) %copy-start.3) | copy-done | bytes 8388632
  61.3 3.4 %copy-done.7 = bf16[1024,4096]{1,0:T(8,128)(2,1)S(1)} copy-done((bf16[1024,4096]{1,0:T(8,128)(2,1)S(1)}, bf16[1024,4096]{1,0:T(8,128)(2,1)}, u32[]{:S(2)}) %copy-start.7) | copy-done | bytes 8388632
  64.7 3.4 %copy-done.11 = bf16[4096,1024]{1,0:T(8,128)(2,1)S(1)} copy-done((bf16[4096,1024]{1,0:T(8,128)(2,1)S(1)}, bf16[4096,1024]{1,0:T(8,128)(2,1)}, u32[]{:S(2)}) %copy-start.11) | copy-done | bytes 8388632
  68.1 1.6 %partials.10 = (f32[3,64,768]{2,1,0:T(8,128)S(1)}, bf16[3,64,768]{2,1,0:T(8,128)(2,1)S(1)}) custom-call(s32[1]{0:T(128)} %bitcast.4.refs_0_, bf16[64,1024]{1,0:T(8,128)(2,1)S(1)} %get-tuple-element.47.refs_1_, bf16[64,1024]{1,0:T(8,128)(2,1)S(1)} %get-tuple-element.48.refs_2_.refs_6_.refs_7_.refs_3_, bf16[1024,4096]{1,0:T(8,128)(2,1)S(1)} %copy-done.3, ...), custom_call_target="tpu_custom_call" | custom-call | flops 301989888 | tf_op jit(solution)/shard_map/partials/pallas_call | solution.py:39
  69.7 0.0 slice-start
  69.7 0.0 slice-start.1
  69.7 1.1 partials.11
  70.8 0.0 collective-permute-done.6.refs_3_
  70.8 1.6 %activate.3.refs_1_ = bf16[3,64,768]{2,1,0:T(8,128)(2,1)S(1)} custom-call(s32[1]{0:T(128)} %constant.24.clone.1.refs_0_, f32[3,64,768]{2,1,0:T(8,128)S(1)} %get-tuple-element.52.refs_6_.refs_1_, f32[3,64,512]{2,1,0:T(8,128)S(1)} %get-tuple-element.54.refs_2_.refs_1_, bf16[3,64,768]{2,1,0:T(8,128)(2,1)} %collective-permute-done.6.refs_3_), custom_call_target="tpu_custom_call" | custom-call | tf_op jit(solution)/shard_map/activate/pallas_call | solution.py:39
  72.5 0.2 collective-permute-start.7
  72.7 0.4 collective-permute-start.8
  73.1 0.1 slice-done.1
  73.3 5.3 %back_rows_grads.4 = (f32[2,64,1024]{2,1,0:T(8,128)S(1)}, f32[1024,4096]{1,0:T(8,128)}, f32[1024,4096]{1,0:T(8,128)}, f32[4096,1024]{1,0:T(8,128)}) custom-call(s32[1]{0:T(128)} %bitcast.5.refs_0_, bf16[3,64,768]{2,1,0:T(8,128)(2,1)S(1)} %activate.3.refs_1_, bf16[1024,4096]{1,0:T(8,128)(2,1)S(1)} %bitcast.13, bf16[1024,4096]{1,0:T(8,128)(2,1)S(1)} %copy-done.7, ...), custom_call_target="tpu_custom_call" | custom-call | flops 603979776 | bytes 9437184 | tf_op jit(solution)/shard_map/back_rows_grads/pallas_call | solution.py:39
  78.5 0.0 collective-permute-done.7.refs_1_
  78.5 5.3 %back_rows_grads.5 = (f32[2,64,1024]{2,1,0:T(8,128)S(1)}, f32[1024,4096]{1,0:T(8,128)}, f32[1024,4096]{1,0:T(8,128)}, f32[4096,1024]{1,0:T(8,128)}) custom-call(s32[1]{0:T(128)} %bitcast.7.refs_0_, bf16[3,64,768]{2,1,0:T(8,128)(2,1)S(1)} %collective-permute-done.7.refs_1_, ...), custom_call_target="tpu_custom_call", output_to_operand_aliasing={{1}: (11, {}), {2}: (12, {}), {3}: (13, {})} | custom-call | flops 603979776 | bytes 9437184 | tf_op jit(solution)/shard_map/back_rows_grads/pallas_call | solution.py:39
  83.8 0.0 collective-permute-done.8.refs_3_
  83.8 0.2 activate.4.refs_1_
  84.0 0.2 collective-permute-start.9
  84.2 1.4 %collective-permute-start.10 = (bf16[3,64,512]{2,1,0:T(8,128)(2,1)S(1)}, bf16[3,64,512]{2,1,0:T(8,128)(2,1)S(1)}, u32[]{:S(2)}, u32[]{:S(2)}) collective-permute-start(bf16[3,64,512]{2,1,0:T(8,128)(2,1)S(1)} %get-tuple-element.73), channel_id=1, source_target_pairs={{0,2},{1,3},{2,0},{3,1},{4,6},{5,7},{6,4},{7,5},{8,10},{9,11},{10,... | collective-permute-start | bytes 589832 | tf_op jit(solution)/shard_map/ppermute | solution.py:199
  85.6 5.3 %back_rows_grads.6 = (f32[2,64,1024]{2,1,0:T(8,128)S(1)}, f32[1024,4096]{1,0:T(8,128)}, f32[1024,4096]{1,0:T(8,128)}, f32[4096,1024]{1,0:T(8,128)}) custom-call(s32[1]{0:T(128)} %bitcast.4.refs_0_, bf16[3,64,768]{2,1,0:T(8,128)(2,1)S(1)} %activate.4.refs_1_, ...), custom_call_target="tpu_custom_call", output_to_operand_aliasing={{1}: (11, {}), {2}: (12, {}), {3}: (13, {})} | custom-call | flops 603979776 | bytes 9437184 | tf_op jit(solution)/shard_map/back_rows_grads/pallas_call | solution.py:39
  90.9 5.3 %back_rows_grads.7 = (f32[2,64,1024]{2,1,0:T(8,128)S(1)}, f32[1024,4096]{1,0:T(8,128)}, f32[1024,4096]{1,0:T(8,128)}, f32[4096,1024]{1,0:T(8,128)}) custom-call(s32[1]{0:T(128)} %bitcast.6.refs_0_, bf16[3,64,768]{2,1,0:T(8,128)(2,1)S(1)} %collective-permute-done.9.refs_1_, ...), custom_call_target="tpu_custom_call", output_to_operand_aliasing={{1}: (11, {}), {2}: (12, {}), {3}: (13, {})} | custom-call | flops 603979776 | bytes 9437184 | tf_op jit(solution)/shard_map/back_rows_grads/pallas_call | solution.py:39
  96.2 0.1 activate.5.refs_1_
  96.3 0.2 collective-permute-start.11
  96.5 1.2 %back_rows.2.refs_5_ = f32[2,64,1024]{2,1,0:T(8,128)S(1)} custom-call(s32[1]{0:T(128)} %bitcast.1.refs_0_, bf16[3,64,512]{2,1,0:T(8,128)(2,1)S(1)} %activate.5.refs_1_, bf16[1024,4096]{1,0:T(8,128)(2,1)S(1)} %bitcast.13, bf16[1024,4096]{1,0:T(8,128)(2,1)S(1)} %copy-done.7, bf16[4096,1024]{1,0:T(8,128)(2,1)S(1)} %copy-done.11, ...), custom_call_target="tpu_custom_call" | custom-call | flops 201326592 | tf_op jit(solution)/shard_map/back_rows/pallas_call | solution.py:39
  97.7 0.1 collective-permute-done.11.refs_1_
  97.8 1.2 %back_rows.3 = (bf16[2,16,1024]{2,1,0:T(8,128)(2,1)S(1)}, bf16[2,16,1024]{2,1,0:T(8,128)(2,1)S(1)}, bf16[2,16,1024]{2,1,0:T(8,128)(2,1)S(1)}, bf16[2,16,1024]{2,1,0:T(8,128)(2,1)S(1)}) custom-call(s32[1]{0:T(128)} %bitcast.refs_0_, bf16[3,64,512]{2,1,0:T(8,128)(2,1)S(1)} %collective-permute-done.11.refs_1_, bf16[1024,4096]{1,0:T(8,128)(2,1)S(1)} %bitcast.13, ...), custom_call_target="tpu_custom_call" | custom-call | flops 201326592 | tf_op jit(solution)/shard_map/back_rows/pallas_call | solution.py:39
  99.0 1.3 %collective-permute-start.12 = (bf16[2,16,1024]{2,1,0:T(8,128)(2,1)S(1)}, bf16[2,16,1024]{2,1,0:T(8,128)(2,1)S(1)}, u32[]{:S(2)}, u32[]{:S(2)}) collective-permute-start(bf16[2,16,1024]{2,1,0:T(8,128)(2,1)S(1)} %get-tuple-element.75), channel_id=1, source_target_pairs={{0,4},{4,0},{8,12},{12,8},{1,5},{5,1},{9,13},{13,9},{2,6},{6,2},{1... | collective-permute-start | bytes 196616 | tf_op jit(solution)/shard_map/ppermute | solution.py:192
  100.3 2.9 %collective-permute-start.13 = (bf16[2,16,1024]{2,1,0:T(8,128)(2,1)S(1)}, bf16[2,16,1024]{2,1,0:T(8,128)(2,1)S(1)}, u32[]{:S(2)}, u32[]{:S(2)}) collective-permute-start(bf16[2,16,1024]{2,1,0:T(8,128)(2,1)S(1)} %get-tuple-element.76), channel_id=1, source_target_pairs={{0,8},{4,12},{8,0},{12,4},{1,9},{5,13},{9,1},{13,5},{2,10},{6,14},... | collective-permute-start | bytes 196616 | tf_op jit(solution)/shard_map/ppermute | solution.py:192
  103.2 0.2 collective-permute-start.14
  103.4 3.1 %back_grads.2 = (f32[1024,4096]{1,0:T(8,128)}, f32[1024,4096]{1,0:T(8,128)}, f32[4096,1024]{1,0:T(8,128)}) custom-call(s32[1]{0:T(128)} %bitcast.1.refs_0_, bf16[3,64,512]{2,1,0:T(8,128)(2,1)S(1)} %activate.5.refs_1_, bf16[1024,64]{1,0:T(8,128)(2,1)S(1)} %get-tuple-element.56.refs_5_.refs_6_.refs_2_, ...), custom_call_target="tpu_custom_call", output_to_operand_aliasing={{0}: (7, {}), {1}: (8, {}), {2}: (9, {})} | custom-call | flops 201326592 | bytes 6291456 | tf_op jit(solution)/shard_map/back_grads/pallas_call | solution.py:39
  106.6 3.1 %back_grads.3 = (f32[1024,4096]{1,0:T(8,128)}, f32[1024,4096]{1,0:T(8,128)}, f32[4096,1024]{1,0:T(8,128)}) custom-call(s32[1]{0:T(128)} %bitcast.refs_0_, bf16[3,64,512]{2,1,0:T(8,128)(2,1)S(1)} %collective-permute-done.11.refs_1_, ...), custom_call_target="tpu_custom_call", output_to_operand_aliasing={{0}: (7, {}), {1}: (8, {}), {2}: (9, {})} | custom-call | flops 201326592 | bytes 6291456 | tf_op jit(solution)/shard_map/back_grads/pallas_call | solution.py:39
  109.7 0.0 collective-permute-done.12
  109.7 0.0 collective-permute-done.13
  109.7 0.6 slice_bitcast_fusion
  (22 shorter events, 0.1 us)
Async XLA Ops:
  1.4 18.3 %collective-permute-start.2 = (bf16[2,16,1024]{2,1,0:T(8,128)(2,1)S(1)}, bf16[2,16,1024]{2,1,0:T(8,128)(2,1)S(1)}, u32[]{:S(2)}, u32[]{:S(2)}) collective-permute-start(bf16[2,16,1024]{2,1,0:T(8,128)(2,1)S(1)} %pad_maximum_fusion.refs_2_), channel_id=1, source_target_pairs={{0,12},{4,8},{8,4},{12,0},{1,13},{5,9},{9,5},{13,1},{2,14},{6,10},... | collective-permute-start | bytes 196616 | tf_op jit(solution)/shard_map/ppermute | solution.py:192
  6.5 13.2 %collective-permute-start.1 = (bf16[2,16,1024]{2,1,0:T(8,128)(2,1)S(1)}, bf16[2,16,1024]{2,1,0:T(8,128)(2,1)S(1)}, u32[]{:S(2)}, u32[]{:S(2)}) collective-permute-start(bf16[2,16,1024]{2,1,0:T(8,128)(2,1)S(1)} %pad_maximum_fusion.refs_2_), channel_id=1, source_target_pairs={{0,8},{4,12},{8,0},{12,4},{1,9},{5,13},{9,1},{13,5},{2,10},{6,14},... | collective-permute-start | bytes 196616 | tf_op jit(solution)/shard_map/ppermute | solution.py:192
  6.5 13.2 %collective-permute-start = (bf16[2,16,1024]{2,1,0:T(8,128)(2,1)S(1)}, bf16[2,16,1024]{2,1,0:T(8,128)(2,1)S(1)}, u32[]{:S(2)}, u32[]{:S(2)}) collective-permute-start(bf16[2,16,1024]{2,1,0:T(8,128)(2,1)S(1)} %pad_maximum_fusion.refs_2_), channel_id=1, source_target_pairs={{0,4},{4,0},{8,12},{12,8},{1,5},{5,1},{9,13},{13,9},{2,6},{6,2},{1... | collective-permute-start | bytes 196616 | tf_op jit(solution)/shard_map/ppermute | solution.py:192
  7.9 0.7 copy-start.12
  8.6 0.7 copy-start.13
  19.7 3.4 %copy-start.4 = (bf16[1024,4096]{1,0:T(8,128)(2,1)}, bf16[1024,4096]{1,0:T(8,128)(2,1)S(1)}, u32[]{:S(2)}) copy-start(bf16[1024,4096]{1,0:T(8,128)(2,1)S(1)} %get-tuple-element.50.refs_4_.refs_3_) | copy-start | bytes 25165828
  19.7 6.1 %copy-start.8 = (bf16[4096,1024]{1,0:T(8,128)(2,1)}, bf16[4096,1024]{1,0:T(8,128)(2,1)S(1)}, u32[]{:S(2)}) copy-start(bf16[4096,1024]{1,0:T(8,128)(2,1)S(1)} %get-tuple-element.51.refs_5_.refs_4_) | copy-start | bytes 25165828
  25.9 3.4 %copy-start = (bf16[1024,4096]{1,0:T(8,128)(2,1)}, bf16[1024,4096]{1,0:T(8,128)(2,1)S(1)}, u32[]{:S(2)}) copy-start(bf16[1024,4096]{1,0:T(8,128)(2,1)S(1)} %get-tuple-element.49.refs_3_.refs_2_) | copy-start | bytes 25165828
  29.3 12.2 %collective-permute-start.3 = (f32[3,64,768]{2,1,0:T(8,128)S(1)}, f32[3,64,768]{2,1,0:T(8,128)}, u32[]{:S(2)}, u32[]{:S(2)}) collective-permute-start(f32[3,64,768]{2,1,0:T(8,128)S(1)} %partials.6.refs_6_), channel_id=1, source_target_pairs={{0,1},{1,0},{2,3},{3,2},{4,5},{5,4},{6,7},{7,6},{8,9},{9,8},{10,11... | collective-permute-start | bytes 1769480 | tf_op jit(solution)/shard_map/ppermute | solution.py:195
  29.3 3.4 %copy-start.1 = (bf16[1024,4096]{1,0:T(8,128)(2,1)S(1)}, bf16[1024,4096]{1,0:T(8,128)(2,1)}, u32[]{:S(2)}) copy-start(bf16[1024,4096]{1,0:T(8,128)(2,1)} %copy-done) | copy-start | bytes 25165828
  32.6 3.4 %copy-start.5 = (bf16[1024,4096]{1,0:T(8,128)(2,1)S(1)}, bf16[1024,4096]{1,0:T(8,128)(2,1)}, u32[]{:S(2)}) copy-start(bf16[1024,4096]{1,0:T(8,128)(2,1)} %copy-done.4) | copy-start | bytes 25165828
  36.0 3.4 %copy-start.9 = (bf16[4096,1024]{1,0:T(8,128)(2,1)S(1)}, bf16[4096,1024]{1,0:T(8,128)(2,1)}, u32[]{:S(2)}) copy-start(bf16[4096,1024]{1,0:T(8,128)(2,1)} %copy-done.8) | copy-start | bytes 25165828
  40.9 17.1 %collective-permute-start.4 = (f32[3,64,768]{2,1,0:T(8,128)S(1)}, f32[3,64,768]{2,1,0:T(8,128)S(1)}, u32[]{:S(2)}, u32[]{:S(2)}) collective-permute-start(f32[3,64,768]{2,1,0:T(8,128)S(1)} %partials.7.refs_6_), channel_id=1, source_target_pairs={{0,1},{1,0},{2,3},{3,2},{4,5},{5,4},{6,7},{7,6},{8,9},{9,8},{10,11... | collective-permute-start | bytes 1769480 | tf_op jit(solution)/shard_map/ppermute | solution.py:195
  41.5 3.4 %copy-start.2 = (bf16[1024,4096]{1,0:T(8,128)(2,1)S(1)}, bf16[1024,4096]{1,0:T(8,128)(2,1)}, u32[]{:S(2)}) copy-start(bf16[1024,4096]{1,0:T(8,128)(2,1)} %copy-done) | copy-start | bytes 25165828
  44.8 3.4 %copy-start.6 = (bf16[1024,4096]{1,0:T(8,128)(2,1)S(1)}, bf16[1024,4096]{1,0:T(8,128)(2,1)}, u32[]{:S(2)}) copy-start(bf16[1024,4096]{1,0:T(8,128)(2,1)} %copy-done.4) | copy-start | bytes 25165828
  48.2 3.4 %copy-start.10 = (bf16[4096,1024]{1,0:T(8,128)(2,1)S(1)}, bf16[4096,1024]{1,0:T(8,128)(2,1)}, u32[]{:S(2)}) copy-start(bf16[4096,1024]{1,0:T(8,128)(2,1)} %copy-done.8) | copy-start | bytes 25165828
  56.2 13.5 %collective-permute-start.5 = (f32[3,64,512]{2,1,0:T(8,128)S(1)}, f32[3,64,512]{2,1,0:T(8,128)S(1)}, u32[]{:S(2)}, u32[]{:S(2)}) collective-permute-start(f32[3,64,512]{2,1,0:T(8,128)S(1)} %partials.9.refs_6_), channel_id=1, source_target_pairs={{0,1},{1,0},{2,3},{3,2},{4,5},{5,4},{6,7},{7,6},{8,9},{9,8},{10,11... | collective-permute-start | bytes 1179656 | tf_op jit(solution)/shard_map/ppermute | solution.py:195
  56.3 14.6 %collective-permute-start.6 = (bf16[3,64,768]{2,1,0:T(8,128)(2,1)}, bf16[3,64,768]{2,1,0:T(8,128)(2,1)}, u32[]{:S(2)}, u32[]{:S(2)}) collective-permute-start(bf16[3,64,768]{2,1,0:T(8,128)(2,1)} %get-tuple-element.55), channel_id=1, source_target_pairs={{0,2},{1,3},{2,0},{3,1},{4,6},{5,7},{6,4},{7,5},{8,10},{9,11},{10,... | collective-permute-start | bytes 884744 | tf_op jit(solution)/shard_map/ppermute | solution.py:199
  57.9 3.4 %copy-start.3 = (bf16[1024,4096]{1,0:T(8,128)(2,1)S(1)}, bf16[1024,4096]{1,0:T(8,128)(2,1)}, u32[]{:S(2)}) copy-start(bf16[1024,4096]{1,0:T(8,128)(2,1)} %copy-done) | copy-start | bytes 25165828
  61.3 3.4 %copy-start.7 = (bf16[1024,4096]{1,0:T(8,128)(2,1)S(1)}, bf16[1024,4096]{1,0:T(8,128)(2,1)}, u32[]{:S(2)}) copy-start(bf16[1024,4096]{1,0:T(8,128)(2,1)} %copy-done.4) | copy-start | bytes 25165828
  64.7 3.4 %copy-start.11 = (bf16[4096,1024]{1,0:T(8,128)(2,1)S(1)}, bf16[4096,1024]{1,0:T(8,128)(2,1)}, u32[]{:S(2)}) copy-start(bf16[4096,1024]{1,0:T(8,128)(2,1)} %copy-done.8) | copy-start | bytes 25165828
  69.7 3.4 %slice-start = ((s8[8388608]{0:T(1024)(128)(4,1)}), s8[4194304]{0:T(1024)(128)(4,1)S(1)}, s32[]{:S(2)}) async-start(s8[8388608]{0:T(1024)(128)(4,1)} %bitcast.12), calls=%async_computation | async-start | bytes 8388608
  69.7 3.5 %slice-start.1 = ((s8[8388608]{0:T(1024)(128)(4,1)}), s8[4194304]{0:T(1024)(128)(4,1)S(1)}, s32[]{:S(2)}) async-start(s8[8388608]{0:T(1024)(128)(4,1)} %bitcast.12), calls=%async_computation.1 | async-start | bytes 8388608
  72.5 6.0 %collective-permute-start.7 = (bf16[3,64,768]{2,1,0:T(8,128)(2,1)S(1)}, bf16[3,64,768]{2,1,0:T(8,128)(2,1)S(1)}, u32[]{:S(2)}, u32[]{:S(2)}) collective-permute-start(bf16[3,64,768]{2,1,0:T(8,128)(2,1)S(1)} %activate.3.refs_1_), channel_id=1, source_target_pairs={{0,1},{1,0},{2,3},{3,2},{4,5},{5,4},{6,7},{7,6},{8,9},{9,8},{10,11... | collective-permute-start | bytes 884744 | tf_op jit(solution)/shard_map/ppermute | solution.py:195
  72.7 11.1 %collective-permute-start.8 = (bf16[3,64,768]{2,1,0:T(8,128)(2,1)S(1)}, bf16[3,64,768]{2,1,0:T(8,128)(2,1)S(1)}, u32[]{:S(2)}, u32[]{:S(2)}) collective-permute-start(bf16[3,64,768]{2,1,0:T(8,128)(2,1)S(1)} %get-tuple-element.64), channel_id=1, source_target_pairs={{0,2},{1,3},{2,0},{3,1},{4,6},{5,7},{6,4},{7,5},{8,10},{9,11},{10,... | collective-permute-start | bytes 884744 | tf_op jit(solution)/shard_map/ppermute | solution.py:199
  84.0 7.0 %collective-permute-start.9 = (bf16[3,64,768]{2,1,0:T(8,128)(2,1)S(1)}, bf16[3,64,768]{2,1,0:T(8,128)(2,1)S(1)}, u32[]{:S(2)}, u32[]{:S(2)}) collective-permute-start(bf16[3,64,768]{2,1,0:T(8,128)(2,1)S(1)} %activate.4.refs_1_), channel_id=1, source_target_pairs={{0,1},{1,0},{2,3},{3,2},{4,5},{5,4},{6,7},{7,6},{8,9},{9,8},{10,11... | collective-permute-start | bytes 884744 | tf_op jit(solution)/shard_map/ppermute | solution.py:195
  84.2 12.0 %collective-permute-start.10 = (bf16[3,64,512]{2,1,0:T(8,128)(2,1)S(1)}, bf16[3,64,512]{2,1,0:T(8,128)(2,1)S(1)}, u32[]{:S(2)}, u32[]{:S(2)}) collective-permute-start(bf16[3,64,512]{2,1,0:T(8,128)(2,1)S(1)} %get-tuple-element.73), channel_id=1, source_target_pairs={{0,2},{1,3},{2,0},{3,1},{4,6},{5,7},{6,4},{7,5},{8,10},{9,11},{10,... | collective-permute-start | bytes 589832 | tf_op jit(solution)/shard_map/ppermute | solution.py:199
  96.3 1.5 %collective-permute-start.11 = (bf16[3,64,512]{2,1,0:T(8,128)(2,1)S(1)}, bf16[3,64,512]{2,1,0:T(8,128)(2,1)S(1)}, u32[]{:S(2)}, u32[]{:S(2)}) collective-permute-start(bf16[3,64,512]{2,1,0:T(8,128)(2,1)S(1)} %activate.5.refs_1_), channel_id=1, source_target_pairs={{0,1},{1,0},{2,3},{3,2},{4,5},{5,4},{6,7},{7,6},{8,9},{9,8},{10,11... | collective-permute-start | bytes 589832 | tf_op jit(solution)/shard_map/ppermute | solution.py:195
  99.0 10.7 %collective-permute-start.12 = (bf16[2,16,1024]{2,1,0:T(8,128)(2,1)S(1)}, bf16[2,16,1024]{2,1,0:T(8,128)(2,1)S(1)}, u32[]{:S(2)}, u32[]{:S(2)}) collective-permute-start(bf16[2,16,1024]{2,1,0:T(8,128)(2,1)S(1)} %get-tuple-element.75), channel_id=1, source_target_pairs={{0,4},{4,0},{8,12},{12,8},{1,5},{5,1},{9,13},{13,9},{2,6},{6,2},{1... | collective-permute-start | bytes 196616 | tf_op jit(solution)/shard_map/ppermute | solution.py:192
  100.3 9.4 %collective-permute-start.13 = (bf16[2,16,1024]{2,1,0:T(8,128)(2,1)S(1)}, bf16[2,16,1024]{2,1,0:T(8,128)(2,1)S(1)}, u32[]{:S(2)}, u32[]{:S(2)}) collective-permute-start(bf16[2,16,1024]{2,1,0:T(8,128)(2,1)S(1)} %get-tuple-element.76), channel_id=1, source_target_pairs={{0,8},{4,12},{8,0},{12,4},{1,9},{5,13},{9,1},{13,5},{2,10},{6,14},... | collective-permute-start | bytes 196616 | tf_op jit(solution)/shard_map/ppermute | solution.py:192
  103.2 6.5 %collective-permute-start.14 = (bf16[2,16,1024]{2,1,0:T(8,128)(2,1)S(1)}, bf16[2,16,1024]{2,1,0:T(8,128)(2,1)S(1)}, u32[]{:S(2)}, u32[]{:S(2)}) collective-permute-start(bf16[2,16,1024]{2,1,0:T(8,128)(2,1)S(1)} %get-tuple-element.77), channel_id=1, source_target_pairs={{0,12},{4,8},{8,4},{12,0},{1,13},{5,9},{9,5},{13,1},{2,14},{6,10},... | collective-permute-start | bytes 196616 | tf_op jit(solution)/shard_map/ppermute | solution.py:192

commit v4 on v3

--- a/solution.py
+++ b/solution.py
@@ -9,7 +9,10 @@
 from jax.sharding import PartitionSpec as P
 
 BLK = 128
+DEPTH = 256
+ANY = pl.BlockSpec(memory_space=pl.ANY)
 PIECES = [3, 3, 2]
+AHEAD = [(1, 0), (1, 1), (1, 2)]
 MIB = 1024 * 1024
 F32 = jnp.float32
 BF16 = jnp.bfloat16
@@ -28,7 +31,7 @@
     return (pltpu.with_memory_space_constraint(array, pltpu.VMEM), spec)
 
 
-def call(kernel, name, scalars, grid, ins, outs, scratch=None, aliases=None, cost=None):
+def call(kernel, name, scalars, grid, ins, outs, scratch=None, aliases=None, cost=None, vmem=4):
     scratch = scratch or {}
     names = ["place", *ins, *outs, *scratch]
     in_names, out_names = list(ins), list(outs)
@@ -49,7 +52,7 @@
         input_output_aliases={
             1 + in_names.index(i): out_names.index(o) for i, o in (aliases or {}).items()
         },
-        compiler_params=pltpu.CompilerParams(vmem_limit_bytes=11 * MIB),
+        compiler_params=pltpu.CompilerParams(vmem_limit_bytes=vmem * MIB),
         cost_estimate=cost,
         name=name,
     )(scalars, *[array for array, _ in ins.values()])
@@ -62,6 +65,27 @@
 
 def whole(array):
     return pl.BlockSpec(array.shape, lambda *_: (0,) * len(array.shape))
+
+
+def stack(rows, bands):
+    return max(1, min(bands, DEPTH // rows))
+
+
+def spread_kernel(r):
+    def pattern(blocks):
+        at = lax.broadcasted_iota(jnp.int32, (blocks, blocks * BLK), 0) * BLK
+        column = lax.broadcasted_iota(jnp.int32, (blocks, blocks * BLK), 1)
+        return ((column >= at) & (column < at + BLK)).astype(F32).astype(BF16)
+
+    def entries(mask):
+        return mask[...].astype(F32).astype(BF16)
+
+    wide = pattern(r.mask_gate.shape[1])
+    gate, up = dot(entries(r.mask_gate), wide), dot(entries(r.mask_up), wide)
+    down = dot(entries(r.mask_down_t), pattern(r.mask_down_t.shape[0]), (0, 0))
+    for value, out in ((gate, r.mg), (up, r.mu), (down, r.md)):
+        for b in range(out.shape[0]):
+            out[b] = value[b : b + 1, :]
 
 
 def assemble_kernel(r):
@@ -73,38 +97,30 @@
     r.tok_t[...] = r.tok[...].T
 
 
-def mask_kernel(r):
-    step = pl.program_id(0)
-
-    @pl.when(step == 0)
-    def _():
-        for mask, out in ((r.mask_gate, r.mg), (r.mask_up, r.mu), (r.mask_down, r.md)):
-            blocks, lanes = mask.shape[1], mask.shape[1] * BLK
-            at = lax.broadcasted_iota(jnp.int32, (blocks, lanes), 0)
-            column = lax.broadcasted_iota(jnp.int32, (blocks, lanes), 1)
-            first = at * BLK
-            spread = ((column >= first) & (column < first + BLK)).astype(F32).astype(BF16)
-            wide = dot(mask[...].astype(F32).astype(BF16), spread)
-            for b in range(mask.shape[0]):
-                out[b] = wide[b : b + 1, :]
-
-    for w, mask, out in ((r.w_gate, r.mg, r.wg), (r.w_up, r.mu, r.wu), (r.w_down, r.md, r.wd)):
-        rows = w.shape[0]
-        for b in range(rows // BLK):
-            keep = mask[step * (rows // BLK) + b].astype(BF16)
-            band = pl.ds(pl.multiple_of(step * rows + b * BLK, BLK), BLK)
-            out[band, :] = w[b * BLK : (b + 1) * BLK, :] * keep
-
-
 def tile_at(r, tile):
     return pl.ds(pl.multiple_of((r.place[0] + pl.program_id(0)) * tile, tile), tile)
 
 
+def keep_masked(r):
+    tile = r.wg.shape[1]
+    step, at = pl.program_id(0), tile_at(r, tile)
+    for w, mask, out in ((r.wg, r.mg, r.kg), (r.wu, r.mu, r.ku)):
+        for b in range(w.shape[0] // BLK):
+            band = slice(b * BLK, (b + 1) * BLK)
+            out[step, band, :] = w[band, :] * mask[b, :, at].astype(BF16)
+    for b in range(tile // BLK):
+        band = slice(b * BLK, (b + 1) * BLK)
+        keep = r.md[(r.place[0] + step) * (tile // BLK) + b].astype(BF16)
+        r.kd[step, band, :] = r.wd[band, :] * keep
+
+
 def partial_kernel(r):
-    at = tile_at(r, r.send.shape[2])
-    gate = dot(r.tok[...], r.wg[:, at])
-    up = dot(r.tok[...], r.wu[:, at])
-    back = dot(r.cot[...], r.wd[at, :], (1, 1))
+    if hasattr(r, "wg"):
+        keep_masked(r)
+    step = pl.program_id(0)
+    gate = dot(r.tok[...], r.kg[step])
+    up = dot(r.tok[...], r.ku[step])
+    back = dot(r.cot[...], r.kd[step], (1, 1))
     for k, value in enumerate((gate, up, back)):
         if hasattr(r, "received"):
             value = value + r.received[k]
@@ -127,14 +143,13 @@
 
 def add_rows(r, tiles):
     step = pl.program_id(0)
-    at = tile_at(r, r.act.shape[2])
 
     @pl.when(step == 0)
     def _():
         r.acc[...] = r.sums[...] if hasattr(r, "sums") else jnp.zeros_like(r.acc)
 
-    r.acc[0] += dot(r.act[0], r.wd[at, :])
-    r.acc[1] += dot(r.act[1], r.wg[:, at], (1, 1)) + dot(r.act[2], r.wu[:, at], (1, 1))
+    r.acc[0] += dot(r.act[0], r.kd[step])
+    r.acc[1] += dot(r.act[1], r.kg[step], (1, 1)) + dot(r.act[2], r.ku[step], (1, 1))
 
     @pl.when(step == tiles - 1)
     def _():
@@ -178,6 +193,7 @@
     split = PIECES if sum(PIECES) * tile == half else [half // tile]
     starts = [sum(split[:p]) for p in range(len(split))]
     direct = n_grid == 4
+    grant = lambda mib: mib if n_grid * tokens.shape[0] <= 64 else min(8 * mib, 40)
 
     core = lax.axis_index("dp") % 2
     firsts = [
@@ -209,79 +225,107 @@
         blocks = [block] + [trade(block, s) for s in range(1, n_grid)]
     else:
         blocks = [lax.all_gather(block, "grid", axis=1, tiled=True)]
-    rows = sum(b.shape[1] for b in blocks)
+    rows = n_grid * tokens.shape[0]
     row_shape = jax.ShapeDtypeStruct((rows, width), BF16)
-    col_shape = jax.ShapeDtypeStruct((width, rows), BF16)
-    bands = width // BLK
-    by_cols = pl.BlockSpec((BLK, units), lambda i, _: (i, 0))
-    by_rows = pl.BlockSpec((units // bands, width), lambda i, _: (i, 0))
-
-    def spread(mask):
-        return pinned(jax.ShapeDtypeStruct((mask.shape[0], 1, mask.shape[1] * BLK), F32))
-
-    kept = call(
-        mask_kernel,
-        "mask",
+    deep_shape = jax.ShapeDtypeStruct((width, rows), BF16)
+    def spread_of(blocks, across):
+        return pinned(jax.ShapeDtypeStruct((blocks, 1, across * BLK), F32))
+
+    spread = call(
+        spread_kernel,
+        "spread",
         none,
-        (bands,),
+        (1,),
         {
-            "mask_gate": (mask_gate, whole(mask_gate)),
-            "mask_up": (mask_up, whole(mask_up)),
-            "mask_down": (mask_down, whole(mask_down)),
-            "w_gate": (hbm(w_gate), by_cols),
-            "w_up": (hbm(w_up), by_cols),
-            "w_down": (hbm(w_down), by_rows),
+            k: (mask, whole(mask))
+            for k, mask in (
+                ("mask_gate", mask_gate),
+                ("mask_up", mask_up),
+                ("mask_down_t", mask_down.T),
+            )
         },
         {
-            "mg": spread(mask_gate),
-            "mu": spread(mask_up),
-            "md": spread(mask_down),
-            "wg": pinned(jax.ShapeDtypeStruct(w_gate.shape, BF16)),
-            "wu": pinned(jax.ShapeDtypeStruct(w_up.shape, BF16)),
-            "wd": pinned(jax.ShapeDtypeStruct(w_down.shape, BF16)),
+            "mg": spread_of(*mask_gate.shape),
+            "mu": spread_of(*mask_up.shape),
+            "md": spread_of(*mask_down.shape),
         },
-        cost=pl.CostEstimate(flops=0, bytes_accessed=6 * width * units, transcendentals=0),
-    )
+    )
+
+    def cost(p, matmuls, mats):
+        step = width * split[p] * tile
+        return pl.CostEstimate(
+            flops=2 * matmuls * rows * step, bytes_accessed=2 * mats * step, transcendentals=0
+        )
+
+    def masking(p):
+        cols = pl.BlockSpec((width, tile), lambda i, first: (0, first[0] + i))
+        downs = pl.BlockSpec((tile, width), lambda i, first: (first[0] + i, 0))
+        by_cols = jax.ShapeDtypeStruct((split[p], width, tile), BF16)
+        by_rows = jax.ShapeDtypeStruct((split[p], tile, width), BF16)
+        ins = {"wg": (hbm(w_gate), cols), "wu": (hbm(w_up), cols), "wd": (hbm(w_down), downs)}
+        ins.update({k: pinned(v) for k, v in spread.items()})
+        return ins, {"kg": pinned(by_cols), "ku": pinned(by_cols), "kd": pinned(by_rows)}
+
+    kept = {}
+    for which, p in AHEAD if direct else []:
+        kept[which, p] = call(
+            keep_masked,
+            "keep_masked",
+            place(which, p),
+            (split[p],),
+            *masking(p),
+            cost=cost(p, 0, 3),
+            vmem=grant(8),
+        )
     gathered = call(
         assemble_kernel,
         "assemble",
         none,
         (1,),
         {
-            "after": (kept["mg"], pl.BlockSpec(memory_space=pl.ANY)),
+            **{f"after{k}": (v["kg"], ANY) for k, v in enumerate(kept.values())},
             **{f"block{k}": (b, whole(b)) for k, b in enumerate(blocks)},
         },
-        {"tok": pinned(row_shape), "cot": pinned(row_shape), "tok_t": pinned(col_shape)},
+        {"tok": pinned(row_shape), "cot": pinned(row_shape), "tok_t": pinned(deep_shape)},
     )
 
     def held(*names):
-        return {k: pinned(kept[k] if k in kept else gathered[k]) for k in names}
+        return {k: pinned(spread[k] if k in spread else gathered[k]) for k in names}
 
     trio = pl.BlockSpec((3, rows, tile), lambda i, idx: (0, 0, i))
 
     def trio_of(p, kind):
         return (jax.ShapeDtypeStruct((3, rows, split[p] * tile), kind), trio)
 
-    def cost(p, matmuls, mats):
-        step = width * split[p] * tile
-        return pl.CostEstimate(
-            flops=2 * matmuls * rows * step, bytes_accessed=2 * mats * step, transcendentals=0
-        )
-
     def partials(which, p, after=None, received=None):
-        ins = held("tok", "cot", "wg", "wu", "wd")
-        outs = {"send": trio_of(p, F32)}
+        ins, outs = held("tok", "cot"), {"send": trio_of(p, F32)}
+        if (which, p) in kept:
+            ins.update({k: pinned(v) for k, v in kept[which, p].items()})
+            masked = {}
+        else:
+            weights, masked = masking(p)
+            ins.update(weights)
         if after is not None:
-            ins["after"] = (after, pl.BlockSpec(memory_space=pl.ANY))
+            ins["after"] = (after, ANY)
         if received is not None:
             ins["received"] = (received, trio)
             outs = {"own": trio_of(p, F32), "send": trio_of(p, BF16)}
-        return call(
-            partial_kernel, "partials", place(which, p), (split[p],), ins, outs, cost=cost(p, 3, 0)
+        got = call(
+            partial_kernel,
+            "partials",
+            place(which, p),
+            (split[p],),
+            ins,
+            {**outs, **masked},
+            cost=cost(p, 3, 3 if masked else 0),
+            vmem=grant(8 if masked else 4),
         )
+        if masked:
+            kept[which, p] = {k: got[k] for k in masked}
+        return got
 
     def activate(own, others, after):
-        ins = {"own": (own, whole(own)), "after": (after, pl.BlockSpec(memory_space=pl.ANY))}
+        ins = {"own": (own, whole(own)), "after": (after, ANY)}
         ins.update({f"other{k}": (a, whole(a)) for k, a in enumerate(others)})
         shape = jax.ShapeDtypeStruct(own.shape, BF16)
         return call(act_kernel, "activate", none, (1,), ins, {"act": (shape, whole(shape))})["act"]
@@ -290,7 +334,7 @@
         ins = {"act": (act, trio)}
         outs, aliases, scratch = {}, {}, {}
         if do_rows:
-            ins.update(held("wg", "wu", "wd"))
+            ins.update({k: pinned(v) for k, v in kept[which, p].items()})
             shape = jax.ShapeDtypeStruct((2, rows, width), F32)
             scratch["acc"] = pltpu.VMEM(shape.shape, F32)
             if "sums" in state:
@@ -310,10 +354,10 @@
             outs["gd"] = (jax.ShapeDtypeStruct((units, width), F32), downs)
             for k in ("gg", "gu", "gd"):
                 if k in state:
-                    ins["old_" + k] = (state[k], pl.BlockSpec(memory_space=pl.ANY))
+                    ins["old_" + k] = (state[k], ANY)
                     aliases["old_" + k] = k
             if "rows0" in state:
-                ins["after"] = (state["rows0"], pl.BlockSpec(memory_space=pl.ANY))
+                ins["after"] = (state["rows0"], ANY)
         got = call(
             functools.partial(back_kernel, do_rows, do_grads, split[p]),
             "_".join(["back"] + ["rows"] * do_rows + ["grads"] * do_grads),
@@ -324,6 +368,7 @@
             scratch=scratch,
             aliases=aliases,
             cost=cost(p, 3 * do_rows + 3 * do_grads, 6 * do_grads),
+            vmem=grant(9 if do_grads else 4),
         )
         return {**state, **{k.replace("new_", ""): v for k, v in got.items()}}
 

time: 111 us -> 88.2 us (0.79)
  local copies, waits for them, and re-layouts: 41.2 us -> 9.91 us
  Pallas kernels: 52.3 us -> 59.5 us
  waiting for transfers between devices: 0.12 us -> 1.51 us
    unnamed x33 -> x70, local copies, waits for them, and re-layouts: 40.6 us -> 9.28 us
    pallas_call x19 -> x22, Pallas kernels: 52.3 us -> 59.5 us  [call(): pl.pallas_call(body, out_shape=[shape for shape, _ in outs.values()], gri...]
    ppermute x3, waiting for transfers between devices: 0.01 us -> 1.29 us  [across(): lax.ppermute(array, 'dp', [(i, (i // 2 + s) % pairs * 2 + i % 2) for i in...]
  transfers between devices with their start and end apart: 15 -> 15, of which waited for: 1 -> 2; matrix products, arithmetic and copies ran while one was open for 1% -> 0% of each run, Pallas kernels for 43% -> 62%
where the time goes in v4:
time: 88.2 us; the launch traced here: 87.6 us
  Pallas kernels  59.5 us (67%)
  starting transfers between devices  14.9 us (17%)
  local copies, waits for them, and re-layouts  9.91 us (11%)
  waiting for transfers between devices  1.51 us (2%)
  between operations  0.98 us (1%)
    pallas_call x22, Pallas kernels, call(): pl.pallas_call(body, out_shape=[shape for shape, _ in outs.values()], gri...  59.5 us
    ppermute x6, starting transfers between devices, trade(): return lax.ppermute(array, 'grid', [(i, i ^ s) for i in range(n_grid)])  10.2 us
    unnamed x70, local copies, waits for them, and re-layouts  9.28 us
    ppermute x3, starting transfers between devices, across(): lax.ppermute(array, 'dp', [(i, (i // 2 + s) % pairs * 2 + i % 2) for i in...  3.68 us
  transfers between devices with their start and end apart: 15, of which 2 were waited for; matrix products, arithmetic and copies ran while one was open for 0% of the time, Pallas kernels for 62%

profile of v4, /device:TPU:0, one launch (start us, length us, event | category | flops | bytes accessed | tf_op | source)
XLA Modules:
  0.0 87.6 jit_solution(14242491899647566958)
XLA Ops:
  0.6 0.8 pad_maximum_fusion.refs_4_
  1.4 5.1 %collective-permute-start.2 = (bf16[2,16,1024]{2,1,0:T(8,128)(2,1)S(1)}, bf16[2,16,1024]{2,1,0:T(8,128)(2,1)S(1)}, u32[]{:S(2)}, u32[]{:S(2)}) collective-permute-start(bf16[2,16,1024]{2,1,0:T(8,128)(2,1)S(1)} %pad_maximum_fusion.refs_4_), channel_id=1, source_target_pairs={{0,12},{4,8},{8,4},{12,0},{1,13},{5,9},{9,5},{13,1},{2,14},{6,10},... | collective-permute-start | bytes 196616 | tf_op jit(solution)/shard_map/ppermute | solution.py:208
  6.5 0.0 collective-permute-start.1
  6.5 0.6 collective-permute-start
  7.2 0.7 copy-done.32
  7.9 0.7 copy-done.33
  8.6 0.7 copy-done.34
  9.2 0.3 spread.1
  9.6 2.1 %keep_masked.5 = (bf16[2,1024,256]{2,1,0:T(8,128)(2,1)S(1)}, bf16[2,1024,256]{2,1,0:T(8,128)(2,1)S(1)}, bf16[2,256,1024]{2,1,0:T(8,128)(2,1)S(1)}) custom-call(s32[1]{0:T(128)} %bitcast.refs_0_, bf16[1024,4096]{1,0:T(8,128)(2,1)} %refs_3_.11, bf16[1024,4096]{1,0:T(8,128)(2,1)} %refs_4_.5, bf16[4096,1024]{1,0:T(8,128)(2,1)} %refs_5_.5, ...), custom_call_target="tpu_custom_call" | custom-call | bytes 3145728 | tf_op jit(solution)/shard_map/keep_masked/pallas_call | solution.py:42
  11.6 1.0 %copy-done.10 = bf16[2,1024,256]{2,1,0:T(8,128)(2,1)} copy-done((bf16[2,1024,256]{2,1,0:T(8,128)(2,1)}, bf16[2,1024,256]{2,1,0:T(8,128)(2,1)S(1)}, u32[]{:S(2)}) %copy-start.10) | copy-done | bytes 1048600
  12.7 3.5 %keep_masked.4 = (bf16[3,1024,256]{2,1,0:T(8,128)(2,1)S(1)}, bf16[3,1024,256]{2,1,0:T(8,128)(2,1)S(1)}, bf16[3,256,1024]{2,1,0:T(8,128)(2,1)S(1)}) custom-call(s32[1]{0:T(128)} %bitcast.4.refs_0_, bf16[1024,4096]{1,0:T(8,128)(2,1)} %refs_3_.11, bf16[1024,4096]{1,0:T(8,128)(2,1)} %refs_4_.5, bf16[4096,1024]{1,0:T(8,128)(2,1)} %refs_5_.5, ...), custom_call_target="tpu_custom_call" | custom-call | bytes 4718592 | tf_op jit(solution)/shard_map/keep_masked/pallas_call | solution.py:42
  16.2 0.0 copy-start.25
  16.2 4.3 %keep_masked.3 = (bf16[3,1024,256]{2,1,0:T(8,128)(2,1)S(1)}, bf16[3,1024,256]{2,1,0:T(8,128)(2,1)S(1)}, bf16[3,256,1024]{2,1,0:T(8,128)(2,1)S(1)}) custom-call(s32[1]{0:T(128)} %bitcast.2.refs_0_, bf16[1024,4096]{1,0:T(8,128)(2,1)} %refs_3_.11, bf16[1024,4096]{1,0:T(8,128)(2,1)} %refs_4_.5, bf16[4096,1024]{1,0:T(8,128)(2,1)} %refs_5_.5, ...), custom_call_target="tpu_custom_call" | custom-call | bytes 4718592 | tf_op jit(solution)/shard_map/keep_masked/pallas_call | solution.py:42
  20.5 0.7 copy-done.26
  21.2 1.1 %copy-done.28 = bf16[2,16,1024]{2,1,0:T(8,128)(2,1)} copy-done((bf16[2,16,1024]{2,1,0:T(8,128)(2,1)}, bf16[2,16,1024]{2,1,0:T(8,128)(2,1)S(1)}, u32[]{:S(2)}) %copy-start.28) | copy-done | bytes 65560
  22.4 0.6 copy-done.30
  23.0 0.8 copy-done.27
  23.8 0.8 copy-done.29
  24.7 0.8 copy-done.31
  25.5 0.1 assemble.1
  25.6 2.3 %partials.6.refs_6_ = f32[3,64,768]{2,1,0:T(8,128)} custom-call(s32[1]{0:T(128)} %bitcast.2.refs_0_, bf16[64,1024]{1,0:T(8,128)(2,1)S(1)} %get-tuple-element.67.refs_1_, bf16[64,1024]{1,0:T(8,128)(2,1)S(1)} %get-tuple-element.68.refs_2_.refs_6_.refs_7_.refs_3_, bf16[3,1024,256]{2,1,0:T(8,128)(2,1)S(1)} %get-tuple-element.64.refs_1_.refs_3_.refs_2_, ...), custom_call_target="tpu_custom_call" | custom-call | flops 301989888 | tf_op jit(solution)/shard_map/partials/pallas_call | solution.py:42
  28.0 0.0 collective-permute-start.3
  28.0 2.4 %partials.7.refs_9_ = f32[3,64,768]{2,1,0:T(8,128)} custom-call(s32[1]{0:T(128)} %bitcast.4.refs_0_, bf16[64,1024]{1,0:T(8,128)(2,1)S(1)} %get-tuple-element.67.refs_1_, bf16[64,1024]{1,0:T(8,128)(2,1)S(1)} %get-tuple-element.68.refs_2_.refs_6_.refs_7_.refs_3_, bf16[3,1024,256]{2,1,0:T(8,128)(2,1)S(1)} %get-tuple-element.65.refs_2_.refs_3_, ...), custom_call_target="tpu_custom_call" | custom-call | flops 301989888 | tf_op jit(solution)/shard_map/partials/pallas_call | solution.py:42
  30.4 0.5 collective-permute-start.4
  30.9 0.0 collective-permute-done.3.refs_10_
  30.9 4.7 %partials.8 = (f32[3,64,768]{2,1,0:T(8,128)S(1)}, bf16[3,64,768]{2,1,0:T(8,128)(2,1)}, bf16[3,1024,256]{2,1,0:T(8,128)(2,1)S(1)}, bf16[3,1024,256]{2,1,0:T(8,128)(2,1)S(1)}, bf16[3,256,1024]{2,1,0:T(8,128)(2,1)S(1)}) custom-call(s32[1]{0:T(128)} %bitcast.8.refs_0_, bf16[64,1024]{1,0:T(8,128)(2,1)S(1)} %get-tuple-element.67.refs_1_, ...), custom_call_target="tpu_custom_call" | custom-call | flops 301989888 | bytes 4718592 | tf_op jit(solution)/shard_map/partials/pallas_call | solution.py:42
  35.6 1.1 %copy-done.22 = bf16[3,256,1024]{2,1,0:T(8,128)(2,1)} copy-done((bf16[3,256,1024]{2,1,0:T(8,128)(2,1)}, bf16[3,256,1024]{2,1,0:T(8,128)(2,1)S(1)}, u32[]{:S(2)}) %copy-start.22) | copy-done | bytes 1572888
  36.8 2.0 %partials.9.refs_9_ = f32[3,64,512]{2,1,0:T(8,128)} custom-call(s32[1]{0:T(128)} %bitcast.refs_0_, bf16[64,1024]{1,0:T(8,128)(2,1)S(1)} %get-tuple-element.67.refs_1_, bf16[64,1024]{1,0:T(8,128)(2,1)S(1)} %get-tuple-element.68.refs_2_.refs_6_.refs_7_.refs_3_, bf16[2,1024,256]{2,1,0:T(8,128)(2,1)S(1)} %get-tuple-element.66.refs_3_.refs_2_, ...), custom_call_target="tpu_custom_call" | custom-call | flops 201326592 | tf_op jit(solution)/shard_map/partials/pallas_call | solution.py:42
  38.8 0.0 collective-permute-start.5
  38.8 1.7 %collective-permute-start.6 = (bf16[3,64,768]{2,1,0:T(8,128)(2,1)}, bf16[3,64,768]{2,1,0:T(8,128)(2,1)}, u32[]{:S(2)}, u32[]{:S(2)}) collective-permute-start(bf16[3,64,768]{2,1,0:T(8,128)(2,1)} %get-tuple-element.78), channel_id=1, source_target_pairs={{0,2},{1,3},{2,0},{3,1},{4,6},{5,7},{6,4},{7,5},{8,10},{9,11},{10,... | collective-permute-start | bytes 884744 | tf_op jit(solution)/shard_map/ppermute | solution.py:215
  40.5 0.0 collective-permute-done.4.refs_10_
  40.5 3.9 %partials.10 = (f32[3,64,768]{2,1,0:T(8,128)S(1)}, bf16[3,64,768]{2,1,0:T(8,128)(2,1)S(1)}, bf16[3,1024,256]{2,1,0:T(8,128)(2,1)S(1)}, bf16[3,1024,256]{2,1,0:T(8,128)(2,1)S(1)}, bf16[3,256,1024]{2,1,0:T(8,128)(2,1)S(1)}) custom-call(s32[1]{0:T(128)} %bitcast.7.refs_0_, bf16[64,1024]{1,0:T(8,128)(2,1)S(1)} %get-tuple-element.67.refs_1_, ...), custom_call_target="tpu_custom_call" | custom-call | flops 301989888 | bytes 4718592 | tf_op jit(solution)/shard_map/partials/pallas_call | solution.py:42
  44.4 0.0 copy-start.19
  44.4 0.0 copy-start.21
  44.4 0.0 copy-start.23
  44.5 0.0 collective-permute-done.5.refs_10_
  44.5 2.7 %partials.11 = (f32[3,64,512]{2,1,0:T(8,128)S(1)}, bf16[3,64,512]{2,1,0:T(8,128)(2,1)S(1)}, bf16[2,1024,256]{2,1,0:T(8,128)(2,1)S(1)}, bf16[2,1024,256]{2,1,0:T(8,128)(2,1)S(1)}, bf16[2,256,1024]{2,1,0:T(8,128)(2,1)S(1)}) custom-call(s32[1]{0:T(128)} %bitcast.1.refs_0_, bf16[64,1024]{1,0:T(8,128)(2,1)S(1)} %get-tuple-element.67.refs_1_, ...), custom_call_target="tpu_custom_call" | custom-call | flops 201326592 | bytes 3145728 | tf_op jit(solution)/shard_map/partials/pallas_call | solution.py:42
  47.2 1.3 %collective-permute-done.6.refs_3_ = bf16[3,64,768]{2,1,0:T(8,128)(2,1)} collective-permute-done((bf16[3,64,768]{2,1,0:T(8,128)(2,1)}, bf16[3,64,768]{2,1,0:T(8,128)(2,1)}, u32[]{:S(2)}, u32[]{:S(2)}) %collective-permute-start.6) | collective-permute-done | bytes 294944 | tf_op jit(solution)/shard_map/ppermute | solution.py:215
  48.5 1.1 %activate.3.refs_1_ = bf16[3,64,768]{2,1,0:T(8,128)(2,1)S(1)} custom-call(s32[1]{0:T(128)} %constant.24.clone.1.refs_0_, f32[3,64,768]{2,1,0:T(8,128)S(1)} %copy-done.17, f32[3,64,512]{2,1,0:T(8,128)S(1)} %get-tuple-element.77.refs_2_.refs_1_, bf16[3,64,768]{2,1,0:T(8,128)(2,1)} %collective-permute-done.6.refs_3_), custom_call_target="tpu_custom_call" | custom-call | tf_op jit(solution)/shard_map/activate/pallas_call | solution.py:42
  49.6 0.1 collective-permute-start.7
  49.8 1.6 %collective-permute-start.8 = (bf16[3,64,768]{2,1,0:T(8,128)(2,1)S(1)}, bf16[3,64,768]{2,1,0:T(8,128)(2,1)S(1)}, u32[]{:S(2)}, u32[]{:S(2)}) collective-permute-start(bf16[3,64,768]{2,1,0:T(8,128)(2,1)S(1)} %get-tuple-element.88), channel_id=1, source_target_pairs={{0,2},{1,3},{2,0},{3,1},{4,6},{5,7},{6,4},{7,5},{8,10},{9,11},{10,... | collective-permute-start | bytes 884744 | tf_op jit(solution)/shard_map/ppermute | solution.py:215
  51.4 5.3 %back_rows_grads.4 = (f32[2,64,1024]{2,1,0:T(8,128)S(1)}, f32[1024,4096]{1,0:T(8,128)}, f32[1024,4096]{1,0:T(8,128)}, f32[4096,1024]{1,0:T(8,128)}) custom-call(s32[1]{0:T(128)} %bitcast.8.refs_0_, bf16[3,64,768]{2,1,0:T(8,128)(2,1)S(1)} %activate.3.refs_1_, bf16[3,1024,256]{2,1,0:T(8,128)(2,1)S(1)} %copy-done.19, bf16[3,1024,256]{2,1,0:T(8,128)(2,1)S(1)} %copy-done.21, ...), custom_call_target="tpu_custom_call" | custom-call | flops 603979776 | bytes 9437184 | tf_op jit(solution)/shard_map/back_rows_grads/pallas_call | solution.py:42
  56.7 0.0 collective-permute-done.7.refs_1_
  56.7 5.3 %back_rows_grads.5 = (f32[2,64,1024]{2,1,0:T(8,128)S(1)}, f32[1024,4096]{1,0:T(8,128)}, f32[1024,4096]{1,0:T(8,128)}, f32[4096,1024]{1,0:T(8,128)}) custom-call(s32[1]{0:T(128)} %bitcast.2.refs_0_, bf16[3,64,768]{2,1,0:T(8,128)(2,1)S(1)} %collective-permute-done.7.refs_1_, ...), custom_call_target="tpu_custom_call", output_to_operand_aliasing={{1}: (11, {}), {2}: (12, {}), {3}: (13, {})} | custom-call | flops 603979776 | bytes 9437184 | tf_op jit(solution)/shard_map/back_rows_grads/pallas_call | solution.py:42
  62.0 0.2 activate.4.refs_1_
  62.2 0.2 collective-permute-start.9
  62.4 0.4 collective-permute-start.10
  62.8 5.3 %back_rows_grads.6 = (f32[2,64,1024]{2,1,0:T(8,128)S(1)}, f32[1024,4096]{1,0:T(8,128)}, f32[1024,4096]{1,0:T(8,128)}, f32[4096,1024]{1,0:T(8,128)}) custom-call(s32[1]{0:T(128)} %bitcast.7.refs_0_, bf16[3,64,768]{2,1,0:T(8,128)(2,1)S(1)} %activate.4.refs_1_, ...), custom_call_target="tpu_custom_call", output_to_operand_aliasing={{1}: (11, {}), {2}: (12, {}), {3}: (13, {})} | custom-call | flops 603979776 | bytes 9437184 | tf_op jit(solution)/shard_map/back_rows_grads/pallas_call | solution.py:42
  68.1 0.0 collective-permute-done.9.refs_1_
  68.1 5.3 %back_rows_grads.7 = (f32[2,64,1024]{2,1,0:T(8,128)S(1)}, f32[1024,4096]{1,0:T(8,128)}, f32[1024,4096]{1,0:T(8,128)}, f32[4096,1024]{1,0:T(8,128)}) custom-call(s32[1]{0:T(128)} %bitcast.4.refs_0_, bf16[3,64,768]{2,1,0:T(8,128)(2,1)S(1)} %collective-permute-done.9.refs_1_, ...), custom_call_target="tpu_custom_call", output_to_operand_aliasing={{1}: (11, {}), {2}: (12, {}), {3}: (13, {})} | custom-call | flops 603979776 | bytes 9437184 | tf_op jit(solution)/shard_map/back_rows_grads/pallas_call | solution.py:42
  73.4 0.1 activate.5.refs_1_
  73.5 0.1 collective-permute-start.11
  73.7 1.2 %back_rows.2.refs_5_ = f32[2,64,1024]{2,1,0:T(8,128)S(1)} custom-call(s32[1]{0:T(128)} %bitcast.1.refs_0_, bf16[3,64,512]{2,1,0:T(8,128)(2,1)S(1)} %activate.5.refs_1_, bf16[2,1024,256]{2,1,0:T(8,128)(2,1)S(1)} %get-tuple-element.101.refs_2_, bf16[2,1024,256]{2,1,0:T(8,128)(2,1)S(1)} %get-tuple-element.102.refs_3_, ...), custom_call_target="tpu_custom_call" | custom-call | flops 201326592 | tf_op jit(solution)/shard_map/back_rows/pallas_call | solution.py:42
  74.9 0.2 collective-permute-done.11.refs_1_
  75.0 1.2 %back_rows.3 = (bf16[2,16,1024]{2,1,0:T(8,128)(2,1)S(1)}, bf16[2,16,1024]{2,1,0:T(8,128)(2,1)S(1)}, bf16[2,16,1024]{2,1,0:T(8,128)(2,1)S(1)}, bf16[2,16,1024]{2,1,0:T(8,128)(2,1)S(1)}) custom-call(s32[1]{0:T(128)} %bitcast.refs_0_, bf16[3,64,512]{2,1,0:T(8,128)(2,1)S(1)} %collective-permute-done.11.refs_1_, ...), custom_call_target="tpu_custom_call" | custom-call | flops 201326592 | tf_op jit(solution)/shard_map/back_rows/pallas_call | solution.py:42
  76.2 1.4 %collective-permute-start.12 = (bf16[2,16,1024]{2,1,0:T(8,128)(2,1)S(1)}, bf16[2,16,1024]{2,1,0:T(8,128)(2,1)S(1)}, u32[]{:S(2)}, u32[]{:S(2)}) collective-permute-start(bf16[2,16,1024]{2,1,0:T(8,128)(2,1)S(1)} %get-tuple-element.105), channel_id=1, source_target_pairs={{0,4},{4,0},{8,12},{12,8},{1,5},{5,1},{9,13},{13,9},{2,6},{6,2},{1... | collective-permute-start | bytes 196616 | tf_op jit(solution)/shard_map/ppermute | solution.py:208
  77.7 2.9 %collective-permute-start.13 = (bf16[2,16,1024]{2,1,0:T(8,128)(2,1)S(1)}, bf16[2,16,1024]{2,1,0:T(8,128)(2,1)S(1)}, u32[]{:S(2)}, u32[]{:S(2)}) collective-permute-start(bf16[2,16,1024]{2,1,0:T(8,128)(2,1)S(1)} %get-tuple-element.106), channel_id=1, source_target_pairs={{0,8},{4,12},{8,0},{12,4},{1,9},{5,13},{9,1},{13,5},{2,10},{6,14},... | collective-permute-start | bytes 196616 | tf_op jit(solution)/shard_map/ppermute | solution.py:208
  80.6 0.1 collective-permute-start.14
  80.7 3.1 %back_grads.2 = (f32[1024,4096]{1,0:T(8,128)}, f32[1024,4096]{1,0:T(8,128)}, f32[4096,1024]{1,0:T(8,128)}) custom-call(s32[1]{0:T(128)} %bitcast.1.refs_0_, bf16[3,64,512]{2,1,0:T(8,128)(2,1)S(1)} %activate.5.refs_1_, bf16[1024,64]{1,0:T(8,128)(2,1)S(1)} %get-tuple-element.82.refs_5_.refs_6_.refs_2_, ...), custom_call_target="tpu_custom_call", output_to_operand_aliasing={{0}: (7, {}), {1}: (8, {}), {2}: (9, {})} | custom-call | flops 201326592 | bytes 6291456 | tf_op jit(solution)/shard_map/back_grads/pallas_call | solution.py:42
  83.8 3.1 %back_grads.3 = (f32[1024,4096]{1,0:T(8,128)}, f32[1024,4096]{1,0:T(8,128)}, f32[4096,1024]{1,0:T(8,128)}) custom-call(s32[1]{0:T(128)} %bitcast.refs_0_, bf16[3,64,512]{2,1,0:T(8,128)(2,1)S(1)} %collective-permute-done.11.refs_1_, ...), custom_call_target="tpu_custom_call", output_to_operand_aliasing={{0}: (7, {}), {1}: (8, {}), {2}: (9, {})} | custom-call | flops 201326592 | bytes 6291456 | tf_op jit(solution)/shard_map/back_grads/pallas_call | solution.py:42
  86.9 0.0 collective-permute-done.12
  86.9 0.0 collective-permute-done.13
  86.9 0.0 collective-permute-done.14
  87.0 0.6 slice_bitcast_fusion
  (61 shorter events, 0.2 us)
Async XLA Ops:
  1.4 14.7 %copy-start.24 = (bf16[2,16,1024]{2,1,0:T(8,128)(2,1)}, bf16[2,16,1024]{2,1,0:T(8,128)(2,1)S(1)}, u32[]{:S(2)}) copy-start(bf16[2,16,1024]{2,1,0:T(8,128)(2,1)S(1)} %pad_maximum_fusion.refs_4_) | copy-start | bytes 196612
  1.4 19.1 %collective-permute-start.2 = (bf16[2,16,1024]{2,1,0:T(8,128)(2,1)S(1)}, bf16[2,16,1024]{2,1,0:T(8,128)(2,1)S(1)}, u32[]{:S(2)}, u32[]{:S(2)}) collective-permute-start(bf16[2,16,1024]{2,1,0:T(8,128)(2,1)S(1)} %pad_maximum_fusion.refs_4_), channel_id=1, source_target_pairs={{0,12},{4,8},{8,4},{12,0},{1,13},{5,9},{9,5},{13,1},{2,14},{6,10},... | collective-permute-start | bytes 196616 | tf_op jit(solution)/shard_map/ppermute | solution.py:208
  6.5 14.7 %collective-permute-start.1 = (bf16[2,16,1024]{2,1,0:T(8,128)(2,1)S(1)}, bf16[2,16,1024]{2,1,0:T(8,128)(2,1)S(1)}, u32[]{:S(2)}, u32[]{:S(2)}) collective-permute-start(bf16[2,16,1024]{2,1,0:T(8,128)(2,1)S(1)} %pad_maximum_fusion.refs_4_), channel_id=1, source_target_pairs={{0,8},{4,12},{8,0},{12,4},{1,9},{5,13},{9,1},{13,5},{2,10},{6,14},... | collective-permute-start | bytes 196616 | tf_op jit(solution)/shard_map/ppermute | solution.py:208
  6.5 15.8 %collective-permute-start = (bf16[2,16,1024]{2,1,0:T(8,128)(2,1)S(1)}, bf16[2,16,1024]{2,1,0:T(8,128)(2,1)S(1)}, u32[]{:S(2)}, u32[]{:S(2)}) collective-permute-start(bf16[2,16,1024]{2,1,0:T(8,128)(2,1)S(1)} %pad_maximum_fusion.refs_4_), channel_id=1, source_target_pairs={{0,4},{4,0},{8,12},{12,8},{1,5},{5,1},{9,13},{13,9},{2,6},{6,2},{1... | collective-permute-start | bytes 196616 | tf_op jit(solution)/shard_map/ppermute | solution.py:208
  7.2 0.7 copy-start.32
  7.9 0.7 copy-start.33
  8.6 0.7 copy-start.34
  11.6 1.0 %copy-start.10 = (bf16[2,1024,256]{2,1,0:T(8,128)(2,1)}, bf16[2,1024,256]{2,1,0:T(8,128)(2,1)S(1)}, u32[]{:S(2)}) copy-start(bf16[2,1024,256]{2,1,0:T(8,128)(2,1)S(1)} %get-tuple-element.69.refs_4_.refs_3_) | copy-start | bytes 3145732
  12.6 3.5 %copy-start.13 = (bf16[2,256,1024]{2,1,0:T(8,128)(2,1)}, bf16[2,256,1024]{2,1,0:T(8,128)(2,1)S(1)}, u32[]{:S(2)}) copy-start(bf16[2,256,1024]{2,1,0:T(8,128)(2,1)S(1)} %get-tuple-element.70.refs_5_.refs_4_) | copy-start | bytes 3145732
  16.2 11.8 %copy-start.2 = (bf16[3,1024,256]{2,1,0:T(8,128)(2,1)}, bf16[3,1024,256]{2,1,0:T(8,128)(2,1)S(1)}, u32[]{:S(2)}) copy-start(bf16[3,1024,256]{2,1,0:T(8,128)(2,1)S(1)} %get-tuple-element.71.refs_4_.refs_3_) | copy-start | bytes 4718596
  16.2 11.8 %copy-start.4 = (bf16[3,256,1024]{2,1,0:T(8,128)(2,1)}, bf16[3,256,1024]{2,1,0:T(8,128)(2,1)S(1)}, u32[]{:S(2)}) copy-start(bf16[3,256,1024]{2,1,0:T(8,128)(2,1)S(1)} %get-tuple-element.72.refs_5_.refs_4_) | copy-start | bytes 4718596
  16.2 6.8 %copy-start.25 = (bf16[2,16,1024]{2,1,0:T(8,128)(2,1)S(1)}, bf16[2,16,1024]{2,1,0:T(8,128)(2,1)}, u32[]{:S(2)}) copy-start(bf16[2,16,1024]{2,1,0:T(8,128)(2,1)} %copy-done.24) | copy-start | bytes 196612
  20.5 5.2 %copy-start = (bf16[3,1024,256]{2,1,0:T(8,128)(2,1)}, bf16[3,1024,256]{2,1,0:T(8,128)(2,1)S(1)}, u32[]{:S(2)}) copy-start(bf16[3,1024,256]{2,1,0:T(8,128)(2,1)S(1)} %get-tuple-element.64.refs_1_.refs_3_.refs_2_) | copy-start | bytes 4718596
  20.5 7.5 %copy-start.6 = (bf16[3,1024,256]{2,1,0:T(8,128)(2,1)}, bf16[3,1024,256]{2,1,0:T(8,128)(2,1)S(1)}, u32[]{:S(2)}) copy-start(bf16[3,1024,256]{2,1,0:T(8,128)(2,1)S(1)} %get-tuple-element.73.refs_4_.refs_3_) | copy-start | bytes 4718596
  20.5 9.9 %copy-start.8 = (bf16[3,256,1024]{2,1,0:T(8,128)(2,1)}, bf16[3,256,1024]{2,1,0:T(8,128)(2,1)S(1)}, u32[]{:S(2)}) copy-start(bf16[3,256,1024]{2,1,0:T(8,128)(2,1)S(1)} %get-tuple-element.74.refs_5_.refs_4_) | copy-start | bytes 4718596
  20.5 0.7 copy-start.26
  21.2 1.1 %copy-start.28 = (bf16[2,16,1024]{2,1,0:T(8,128)(2,1)}, bf16[2,16,1024]{2,1,0:T(8,128)(2,1)S(1)}, u32[]{:S(2)}) copy-start(bf16[2,16,1024]{2,1,0:T(8,128)(2,1)S(1)} %collective-permute-done.1.refs_6_) | copy-start | bytes 196612
  22.4 0.6 copy-start.30
  23.0 0.8 copy-start.27
  23.8 0.8 copy-start.29
  24.7 0.8 copy-start.31
  28.0 2.9 %collective-permute-start.3 = (f32[3,64,768]{2,1,0:T(8,128)}, f32[3,64,768]{2,1,0:T(8,128)}, u32[]{:S(2)}, u32[]{:S(2)}) collective-permute-start(f32[3,64,768]{2,1,0:T(8,128)} %partials.6.refs_6_), channel_id=1, source_target_pairs={{0,1},{1,0},{2,3},{3,2},{4,5},{5,4},{6,7},{7,6},{8,9},{9,8},{10,11... | collective-permute-start | bytes 1769480 | tf_op jit(solution)/shard_map/ppermute | solution.py:211
  30.4 10.1 %collective-permute-start.4 = (f32[3,64,768]{2,1,0:T(8,128)}, f32[3,64,768]{2,1,0:T(8,128)}, u32[]{:S(2)}, u32[]{:S(2)}) collective-permute-start(f32[3,64,768]{2,1,0:T(8,128)} %partials.7.refs_9_), channel_id=1, source_target_pairs={{0,1},{1,0},{2,3},{3,2},{4,5},{5,4},{6,7},{7,6},{8,9},{9,8},{10,11... | collective-permute-start | bytes 1769480 | tf_op jit(solution)/shard_map/ppermute | solution.py:211
  30.9 5.9 %copy-start.11 = (bf16[2,1024,256]{2,1,0:T(8,128)(2,1)S(1)}, bf16[2,1024,256]{2,1,0:T(8,128)(2,1)}, u32[]{:S(2)}) copy-start(bf16[2,1024,256]{2,1,0:T(8,128)(2,1)} %copy-done.10) | copy-start | bytes 3145732
  30.9 5.9 %copy-start.14 = (bf16[2,256,1024]{2,1,0:T(8,128)(2,1)S(1)}, bf16[2,256,1024]{2,1,0:T(8,128)(2,1)}, u32[]{:S(2)}) copy-start(bf16[2,256,1024]{2,1,0:T(8,128)(2,1)} %copy-done.13) | copy-start | bytes 3145732
  35.6 1.1 %copy-start.22 = (bf16[3,256,1024]{2,1,0:T(8,128)(2,1)}, bf16[3,256,1024]{2,1,0:T(8,128)(2,1)S(1)}, u32[]{:S(2)}) copy-start(bf16[3,256,1024]{2,1,0:T(8,128)(2,1)S(1)} %get-tuple-element.81.refs_4_) | copy-start | bytes 4718596
  36.7 2.0 %copy-start.16 = (f32[3,64,768]{2,1,0:T(8,128)}, f32[3,64,768]{2,1,0:T(8,128)S(1)}, u32[]{:S(2)}) copy-start(f32[3,64,768]{2,1,0:T(8,128)S(1)} %get-tuple-element.75.refs_6_.refs_1_) | copy-start | bytes 1769476
  36.7 2.1 %copy-start.18 = (bf16[3,1024,256]{2,1,0:T(8,128)(2,1)}, bf16[3,1024,256]{2,1,0:T(8,128)(2,1)S(1)}, u32[]{:S(2)}) copy-start(bf16[3,1024,256]{2,1,0:T(8,128)(2,1)S(1)} %get-tuple-element.79.refs_2_) | copy-start | bytes 4718596
  36.8 2.1 %copy-start.20 = (bf16[3,1024,256]{2,1,0:T(8,128)(2,1)}, bf16[3,1024,256]{2,1,0:T(8,128)(2,1)S(1)}, u32[]{:S(2)}) copy-start(bf16[3,1024,256]{2,1,0:T(8,128)(2,1)S(1)} %get-tuple-element.80.refs_3_) | copy-start | bytes 4718596
  38.8 5.7 %collective-permute-start.5 = (f32[3,64,512]{2,1,0:T(8,128)}, f32[3,64,512]{2,1,0:T(8,128)}, u32[]{:S(2)}, u32[]{:S(2)}) collective-permute-start(f32[3,64,512]{2,1,0:T(8,128)} %partials.9.refs_9_), channel_id=1, source_target_pairs={{0,1},{1,0},{2,3},{3,2},{4,5},{5,4},{6,7},{7,6},{8,9},{9,8},{10,11... | collective-permute-start | bytes 1179656 | tf_op jit(solution)/shard_map/ppermute | solution.py:211
  38.8 9.7 %collective-permute-start.6 = (bf16[3,64,768]{2,1,0:T(8,128)(2,1)}, bf16[3,64,768]{2,1,0:T(8,128)(2,1)}, u32[]{:S(2)}, u32[]{:S(2)}) collective-permute-start(bf16[3,64,768]{2,1,0:T(8,128)(2,1)} %get-tuple-element.78), channel_id=1, source_target_pairs={{0,2},{1,3},{2,0},{3,1},{4,6},{5,7},{6,4},{7,5},{8,10},{9,11},{10,... | collective-permute-start | bytes 884744 | tf_op jit(solution)/shard_map/ppermute | solution.py:215
  44.4 4.1 %copy-start.17 = (f32[3,64,768]{2,1,0:T(8,128)S(1)}, f32[3,64,768]{2,1,0:T(8,128)}, u32[]{:S(2)}) copy-start(f32[3,64,768]{2,1,0:T(8,128)} %copy-done.16) | copy-start | bytes 1769476
  44.4 7.0 %copy-start.19 = (bf16[3,1024,256]{2,1,0:T(8,128)(2,1)S(1)}, bf16[3,1024,256]{2,1,0:T(8,128)(2,1)}, u32[]{:S(2)}) copy-start(bf16[3,1024,256]{2,1,0:T(8,128)(2,1)} %copy-done.18) | copy-start | bytes 4718596
  44.4 7.0 %copy-start.21 = (bf16[3,1024,256]{2,1,0:T(8,128)(2,1)S(1)}, bf16[3,1024,256]{2,1,0:T(8,128)(2,1)}, u32[]{:S(2)}) copy-start(bf16[3,1024,256]{2,1,0:T(8,128)(2,1)} %copy-done.20) | copy-start | bytes 4718596
  44.4 7.0 %copy-start.23 = (bf16[3,256,1024]{2,1,0:T(8,128)(2,1)S(1)}, bf16[3,256,1024]{2,1,0:T(8,128)(2,1)}, u32[]{:S(2)}) copy-start(bf16[3,256,1024]{2,1,0:T(8,128)(2,1)} %copy-done.22) | copy-start | bytes 4718596
  44.5 12.2 %copy-start.1 = (bf16[3,1024,256]{2,1,0:T(8,128)(2,1)S(1)}, bf16[3,1024,256]{2,1,0:T(8,128)(2,1)}, u32[]{:S(2)}) copy-start(bf16[3,1024,256]{2,1,0:T(8,128)(2,1)} %copy-done) | copy-start | bytes 4718596
  44.5 12.2 %copy-start.7 = (bf16[3,1024,256]{2,1,0:T(8,128)(2,1)S(1)}, bf16[3,1024,256]{2,1,0:T(8,128)(2,1)}, u32[]{:S(2)}) copy-start(bf16[3,1024,256]{2,1,0:T(8,128)(2,1)} %copy-done.6) | copy-start | bytes 4718596
  44.5 12.2 %copy-start.9 = (bf16[3,256,1024]{2,1,0:T(8,128)(2,1)S(1)}, bf16[3,256,1024]{2,1,0:T(8,128)(2,1)}, u32[]{:S(2)}) copy-start(bf16[3,256,1024]{2,1,0:T(8,128)(2,1)} %copy-done.8) | copy-start | bytes 4718596
  49.6 7.1 %collective-permute-start.7 = (bf16[3,64,768]{2,1,0:T(8,128)(2,1)S(1)}, bf16[3,64,768]{2,1,0:T(8,128)(2,1)S(1)}, u32[]{:S(2)}, u32[]{:S(2)}) collective-permute-start(bf16[3,64,768]{2,1,0:T(8,128)(2,1)S(1)} %activate.3.refs_1_), channel_id=1, source_target_pairs={{0,1},{1,0},{2,3},{3,2},{4,5},{5,4},{6,7},{7,6},{8,9},{9,8},{10,11... | collective-permute-start | bytes 884744 | tf_op jit(solution)/shard_map/ppermute | solution.py:211
  49.8 12.3 %collective-permute-start.8 = (bf16[3,64,768]{2,1,0:T(8,128)(2,1)S(1)}, bf16[3,64,768]{2,1,0:T(8,128)(2,1)S(1)}, u32[]{:S(2)}, u32[]{:S(2)}) collective-permute-start(bf16[3,64,768]{2,1,0:T(8,128)(2,1)S(1)} %get-tuple-element.88), channel_id=1, source_target_pairs={{0,2},{1,3},{2,0},{3,1},{4,6},{5,7},{6,4},{7,5},{8,10},{9,11},{10,... | collective-permute-start | bytes 884744 | tf_op jit(solution)/shard_map/ppermute | solution.py:215
  62.2 5.9 %collective-permute-start.9 = (bf16[3,64,768]{2,1,0:T(8,128)(2,1)S(1)}, bf16[3,64,768]{2,1,0:T(8,128)(2,1)S(1)}, u32[]{:S(2)}, u32[]{:S(2)}) collective-permute-start(bf16[3,64,768]{2,1,0:T(8,128)(2,1)S(1)} %activate.4.refs_1_), channel_id=1, source_target_pairs={{0,1},{1,0},{2,3},{3,2},{4,5},{5,4},{6,7},{7,6},{8,9},{9,8},{10,11... | collective-permute-start | bytes 884744 | tf_op jit(solution)/shard_map/ppermute | solution.py:211
  62.4 11.0 %collective-permute-start.10 = (bf16[3,64,512]{2,1,0:T(8,128)(2,1)S(1)}, bf16[3,64,512]{2,1,0:T(8,128)(2,1)S(1)}, u32[]{:S(2)}, u32[]{:S(2)}) collective-permute-start(bf16[3,64,512]{2,1,0:T(8,128)(2,1)S(1)} %get-tuple-element.100), channel_id=1, source_target_pairs={{0,2},{1,3},{2,0},{3,1},{4,6},{5,7},{6,4},{7,5},{8,10},{9,11},{10,... | collective-permute-start | bytes 589832 | tf_op jit(solution)/shard_map/ppermute | solution.py:215
  62.8 5.3 %copy-start.3 = (bf16[3,1024,256]{2,1,0:T(8,128)(2,1)S(1)}, bf16[3,1024,256]{2,1,0:T(8,128)(2,1)}, u32[]{:S(2)}) copy-start(bf16[3,1024,256]{2,1,0:T(8,128)(2,1)} %copy-done.2) | copy-start | bytes 4718596
  62.8 5.3 %copy-start.5 = (bf16[3,256,1024]{2,1,0:T(8,128)(2,1)S(1)}, bf16[3,256,1024]{2,1,0:T(8,128)(2,1)}, u32[]{:S(2)}) copy-start(bf16[3,256,1024]{2,1,0:T(8,128)(2,1)} %copy-done.4) | copy-start | bytes 4718596
  68.1 6.9 %copy-start.12 = (bf16[2,1024,256]{2,1,0:T(8,128)(2,1)S(1)}, bf16[2,1024,256]{2,1,0:T(8,128)(2,1)}, u32[]{:S(2)}) copy-start(bf16[2,1024,256]{2,1,0:T(8,128)(2,1)} %copy-done.10) | copy-start | bytes 3145732
  68.1 6.9 %copy-start.15 = (bf16[2,256,1024]{2,1,0:T(8,128)(2,1)S(1)}, bf16[2,256,1024]{2,1,0:T(8,128)(2,1)}, u32[]{:S(2)}) copy-start(bf16[2,256,1024]{2,1,0:T(8,128)(2,1)} %copy-done.13) | copy-start | bytes 3145732
  73.5 1.5 %collective-permute-start.11 = (bf16[3,64,512]{2,1,0:T(8,128)(2,1)S(1)}, bf16[3,64,512]{2,1,0:T(8,128)(2,1)S(1)}, u32[]{:S(2)}, u32[]{:S(2)}) collective-permute-start(bf16[3,64,512]{2,1,0:T(8,128)(2,1)S(1)} %activate.5.refs_1_), channel_id=1, source_target_pairs={{0,1},{1,0},{2,3},{3,2},{4,5},{5,4},{6,7},{7,6},{8,9},{9,8},{10,11... | collective-permute-start | bytes 589832 | tf_op jit(solution)/shard_map/ppermute | solution.py:211
  76.2 10.7 %collective-permute-start.12 = (bf16[2,16,1024]{2,1,0:T(8,128)(2,1)S(1)}, bf16[2,16,1024]{2,1,0:T(8,128)(2,1)S(1)}, u32[]{:S(2)}, u32[]{:S(2)}) collective-permute-start(bf16[2,16,1024]{2,1,0:T(8,128)(2,1)S(1)} %get-tuple-element.105), channel_id=1, source_target_pairs={{0,4},{4,0},{8,12},{12,8},{1,5},{5,1},{9,13},{13,9},{2,6},{6,2},{1... | collective-permute-start | bytes 196616 | tf_op jit(solution)/shard_map/ppermute | solution.py:208
  77.7 9.3 %collective-permute-start.13 = (bf16[2,16,1024]{2,1,0:T(8,128)(2,1)S(1)}, bf16[2,16,1024]{2,1,0:T(8,128)(2,1)S(1)}, u32[]{:S(2)}, u32[]{:S(2)}) collective-permute-start(bf16[2,16,1024]{2,1,0:T(8,128)(2,1)S(1)} %get-tuple-element.106), channel_id=1, source_target_pairs={{0,8},{4,12},{8,0},{12,4},{1,9},{5,13},{9,1},{13,5},{2,10},{6,14},... | collective-permute-start | bytes 196616 | tf_op jit(solution)/shard_map/ppermute | solution.py:208
  80.6 6.3 %collective-permute-start.14 = (bf16[2,16,1024]{2,1,0:T(8,128)(2,1)S(1)}, bf16[2,16,1024]{2,1,0:T(8,128)(2,1)S(1)}, u32[]{:S(2)}, u32[]{:S(2)}) collective-permute-start(bf16[2,16,1024]{2,1,0:T(8,128)(2,1)S(1)} %get-tuple-element.107), channel_id=1, source_target_pairs={{0,12},{4,8},{8,4},{12,0},{1,13},{5,9},{9,5},{13,1},{2,14},{6,10},... | collective-permute-start | bytes 196616 | tf_op jit(solution)/shard_map/ppermute | solution.py:208

commit v5 on v4

--- a/solution.py
+++ b/solution.py
@@ -9,11 +9,10 @@
 from jax.sharding import PartitionSpec as P
 
 BLK = 128
+MIB = 1024 * 1024
 DEPTH = 256
 ANY = pl.BlockSpec(memory_space=pl.ANY)
 PIECES = [3, 3, 2]
-AHEAD = [(1, 0), (1, 1), (1, 2)]
-MIB = 1024 * 1024
 F32 = jnp.float32
 BF16 = jnp.bfloat16
 
@@ -77,51 +76,78 @@
         column = lax.broadcasted_iota(jnp.int32, (blocks, blocks * BLK), 1)
         return ((column >= at) & (column < at + BLK)).astype(F32).astype(BF16)
 
-    def entries(mask):
-        return mask[...].astype(F32).astype(BF16)
-
-    wide = pattern(r.mask_gate.shape[1])
-    gate, up = dot(entries(r.mask_gate), wide), dot(entries(r.mask_up), wide)
-    down = dot(entries(r.mask_down_t), pattern(r.mask_down_t.shape[0]), (0, 0))
-    for value, out in ((gate, r.mg), (up, r.mu), (down, r.md)):
-        for b in range(out.shape[0]):
-            out[b] = value[b : b + 1, :]
+    across, along = r.mask_gate.shape
+    units, features = pattern(along), pattern(across)
+    for mask, by_units, by_features in (
+        (r.mask_gate, r.mg, r.mgt),
+        (r.mask_up, r.mu, r.mut),
+        (r.mask_down_t, r.mdt, r.md),
+    ):
+        entries = mask[...].astype(F32).astype(BF16)
+        value = dot(entries, units)
+        for b in range(across):
+            by_units[b] = value[b : b + 1, :]
+        value = dot(entries, features, (0, 0))
+        for b in range(along):
+            by_features[b] = value[b : b + 1, :]
+
+
+def diagonal(out, value, start=0):
+    rows, size = value.shape
+    for b in range(size // BLK):
+        band = slice(b * BLK, (b + 1) * BLK)
+        out[start + b * rows : start + (b + 1) * rows, band] = value[:, band]
 
 
 def assemble_kernel(r):
     blocks = [ref for name, ref in vars(r).items() if name.startswith("block")]
     rows = blocks[0].shape[1]
-    for k, block in enumerate(blocks):
-        r.tok[k * rows : (k + 1) * rows, :] = block[0]
-        r.cot[k * rows : (k + 1) * rows, :] = block[1]
-    r.tok_t[...] = r.tok[...].T
+    tok = jnp.concatenate([block[0] for block in blocks], axis=0)
+    cot = jnp.concatenate([block[1] for block in blocks], axis=0)
+    r.cot[...] = cot
+    rows, width = cot.shape
+    pair = r.tok_d.shape[2] // BLK
+    r.tok_d[...] = jnp.zeros_like(r.tok_d)
+    r.cot_d[...] = jnp.zeros_like(r.cot_d)
+    for p in range(width // (pair * BLK)):
+        part = slice(p * pair * BLK, (p + 1) * pair * BLK)
+        diagonal(r.tok_d.at[p], tok[:, part])
+        diagonal(r.cot_d.at[p], cot[:, part])
+    deep = stack(rows, width // BLK)
+    r.bands[...] = jnp.zeros_like(r.bands)
+    for b in range(width // BLK):
+        band = slice(b * BLK, (b + 1) * BLK)
+        slot = slice((b % deep) * rows, (b % deep + 1) * rows)
+        r.bands[slot, band] = tok[:, band]
+    r.tok_t[...] = r.bands[...].T
 
 
 def tile_at(r, tile):
     return pl.ds(pl.multiple_of((r.place[0] + pl.program_id(0)) * tile, tile), tile)
 
 
-def keep_masked(r):
-    tile = r.wg.shape[1]
-    step, at = pl.program_id(0), tile_at(r, tile)
-    for w, mask, out in ((r.wg, r.mg, r.kg), (r.wu, r.mu, r.ku)):
-        for b in range(w.shape[0] // BLK):
-            band = slice(b * BLK, (b + 1) * BLK)
-            out[step, band, :] = w[band, :] * mask[b, :, at].astype(BF16)
-    for b in range(tile // BLK):
-        band = slice(b * BLK, (b + 1) * BLK)
-        keep = r.md[(r.place[0] + step) * (tile // BLK) + b].astype(BF16)
-        r.kd[step, band, :] = r.wd[band, :] * keep
+def masked_sum(left, right, masks, dims=(1, 0)):
+    value = dot(left, right, dims)
+    rows = value.shape[0] // len(masks)
+    return sum(value[b * rows : (b + 1) * rows, :] * m for b, m in enumerate(masks))
 
 
 def partial_kernel(r):
-    if hasattr(r, "wg"):
-        keep_masked(r)
-    step = pl.program_id(0)
-    gate = dot(r.tok[...], r.kg[step])
-    up = dot(r.tok[...], r.ku[step])
-    back = dot(r.cot[...], r.kd[step], (1, 1))
-    for k, value in enumerate((gate, up, back)):
+    at = tile_at(r, r.send.shape[2])
+    pairs, _, size = r.tok_d.shape
+    totals = [0.0, 0.0, 0.0]
+    for p in range(pairs):
+        part = slice(p * size, (p + 1) * size)
+        bands = range(p * size // BLK, (p + 1) * size // BLK)
+        for k, (left, right, mask, dims) in enumerate(
+            (
+                (r.tok_d[p], r.wg[part, :], r.mg, (1, 0)),
+                (r.tok_d[p], r.wu[part, :], r.mu, (1, 0)),
+                (r.cot_d[p], r.wd[:, part], r.mdt, (1, 1)),
+            )
+        ):
+            totals[k] += masked_sum(left, right, [mask[b, :, at] for b in bands], dims)
+    for k, value in enumerate(totals):
         if hasattr(r, "received"):
             value = value + r.received[k]
             r.own[k] = value
@@ -143,13 +169,25 @@
 
 def add_rows(r, tiles):
     step = pl.program_id(0)
+    width = r.acc.shape[2]
+    tile = r.act.shape[2]
 
     @pl.when(step == 0)
     def _():
         r.acc[...] = r.sums[...] if hasattr(r, "sums") else jnp.zeros_like(r.acc)
 
-    r.acc[0] += dot(r.act[0], r.kd[step])
-    r.acc[1] += dot(r.act[1], r.kg[step], (1, 1)) + dot(r.act[2], r.ku[step], (1, 1))
+    first = (r.place[0] + step) * (tile // BLK)
+    size = min(DEPTH, width)
+    for f in range(0, width, size):
+        part = slice(f, f + size)
+
+        def masks(mask):
+            return [mask[first + b][:, part] for b in range(tile // BLK)]
+
+        r.acc[0, :, part] += masked_sum(r.act_d[0], r.wd[:, part], masks(r.md))
+        r.acc[1, :, part] += masked_sum(
+            r.act_d[1], r.wg[part, :], masks(r.mgt), (1, 1)
+        ) + masked_sum(r.act_d[2], r.wu[part, :], masks(r.mut), (1, 1))
 
     @pl.when(step == tiles - 1)
     def _():
@@ -163,21 +201,30 @@
 
 
 def weight_grads(r):
-    tile = r.act.shape[2]
+    _, rows, tile = r.act.shape
     at = tile_at(r, tile)
+    deep = r.tok_t.shape[1] // rows
     for out, k, mask in ((r.gg, 1, r.mg), (r.gu, 2, r.mu)):
-        value = dot(r.tok_t[...], r.act[k])
-        for b in range(out.shape[0] // BLK):
-            band = slice(b * BLK, (b + 1) * BLK)
-            out[band, :] = value[band, :] * mask[b, :, at]
-    value = dot(r.act[0].T, r.cot[...])
+        for g in range(out.shape[0] // (deep * BLK)):
+            right = r.masked_act.at[k - 1, g]
+            for j in range(deep):
+                keep = mask[g * deep + j, :, at].astype(BF16)
+                right[j * rows : (j + 1) * rows, :] = r.act[k] * keep
+            group = slice(g * deep * BLK, (g + 1) * deep * BLK)
+            out[group, :] = dot(r.tok_t[group, :], right[...])
+    first = (r.place[0] + pl.program_id(0)) * (tile // BLK)
     for b in range(tile // BLK):
-        band = slice(b * BLK, (b + 1) * BLK)
-        row = (r.place[0] + pl.program_id(0)) * (tile // BLK) + b
-        r.gd[band, :] = value[band, :] * r.md[row]
+        r.masked_cot[b * rows : (b + 1) * rows, :] = r.cot[...] * r.md[first + b].astype(BF16)
+    r.gd[...] = dot(r.act_d[0].T, r.masked_cot[...])
 
 
 def back_kernel(do_rows, do_grads, tiles, r):
+    @pl.when(pl.program_id(0) == 0)
+    def _():
+        r.act_d[...] = jnp.zeros_like(r.act_d)
+
+    for k in range(3 if do_rows else 1):
+        diagonal(r.act_d.at[k], r.act[k])
     if do_rows:
         add_rows(r, tiles)
     if do_grads:
@@ -226,8 +273,12 @@
     else:
         blocks = [lax.all_gather(block, "grid", axis=1, tiled=True)]
     rows = n_grid * tokens.shape[0]
+    pair = min(2, width // BLK)
+    deep = stack(rows, width // BLK)
     row_shape = jax.ShapeDtypeStruct((rows, width), BF16)
-    deep_shape = jax.ShapeDtypeStruct((width, rows), BF16)
+    pair_shape = jax.ShapeDtypeStruct((width // (pair * BLK), pair * rows, pair * BLK), BF16)
+    deep_shape = jax.ShapeDtypeStruct((width, deep * rows), BF16)
+
     def spread_of(blocks, across):
         return pinned(jax.ShapeDtypeStruct((blocks, 1, across * BLK), F32))
 
@@ -245,10 +296,14 @@
             )
         },
         {
-            "mg": spread_of(*mask_gate.shape),
-            "mu": spread_of(*mask_up.shape),
-            "md": spread_of(*mask_down.shape),
+            "mg": spread_of(width // BLK, units // BLK),
+            "mu": spread_of(width // BLK, units // BLK),
+            "mdt": spread_of(width // BLK, units // BLK),
+            "mgt": spread_of(units // BLK, width // BLK),
+            "mut": spread_of(units // BLK, width // BLK),
+            "md": spread_of(units // BLK, width // BLK),
         },
+        vmem=grant(4),
     )
 
     def cost(p, matmuls, mats):
@@ -257,36 +312,28 @@
             flops=2 * matmuls * rows * step, bytes_accessed=2 * mats * step, transcendentals=0
         )
 
-    def masking(p):
+    def weights():
         cols = pl.BlockSpec((width, tile), lambda i, first: (0, first[0] + i))
         downs = pl.BlockSpec((tile, width), lambda i, first: (first[0] + i, 0))
-        by_cols = jax.ShapeDtypeStruct((split[p], width, tile), BF16)
-        by_rows = jax.ShapeDtypeStruct((split[p], tile, width), BF16)
-        ins = {"wg": (hbm(w_gate), cols), "wu": (hbm(w_up), cols), "wd": (hbm(w_down), downs)}
-        ins.update({k: pinned(v) for k, v in spread.items()})
-        return ins, {"kg": pinned(by_cols), "ku": pinned(by_cols), "kd": pinned(by_rows)}
-
-    kept = {}
-    for which, p in AHEAD if direct else []:
-        kept[which, p] = call(
-            keep_masked,
-            "keep_masked",
-            place(which, p),
-            (split[p],),
-            *masking(p),
-            cost=cost(p, 0, 3),
-            vmem=grant(8),
-        )
+        return {"wg": (hbm(w_gate), cols), "wu": (hbm(w_up), cols), "wd": (hbm(w_down), downs)}
+
     gathered = call(
         assemble_kernel,
         "assemble",
         none,
         (1,),
         {
-            **{f"after{k}": (v["kg"], ANY) for k, v in enumerate(kept.values())},
+            "after": (spread["mg"], ANY),
             **{f"block{k}": (b, whole(b)) for k, b in enumerate(blocks)},
         },
-        {"tok": pinned(row_shape), "cot": pinned(row_shape), "tok_t": pinned(deep_shape)},
+        {
+            "cot": pinned(row_shape),
+            "tok_d": pinned(pair_shape),
+            "cot_d": pinned(pair_shape),
+            "tok_t": pinned(deep_shape),
+        },
+        scratch={"bands": pltpu.VMEM(deep_shape.shape[::-1], BF16)},
+        vmem=grant(4),
     )
 
     def held(*names):
@@ -298,31 +345,23 @@
         return (jax.ShapeDtypeStruct((3, rows, split[p] * tile), kind), trio)
 
     def partials(which, p, after=None, received=None):
-        ins, outs = held("tok", "cot"), {"send": trio_of(p, F32)}
-        if (which, p) in kept:
-            ins.update({k: pinned(v) for k, v in kept[which, p].items()})
-            masked = {}
-        else:
-            weights, masked = masking(p)
-            ins.update(weights)
+        ins = {**held("tok_d", "cot_d", "mg", "mu", "mdt"), **weights()}
+        outs = {"send": trio_of(p, F32)}
         if after is not None:
             ins["after"] = (after, ANY)
         if received is not None:
             ins["received"] = (received, trio)
             outs = {"own": trio_of(p, F32), "send": trio_of(p, BF16)}
-        got = call(
+        return call(
             partial_kernel,
             "partials",
             place(which, p),
             (split[p],),
             ins,
-            {**outs, **masked},
-            cost=cost(p, 3, 3 if masked else 0),
-            vmem=grant(8 if masked else 4),
+            outs,
+            cost=cost(p, 3, 3),
+            vmem=grant(6),
         )
-        if masked:
-            kept[which, p] = {k: got[k] for k in masked}
-        return got
 
     def activate(own, others, after):
         ins = {"own": (own, whole(own)), "after": (after, ANY)}
@@ -332,9 +371,11 @@
 
     def back(which, p, act, do_rows, do_grads, state, last=False):
         ins = {"act": (act, trio)}
-        outs, aliases, scratch = {}, {}, {}
+        outs, aliases = {}, {}
+        spots = tile // BLK
+        scratch = {"act_d": pltpu.VMEM((3, spots * rows, tile), BF16)}
         if do_rows:
-            ins.update({k: pinned(v) for k, v in kept[which, p].items()})
+            ins.update({**weights(), **held("md", "mgt", "mut")})
             shape = jax.ShapeDtypeStruct((2, rows, width), F32)
             scratch["acc"] = pltpu.VMEM(shape.shape, F32)
             if "sums" in state:
@@ -352,6 +393,8 @@
             outs["gg"] = (jax.ShapeDtypeStruct((width, units), F32), cols)
             outs["gu"] = (jax.ShapeDtypeStruct((width, units), F32), cols)
             outs["gd"] = (jax.ShapeDtypeStruct((units, width), F32), downs)
+            scratch["masked_act"] = pltpu.VMEM((2, width // (deep * BLK), deep * rows, tile), BF16)
+            scratch["masked_cot"] = pltpu.VMEM((spots * rows, width), BF16)
             for k in ("gg", "gu", "gd"):
                 if k in state:
                     ins["old_" + k] = (state[k], ANY)
@@ -367,8 +410,8 @@
             outs,
             scratch=scratch,
             aliases=aliases,
-            cost=cost(p, 3 * do_rows + 3 * do_grads, 6 * do_grads),
-            vmem=grant(9 if do_grads else 4),
+            cost=cost(p, 3 * do_rows + 3 * do_grads, 3 * do_rows + 6 * do_grads),
+            vmem=grant(14 if do_rows and do_grads else 10),
         )
         return {**state, **{k.replace("new_", ""): v for k, v in got.items()}}
 

time: 88.2 us -> 90.4 us (1.025)
  local copies, waits for them, and re-layouts: 9.91 us -> 2.69 us
  Pallas kernels: 59.5 us -> 66 us
  waiting for transfers between devices: 1.51 us -> 4.34 us
    unnamed x70 -> x6, local copies, waits for them, and re-layouts: 9.28 us -> 2.06 us
    pallas_call x22 -> x19, Pallas kernels: 59.5 us -> 66 us  [call(): pl.pallas_call(body, out_shape=[shape for shape, _ in outs.values()], gri...]
    ppermute x6, waiting for transfers between devices: 0.02 us -> 2.52 us  [trade(): return lax.ppermute(array, 'grid', [(i, i ^ s) for i in range(n_grid)])]
  transfers between devices with their start and end apart: 15 -> 15, of which waited for: 2 -> 2; matrix products, arithmetic and copies ran while one was open for 0% -> 0% of each run, Pallas kernels for 62% -> 65%
where the time goes in v5:
time: 90.4 us; the launch traced here: 89.6 us
  Pallas kernels  66 us (73%)
  starting transfers between devices  15 us (17%)
  waiting for transfers between devices  4.34 us (5%)
  local copies, waits for them, and re-layouts  2.69 us (3%)
    pallas_call x19, Pallas kernels, call(): pl.pallas_call(body, out_shape=[shape for shape, _ in outs.values()], gri...  66 us
    ppermute x6, starting transfers between devices, trade(): return lax.ppermute(array, 'grid', [(i, i ^ s) for i in range(n_grid)])  10.2 us
    ppermute x3, starting transfers between devices, across(): lax.ppermute(array, 'dp', [(i, (i // 2 + s) % pairs * 2 + i % 2) for i in...  3.6 us
    ppermute x6, waiting for transfers between devices, trade(): return lax.ppermute(array, 'grid', [(i, i ^ s) for i in range(n_grid)])  2.52 us
    unnamed x6, local copies, waits for them, and re-layouts  2.06 us
  transfers between devices with their start and end apart: 15, of which 2 were waited for; matrix products, arithmetic and copies ran while one was open for 0% of the time, Pallas kernels for 65%

profile of v5, /device:TPU:0, one launch (start us, length us, event | category | flops | bytes accessed | tf_op | source)
XLA Modules:
  0.0 89.6 jit_solution(3537774694909529136)
XLA Ops:
  0.6 0.8 pad_maximum_fusion.refs_2_
  1.4 5.1 %collective-permute-start.2 = (bf16[2,16,1024]{2,1,0:T(8,128)(2,1)S(1)}, bf16[2,16,1024]{2,1,0:T(8,128)(2,1)S(1)}, u32[]{:S(2)}, u32[]{:S(2)}) collective-permute-start(bf16[2,16,1024]{2,1,0:T(8,128)(2,1)S(1)} %pad_maximum_fusion.refs_2_), channel_id=1, source_target_pairs={{0,12},{4,8},{8,4},{12,0},{1,13},{5,9},{9,5},{13,1},{2,14},{6,10},... | collective-permute-start | bytes 196616 | tf_op jit(solution)/shard_map/ppermute | solution.py:255
  6.5 0.0 collective-permute-start.1
  6.5 0.6 collective-permute-start
  7.2 0.0 copy-start
  7.2 0.7 copy-done
  7.8 0.0 copy-start.1
  7.8 0.7 copy-done.1
  8.5 0.0 copy-start.2
  8.5 0.7 copy-done.2
  9.2 0.4 spread.1
  9.6 0.0 collective-permute-done.2.refs_5_
  9.6 2.5 %collective-permute-done.1.refs_4_ = bf16[2,16,1024]{2,1,0:T(8,128)(2,1)S(1)} collective-permute-done((bf16[2,16,1024]{2,1,0:T(8,128)(2,1)S(1)}, bf16[2,16,1024]{2,1,0:T(8,128)(2,1)S(1)}, u32[]{:S(2)}, u32[]{:S(2)}) %collective-permute-start.1) | collective-permute-done | bytes 65568 | tf_op jit(solution)/shard_map/ppermute | solution.py:255
  12.1 0.0 collective-permute-done.refs_3_
  12.1 0.3 assemble.1
  12.4 3.7 %partials.6.refs_9_ = f32[3,64,768]{2,1,0:T(8,128)S(1)} custom-call(s32[1]{0:T(128)} %bitcast.8.refs_0_, bf16[4,128,256]{2,1,0:T(8,128)(2,1)S(1)} %get-tuple-element.48.refs_1_, bf16[4,128,256]{2,1,0:T(8,128)(2,1)S(1)} %get-tuple-element.49.refs_2_, f32[8,1,4096]{2,1,0:T(1,128)S(1)} %get-tuple-element.47.refs_1_.refs_3_.refs_10_.refs_11_.refs_4_, ...), custom_call_target="tpu_custom_call" | custom-call | flops 301989888 | bytes 4718592 | tf_op jit(solution)/shard_map/partials/pallas_call | solution.py:41
  16.2 0.1 collective-permute-start.3
  16.2 3.7 %partials.7.refs_9_ = f32[3,64,768]{2,1,0:T(8,128)S(1)} custom-call(s32[1]{0:T(128)} %bitcast.7.refs_0_, bf16[4,128,256]{2,1,0:T(8,128)(2,1)S(1)} %get-tuple-element.48.refs_1_, bf16[4,128,256]{2,1,0:T(8,128)(2,1)S(1)} %get-tuple-element.49.refs_2_, f32[8,1,4096]{2,1,0:T(1,128)S(1)} %get-tuple-element.47.refs_1_.refs_3_.refs_10_.refs_11_.refs_4_, ...), custom_call_target="tpu_custom_call" | custom-call | flops 301989888 | bytes 4718592 | tf_op jit(solution)/shard_map/partials/pallas_call | solution.py:41
  20.0 0.5 collective-permute-start.4
  20.5 0.0 collective-permute-done.3.refs_10_
  20.5 4.5 %partials.8 = (f32[3,64,768]{2,1,0:T(8,128)S(1)}, bf16[3,64,768]{2,1,0:T(8,128)(2,1)}) custom-call(s32[1]{0:T(128)} %bitcast.6.refs_0_, bf16[4,128,256]{2,1,0:T(8,128)(2,1)S(1)} %get-tuple-element.48.refs_1_, bf16[4,128,256]{2,1,0:T(8,128)(2,1)S(1)} %get-tuple-element.49.refs_2_, ...), custom_call_target="tpu_custom_call" | custom-call | flops 301989888 | bytes 4718592 | tf_op jit(solution)/shard_map/partials/pallas_call | solution.py:41
  25.0 2.4 %partials.9.refs_9_ = f32[3,64,512]{2,1,0:T(8,128)S(1)} custom-call(s32[1]{0:T(128)} %bitcast.refs_0_, bf16[4,128,256]{2,1,0:T(8,128)(2,1)S(1)} %get-tuple-element.48.refs_1_, bf16[4,128,256]{2,1,0:T(8,128)(2,1)S(1)} %get-tuple-element.49.refs_2_, f32[8,1,4096]{2,1,0:T(1,128)S(1)} %get-tuple-element.47.refs_1_.refs_3_.refs_10_.refs_11_.refs_4_, ...), custom_call_target="tpu_custom_call" | custom-call | flops 201326592 | bytes 3145728 | tf_op jit(solution)/shard_map/partials/pallas_call | solution.py:41
  27.4 0.1 collective-permute-start.5
  27.5 1.5 %collective-permute-start.6 = (bf16[3,64,768]{2,1,0:T(8,128)(2,1)}, bf16[3,64,768]{2,1,0:T(8,128)(2,1)}, u32[]{:S(2)}, u32[]{:S(2)}) collective-permute-start(bf16[3,64,768]{2,1,0:T(8,128)(2,1)} %get-tuple-element.55), channel_id=1, source_target_pairs={{0,2},{1,3},{2,0},{3,1},{4,6},{5,7},{6,4},{7,5},{8,10},{9,11},{10,... | collective-permute-start | bytes 884744 | tf_op jit(solution)/shard_map/ppermute | solution.py:262
  29.0 0.0 collective-permute-done.4.refs_10_
  29.0 3.8 %partials.10 = (f32[3,64,768]{2,1,0:T(8,128)S(1)}, bf16[3,64,768]{2,1,0:T(8,128)(2,1)S(1)}) custom-call(s32[1]{0:T(128)} %bitcast.5.refs_0_, bf16[4,128,256]{2,1,0:T(8,128)(2,1)S(1)} %get-tuple-element.48.refs_1_, bf16[4,128,256]{2,1,0:T(8,128)(2,1)S(1)} %get-tuple-element.49.refs_2_, ...), custom_call_target="tpu_custom_call" | custom-call | flops 301989888 | bytes 4718592 | tf_op jit(solution)/shard_map/partials/pallas_call | solution.py:41
  32.9 0.0 collective-permute-done.5.refs_10_
  32.9 2.5 %partials.11 = (f32[3,64,512]{2,1,0:T(8,128)S(1)}, bf16[3,64,512]{2,1,0:T(8,128)(2,1)S(1)}) custom-call(s32[1]{0:T(128)} %bitcast.1.refs_0_, bf16[4,128,256]{2,1,0:T(8,128)(2,1)S(1)} %get-tuple-element.48.refs_1_, bf16[4,128,256]{2,1,0:T(8,128)(2,1)S(1)} %get-tuple-element.49.refs_2_, ...), custom_call_target="tpu_custom_call" | custom-call | flops 201326592 | bytes 3145728 | tf_op jit(solution)/shard_map/partials/pallas_call | solution.py:41
  35.4 1.8 %collective-permute-done.6.refs_3_ = bf16[3,64,768]{2,1,0:T(8,128)(2,1)} collective-permute-done((bf16[3,64,768]{2,1,0:T(8,128)(2,1)}, bf16[3,64,768]{2,1,0:T(8,128)(2,1)}, u32[]{:S(2)}, u32[]{:S(2)}) %collective-permute-start.6) | collective-permute-done | bytes 294944 | tf_op jit(solution)/shard_map/ppermute | solution.py:262
  37.2 1.1 %activate.3.refs_1_ = bf16[3,64,768]{2,1,0:T(8,128)(2,1)S(1)} custom-call(s32[1]{0:T(128)} %constant.24.clone.1.refs_0_, f32[3,64,768]{2,1,0:T(8,128)S(1)} %get-tuple-element.52.refs_9_.refs_1_, f32[3,64,512]{2,1,0:T(8,128)S(1)} %get-tuple-element.54.refs_2_.refs_1_, bf16[3,64,768]{2,1,0:T(8,128)(2,1)} %collective-permute-done.6.refs_3_), custom_call_target="tpu_custom_call" | custom-call | tf_op jit(solution)/shard_map/activate/pallas_call | solution.py:41
  38.3 0.1 collective-permute-start.7
  38.4 1.6 %collective-permute-start.8 = (bf16[3,64,768]{2,1,0:T(8,128)(2,1)S(1)}, bf16[3,64,768]{2,1,0:T(8,128)(2,1)S(1)}, u32[]{:S(2)}, u32[]{:S(2)}) collective-permute-start(bf16[3,64,768]{2,1,0:T(8,128)(2,1)S(1)} %get-tuple-element.66), channel_id=1, source_target_pairs={{0,2},{1,3},{2,0},{3,1},{4,6},{5,7},{6,4},{7,5},{8,10},{9,11},{10,... | collective-permute-start | bytes 884744 | tf_op jit(solution)/shard_map/ppermute | solution.py:262
  40.0 7.9 %back_rows_grads.4 = (f32[2,64,1024]{2,1,0:T(8,128)S(1)}, f32[1024,4096]{1,0:T(8,128)}, f32[1024,4096]{1,0:T(8,128)}, f32[4096,1024]{1,0:T(8,128)}) custom-call(s32[1]{0:T(128)} %bitcast.6.refs_0_, bf16[3,64,768]{2,1,0:T(8,128)(2,1)S(1)} %activate.3.refs_1_, bf16[1024,4096]{1,0:T(8,128)(2,1)} %refs_2_.13, bf16[1024,4096]{1,0:T(8,128)(2,1)} %refs_3_.11, ...), custom_call_target="tpu_custom_call" | custom-call | flops 603979776 | bytes 14155776 | tf_op jit(solution)/shard_map/back_rows_grads/pallas_call | solution.py:41
  47.9 0.0 collective-permute-done.7.refs_1_
  47.9 7.9 %back_rows_grads.5 = (f32[2,64,1024]{2,1,0:T(8,128)S(1)}, f32[1024,4096]{1,0:T(8,128)}, f32[1024,4096]{1,0:T(8,128)}, f32[4096,1024]{1,0:T(8,128)}) custom-call(s32[1]{0:T(128)} %bitcast.8.refs_0_, bf16[3,64,768]{2,1,0:T(8,128)(2,1)S(1)} %collective-permute-done.7.refs_1_, ...), custom_call_target="tpu_custom_call", output_to_operand_aliasing={{1}: (13, {}), {2}: (14, {}), {3}: (15, {})} | custom-call | flops 603979776 | bytes 14155776 | tf_op jit(solution)/shard_map/back_rows_grads/pallas_call | solution.py:41
  55.8 0.0 collective-permute-done.8.refs_3_
  55.8 0.1 activate.4.refs_1_
  56.0 0.2 collective-permute-start.9
  56.2 0.5 collective-permute-start.10
  56.7 7.9 %back_rows_grads.6 = (f32[2,64,1024]{2,1,0:T(8,128)S(1)}, f32[1024,4096]{1,0:T(8,128)}, f32[1024,4096]{1,0:T(8,128)}, f32[4096,1024]{1,0:T(8,128)}) custom-call(s32[1]{0:T(128)} %bitcast.5.refs_0_, bf16[3,64,768]{2,1,0:T(8,128)(2,1)S(1)} %activate.4.refs_1_, ...), custom_call_target="tpu_custom_call", output_to_operand_aliasing={{1}: (13, {}), {2}: (14, {}), {3}: (15, {})} | custom-call | flops 603979776 | bytes 14155776 | tf_op jit(solution)/shard_map/back_rows_grads/pallas_call | solution.py:41
  64.6 0.0 collective-permute-done.9.refs_1_
  64.6 7.9 %back_rows_grads.7 = (f32[2,64,1024]{2,1,0:T(8,128)S(1)}, f32[1024,4096]{1,0:T(8,128)}, f32[1024,4096]{1,0:T(8,128)}, f32[4096,1024]{1,0:T(8,128)}) custom-call(s32[1]{0:T(128)} %bitcast.7.refs_0_, bf16[3,64,768]{2,1,0:T(8,128)(2,1)S(1)} %collective-permute-done.9.refs_1_, ...), custom_call_target="tpu_custom_call", output_to_operand_aliasing={{1}: (13, {}), {2}: (14, {}), {3}: (15, {})} | custom-call | flops 603979776 | bytes 14155776 | tf_op jit(solution)/shard_map/back_rows_grads/pallas_call | solution.py:41
  72.6 0.0 collective-permute-done.10.refs_3_
  72.6 0.1 activate.5.refs_1_
  72.7 0.1 collective-permute-start.11
  72.8 2.6 %back_rows.2.refs_8_ = f32[2,64,1024]{2,1,0:T(8,128)S(1)} custom-call(s32[1]{0:T(128)} %bitcast.1.refs_0_, bf16[3,64,512]{2,1,0:T(8,128)(2,1)S(1)} %activate.5.refs_1_, bf16[1024,4096]{1,0:T(8,128)(2,1)} %refs_2_.13, bf16[1024,4096]{1,0:T(8,128)(2,1)} %refs_3_.11, bf16[4096,1024]{1,0:T(8,128)(2,1)} %refs_4_.11, ...), custom_call_target="tpu_custom_call" | custom-call | flops 201326592 | bytes 3145728 | tf_op jit(solution)/shard_map/back_rows/pallas_call | solution.py:41
  75.4 0.0 collective-permute-done.11.refs_1_
  75.4 2.7 %back_rows.3 = (bf16[2,16,1024]{2,1,0:T(8,128)(2,1)S(1)}, bf16[2,16,1024]{2,1,0:T(8,128)(2,1)S(1)}, bf16[2,16,1024]{2,1,0:T(8,128)(2,1)S(1)}, bf16[2,16,1024]{2,1,0:T(8,128)(2,1)S(1)}) custom-call(s32[1]{0:T(128)} %bitcast.refs_0_, bf16[3,64,512]{2,1,0:T(8,128)(2,1)S(1)} %collective-permute-done.11.refs_1_, bf16[1024,4096]{1,0:T(8,128)(2,1)} %refs_2_.13, ...), custom_call_target="tpu_custom_call" | custom-call | flops 201326592 | bytes 3145728 | tf_op jit(solution)/shard_map/back_rows/pallas_call | solution.py:41
  78.1 1.1 %collective-permute-start.12 = (bf16[2,16,1024]{2,1,0:T(8,128)(2,1)S(1)}, bf16[2,16,1024]{2,1,0:T(8,128)(2,1)S(1)}, u32[]{:S(2)}, u32[]{:S(2)}) collective-permute-start(bf16[2,16,1024]{2,1,0:T(8,128)(2,1)S(1)} %get-tuple-element.77), channel_id=1, source_target_pairs={{0,4},{4,0},{8,12},{12,8},{1,5},{5,1},{9,13},{13,9},{2,6},{6,2},{1... | collective-permute-start | bytes 196616 | tf_op jit(solution)/shard_map/ppermute | solution.py:255
  79.3 2.2 %collective-permute-start.13 = (bf16[2,16,1024]{2,1,0:T(8,128)(2,1)S(1)}, bf16[2,16,1024]{2,1,0:T(8,128)(2,1)S(1)}, u32[]{:S(2)}, u32[]{:S(2)}) collective-permute-start(bf16[2,16,1024]{2,1,0:T(8,128)(2,1)S(1)} %get-tuple-element.78), channel_id=1, source_target_pairs={{0,8},{4,12},{8,0},{12,4},{1,9},{5,13},{9,1},{13,5},{2,10},{6,14},... | collective-permute-start | bytes 196616 | tf_op jit(solution)/shard_map/ppermute | solution.py:255
  81.5 1.1 %collective-permute-start.14 = (bf16[2,16,1024]{2,1,0:T(8,128)(2,1)S(1)}, bf16[2,16,1024]{2,1,0:T(8,128)(2,1)S(1)}, u32[]{:S(2)}, u32[]{:S(2)}) collective-permute-start(bf16[2,16,1024]{2,1,0:T(8,128)(2,1)S(1)} %get-tuple-element.79), channel_id=1, source_target_pairs={{0,12},{4,8},{8,4},{12,0},{1,13},{5,9},{9,5},{13,1},{2,14},{6,10},... | collective-permute-start | bytes 196616 | tf_op jit(solution)/shard_map/ppermute | solution.py:255
  82.6 3.2 %back_grads.2 = (f32[1024,4096]{1,0:T(8,128)}, f32[1024,4096]{1,0:T(8,128)}, f32[4096,1024]{1,0:T(8,128)}) custom-call(s32[1]{0:T(128)} %bitcast.1.refs_0_, bf16[3,64,512]{2,1,0:T(8,128)(2,1)S(1)} %activate.5.refs_1_, bf16[1024,256]{1,0:T(8,128)(2,1)S(1)} %get-tuple-element.59.refs_8_.refs_9_.refs_2_, ...), custom_call_target="tpu_custom_call", output_to_operand_aliasing={{0}: (7, {}), {1}: (8, {}), {2}: (9, {})} | custom-call | flops 201326592 | bytes 6291456 | tf_op jit(solution)/shard_map/back_grads/pallas_call | solution.py:41
  85.8 3.2 %back_grads.3 = (f32[1024,4096]{1,0:T(8,128)}, f32[1024,4096]{1,0:T(8,128)}, f32[4096,1024]{1,0:T(8,128)}) custom-call(s32[1]{0:T(128)} %bitcast.refs_0_, bf16[3,64,512]{2,1,0:T(8,128)(2,1)S(1)} %collective-permute-done.11.refs_1_, ...), custom_call_target="tpu_custom_call", output_to_operand_aliasing={{0}: (7, {}), {1}: (8, {}), {2}: (9, {})} | custom-call | flops 201326592 | bytes 6291456 | tf_op jit(solution)/shard_map/back_grads/pallas_call | solution.py:41
  88.9 0.0 collective-permute-done.12
  88.9 0.0 collective-permute-done.13
  88.9 0.0 collective-permute-done.14
  89.0 0.6 slice_bitcast_fusion
  (1 shorter events, 0.0 us)
Async XLA Ops:
  1.4 8.2 %collective-permute-start.2 = (bf16[2,16,1024]{2,1,0:T(8,128)(2,1)S(1)}, bf16[2,16,1024]{2,1,0:T(8,128)(2,1)S(1)}, u32[]{:S(2)}, u32[]{:S(2)}) collective-permute-start(bf16[2,16,1024]{2,1,0:T(8,128)(2,1)S(1)} %pad_maximum_fusion.refs_2_), channel_id=1, source_target_pairs={{0,12},{4,8},{8,4},{12,0},{1,13},{5,9},{9,5},{13,1},{2,14},{6,10},... | collective-permute-start | bytes 196616 | tf_op jit(solution)/shard_map/ppermute | solution.py:255
  6.5 5.6 %collective-permute-start.1 = (bf16[2,16,1024]{2,1,0:T(8,128)(2,1)S(1)}, bf16[2,16,1024]{2,1,0:T(8,128)(2,1)S(1)}, u32[]{:S(2)}, u32[]{:S(2)}) collective-permute-start(bf16[2,16,1024]{2,1,0:T(8,128)(2,1)S(1)} %pad_maximum_fusion.refs_2_), channel_id=1, source_target_pairs={{0,8},{4,12},{8,0},{12,4},{1,9},{5,13},{9,1},{13,5},{2,10},{6,14},... | collective-permute-start | bytes 196616 | tf_op jit(solution)/shard_map/ppermute | solution.py:255
  6.5 5.6 %collective-permute-start = (bf16[2,16,1024]{2,1,0:T(8,128)(2,1)S(1)}, bf16[2,16,1024]{2,1,0:T(8,128)(2,1)S(1)}, u32[]{:S(2)}, u32[]{:S(2)}) collective-permute-start(bf16[2,16,1024]{2,1,0:T(8,128)(2,1)S(1)} %pad_maximum_fusion.refs_2_), channel_id=1, source_target_pairs={{0,4},{4,0},{8,12},{12,8},{1,5},{5,1},{9,13},{13,9},{2,6},{6,2},{1... | collective-permute-start | bytes 196616 | tf_op jit(solution)/shard_map/ppermute | solution.py:255
  7.2 0.7 copy-start
  7.8 0.7 copy-start.1
  8.5 0.7 copy-start.2
  16.2 4.4 %collective-permute-start.3 = (f32[3,64,768]{2,1,0:T(8,128)S(1)}, f32[3,64,768]{2,1,0:T(8,128)}, u32[]{:S(2)}, u32[]{:S(2)}) collective-permute-start(f32[3,64,768]{2,1,0:T(8,128)S(1)} %partials.6.refs_9_), channel_id=1, source_target_pairs={{0,1},{1,0},{2,3},{3,2},{4,5},{5,4},{6,7},{7,6},{8,9},{9,8},{10,11... | collective-permute-start | bytes 1769480 | tf_op jit(solution)/shard_map/ppermute | solution.py:258
  20.0 9.1 %collective-permute-start.4 = (f32[3,64,768]{2,1,0:T(8,128)S(1)}, f32[3,64,768]{2,1,0:T(8,128)}, u32[]{:S(2)}, u32[]{:S(2)}) collective-permute-start(f32[3,64,768]{2,1,0:T(8,128)S(1)} %partials.7.refs_9_), channel_id=1, source_target_pairs={{0,1},{1,0},{2,3},{3,2},{4,5},{5,4},{6,7},{7,6},{8,9},{9,8},{10,11... | collective-permute-start | bytes 1769480 | tf_op jit(solution)/shard_map/ppermute | solution.py:258
  27.4 5.5 %collective-permute-start.5 = (f32[3,64,512]{2,1,0:T(8,128)S(1)}, f32[3,64,512]{2,1,0:T(8,128)}, u32[]{:S(2)}, u32[]{:S(2)}) collective-permute-start(f32[3,64,512]{2,1,0:T(8,128)S(1)} %partials.9.refs_9_), channel_id=1, source_target_pairs={{0,1},{1,0},{2,3},{3,2},{4,5},{5,4},{6,7},{7,6},{8,9},{9,8},{10,11... | collective-permute-start | bytes 1179656 | tf_op jit(solution)/shard_map/ppermute | solution.py:258
  27.5 9.7 %collective-permute-start.6 = (bf16[3,64,768]{2,1,0:T(8,128)(2,1)}, bf16[3,64,768]{2,1,0:T(8,128)(2,1)}, u32[]{:S(2)}, u32[]{:S(2)}) collective-permute-start(bf16[3,64,768]{2,1,0:T(8,128)(2,1)} %get-tuple-element.55), channel_id=1, source_target_pairs={{0,2},{1,3},{2,0},{3,1},{4,6},{5,7},{6,4},{7,5},{8,10},{9,11},{10,... | collective-permute-start | bytes 884744 | tf_op jit(solution)/shard_map/ppermute | solution.py:262
  38.3 9.5 %collective-permute-start.7 = (bf16[3,64,768]{2,1,0:T(8,128)(2,1)S(1)}, bf16[3,64,768]{2,1,0:T(8,128)(2,1)S(1)}, u32[]{:S(2)}, u32[]{:S(2)}) collective-permute-start(bf16[3,64,768]{2,1,0:T(8,128)(2,1)S(1)} %activate.3.refs_1_), channel_id=1, source_target_pairs={{0,1},{1,0},{2,3},{3,2},{4,5},{5,4},{6,7},{7,6},{8,9},{9,8},{10,11... | collective-permute-start | bytes 884744 | tf_op jit(solution)/shard_map/ppermute | solution.py:258
  38.4 17.4 %collective-permute-start.8 = (bf16[3,64,768]{2,1,0:T(8,128)(2,1)S(1)}, bf16[3,64,768]{2,1,0:T(8,128)(2,1)S(1)}, u32[]{:S(2)}, u32[]{:S(2)}) collective-permute-start(bf16[3,64,768]{2,1,0:T(8,128)(2,1)S(1)} %get-tuple-element.66), channel_id=1, source_target_pairs={{0,2},{1,3},{2,0},{3,1},{4,6},{5,7},{6,4},{7,5},{8,10},{9,11},{10,... | collective-permute-start | bytes 884744 | tf_op jit(solution)/shard_map/ppermute | solution.py:262
  56.0 8.7 %collective-permute-start.9 = (bf16[3,64,768]{2,1,0:T(8,128)(2,1)S(1)}, bf16[3,64,768]{2,1,0:T(8,128)(2,1)S(1)}, u32[]{:S(2)}, u32[]{:S(2)}) collective-permute-start(bf16[3,64,768]{2,1,0:T(8,128)(2,1)S(1)} %activate.4.refs_1_), channel_id=1, source_target_pairs={{0,1},{1,0},{2,3},{3,2},{4,5},{5,4},{6,7},{7,6},{8,9},{9,8},{10,11... | collective-permute-start | bytes 884744 | tf_op jit(solution)/shard_map/ppermute | solution.py:258
  56.2 16.4 %collective-permute-start.10 = (bf16[3,64,512]{2,1,0:T(8,128)(2,1)S(1)}, bf16[3,64,512]{2,1,0:T(8,128)(2,1)S(1)}, u32[]{:S(2)}, u32[]{:S(2)}) collective-permute-start(bf16[3,64,512]{2,1,0:T(8,128)(2,1)S(1)} %get-tuple-element.75), channel_id=1, source_target_pairs={{0,2},{1,3},{2,0},{3,1},{4,6},{5,7},{6,4},{7,5},{8,10},{9,11},{10,... | collective-permute-start | bytes 589832 | tf_op jit(solution)/shard_map/ppermute | solution.py:262
  72.7 2.8 %collective-permute-start.11 = (bf16[3,64,512]{2,1,0:T(8,128)(2,1)S(1)}, bf16[3,64,512]{2,1,0:T(8,128)(2,1)S(1)}, u32[]{:S(2)}, u32[]{:S(2)}) collective-permute-start(bf16[3,64,512]{2,1,0:T(8,128)(2,1)S(1)} %activate.5.refs_1_), channel_id=1, source_target_pairs={{0,1},{1,0},{2,3},{3,2},{4,5},{5,4},{6,7},{7,6},{8,9},{9,8},{10,11... | collective-permute-start | bytes 589832 | tf_op jit(solution)/shard_map/ppermute | solution.py:258
  78.1 10.8 %collective-permute-start.12 = (bf16[2,16,1024]{2,1,0:T(8,128)(2,1)S(1)}, bf16[2,16,1024]{2,1,0:T(8,128)(2,1)S(1)}, u32[]{:S(2)}, u32[]{:S(2)}) collective-permute-start(bf16[2,16,1024]{2,1,0:T(8,128)(2,1)S(1)} %get-tuple-element.77), channel_id=1, source_target_pairs={{0,4},{4,0},{8,12},{12,8},{1,5},{5,1},{9,13},{13,9},{2,6},{6,2},{1... | collective-permute-start | bytes 196616 | tf_op jit(solution)/shard_map/ppermute | solution.py:255
  79.3 9.7 %collective-permute-start.13 = (bf16[2,16,1024]{2,1,0:T(8,128)(2,1)S(1)}, bf16[2,16,1024]{2,1,0:T(8,128)(2,1)S(1)}, u32[]{:S(2)}, u32[]{:S(2)}) collective-permute-start(bf16[2,16,1024]{2,1,0:T(8,128)(2,1)S(1)} %get-tuple-element.78), channel_id=1, source_target_pairs={{0,8},{4,12},{8,0},{12,4},{1,9},{5,13},{9,1},{13,5},{2,10},{6,14},... | collective-permute-start | bytes 196616 | tf_op jit(solution)/shard_map/ppermute | solution.py:255
  81.5 7.5 %collective-permute-start.14 = (bf16[2,16,1024]{2,1,0:T(8,128)(2,1)S(1)}, bf16[2,16,1024]{2,1,0:T(8,128)(2,1)S(1)}, u32[]{:S(2)}, u32[]{:S(2)}) collective-permute-start(bf16[2,16,1024]{2,1,0:T(8,128)(2,1)S(1)} %get-tuple-element.79), channel_id=1, source_target_pairs={{0,12},{4,8},{8,4},{12,0},{1,13},{5,9},{9,5},{13,1},{2,14},{6,10},... | collective-permute-start | bytes 196616 | tf_op jit(solution)/shard_map/ppermute | solution.py:255

commit v6 on v5

v6 whole, which is shorter than its diff:
```python
import functools
import types

import jax
import jax.numpy as jnp
from jax import lax
from jax.experimental import pallas as pl
from jax.experimental.pallas import tpu as pltpu
from jax.sharding import PartitionSpec as P

BLK = 128
MIB = 1024 * 1024
DEPTH = 256
ANY = pl.BlockSpec(memory_space=pl.ANY)
PIECES = [3, 3, 2]
KEPT = ("kg", "ku", "kd")
F32 = jnp.float32
BF16 = jnp.bfloat16


def dot(left, right, dims=(1, 0)):
    return lax.dot_general(
        left, right, (((dims[0],), (dims[1],)), ((), ())), preferred_element_type=F32
    )


def pinned(array):
    spec = pl.BlockSpec(memory_space=pltpu.VMEM)
    if isinstance(array, jax.ShapeDtypeStruct):
        return (pltpu.VMEM(array.shape, array.dtype), spec)
    return (pltpu.with_memory_space_constraint(array, pltpu.VMEM), spec)


def call(kernel, name, scalars, ins, outs, scratch=None, aliases=None, cost=None, vmem=2):
    scratch = scratch or {}
    names = ["place", *ins, *outs, *scratch]
    in_names, out_names = list(ins), list(outs)

    def body(*refs):
        kernel(types.SimpleNamespace(**dict(zip(names, refs))))

    results = pl.pallas_call(
        body,
        out_shape=[shape for shape, _ in outs.values()],
        grid_spec=pltpu.PrefetchScalarGridSpec(
            num_scalar_prefetch=1,
            grid=(1,),
            in_specs=[spec for _, spec in ins.values()],
            out_specs=[spec for _, spec in outs.values()],
            scratch_shapes=list(scratch.values()),
        ),
        input_output_aliases={
            1 + in_names.index(i): out_names.index(o) for i, o in (aliases or {}).items()
        },
        compiler_params=pltpu.CompilerParams(vmem_limit_bytes=vmem * MIB),
        cost_estimate=cost,
        name=name,
    )(scalars, *[array for array, _ in ins.values()])
    return dict(zip(out_names, results))


def hbm(array):
    return pltpu.with_memory_space_constraint(array, pltpu.HBM)


def whole(array):
    return pl.BlockSpec(array.shape, lambda *_: (0,) * len(array.shape))


def spread(r):
    def pattern(blocks):
        at = lax.broadcasted_iota(jnp.int32, (blocks, blocks * BLK), 0) * BLK
        column = lax.broadcasted_iota(jnp.int32, (blocks, blocks * BLK), 1)
        return ((column >= at) & (column < at + BLK)).astype(F32).astype(BF16)

    across, along = r.mask_gate.shape
    units, features = pattern(along), pattern(across)
    for mask, by_units, by_features in (
        (r.mask_gate, r.mg, r.mgt),
        (r.mask_up, r.mu, r.mut),
        (r.mask_down_t, r.mdt, r.md),
    ):
        entries = mask[...].astype(F32).astype(BF16)
        value = dot(entries, units)
        for b in range(across):
            by_units[b] = value[b : b + 1, :]
        value = dot(entries, features, (0, 0))
        for b in range(along):
            by_features[b] = value[b : b + 1, :]


def span(start, size):
    return pl.ds(pl.multiple_of(start, BLK), size)


def fetch(r, which, starts, into, sems):
    copies = []
    for start, (gate, up, down) in zip(starts, into):
        at = span(r.place[which] + start, down.shape[0])
        for source, target in (
            (r.w_gate.at[:, at], gate),
            (r.w_up.at[:, at], up),
            (r.w_down.at[at, :], down),
        ):
            copies.append(pltpu.make_async_copy(source, target, sems.at[len(copies)]))
            copies[-1].start()
    return copies


def fetch_kernel(starts, r):
    into = [[getattr(r, f"{k}{p}") for k in KEPT] for p in range(len(starts))]
    copies = fetch(r, 1, starts, into, r.sems)
    spread(r)
    for copy in copies:
        copy.wait()


def diagonal(out, value):
    rows, size = value.shape
    for b in range(size // BLK):
        band = slice(b * BLK, (b + 1) * BLK)
        out[b * rows : (b + 1) * rows, band] = value[:, band]


def assemble_kernel(r):
    blocks = [ref for name, ref in vars(r).items() if name.startswith("block")]
    tok = jnp.concatenate([block[0] for block in blocks], axis=0)
    cot = jnp.concatenate([block[1] for block in blocks], axis=0)
    r.cot[...] = cot
    size = r.tok_d.shape[2]
    r.tok_d[...] = jnp.zeros_like(r.tok_d)
    r.cot_d[...] = jnp.zeros_like(r.cot_d)
    for p in range(r.tok_d.shape[0]):
        part = slice(p * size, (p + 1) * size)
        diagonal(r.tok_d.at[p], tok[:, part])
        diagonal(r.cot_d.at[p], cot[:, part])
    for p in range(r.tok_d.shape[0]):
        r.tok_t[p] = r.tok_d[p].T


def masked_sum(left, right, masks, dims=(1, 0)):
    value = dot(left, right, dims)
    rows = value.shape[0] // len(masks)
    return sum(value[b * rows : (b + 1) * rows, :] * m for b, m in enumerate(masks))


def partial_kernel(which, start, tile, r):
    copies = []
    if hasattr(r, "sems"):
        copies = fetch(r, 0, [start], [(r.new_kg, r.new_ku, r.new_kd)], r.sems)
    pairs, _, size = r.tok_d.shape
    for first in range(0, r.send.shape[2], tile):
        at = span(r.place[which] + start + first, tile)
        local = slice(first, first + tile)
        totals = [0.0, 0.0, 0.0]
        for p in range(pairs):
            part = slice(p * size, (p + 1) * size)
            bands = range(p * size // BLK, (p + 1) * size // BLK)
            for k, (left, right, mask, dims) in enumerate(
                (
                    (r.tok_d[p], r.kg[part, local], r.mg, (1, 0)),
                    (r.tok_d[p], r.ku[part, local], r.mu, (1, 0)),
                    (r.cot_d[p], r.kd[local, part], r.mdt, (1, 1)),
                )
            ):
                totals[k] += masked_sum(left, right, [mask[b, :, at] for b in bands], dims)
        for k, value in enumerate(totals):
            if hasattr(r, "received"):
                value = value + r.received[k, :, local]
                r.own[k, :, local] = value
            r.send[k, :, local] = value.astype(r.send.dtype)
    for copy in copies:
        copy.wait()


def act_kernel(r):
    others = [ref for name, ref in vars(r).items() if name.startswith("other")]
    gate, up, back = (
        sum((other[k].astype(F32) for other in others), r.own[k]) for k in range(3)
    )
    sigma = 1.0 / (1.0 + jnp.exp(-gate))
    silu = gate * sigma
    slope = sigma * (1.0 + gate * (1.0 - sigma))
    r.act[0] = (silu * up).astype(BF16)
    r.act[1] = (back * up * slope).astype(BF16)
    r.act[2] = (back * silu).astype(BF16)


def add_rows(r, block, local):
    width, tile = r.acc.shape[2], r.act_d.shape[2]
    size = min(DEPTH, width)
    for f in range(0, width, size):
        part = slice(f, f + size)

        def masks(mask):
            return [mask[block + b][:, part] for b in range(tile // BLK)]

        r.acc[0, :, part] += masked_sum(r.act_d[0], r.kd[local, part], masks(r.md))
        r.acc[1, :, part] += masked_sum(
            r.act_d[1], r.kg[part, local], masks(r.mgt), (1, 1)
        ) + masked_sum(r.act_d[2], r.ku[part, local], masks(r.mut), (1, 1))


class Outbox:
    def __init__(self, slots, sems):
        self.slots, self.sems = slots, sems
        self.flying, self.count = [None] * slots.shape[0], 0

    def put(self, value, target):
        k = self.count % len(self.flying)
        self.count += 1
        if self.flying[k] is not None:
            self.flying[k].wait()
        self.slots[k] = value
        self.flying[k] = pltpu.make_async_copy(self.slots.at[k], target, self.sems.at[k])
        self.flying[k].start()

    def close(self):
        for copy in self.flying:
            if copy is not None:
                copy.wait()


def back_kernel(which, start, do_rows, do_grads, r):
    _, rows, size = r.act.shape
    tile = r.act_d.shape[2]
    base = r.place[which] + start
    at = span(base, size)
    r.act_d[...] = jnp.zeros_like(r.act_d)
    groups = 0
    if do_rows:
        r.acc[...] = r.sums[...] if hasattr(r, "sums") else jnp.zeros_like(r.acc)
    if do_grads:
        groups, height, _ = r.tok_t.shape
        by_cols, by_rows = Outbox(r.col_slots, r.col_sems), Outbox(r.row_slots, r.row_sems)
    for i in range(max(groups, size // tile)):
        if i < groups:
            band = slice(i * height, (i + 1) * height)
            for out, k, mask in ((r.gg, 1, r.mg), (r.gu, 2, r.mu)):
                right = r.masked_act.at[k - 1]
                for j in range(height // BLK):
                    keep = mask[i * (height // BLK) + j, :, at].astype(BF16)
                    right[j * rows : (j + 1) * rows, :] = r.act[k] * keep
                by_cols.put(dot(r.tok_t[i], right[...]), out.at[band, at])
        if i < size // tile:
            local = slice(i * tile, (i + 1) * tile)
            for k in range(3 if do_rows else 1):
                diagonal(r.act_d.at[k], r.act[k, :, local])
            block = lax.div(base, BLK) + i * (tile // BLK)
            if do_grads:
                for b in range(tile // BLK):
                    keep = r.md[block + b].astype(BF16)
                    r.masked_cot[b * rows : (b + 1) * rows, :] = r.cot[...] * keep
                value = dot(r.act_d[0].T, r.masked_cot[...])
                by_rows.put(value, r.gd.at[span(base + i * tile, tile), :])
            if do_rows:
                add_rows(r, block, local)
    if do_rows:
        if hasattr(r, "new_sums"):
            r.new_sums[...] = r.acc[...]
        else:
            outs = [ref for name, ref in vars(r).items() if name.startswith("rows")]
            count = outs[0].shape[1]
            for k, out in enumerate(outs):
                out[...] = r.acc[:, k * count : (k + 1) * count, :].astype(out.dtype)
    if do_grads:
        by_cols.close()
        by_rows.close()


def shards(sizes, tokens, w_gate, w_up, w_down, mask_gate, mask_up, mask_down, grad_out):
    n_grid, n_dp = sizes
    width, units = w_gate.shape
    rows = n_grid * tokens.shape[0]
    pairs = n_dp // 2
    half = units // 2
    tile = min(DEPTH, half)
    split = PIECES if sum(PIECES) * tile == half else [half // tile]
    split = [tile * count for count in split]
    starts = [sum(split[:p]) for p in range(len(split))]
    n = len(split)
    direct = n_grid == 4
    grant = lambda mib: mib if rows <= 64 else 32

    core = lax.axis_index("dp") % 2
    place = jnp.stack([core * half, (1 - core) * half]).astype(jnp.int32)

    def trade(array, s):
        return lax.ppermute(array, "grid", [(i, i ^ s) for i in range(n_grid)])

    def swap(array):
        return lax.ppermute(array, "dp", [(i, i ^ 1) for i in range(n_dp)])

    def across(array):
        return [
            lax.ppermute(
                array,
                "dp",
                [(i, ((i // 2 + s) % pairs) * 2 + i % 2) for i in range(n_dp)],
            )
            for s in range(1, pairs)
        ]

    def cost(p, matmuls, mats):
        step = width * split[p]
        return pl.CostEstimate(
            flops=2 * matmuls * rows * step, bytes_accessed=2 * mats * step, transcendentals=0
        )

    def shape(*dims, kind=BF16):
        return jax.ShapeDtypeStruct(dims, kind)

    weights = {"w_gate": (w_gate, ANY), "w_up": (w_up, ANY), "w_down": (w_down, ANY)}
    weights = {k: (hbm(w), spec) for k, (w, spec) in weights.items()}

    def kept_shapes(p):
        return [shape(width, split[p]), shape(width, split[p]), shape(split[p], width)]

    block = jnp.stack([tokens, grad_out])
    if direct:
        blocks = [block] + [trade(block, s) for s in range(1, n_grid)]
    else:
        blocks = [lax.all_gather(block, "grid", axis=1, tiled=True)]

    across_shape = shape(width // BLK, 1, units, kind=F32)
    along_shape = shape(units // BLK, 1, width, kind=F32)
    masks = {"mask_gate": mask_gate, "mask_up": mask_up, "mask_down_t": mask_down.T}
    got = call(
        functools.partial(fetch_kernel, starts),
        "fetch",
        place,
        {**weights, **{k: (hbm(m), whole(m)) for k, m in masks.items()}},
        {
            **{k: pinned(across_shape) for k in ("mg", "mu", "mdt")},
            **{k: pinned(along_shape) for k in ("mgt", "mut", "md")},
            **{f"{k}{p}": pinned(s) for p in range(n) for k, s in zip(KEPT, kept_shapes(p))},
        },
        scratch={"sems": pltpu.SemaphoreType.DMA((3 * n,))},
        cost=pl.CostEstimate(flops=0, bytes_accessed=6 * width * half, transcendentals=0),
        vmem=grant(4),
    )
    values = {k: got[k] for k in ("mg", "mu", "mdt", "mgt", "mut", "md")}
    kept = {(1, p): {k: got[f"{k}{p}"] for k in KEPT} for p in range(n)}

    pair = min(DEPTH, width) // BLK
    pair_shape = shape(width // (pair * BLK), pair * rows, pair * BLK)
    values |= call(
        assemble_kernel,
        "assemble",
        place,
        {
            "after": (values["mg"], ANY),
            **{f"block{k}": (b, whole(b)) for k, b in enumerate(blocks)},
        },
        {
            "cot": pinned(shape(rows, width)),
            "tok_d": pinned(pair_shape),
            "cot_d": pinned(pair_shape),
            "tok_t": pinned(shape(pair_shape.shape[0], pair * BLK, pair * rows)),
        },
        vmem=grant(4),
    )

    def held(*names):
        return {k: pinned(values[k]) for k in names}

    def partials(which, p, after=None, received=None):
        trio = (3, rows, split[p])
        ins = held("tok_d", "cot_d", "mg", "mu", "mdt")
        ins.update({k: pinned(v) for k, v in kept[which, p].items()})
        outs, scratch = {"send": pinned(shape(*trio, kind=F32))}, {}
        if after is not None:
            ins["after"] = (after, ANY)
        if received is None:
            ins.update(weights)
            outs.update({"new_" + k: pinned(s) for k, s in zip(KEPT, kept_shapes(p))})
            scratch["sems"] = pltpu.SemaphoreType.DMA((3,))
        else:
            ins["received"] = pinned(received)
            outs = {"own": pinned(shape(*trio, kind=F32)), "send": pinned(shape(*trio))}
        got = call(
            functools.partial(partial_kernel, which, starts[p], tile),
            "partials",
            place,
            ins,
            outs,
            scratch=scratch,
            cost=cost(p, 3, 3),
            vmem=grant(2),
        )
        if received is None:
            kept[0, p] = {k: got["new_" + k] for k in KEPT}
        return got

    def activate(own, others, after):
        ins = {"own": pinned(own), "after": (after, ANY)}
        ins.update({f"other{k}": pinned(a) for k, a in enumerate(others)})
        outs = {"act": pinned(shape(*own.shape))}
        return call(act_kernel, "activate", place, ins, outs, vmem=grant(2))["act"]

    def back(which, p, act, do_rows, do_grads, state, last=False):
        ins = {"act": pinned(act), **held("md")}
        outs, aliases = {}, {}
        spots, size = tile // BLK, split[p]
        scratch = {"act_d": pltpu.VMEM((3, spots * rows, tile), BF16)}
        if do_rows:
            ins.update({k: pinned(v) for k, v in kept[which, p].items()})
            ins.update(held("mgt", "mut"))
            scratch["acc"] = pltpu.VMEM((2, rows, width), F32)
            if "sums" in state:
                ins["sums"] = pinned(state["sums"])
            if last:
                n_out = n_grid if direct else 1
                out = shape(2, rows // n_out, width, kind=BF16 if direct else F32)
                outs.update({f"rows{k}": pinned(out) for k in range(n_out)})
            else:
                outs["new_sums"] = pinned(shape(2, rows, width, kind=F32))
        if do_grads:
            ins.update(held("tok_t", "cot", "mg", "mu"))
            outs["gg"] = (shape(width, units, kind=F32), ANY)
            outs["gu"] = (shape(width, units, kind=F32), ANY)
            outs["gd"] = (shape(units, width, kind=F32), ANY)
            scratch["masked_act"] = pltpu.VMEM((2, pair * rows, size), BF16)
            scratch["masked_cot"] = pltpu.VMEM((spots * rows, width), BF16)
            scratch["col_slots"] = pltpu.VMEM((4, pair * BLK, size), F32)
            scratch["row_slots"] = pltpu.VMEM((2, tile, width), F32)
            scratch["col_sems"] = pltpu.SemaphoreType.DMA((4,))
            scratch["row_sems"] = pltpu.SemaphoreType.DMA((2,))
            for k in ("gg", "gu", "gd"):
                if k in state:
                    ins["old_" + k] = (state[k], ANY)
                    aliases["old_" + k] = k
            if "rows0" in state:
                ins["after"] = (state["rows0"], ANY)
        got = call(
            functools.partial(back_kernel, which, starts[p], do_rows, do_grads),
            "_".join(["back"] + ["rows"] * do_rows + ["grads"] * do_grads),
            place,
            ins,
            outs,
            scratch=scratch,
            aliases=aliases,
            cost=cost(p, 3 * do_rows + 3 * do_grads, 6 * do_grads),
            vmem=grant(9 if do_grads else 3),
        )
        return {**state, **{k.replace("new_", ""): v for k, v in got.items()}}

    sent, sums, theirs, after = [], [], [], None
    for p in range(n + 1):
        if p < n:
            after = partials(1, p, after)["send"]
            sent.append(swap(after))
        if p > 0:
            got = partials(0, p - 1, after, sent[p - 1])
            after = got["own"]
            sums.append(after)
            theirs.append(across(got["send"]))

    state = {}
    for p in range(n):
        last = p == n - 1
        act = activate(sums[p], theirs[p], state.get("sums", after))
        act_other = swap(act)
        state = back(0, p, act, True, not last, state)
        state = back(1, p, act_other, True, not last, state, last)
        if last:
            state = back(0, p, act, False, True, state)
            state = back(1, p, act_other, False, True, state)

    if direct:
        both = state["rows0"].astype(F32)
        for s in range(1, n_grid):
            both += trade(state[f"rows{s}"], s).astype(F32)
    else:
        both = lax.psum_scatter(state["rows0"], "grid", scatter_dimension=1, tiled=True)
    both = both.astype(BF16)
    return (both[0], both[1], state["gg"], state["gu"], state["gd"])


def solution(mesh):
    in_specs = (
        P(("groups", "grid"), "dp"),
        P("dp", "grid"),
        P("dp", "grid"),
        P("grid", "dp"),
        P(("groups", "dp"), "grid"),
        P(("groups", "dp"), "grid"),
        P(("groups", "grid"), "dp"),
        P(("groups", "grid"), "dp"),
    )
    out_specs = (
        P(("groups", "grid"), "dp"),
        P(("groups", "grid"), "dp"),
        P(("groups", "dp"), "grid"),
        P(("groups", "dp"), "grid"),
        P(("groups", "grid"), "dp"),
    )
    sizes = (mesh.shape["grid"], mesh.shape["dp"])
    return jax.shard_map(
        functools.partial(shards, sizes),
        mesh=mesh,
        in_specs=in_specs,
        out_specs=out_specs,
        check_vma=False,
    )
```

time: 90.4 us -> 77.7 us (0.86)
  Pallas kernels: 66 us -> 55.2 us
  local copies, waits for them, and re-layouts: 2.69 us -> 0.63 us
    pallas_call x19, Pallas kernels: 66 us -> 55.2 us  [call(): pl.pallas_call(body, out_shape=[shape for shape, _ in outs.values()], gri...]
    ppermute x3, waiting for transfers between devices: 1.8 us -> 4.75 us  [across(): lax.ppermute(array, 'dp', [(i, (i // 2 + s) % pairs * 2 + i % 2) for i in...]
    ppermute x6, waiting for transfers between devices: 2.52 us -> 0.02 us  [trade(): return lax.ppermute(array, 'grid', [(i, i ^ s) for i in range(n_grid)])]
    unnamed x6 -> x0, local copies, waits for them, and re-layouts: 2.06 us -> none
  transfers between devices with their start and end apart: 15 -> 15, of which waited for: 2 -> 1; matrix products, arithmetic and copies ran while one was open for 0% -> 0% of each run, Pallas kernels for 65% -> 61%
where the time goes in v6:
time: 77.7 us; the launch traced here: 77.5 us
  Pallas kernels  55.2 us (71%)
  starting transfers between devices  15.1 us (19%)
  waiting for transfers between devices  4.78 us (6%)
  other arithmetic  0.9 us (1%)
  between operations  0.89 us (1%)
    pallas_call x19, Pallas kernels, call(): pl.pallas_call(body, out_shape=[shape for shape, _ in outs.values()], gri...  55.2 us
    ppermute x6, starting transfers between devices, trade(): return lax.ppermute(array, 'grid', [(i, i ^ s) for i in range(n_grid)])  10.2 us
    ppermute x3, waiting for transfers between devices, across(): lax.ppermute(array, 'dp', [(i, (i // 2 + s) % pairs * 2 + i % 2) for i in...  4.75 us
    ppermute x3, starting transfers between devices, across(): lax.ppermute(array, 'dp', [(i, (i // 2 + s) % pairs * 2 + i % 2) for i in...  3.77 us
  transfers between devices with their start and end apart: 15, of which 1 were waited for; matrix products, arithmetic and copies ran while one was open for 0% of the time, Pallas kernels for 61%

profile of v6, /device:TPU:0, one launch (start us, length us, event | category | flops | bytes accessed | tf_op | source)
XLA Modules:
  0.0 77.5 jit_solution(12663160103775833419)
XLA Ops:
  0.6 0.8 %pad_maximum_fusion.refs_2_ = bf16[2,16,1024]{2,1,0:T(8,128)(2,1)S(1)} fusion(bf16[1,16,1024]{2,1,0:T(8,128)(2,1)} %bitcast.9, bf16[1,16,1024]{2,1,0:T(8,128)(2,1)} %bitcast.10), kind=kLoop, calls=%fused_computation.1 | loop fusion | flops 32768 | bytes 131072 | tf_op jit(solution)/shard_map/stack | solution.py:319
  1.4 5.1 %collective-permute-start.2 = (bf16[2,16,1024]{2,1,0:T(8,128)(2,1)S(1)}, bf16[2,16,1024]{2,1,0:T(8,128)(2,1)S(1)}, u32[]{:S(2)}, u32[]{:S(2)}) collective-permute-start(bf16[2,16,1024]{2,1,0:T(8,128)(2,1)S(1)} %pad_maximum_fusion.refs_2_), channel_id=1, source_target_pairs={{0,12},{4,8},{8,4},{12,0},{1,13},{5,9},{9,5},{13,1},{2,14},{6,10},... | collective-permute-start | bytes 196616 | tf_op jit(solution)/shard_map/ppermute | solution.py:289
  6.5 0.0 collective-permute-start.1
  6.5 0.6 collective-permute-start
  7.2 0.1 pad_add_fusion.refs_0_
  7.2 6.2 %fetch.1 = (f32[8,1,4096]{2,1,0:T(1,128)S(1)}, f32[8,1,4096]{2,1,0:T(1,128)S(1)}, f32[8,1,4096]{2,1,0:T(1,128)S(1)}, f32[32,1,1024]{2,1,0:T(1,128)S(1)}, f32[32,...) custom-call(s32[2]{0:T(128)S(1)} %pad_add_fusion.refs_0_, ...), custom_call_target="tpu_custom_call" | custom-call | bytes 12582912 | tf_op jit(solution)/shard_map/fetch/pallas_call | solution.py:42
  13.5 0.0 collective-permute-done.2.refs_5_
  13.5 0.0 collective-permute-done.1.refs_4_
  13.5 0.0 collective-permute-done.refs_3_
  13.5 0.7 assemble.1
  14.2 3.9 %partials.6 = (f32[3,64,768]{2,1,0:T(8,128)S(1)}, bf16[1024,768]{1,0:T(8,128)(2,1)S(1)}, bf16[1024,768]{1,0:T(8,128)(2,1)S(1)}, bf16[768,1024]{1,0:T(8,128)(2,1)S(1)}) custom-call(s32[2]{0:T(128)S(1)} %pad_add_fusion.refs_0_, bf16[4,128,256]{2,1,0:T(8,128)(2,1)S(1)} %get-tuple-element.69.refs_1_, bf16[4,128,256]{2,1,0:T(8,128)(2,1)S(1)} %get-tuple-element.70.refs_2_, ...), custom_call_target="tpu_custom_call" | custom-call | flops 301989888 | bytes 4718592 | tf_op jit(solution)/shard_map/partials/pallas_call | solution.py:42
  18.1 0.1 collective-permute-start.3
  18.2 3.9 %partials.7 = (f32[3,64,768]{2,1,0:T(8,128)S(1)}, bf16[1024,768]{1,0:T(8,128)(2,1)S(1)}, bf16[1024,768]{1,0:T(8,128)(2,1)S(1)}, bf16[768,1024]{1,0:T(8,128)(2,1)S(1)}) custom-call(s32[2]{0:T(128)S(1)} %pad_add_fusion.refs_0_, bf16[4,128,256]{2,1,0:T(8,128)(2,1)S(1)} %get-tuple-element.69.refs_1_, bf16[4,128,256]{2,1,0:T(8,128)(2,1)S(1)} %get-tuple-element.70.refs_2_, ...), custom_call_target="tpu_custom_call" | custom-call | flops 301989888 | bytes 4718592 | tf_op jit(solution)/shard_map/partials/pallas_call | solution.py:42
  22.1 0.5 collective-permute-start.4
  22.6 0.0 collective-permute-done.3.refs_10_
  22.6 1.6 %partials.8 = (f32[3,64,768]{2,1,0:T(8,128)S(1)}, bf16[3,64,768]{2,1,0:T(8,128)(2,1)S(1)}) custom-call(s32[2]{0:T(128)S(1)} %pad_add_fusion.refs_0_, bf16[4,128,256]{2,1,0:T(8,128)(2,1)S(1)} %get-tuple-element.69.refs_1_, bf16[4,128,256]{2,1,0:T(8,128)(2,1)S(1)} %get-tuple-element.70.refs_2_, ...), custom_call_target="tpu_custom_call" | custom-call | flops 301989888 | bytes 4718592 | tf_op jit(solution)/shard_map/partials/pallas_call | solution.py:42
  24.3 3.1 %partials.9 = (f32[3,64,512]{2,1,0:T(8,128)S(1)}, bf16[1024,512]{1,0:T(8,128)(2,1)S(1)}, bf16[1024,512]{1,0:T(8,128)(2,1)S(1)}, bf16[512,1024]{1,0:T(8,128)(2,1)S(1)}) custom-call(s32[2]{0:T(128)S(1)} %pad_add_fusion.refs_0_, bf16[4,128,256]{2,1,0:T(8,128)(2,1)S(1)} %get-tuple-element.69.refs_1_, bf16[4,128,256]{2,1,0:T(8,128)(2,1)S(1)} %get-tuple-element.70.refs_2_, ...), custom_call_target="tpu_custom_call" | custom-call | flops 201326592 | bytes 3145728 | tf_op jit(solution)/shard_map/partials/pallas_call | solution.py:42
  27.4 0.1 collective-permute-start.5
  27.5 1.7 %collective-permute-start.6 = (bf16[3,64,768]{2,1,0:T(8,128)(2,1)S(1)}, bf16[3,64,768]{2,1,0:T(8,128)(2,1)S(1)}, u32[]{:S(2)}, u32[]{:S(2)}) collective-permute-start(bf16[3,64,768]{2,1,0:T(8,128)(2,1)S(1)} %get-tuple-element.97), channel_id=1, source_target_pairs={{0,2},{1,3},{2,0},{3,1},{4,6},{5,7},{6,4},{7,5},{8,10},{9,11},{10,... | collective-permute-start | bytes 884744 | tf_op jit(solution)/shard_map/ppermute | solution.py:296
  29.1 0.0 collective-permute-done.4.refs_10_
  29.2 1.6 %partials.10 = (f32[3,64,768]{2,1,0:T(8,128)S(1)}, bf16[3,64,768]{2,1,0:T(8,128)(2,1)S(1)}) custom-call(s32[2]{0:T(128)S(1)} %pad_add_fusion.refs_0_, bf16[4,128,256]{2,1,0:T(8,128)(2,1)S(1)} %get-tuple-element.69.refs_1_, bf16[4,128,256]{2,1,0:T(8,128)(2,1)S(1)} %get-tuple-element.70.refs_2_, ...), custom_call_target="tpu_custom_call" | custom-call | flops 301989888 | bytes 4718592 | tf_op jit(solution)/shard_map/partials/pallas_call | solution.py:42
  30.8 0.0 collective-permute-done.5.refs_10_
  30.8 1.3 %partials.11 = (f32[3,64,512]{2,1,0:T(8,128)S(1)}, bf16[3,64,512]{2,1,0:T(8,128)(2,1)S(1)}) custom-call(s32[2]{0:T(128)S(1)} %pad_add_fusion.refs_0_, bf16[4,128,256]{2,1,0:T(8,128)(2,1)S(1)} %get-tuple-element.69.refs_1_, bf16[4,128,256]{2,1,0:T(8,128)(2,1)S(1)} %get-tuple-element.70.refs_2_, ...), custom_call_target="tpu_custom_call" | custom-call | flops 201326592 | bytes 3145728 | tf_op jit(solution)/shard_map/partials/pallas_call | solution.py:42
  32.1 4.7 %collective-permute-done.6.refs_3_ = bf16[3,64,768]{2,1,0:T(8,128)(2,1)S(1)} collective-permute-done((bf16[3,64,768]{2,1,0:T(8,128)(2,1)S(1)}, bf16[3,64,768]{2,1,0:T(8,128)(2,1)S(1)}, u32[]{:S(2)}, u32[]{:S(2)}) %collective-permute-start.6) | collective-permute-done | bytes 294944 | tf_op jit(solution)/shard_map/ppermute | solution.py:296
  36.9 0.7 activate.3.refs_1_
  37.6 0.1 collective-permute-start.7
  37.6 1.7 %collective-permute-start.8 = (bf16[3,64,768]{2,1,0:T(8,128)(2,1)S(1)}, bf16[3,64,768]{2,1,0:T(8,128)(2,1)S(1)}, u32[]{:S(2)}, u32[]{:S(2)}) collective-permute-start(bf16[3,64,768]{2,1,0:T(8,128)(2,1)S(1)} %get-tuple-element.108), channel_id=1, source_target_pairs={{0,2},{1,3},{2,0},{3,1},{4,6},{5,7},{6,4},{7,5},{8,10},{9,11},{10,... | collective-permute-start | bytes 884744 | tf_op jit(solution)/shard_map/ppermute | solution.py:296
  39.3 5.1 %back_rows_grads.4 = (f32[2,64,1024]{2,1,0:T(8,128)S(1)}, f32[1024,4096]{1,0:T(8,128)}, f32[1024,4096]{1,0:T(8,128)}, f32[4096,1024]{1,0:T(8,128)}) custom-call(s32[2]{0:T(128)S(1)} %pad_add_fusion.refs_0_, bf16[3,64,768]{2,1,0:T(8,128)(2,1)S(1)} %activate.3.refs_1_, f32[32,1,1024]{2,1,0:T(1,128)S(1)} %get-tuple-element.98.refs_2_, ...), custom_call_target="tpu_custom_call" | custom-call | flops 603979776 | bytes 9437184 | tf_op jit(solution)/shard_map/back_rows_grads/pallas_call | solution.py:42
  44.5 0.0 collective-permute-done.7.refs_1_
  44.5 5.3 %back_rows_grads.5 = (f32[2,64,1024]{2,1,0:T(8,128)S(1)}, f32[1024,4096]{1,0:T(8,128)}, f32[1024,4096]{1,0:T(8,128)}, f32[4096,1024]{1,0:T(8,128)}) custom-call(s32[2]{0:T(128)S(1)} %pad_add_fusion.refs_0_, bf16[3,64,768]{2,1,0:T(8,128)(2,1)S(1)} %collective-permute-done.7.refs_1_, ...), custom_call_target="tpu_custom_call", output_to_operand_aliasing={{1}: (13, {}), {2}: (14, {}), {3}: (15, {})} | custom-call | flops 603979776 | bytes 9437184 | tf_op jit(solution)/shard_map/back_rows_grads/pallas_call | solution.py:42
  49.8 0.0 collective-permute-done.8.refs_3_
  49.8 0.7 activate.4.refs_1_
  50.5 0.2 collective-permute-start.9
  50.8 0.4 collective-permute-start.10
  51.1 5.2 %back_rows_grads.6 = (f32[2,64,1024]{2,1,0:T(8,128)S(1)}, f32[1024,4096]{1,0:T(8,128)}, f32[1024,4096]{1,0:T(8,128)}, f32[4096,1024]{1,0:T(8,128)}) custom-call(s32[2]{0:T(128)S(1)} %pad_add_fusion.refs_0_, bf16[3,64,768]{2,1,0:T(8,128)(2,1)S(1)} %activate.4.refs_1_, ...), custom_call_target="tpu_custom_call", output_to_operand_aliasing={{1}: (13, {}), {2}: (14, {}), {3}: (15, {})} | custom-call | flops 603979776 | bytes 9437184 | tf_op jit(solution)/shard_map/back_rows_grads/pallas_call | solution.py:42
  56.3 0.0 collective-permute-done.9.refs_1_
  56.3 5.2 %back_rows_grads.7 = (f32[2,64,1024]{2,1,0:T(8,128)S(1)}, f32[1024,4096]{1,0:T(8,128)}, f32[1024,4096]{1,0:T(8,128)}, f32[4096,1024]{1,0:T(8,128)}) custom-call(s32[2]{0:T(128)S(1)} %pad_add_fusion.refs_0_, bf16[3,64,768]{2,1,0:T(8,128)(2,1)S(1)} %collective-permute-done.9.refs_1_, ...), custom_call_target="tpu_custom_call", output_to_operand_aliasing={{1}: (13, {}), {2}: (14, {}), {3}: (15, {})} | custom-call | flops 603979776 | bytes 9437184 | tf_op jit(solution)/shard_map/back_rows_grads/pallas_call | solution.py:42
  61.5 0.0 collective-permute-done.10.refs_3_
  61.5 0.6 activate.5.refs_1_
  62.1 0.1 collective-permute-start.11
  62.3 1.5 %back_rows.2.refs_8_ = f32[2,64,1024]{2,1,0:T(8,128)S(1)} custom-call(s32[2]{0:T(128)S(1)} %pad_add_fusion.refs_0_, bf16[3,64,512]{2,1,0:T(8,128)(2,1)S(1)} %activate.5.refs_1_, f32[32,1,1024]{2,1,0:T(1,128)S(1)} %get-tuple-element.98.refs_2_, bf16[1024,512]{1,0:T(8,128)(2,1)S(1)} %get-tuple-element.88.refs_6_.refs_3_, ...), custom_call_target="tpu_custom_call" | custom-call | flops 201326592 | tf_op jit(solution)/shard_map/back_rows/pallas_call | solution.py:42
  63.8 0.0 collective-permute-done.11.refs_1_
  63.8 1.5 %back_rows.3 = (bf16[2,16,1024]{2,1,0:T(8,128)(2,1)S(1)}, bf16[2,16,1024]{2,1,0:T(8,128)(2,1)S(1)}, bf16[2,16,1024]{2,1,0:T(8,128)(2,1)S(1)}, bf16[2,16,1024]{2,1,0:T(8,128)(2,1)S(1)}) custom-call(s32[2]{0:T(128)S(1)} %pad_add_fusion.refs_0_, bf16[3,64,512]{2,1,0:T(8,128)(2,1)S(1)} %collective-permute-done.11.refs_1_, ...), custom_call_target="tpu_custom_call" | custom-call | flops 201326592 | tf_op jit(solution)/shard_map/back_rows/pallas_call | solution.py:42
  65.4 1.5 %collective-permute-start.12 = (bf16[2,16,1024]{2,1,0:T(8,128)(2,1)S(1)}, bf16[2,16,1024]{2,1,0:T(8,128)(2,1)S(1)}, u32[]{:S(2)}, u32[]{:S(2)}) collective-permute-start(bf16[2,16,1024]{2,1,0:T(8,128)(2,1)S(1)} %get-tuple-element.119), channel_id=1, source_target_pairs={{0,4},{4,0},{8,12},{12,8},{1,5},{5,1},{9,13},{13,9},{2,6},{6,2},{1... | collective-permute-start | bytes 196616 | tf_op jit(solution)/shard_map/ppermute | solution.py:289
  66.8 2.9 %collective-permute-start.13 = (bf16[2,16,1024]{2,1,0:T(8,128)(2,1)S(1)}, bf16[2,16,1024]{2,1,0:T(8,128)(2,1)S(1)}, u32[]{:S(2)}, u32[]{:S(2)}) collective-permute-start(bf16[2,16,1024]{2,1,0:T(8,128)(2,1)S(1)} %get-tuple-element.120), channel_id=1, source_target_pairs={{0,8},{4,12},{8,0},{12,4},{1,9},{5,13},{9,1},{13,5},{2,10},{6,14},... | collective-permute-start | bytes 196616 | tf_op jit(solution)/shard_map/ppermute | solution.py:289
  69.7 0.1 collective-permute-start.14
  69.8 3.5 %back_grads.2 = (f32[1024,4096]{1,0:T(8,128)}, f32[1024,4096]{1,0:T(8,128)}, f32[4096,1024]{1,0:T(8,128)}) custom-call(s32[2]{0:T(128)S(1)} %pad_add_fusion.refs_0_, bf16[3,64,512]{2,1,0:T(8,128)(2,1)S(1)} %activate.5.refs_1_, f32[32,1,1024]{2,1,0:T(1,128)S(1)} %get-tuple-element.98.refs_2_, ...), custom_call_target="tpu_custom_call", output_to_operand_aliasing={{0}: (7, {}), {1}: (8, {}), {2}: (9, {})} | custom-call | flops 201326592 | bytes 6291456 | tf_op jit(solution)/shard_map/back_grads/pallas_call | solution.py:42
  73.3 3.5 %back_grads.3 = (f32[1024,4096]{1,0:T(8,128)}, f32[1024,4096]{1,0:T(8,128)}, f32[4096,1024]{1,0:T(8,128)}) custom-call(s32[2]{0:T(128)S(1)} %pad_add_fusion.refs_0_, bf16[3,64,512]{2,1,0:T(8,128)(2,1)S(1)} %collective-permute-done.11.refs_1_, ...), custom_call_target="tpu_custom_call", output_to_operand_aliasing={{0}: (7, {}), {1}: (8, {}), {2}: (9, {})} | custom-call | flops 201326592 | bytes 6291456 | tf_op jit(solution)/shard_map/back_grads/pallas_call | solution.py:42
  76.8 0.0 collective-permute-done.12
  76.8 0.0 collective-permute-done.13
  76.8 0.0 collective-permute-done.14
  76.9 0.6 slice_bitcast_fusion
  (1 shorter events, 0.0 us)
Async XLA Ops:
  1.4 12.1 %collective-permute-start.2 = (bf16[2,16,1024]{2,1,0:T(8,128)(2,1)S(1)}, bf16[2,16,1024]{2,1,0:T(8,128)(2,1)S(1)}, u32[]{:S(2)}, u32[]{:S(2)}) collective-permute-start(bf16[2,16,1024]{2,1,0:T(8,128)(2,1)S(1)} %pad_maximum_fusion.refs_2_), channel_id=1, source_target_pairs={{0,12},{4,8},{8,4},{12,0},{1,13},{5,9},{9,5},{13,1},{2,14},{6,10},... | collective-permute-start | bytes 196616 | tf_op jit(solution)/shard_map/ppermute | solution.py:289
  6.5 7.0 %collective-permute-start.1 = (bf16[2,16,1024]{2,1,0:T(8,128)(2,1)S(1)}, bf16[2,16,1024]{2,1,0:T(8,128)(2,1)S(1)}, u32[]{:S(2)}, u32[]{:S(2)}) collective-permute-start(bf16[2,16,1024]{2,1,0:T(8,128)(2,1)S(1)} %pad_maximum_fusion.refs_2_), channel_id=1, source_target_pairs={{0,8},{4,12},{8,0},{12,4},{1,9},{5,13},{9,1},{13,5},{2,10},{6,14},... | collective-permute-start | bytes 196616 | tf_op jit(solution)/shard_map/ppermute | solution.py:289
  6.5 7.0 %collective-permute-start = (bf16[2,16,1024]{2,1,0:T(8,128)(2,1)S(1)}, bf16[2,16,1024]{2,1,0:T(8,128)(2,1)S(1)}, u32[]{:S(2)}, u32[]{:S(2)}) collective-permute-start(bf16[2,16,1024]{2,1,0:T(8,128)(2,1)S(1)} %pad_maximum_fusion.refs_2_), channel_id=1, source_target_pairs={{0,4},{4,0},{8,12},{12,8},{1,5},{5,1},{9,13},{13,9},{2,6},{6,2},{1... | collective-permute-start | bytes 196616 | tf_op jit(solution)/shard_map/ppermute | solution.py:289
  18.1 4.5 %collective-permute-start.3 = (f32[3,64,768]{2,1,0:T(8,128)S(1)}, f32[3,64,768]{2,1,0:T(8,128)S(1)}, u32[]{:S(2)}, u32[]{:S(2)}) collective-permute-start(f32[3,64,768]{2,1,0:T(8,128)S(1)} %get-tuple-element.85.refs_9_), channel_id=1, source_target_pairs={{0,1},{1,0},{2,3},{3,2},{4,5},{5,4},{6,7},{7,6},{8,9},{9,8},{10,11... | collective-permute-start | bytes 1769480 | tf_op jit(solution)/shard_map/ppermute | solution.py:292
  22.1 7.1 %collective-permute-start.4 = (f32[3,64,768]{2,1,0:T(8,128)S(1)}, f32[3,64,768]{2,1,0:T(8,128)S(1)}, u32[]{:S(2)}, u32[]{:S(2)}) collective-permute-start(f32[3,64,768]{2,1,0:T(8,128)S(1)} %get-tuple-element.86.refs_9_), channel_id=1, source_target_pairs={{0,1},{1,0},{2,3},{3,2},{4,5},{5,4},{6,7},{7,6},{8,9},{9,8},{10,11... | collective-permute-start | bytes 1769480 | tf_op jit(solution)/shard_map/ppermute | solution.py:292
  27.4 3.4 %collective-permute-start.5 = (f32[3,64,512]{2,1,0:T(8,128)S(1)}, f32[3,64,512]{2,1,0:T(8,128)S(1)}, u32[]{:S(2)}, u32[]{:S(2)}) collective-permute-start(f32[3,64,512]{2,1,0:T(8,128)S(1)} %get-tuple-element.94.refs_9_), channel_id=1, source_target_pairs={{0,1},{1,0},{2,3},{3,2},{4,5},{5,4},{6,7},{7,6},{8,9},{9,8},{10,11... | collective-permute-start | bytes 1179656 | tf_op jit(solution)/shard_map/ppermute | solution.py:292
  27.5 9.4 %collective-permute-start.6 = (bf16[3,64,768]{2,1,0:T(8,128)(2,1)S(1)}, bf16[3,64,768]{2,1,0:T(8,128)(2,1)S(1)}, u32[]{:S(2)}, u32[]{:S(2)}) collective-permute-start(bf16[3,64,768]{2,1,0:T(8,128)(2,1)S(1)} %get-tuple-element.97), channel_id=1, source_target_pairs={{0,2},{1,3},{2,0},{3,1},{4,6},{5,7},{6,4},{7,5},{8,10},{9,11},{10,... | collective-permute-start | bytes 884744 | tf_op jit(solution)/shard_map/ppermute | solution.py:296
  37.6 6.9 %collective-permute-start.7 = (bf16[3,64,768]{2,1,0:T(8,128)(2,1)S(1)}, bf16[3,64,768]{2,1,0:T(8,128)(2,1)S(1)}, u32[]{:S(2)}, u32[]{:S(2)}) collective-permute-start(bf16[3,64,768]{2,1,0:T(8,128)(2,1)S(1)} %activate.3.refs_1_), channel_id=1, source_target_pairs={{0,1},{1,0},{2,3},{3,2},{4,5},{5,4},{6,7},{7,6},{8,9},{9,8},{10,11... | collective-permute-start | bytes 884744 | tf_op jit(solution)/shard_map/ppermute | solution.py:292
  37.6 12.2 %collective-permute-start.8 = (bf16[3,64,768]{2,1,0:T(8,128)(2,1)S(1)}, bf16[3,64,768]{2,1,0:T(8,128)(2,1)S(1)}, u32[]{:S(2)}, u32[]{:S(2)}) collective-permute-start(bf16[3,64,768]{2,1,0:T(8,128)(2,1)S(1)} %get-tuple-element.108), channel_id=1, source_target_pairs={{0,2},{1,3},{2,0},{3,1},{4,6},{5,7},{6,4},{7,5},{8,10},{9,11},{10,... | collective-permute-start | bytes 884744 | tf_op jit(solution)/shard_map/ppermute | solution.py:296
  50.5 5.8 %collective-permute-start.9 = (bf16[3,64,768]{2,1,0:T(8,128)(2,1)S(1)}, bf16[3,64,768]{2,1,0:T(8,128)(2,1)S(1)}, u32[]{:S(2)}, u32[]{:S(2)}) collective-permute-start(bf16[3,64,768]{2,1,0:T(8,128)(2,1)S(1)} %activate.4.refs_1_), channel_id=1, source_target_pairs={{0,1},{1,0},{2,3},{3,2},{4,5},{5,4},{6,7},{7,6},{8,9},{9,8},{10,11... | collective-permute-start | bytes 884744 | tf_op jit(solution)/shard_map/ppermute | solution.py:292
  50.8 10.7 %collective-permute-start.10 = (bf16[3,64,512]{2,1,0:T(8,128)(2,1)S(1)}, bf16[3,64,512]{2,1,0:T(8,128)(2,1)S(1)}, u32[]{:S(2)}, u32[]{:S(2)}) collective-permute-start(bf16[3,64,512]{2,1,0:T(8,128)(2,1)S(1)} %get-tuple-element.117), channel_id=1, source_target_pairs={{0,2},{1,3},{2,0},{3,1},{4,6},{5,7},{6,4},{7,5},{8,10},{9,11},{10,... | collective-permute-start | bytes 589832 | tf_op jit(solution)/shard_map/ppermute | solution.py:296
  62.1 1.7 %collective-permute-start.11 = (bf16[3,64,512]{2,1,0:T(8,128)(2,1)S(1)}, bf16[3,64,512]{2,1,0:T(8,128)(2,1)S(1)}, u32[]{:S(2)}, u32[]{:S(2)}) collective-permute-start(bf16[3,64,512]{2,1,0:T(8,128)(2,1)S(1)} %activate.5.refs_1_), channel_id=1, source_target_pairs={{0,1},{1,0},{2,3},{3,2},{4,5},{5,4},{6,7},{7,6},{8,9},{9,8},{10,11... | collective-permute-start | bytes 589832 | tf_op jit(solution)/shard_map/ppermute | solution.py:292
  65.4 11.4 %collective-permute-start.12 = (bf16[2,16,1024]{2,1,0:T(8,128)(2,1)S(1)}, bf16[2,16,1024]{2,1,0:T(8,128)(2,1)S(1)}, u32[]{:S(2)}, u32[]{:S(2)}) collective-permute-start(bf16[2,16,1024]{2,1,0:T(8,128)(2,1)S(1)} %get-tuple-element.119), channel_id=1, source_target_pairs={{0,4},{4,0},{8,12},{12,8},{1,5},{5,1},{9,13},{13,9},{2,6},{6,2},{1... | collective-permute-start | bytes 196616 | tf_op jit(solution)/shard_map/ppermute | solution.py:289
  66.8 10.0 %collective-permute-start.13 = (bf16[2,16,1024]{2,1,0:T(8,128)(2,1)S(1)}, bf16[2,16,1024]{2,1,0:T(8,128)(2,1)S(1)}, u32[]{:S(2)}, u32[]{:S(2)}) collective-permute-start(bf16[2,16,1024]{2,1,0:T(8,128)(2,1)S(1)} %get-tuple-element.120), channel_id=1, source_target_pairs={{0,8},{4,12},{8,0},{12,4},{1,9},{5,13},{9,1},{13,5},{2,10},{6,14},... | collective-permute-start | bytes 196616 | tf_op jit(solution)/shard_map/ppermute | solution.py:289
  69.7 7.1 %collective-permute-start.14 = (bf16[2,16,1024]{2,1,0:T(8,128)(2,1)S(1)}, bf16[2,16,1024]{2,1,0:T(8,128)(2,1)S(1)}, u32[]{:S(2)}, u32[]{:S(2)}) collective-permute-start(bf16[2,16,1024]{2,1,0:T(8,128)(2,1)S(1)} %get-tuple-element.121), channel_id=1, source_target_pairs={{0,12},{4,8},{8,4},{12,0},{1,13},{5,9},{9,5},{13,1},{2,14},{6,10},... | collective-permute-start | bytes 196616 | tf_op jit(solution)/shard_map/ppermute | solution.py:289

commit v7 on v6

--- a/solution.py
+++ b/solution.py
@@ -12,7 +12,8 @@
 MIB = 1024 * 1024
 DEPTH = 256
 ANY = pl.BlockSpec(memory_space=pl.ANY)
-PIECES = [3, 3, 2]
+PIECES = [2, 3, 3]
+SPLIT = 4
 KEPT = ("kg", "ku", "kd")
 F32 = jnp.float32
 BF16 = jnp.bfloat16
@@ -31,7 +32,7 @@
     return (pltpu.with_memory_space_constraint(array, pltpu.VMEM), spec)
 
 
-def call(kernel, name, scalars, ins, outs, scratch=None, aliases=None, cost=None, vmem=2):
+def call(kernel, name, scalars, ins, outs, scratch=None, aliases=None, vmem=2):
     scratch = scratch or {}
     names = ["place", *ins, *outs, *scratch]
     in_names, out_names = list(ins), list(outs)
@@ -53,7 +54,7 @@
             1 + in_names.index(i): out_names.index(o) for i, o in (aliases or {}).items()
         },
         compiler_params=pltpu.CompilerParams(vmem_limit_bytes=vmem * MIB),
-        cost_estimate=cost,
+        cost_estimate=pl.CostEstimate(flops=1, bytes_accessed=1, transcendentals=0),
         name=name,
     )(scalars, *[array for array, _ in ins.values()])
     return dict(zip(out_names, results))
@@ -93,23 +94,31 @@
     return pl.ds(pl.multiple_of(start, BLK), size)
 
 
-def fetch(r, which, starts, into, sems):
+def fetch(r, loads, sems):
     copies = []
-    for start, (gate, up, down) in zip(starts, into):
-        at = span(r.place[which] + start, down.shape[0])
-        for source, target in (
-            (r.w_gate.at[:, at], gate),
-            (r.w_up.at[:, at], up),
-            (r.w_down.at[at, :], down),
-        ):
-            copies.append(pltpu.make_async_copy(source, target, sems.at[len(copies)]))
-            copies[-1].start()
+
+    for which, first, targets in loads:
+        gate, up, down = (getattr(r, name) for name in targets)
+        size, width = down.shape
+        base = r.place[which] + first
+        for source, target in ((r.w_gate, gate), (r.w_up, up)):
+            for row in range(0, width, width // SPLIT):
+                rows = slice(row, row + width // SPLIT)
+                copies.append((source.at[rows, span(base, size)], target.at[rows, :]))
+        for row in range(0, size, BLK):
+            copies.append((r.w_down.at[span(base + row, BLK), :], down.at[row : row + BLK, :]))
+    copies = [pltpu.make_async_copy(a, b, sems.at[k]) for k, (a, b) in enumerate(copies)]
+    for copy in copies:
+        copy.start()
     return copies
 
 
-def fetch_kernel(starts, r):
-    into = [[getattr(r, f"{k}{p}") for k in KEPT] for p in range(len(starts))]
-    copies = fetch(r, 1, starts, into, r.sems)
+def count_copies(sizes):
+    return sum(2 * SPLIT + size // BLK for size in sizes)
+
+
+def fetch_kernel(loads, r):
+    copies = fetch(r, loads, r.sems)
     spread(r)
     for copy in copies:
         copy.wait()
@@ -144,10 +153,8 @@
     return sum(value[b * rows : (b + 1) * rows, :] * m for b, m in enumerate(masks))
 
 
-def partial_kernel(which, start, tile, r):
-    copies = []
-    if hasattr(r, "sems"):
-        copies = fetch(r, 0, [start], [(r.new_kg, r.new_ku, r.new_kd)], r.sems)
+def partial_kernel(which, start, tile, loads, r):
+    copies = fetch(r, loads, r.sems) if loads else []
     pairs, _, size = r.tok_d.shape
     for first in range(0, r.send.shape[2], tile):
         at = span(r.place[which] + start + first, tile)
@@ -186,8 +193,8 @@
     r.act[2] = (back * silu).astype(BF16)
 
 
-def add_rows(r, block, local):
-    width, tile = r.acc.shape[2], r.act_d.shape[2]
+def add_rows(r, i, block, local):
+    width, tile = r.acc.shape[2], r.act_d.shape[3]
     size = min(DEPTH, width)
     for f in range(0, width, size):
         part = slice(f, f + size)
@@ -195,10 +202,10 @@
         def masks(mask):
             return [mask[block + b][:, part] for b in range(tile // BLK)]
 
-        r.acc[0, :, part] += masked_sum(r.act_d[0], r.kd[local, part], masks(r.md))
+        r.acc[0, :, part] += masked_sum(r.act_d[i, 0], r.kd[local, part], masks(r.md))
         r.acc[1, :, part] += masked_sum(
-            r.act_d[1], r.kg[part, local], masks(r.mgt), (1, 1)
-        ) + masked_sum(r.act_d[2], r.ku[part, local], masks(r.mut), (1, 1))
+            r.act_d[i, 1], r.kg[part, local], masks(r.mgt), (1, 1)
+        ) + masked_sum(r.act_d[i, 2], r.ku[part, local], masks(r.mut), (1, 1))
 
 
 class Outbox:
@@ -223,7 +230,7 @@
 
 def back_kernel(which, start, do_rows, do_grads, r):
     _, rows, size = r.act.shape
-    tile = r.act_d.shape[2]
+    tile = r.act_d.shape[3]
     base = r.place[which] + start
     at = span(base, size)
     r.act_d[...] = jnp.zeros_like(r.act_d)
@@ -233,7 +240,13 @@
     if do_grads:
         groups, height, _ = r.tok_t.shape
         by_cols, by_rows = Outbox(r.col_slots, r.col_sems), Outbox(r.row_slots, r.row_sems)
-    for i in range(max(groups, size // tile)):
+    tiles = [slice(i * tile, (i + 1) * tile) for i in range(size // tile)]
+    block = lax.div(base, BLK)
+    spots = tile // BLK
+    for i, local in enumerate(tiles):
+        for k in range(3 if do_rows else 1):
+            diagonal(r.act_d.at[i, k], r.act[k, :, local])
+    for i in range(max(groups, len(tiles)) if do_grads else 0):
         if i < groups:
             band = slice(i * height, (i + 1) * height)
             for out, k, mask in ((r.gg, 1, r.mg), (r.gu, 2, r.mu)):
@@ -242,19 +255,14 @@
                     keep = mask[i * (height // BLK) + j, :, at].astype(BF16)
                     right[j * rows : (j + 1) * rows, :] = r.act[k] * keep
                 by_cols.put(dot(r.tok_t[i], right[...]), out.at[band, at])
-        if i < size // tile:
-            local = slice(i * tile, (i + 1) * tile)
-            for k in range(3 if do_rows else 1):
-                diagonal(r.act_d.at[k], r.act[k, :, local])
-            block = lax.div(base, BLK) + i * (tile // BLK)
-            if do_grads:
-                for b in range(tile // BLK):
-                    keep = r.md[block + b].astype(BF16)
-                    r.masked_cot[b * rows : (b + 1) * rows, :] = r.cot[...] * keep
-                value = dot(r.act_d[0].T, r.masked_cot[...])
-                by_rows.put(value, r.gd.at[span(base + i * tile, tile), :])
-            if do_rows:
-                add_rows(r, block, local)
+        if i < len(tiles):
+            for b in range(spots):
+                keep = r.md[block + i * spots + b].astype(BF16)
+                r.masked_cot[b * rows : (b + 1) * rows, :] = r.cot[...] * keep
+            value = dot(r.act_d[i, 0].T, r.masked_cot[...])
+            by_rows.put(value, r.gd.at[span(base + i * tile, tile), :])
+    for i, local in enumerate(tiles if do_rows else []):
+        add_rows(r, i, block + i * spots, local)
     if do_rows:
         if hasattr(r, "new_sums"):
             r.new_sums[...] = r.acc[...]
@@ -301,12 +309,6 @@
             for s in range(1, pairs)
         ]
 
-    def cost(p, matmuls, mats):
-        step = width * split[p]
-        return pl.CostEstimate(
-            flops=2 * matmuls * rows * step, bytes_accessed=2 * mats * step, transcendentals=0
-        )
-
     def shape(*dims, kind=BF16):
         return jax.ShapeDtypeStruct(dims, kind)
 
@@ -325,22 +327,38 @@
     across_shape = shape(width // BLK, 1, units, kind=F32)
     along_shape = shape(units // BLK, 1, width, kind=F32)
     masks = {"mask_gate": mask_gate, "mask_up": mask_up, "mask_down_t": mask_down.T}
+    kept = {}
+
+    def loading(pieces):
+        loads, outs = [], {}
+        for which, p in pieces:
+            names = [f"{k}_{which}_{p}" for k in KEPT]
+            loads.append((which, starts[p], names))
+            outs.update({k: pinned(s) for k, s in zip(names, kept_shapes(p))})
+        count = count_copies([split[p] for _, p in pieces])
+        return loads, outs, {"sems": pltpu.SemaphoreType.DMA((count,))} if pieces else {}
+
+    def keep(got, pieces):
+        for which, p in pieces:
+            kept[which, p] = {k: got[f"{k}_{which}_{p}"] for k in KEPT}
+
+    first = [(1, p) for p in range(min(n, 2))]
+    loads, outs, scratch = loading(first)
     got = call(
-        functools.partial(fetch_kernel, starts),
+        functools.partial(fetch_kernel, loads),
         "fetch",
         place,
         {**weights, **{k: (hbm(m), whole(m)) for k, m in masks.items()}},
         {
             **{k: pinned(across_shape) for k in ("mg", "mu", "mdt")},
             **{k: pinned(along_shape) for k in ("mgt", "mut", "md")},
-            **{f"{k}{p}": pinned(s) for p in range(n) for k, s in zip(KEPT, kept_shapes(p))},
+            **outs,
         },
-        scratch={"sems": pltpu.SemaphoreType.DMA((3 * n,))},
-        cost=pl.CostEstimate(flops=0, bytes_accessed=6 * width * half, transcendentals=0),
+        scratch=scratch,
         vmem=grant(4),
     )
     values = {k: got[k] for k in ("mg", "mu", "mdt", "mgt", "mut", "md")}
-    kept = {(1, p): {k: got[f"{k}{p}"] for k in KEPT} for p in range(n)}
+    keep(got, first)
 
     pair = min(DEPTH, width) // BLK
     pair_shape = shape(width // (pair * BLK), pair * rows, pair * BLK)
@@ -364,32 +382,27 @@
     def held(*names):
         return {k: pinned(values[k]) for k in names}
 
-    def partials(which, p, after=None, received=None):
+    def partials(which, p, pieces, after=None, received=None):
         trio = (3, rows, split[p])
         ins = held("tok_d", "cot_d", "mg", "mu", "mdt")
         ins.update({k: pinned(v) for k, v in kept[which, p].items()})
-        outs, scratch = {"send": pinned(shape(*trio, kind=F32))}, {}
+        outs = {"send": pinned(shape(*trio, kind=F32))}
         if after is not None:
             ins["after"] = (after, ANY)
-        if received is None:
-            ins.update(weights)
-            outs.update({"new_" + k: pinned(s) for k, s in zip(KEPT, kept_shapes(p))})
-            scratch["sems"] = pltpu.SemaphoreType.DMA((3,))
-        else:
+        if received is not None:
             ins["received"] = pinned(received)
             outs = {"own": pinned(shape(*trio, kind=F32)), "send": pinned(shape(*trio))}
+        loads, fetched, scratch = loading(pieces)
         got = call(
-            functools.partial(partial_kernel, which, starts[p], tile),
+            functools.partial(partial_kernel, which, starts[p], tile, loads),
             "partials",
             place,
-            ins,
-            outs,
+            {**ins, **(weights if loads else {})},
+            {**outs, **fetched},
             scratch=scratch,
-            cost=cost(p, 3, 3),
             vmem=grant(2),
         )
-        if received is None:
-            kept[0, p] = {k: got["new_" + k] for k in KEPT}
+        keep(got, pieces)
         return got
 
     def activate(own, others, after):
@@ -402,7 +415,7 @@
         ins = {"act": pinned(act), **held("md")}
         outs, aliases = {}, {}
         spots, size = tile // BLK, split[p]
-        scratch = {"act_d": pltpu.VMEM((3, spots * rows, tile), BF16)}
+        scratch = {"act_d": pltpu.VMEM((size // tile, 3, spots * rows, tile), BF16)}
         if do_rows:
             ins.update({k: pinned(v) for k, v in kept[which, p].items()})
             ins.update(held("mgt", "mut"))
@@ -422,10 +435,11 @@
             outs["gd"] = (shape(units, width, kind=F32), ANY)
             scratch["masked_act"] = pltpu.VMEM((2, pair * rows, size), BF16)
             scratch["masked_cot"] = pltpu.VMEM((spots * rows, width), BF16)
-            scratch["col_slots"] = pltpu.VMEM((4, pair * BLK, size), F32)
-            scratch["row_slots"] = pltpu.VMEM((2, tile, width), F32)
-            scratch["col_sems"] = pltpu.SemaphoreType.DMA((4,))
-            scratch["row_sems"] = pltpu.SemaphoreType.DMA((2,))
+            by_cols, by_rows = 2 * width // (pair * BLK), size // tile
+            scratch["col_slots"] = pltpu.VMEM((by_cols, pair * BLK, size), F32)
+            scratch["row_slots"] = pltpu.VMEM((by_rows, tile, width), F32)
+            scratch["col_sems"] = pltpu.SemaphoreType.DMA((by_cols,))
+            scratch["row_sems"] = pltpu.SemaphoreType.DMA((by_rows,))
             for k in ("gg", "gu", "gd"):
                 if k in state:
                     ins["old_" + k] = (state[k], ANY)
@@ -440,18 +454,18 @@
             outs,
             scratch=scratch,
             aliases=aliases,
-            cost=cost(p, 3 * do_rows + 3 * do_grads, 6 * do_grads),
-            vmem=grant(9 if do_grads else 3),
+            vmem=grant(12 if do_grads else 3),
         )
         return {**state, **{k.replace("new_", ""): v for k, v in got.items()}}
 
     sent, sums, theirs, after = [], [], [], None
     for p in range(n + 1):
         if p < n:
-            after = partials(1, p, after)["send"]
+            after = partials(1, p, [(0, p)], after)["send"]
             sent.append(swap(after))
         if p > 0:
-            got = partials(0, p - 1, after, sent[p - 1])
+            ahead = [(1, p + 1)] if p + 1 < n else []
+            got = partials(0, p - 1, ahead, after, sent[p - 1])
             after = got["own"]
             sums.append(after)
             theirs.append(across(got["send"]))

time: 77.7 us -> 75.1 us (0.967)
  waiting for transfers between devices: 4.78 us -> 2.37 us
    ppermute x3, waiting for transfers between devices: 4.75 us -> 2.34 us  [across(): lax.ppermute(array, 'dp', [(i, (i // 2 + s) % pairs * 2 + i % 2) for i in...]
  transfers between devices with their start and end apart: 15 -> 15, of which waited for: 1 -> 1; matrix products, arithmetic and copies ran while one was open for 0% -> 0% of each run, Pallas kernels for 61% -> 63%
where the time goes in v7:
time: 75.1 us; the launch traced here: 74.9 us
  Pallas kernels  54.7 us (73%)
  starting transfers between devices  15.4 us (21%)
  waiting for transfers between devices  2.37 us (3%)
  other arithmetic  0.9 us (1%)
  between operations  0.89 us (1%)
    pallas_call x19, Pallas kernels, call(): pl.pallas_call(body, out_shape=[shape for shape, _ in outs.values()], gri...  54.7 us
    ppermute x6, starting transfers between devices, trade(): return lax.ppermute(array, 'grid', [(i, i ^ s) for i in range(n_grid)])  10.2 us
    ppermute x3, starting transfers between devices, across(): lax.ppermute(array, 'dp', [(i, (i // 2 + s) % pairs * 2 + i % 2) for i in...  3.77 us
    ppermute x3, waiting for transfers between devices, across(): lax.ppermute(array, 'dp', [(i, (i // 2 + s) % pairs * 2 + i % 2) for i in...  2.34 us
  transfers between devices with their start and end apart: 15, of which 1 were waited for; matrix products, arithmetic and copies ran while one was open for 0% of the time, Pallas kernels for 63%

profile of v7, /device:TPU:0, one launch (start us, length us, event | category | flops | bytes accessed | tf_op | source)
XLA Modules:
  0.0 74.9 jit_solution(12196636371350465546)
XLA Ops:
  0.6 0.8 %pad_maximum_fusion.refs_2_ = bf16[2,16,1024]{2,1,0:T(8,128)(2,1)S(1)} fusion(bf16[1,16,1024]{2,1,0:T(8,128)(2,1)} %bitcast.9, bf16[1,16,1024]{2,1,0:T(8,128)(2,1)} %bitcast.10), kind=kLoop, calls=%fused_computation.1 | loop fusion | flops 32768 | bytes 131072 | tf_op jit(solution)/shard_map/stack | solution.py:321
  1.4 5.1 %collective-permute-start.2 = (bf16[2,16,1024]{2,1,0:T(8,128)(2,1)S(1)}, bf16[2,16,1024]{2,1,0:T(8,128)(2,1)S(1)}, u32[]{:S(2)}, u32[]{:S(2)}) collective-permute-start(bf16[2,16,1024]{2,1,0:T(8,128)(2,1)S(1)} %pad_maximum_fusion.refs_2_), channel_id=1, source_target_pairs={{0,12},{4,8},{8,4},{12,0},{1,13},{5,9},{9,5},{13,1},{2,14},{6,10},... | collective-permute-start | bytes 196616 | tf_op jit(solution)/shard_map/ppermute | solution.py:297
  6.5 0.0 collective-permute-start.1
  6.5 0.6 collective-permute-start
  7.2 0.1 pad_add_fusion.refs_0_
  7.2 5.0 %fetch.1 = (f32[8,1,4096]{2,1,0:T(1,128)S(1)}, f32[8,1,4096]{2,1,0:T(1,128)S(1)}, f32[8,1,4096]{2,1,0:T(1,128)S(1)}, f32[32,1,1024]{2,1,0:T(1,128)S(1)}, f32[32,...) custom-call(s32[2]{0:T(128)S(1)} %pad_add_fusion.refs_0_, ...), custom_call_target="tpu_custom_call" | custom-call | flops 1 | bytes 1 | tf_op jit(solution)/shard_map/fetch/pallas_call | solution.py:43
  12.2 0.0 collective-permute-done.2.refs_5_
  12.2 0.0 collective-permute-done.1.refs_4_
  12.2 0.0 collective-permute-done.refs_3_
  12.3 0.7 assemble.1
  13.0 3.1 %partials.6 = (f32[3,64,512]{2,1,0:T(8,128)S(1)}, bf16[1024,512]{1,0:T(8,128)(2,1)S(1)}, bf16[1024,512]{1,0:T(8,128)(2,1)S(1)}, bf16[512,1024]{1,0:T(8,128)(2,1)S(1)}) custom-call(s32[2]{0:T(128)S(1)} %pad_add_fusion.refs_0_, bf16[4,128,256]{2,1,0:T(8,128)(2,1)S(1)} %get-tuple-element.69.refs_1_, bf16[4,128,256]{2,1,0:T(8,128)(2,1)S(1)} %get-tuple-element.70.refs_2_, ...), custom_call_target="tpu_custom_call" | custom-call | flops 1 | bytes 1 | tf_op jit(solution)/shard_map/partials/pallas_call | solution.py:43
  16.1 0.1 collective-permute-start.3
  16.2 3.9 %partials.7 = (f32[3,64,768]{2,1,0:T(8,128)S(1)}, bf16[1024,768]{1,0:T(8,128)(2,1)S(1)}, bf16[1024,768]{1,0:T(8,128)(2,1)S(1)}, bf16[768,1024]{1,0:T(8,128)(2,1)S(1)}) custom-call(s32[2]{0:T(128)S(1)} %pad_add_fusion.refs_0_, bf16[4,128,256]{2,1,0:T(8,128)(2,1)S(1)} %get-tuple-element.69.refs_1_, bf16[4,128,256]{2,1,0:T(8,128)(2,1)S(1)} %get-tuple-element.70.refs_2_, ...), custom_call_target="tpu_custom_call" | custom-call | flops 1 | bytes 1 | tf_op jit(solution)/shard_map/partials/pallas_call | solution.py:43
  20.1 0.5 collective-permute-start.4
  20.7 0.0 collective-permute-done.3.refs_10_
  20.7 3.6 %partials.8 = (f32[3,64,512]{2,1,0:T(8,128)S(1)}, bf16[3,64,512]{2,1,0:T(8,128)(2,1)S(1)}, bf16[1024,768]{1,0:T(8,128)(2,1)S(1)}, bf16[1024,768]{1,0:T(8,128)(2,1)S(1)}, bf16[768,1024]{1,0:T(8,128)(2,1)S(1)}) custom-call(s32[2]{0:T(128)S(1)} %pad_add_fusion.refs_0_, bf16[4,128,256]{2,1,0:T(8,128)(2,1)S(1)} %get-tuple-element.69.refs_1_, ...), custom_call_target="tpu_custom_call" | custom-call | flops 1 | bytes 1 | tf_op jit(solution)/shard_map/partials/pallas_call | solution.py:43
  24.3 3.9 %partials.9 = (f32[3,64,768]{2,1,0:T(8,128)S(1)}, bf16[1024,768]{1,0:T(8,128)(2,1)S(1)}, bf16[1024,768]{1,0:T(8,128)(2,1)S(1)}, bf16[768,1024]{1,0:T(8,128)(2,1)S(1)}) custom-call(s32[2]{0:T(128)S(1)} %pad_add_fusion.refs_0_, bf16[4,128,256]{2,1,0:T(8,128)(2,1)S(1)} %get-tuple-element.69.refs_1_, bf16[4,128,256]{2,1,0:T(8,128)(2,1)S(1)} %get-tuple-element.70.refs_2_, ...), custom_call_target="tpu_custom_call" | custom-call | flops 1 | bytes 1 | tf_op jit(solution)/shard_map/partials/pallas_call | solution.py:43
  28.2 0.1 collective-permute-start.5
  28.3 1.7 %collective-permute-start.6 = (bf16[3,64,512]{2,1,0:T(8,128)(2,1)S(1)}, bf16[3,64,512]{2,1,0:T(8,128)(2,1)S(1)}, u32[]{:S(2)}, u32[]{:S(2)}) collective-permute-start(bf16[3,64,512]{2,1,0:T(8,128)(2,1)S(1)} %get-tuple-element.97), channel_id=1, source_target_pairs={{0,2},{1,3},{2,0},{3,1},{4,6},{5,7},{6,4},{7,5},{8,10},{9,11},{10,... | collective-permute-start | bytes 589832 | tf_op jit(solution)/shard_map/ppermute | solution.py:304
  30.0 0.0 collective-permute-done.4.refs_10_
  30.0 1.6 %partials.10 = (f32[3,64,768]{2,1,0:T(8,128)S(1)}, bf16[3,64,768]{2,1,0:T(8,128)(2,1)S(1)}) custom-call(s32[2]{0:T(128)S(1)} %pad_add_fusion.refs_0_, bf16[4,128,256]{2,1,0:T(8,128)(2,1)S(1)} %get-tuple-element.69.refs_1_, bf16[4,128,256]{2,1,0:T(8,128)(2,1)S(1)} %get-tuple-element.70.refs_2_, ...), custom_call_target="tpu_custom_call" | custom-call | flops 1 | bytes 1 | tf_op jit(solution)/shard_map/partials/pallas_call | solution.py:43
  31.7 0.5 collective-permute-start.8
  32.1 0.0 collective-permute-done.5.refs_10_
  32.1 1.6 %partials.11 = (f32[3,64,768]{2,1,0:T(8,128)S(1)}, bf16[3,64,768]{2,1,0:T(8,128)(2,1)S(1)}) custom-call(s32[2]{0:T(128)S(1)} %pad_add_fusion.refs_0_, bf16[4,128,256]{2,1,0:T(8,128)(2,1)S(1)} %get-tuple-element.69.refs_1_, bf16[4,128,256]{2,1,0:T(8,128)(2,1)S(1)} %get-tuple-element.70.refs_2_, ...), custom_call_target="tpu_custom_call" | custom-call | flops 1 | bytes 1 | tf_op jit(solution)/shard_map/partials/pallas_call | solution.py:43
  33.8 2.3 %collective-permute-done.6.refs_3_ = bf16[3,64,512]{2,1,0:T(8,128)(2,1)S(1)} collective-permute-done((bf16[3,64,512]{2,1,0:T(8,128)(2,1)S(1)}, bf16[3,64,512]{2,1,0:T(8,128)(2,1)S(1)}, u32[]{:S(2)}, u32[]{:S(2)}) %collective-permute-start.6) | collective-permute-done | bytes 196640 | tf_op jit(solution)/shard_map/ppermute | solution.py:304
  36.1 0.6 activate.3.refs_1_
  36.7 0.1 collective-permute-start.7
  36.8 3.5 %back_rows_grads.4 = (f32[2,64,1024]{2,1,0:T(8,128)S(1)}, f32[1024,4096]{1,0:T(8,128)}, f32[1024,4096]{1,0:T(8,128)}, f32[4096,1024]{1,0:T(8,128)}) custom-call(s32[2]{0:T(128)S(1)} %pad_add_fusion.refs_0_, bf16[3,64,512]{2,1,0:T(8,128)(2,1)S(1)} %activate.3.refs_1_, f32[32,1,1024]{2,1,0:T(1,128)S(1)} %get-tuple-element.98.refs_2_, ...), custom_call_target="tpu_custom_call" | custom-call | flops 1 | bytes 1 | tf_op jit(solution)/shard_map/back_rows_grads/pallas_call | solution.py:43
  40.3 0.0 collective-permute-done.7.refs_1_
  40.4 3.5 %back_rows_grads.5 = (f32[2,64,1024]{2,1,0:T(8,128)S(1)}, f32[1024,4096]{1,0:T(8,128)}, f32[1024,4096]{1,0:T(8,128)}, f32[4096,1024]{1,0:T(8,128)}) custom-call(s32[2]{0:T(128)S(1)} %pad_add_fusion.refs_0_, bf16[3,64,512]{2,1,0:T(8,128)(2,1)S(1)} %collective-permute-done.7.refs_1_, ...), custom_call_target="tpu_custom_call", output_to_operand_aliasing={{1}: (13, {}), {2}: (14, {}), {3}: (15, {})} | custom-call | flops 1 | bytes 1 | tf_op jit(solution)/shard_map/back_rows_grads/pallas_call | solution.py:43
  43.9 0.0 collective-permute-done.8.refs_3_
  43.9 0.7 activate.4.refs_1_
  44.6 0.6 collective-permute-start.9
  45.2 1.6 %collective-permute-start.10 = (bf16[3,64,768]{2,1,0:T(8,128)(2,1)S(1)}, bf16[3,64,768]{2,1,0:T(8,128)(2,1)S(1)}, u32[]{:S(2)}, u32[]{:S(2)}) collective-permute-start(bf16[3,64,768]{2,1,0:T(8,128)(2,1)S(1)} %get-tuple-element.117), channel_id=1, source_target_pairs={{0,2},{1,3},{2,0},{3,1},{4,6},{5,7},{6,4},{7,5},{8,10},{9,11},{10,... | collective-permute-start | bytes 884744 | tf_op jit(solution)/shard_map/ppermute | solution.py:304
  46.8 4.5 %back_rows_grads.6 = (f32[2,64,1024]{2,1,0:T(8,128)S(1)}, f32[1024,4096]{1,0:T(8,128)}, f32[1024,4096]{1,0:T(8,128)}, f32[4096,1024]{1,0:T(8,128)}) custom-call(s32[2]{0:T(128)S(1)} %pad_add_fusion.refs_0_, bf16[3,64,768]{2,1,0:T(8,128)(2,1)S(1)} %activate.4.refs_1_, ...), custom_call_target="tpu_custom_call", output_to_operand_aliasing={{1}: (13, {}), {2}: (14, {}), {3}: (15, {})} | custom-call | flops 1 | bytes 1 | tf_op jit(solution)/shard_map/back_rows_grads/pallas_call | solution.py:43
  51.3 0.0 collective-permute-done.9.refs_1_
  51.3 4.5 %back_rows_grads.7 = (f32[2,64,1024]{2,1,0:T(8,128)S(1)}, f32[1024,4096]{1,0:T(8,128)}, f32[1024,4096]{1,0:T(8,128)}, f32[4096,1024]{1,0:T(8,128)}) custom-call(s32[2]{0:T(128)S(1)} %pad_add_fusion.refs_0_, bf16[3,64,768]{2,1,0:T(8,128)(2,1)S(1)} %collective-permute-done.9.refs_1_, ...), custom_call_target="tpu_custom_call", output_to_operand_aliasing={{1}: (13, {}), {2}: (14, {}), {3}: (15, {})} | custom-call | flops 1 | bytes 1 | tf_op jit(solution)/shard_map/back_rows_grads/pallas_call | solution.py:43
  55.9 0.0 collective-permute-done.10.refs_3_
  55.9 0.7 activate.5.refs_1_
  56.6 0.1 collective-permute-start.11
  56.7 2.0 %back_rows.2.refs_8_ = f32[2,64,1024]{2,1,0:T(8,128)S(1)} custom-call(s32[2]{0:T(128)S(1)} %pad_add_fusion.refs_0_, bf16[3,64,768]{2,1,0:T(8,128)(2,1)S(1)} %activate.5.refs_1_, f32[32,1,1024]{2,1,0:T(1,128)S(1)} %get-tuple-element.98.refs_2_, bf16[1024,768]{1,0:T(8,128)(2,1)S(1)} %get-tuple-element.88.refs_6_.refs_3_, ...), custom_call_target="tpu_custom_call" | custom-call | flops 1 | bytes 1 | tf_op jit(solution)/shard_map/back_rows/pallas_call | solution.py:43
  58.6 0.0 collective-permute-done.11.refs_1_
  58.6 2.0 %back_rows.3 = (bf16[2,16,1024]{2,1,0:T(8,128)(2,1)S(1)}, bf16[2,16,1024]{2,1,0:T(8,128)(2,1)S(1)}, bf16[2,16,1024]{2,1,0:T(8,128)(2,1)S(1)}, bf16[2,16,1024]{2,1,0:T(8,128)(2,1)S(1)}) custom-call(s32[2]{0:T(128)S(1)} %pad_add_fusion.refs_0_, bf16[3,64,768]{2,1,0:T(8,128)(2,1)S(1)} %collective-permute-done.11.refs_1_, ...), custom_call_target="tpu_custom_call" | custom-call | flops 1 | bytes 1 | tf_op jit(solution)/shard_map/back_rows/pallas_call | solution.py:43
  60.6 1.3 %collective-permute-start.12 = (bf16[2,16,1024]{2,1,0:T(8,128)(2,1)S(1)}, bf16[2,16,1024]{2,1,0:T(8,128)(2,1)S(1)}, u32[]{:S(2)}, u32[]{:S(2)}) collective-permute-start(bf16[2,16,1024]{2,1,0:T(8,128)(2,1)S(1)} %get-tuple-element.119), channel_id=1, source_target_pairs={{0,4},{4,0},{8,12},{12,8},{1,5},{5,1},{9,13},{13,9},{2,6},{6,2},{1... | collective-permute-start | bytes 196616 | tf_op jit(solution)/shard_map/ppermute | solution.py:297
  61.9 2.9 %collective-permute-start.13 = (bf16[2,16,1024]{2,1,0:T(8,128)(2,1)S(1)}, bf16[2,16,1024]{2,1,0:T(8,128)(2,1)S(1)}, u32[]{:S(2)}, u32[]{:S(2)}) collective-permute-start(bf16[2,16,1024]{2,1,0:T(8,128)(2,1)S(1)} %get-tuple-element.120), channel_id=1, source_target_pairs={{0,8},{4,12},{8,0},{12,4},{1,9},{5,13},{9,1},{13,5},{2,10},{6,14},... | collective-permute-start | bytes 196616 | tf_op jit(solution)/shard_map/ppermute | solution.py:297
  64.8 0.2 collective-permute-start.14
  65.1 4.5 %back_grads.2 = (f32[1024,4096]{1,0:T(8,128)}, f32[1024,4096]{1,0:T(8,128)}, f32[4096,1024]{1,0:T(8,128)}) custom-call(s32[2]{0:T(128)S(1)} %pad_add_fusion.refs_0_, bf16[3,64,768]{2,1,0:T(8,128)(2,1)S(1)} %activate.5.refs_1_, f32[32,1,1024]{2,1,0:T(1,128)S(1)} %get-tuple-element.98.refs_2_, ...), custom_call_target="tpu_custom_call", output_to_operand_aliasing={{0}: (7, {}), {1}: (8, {}), {2}: (9, {})} | custom-call | flops 1 | bytes 1 | tf_op jit(solution)/shard_map/back_grads/pallas_call | solution.py:43
  69.6 4.5 %back_grads.3 = (f32[1024,4096]{1,0:T(8,128)}, f32[1024,4096]{1,0:T(8,128)}, f32[4096,1024]{1,0:T(8,128)}) custom-call(s32[2]{0:T(128)S(1)} %pad_add_fusion.refs_0_, bf16[3,64,768]{2,1,0:T(8,128)(2,1)S(1)} %collective-permute-done.11.refs_1_, ...), custom_call_target="tpu_custom_call", output_to_operand_aliasing={{0}: (7, {}), {1}: (8, {}), {2}: (9, {})} | custom-call | flops 1 | bytes 1 | tf_op jit(solution)/shard_map/back_grads/pallas_call | solution.py:43
  74.1 0.0 collective-permute-done.12
  74.2 0.0 collective-permute-done.13
  74.2 0.0 collective-permute-done.14
  74.2 0.6 slice_bitcast_fusion
  (1 shorter events, 0.0 us)
Async XLA Ops:
  1.4 10.8 %collective-permute-start.2 = (bf16[2,16,1024]{2,1,0:T(8,128)(2,1)S(1)}, bf16[2,16,1024]{2,1,0:T(8,128)(2,1)S(1)}, u32[]{:S(2)}, u32[]{:S(2)}) collective-permute-start(bf16[2,16,1024]{2,1,0:T(8,128)(2,1)S(1)} %pad_maximum_fusion.refs_2_), channel_id=1, source_target_pairs={{0,12},{4,8},{8,4},{12,0},{1,13},{5,9},{9,5},{13,1},{2,14},{6,10},... | collective-permute-start | bytes 196616 | tf_op jit(solution)/shard_map/ppermute | solution.py:297
  6.5 5.7 %collective-permute-start.1 = (bf16[2,16,1024]{2,1,0:T(8,128)(2,1)S(1)}, bf16[2,16,1024]{2,1,0:T(8,128)(2,1)S(1)}, u32[]{:S(2)}, u32[]{:S(2)}) collective-permute-start(bf16[2,16,1024]{2,1,0:T(8,128)(2,1)S(1)} %pad_maximum_fusion.refs_2_), channel_id=1, source_target_pairs={{0,8},{4,12},{8,0},{12,4},{1,9},{5,13},{9,1},{13,5},{2,10},{6,14},... | collective-permute-start | bytes 196616 | tf_op jit(solution)/shard_map/ppermute | solution.py:297
  6.5 5.7 %collective-permute-start = (bf16[2,16,1024]{2,1,0:T(8,128)(2,1)S(1)}, bf16[2,16,1024]{2,1,0:T(8,128)(2,1)S(1)}, u32[]{:S(2)}, u32[]{:S(2)}) collective-permute-start(bf16[2,16,1024]{2,1,0:T(8,128)(2,1)S(1)} %pad_maximum_fusion.refs_2_), channel_id=1, source_target_pairs={{0,4},{4,0},{8,12},{12,8},{1,5},{5,1},{9,13},{13,9},{2,6},{6,2},{1... | collective-permute-start | bytes 196616 | tf_op jit(solution)/shard_map/ppermute | solution.py:297
  16.1 4.6 %collective-permute-start.3 = (f32[3,64,512]{2,1,0:T(8,128)S(1)}, f32[3,64,512]{2,1,0:T(8,128)S(1)}, u32[]{:S(2)}, u32[]{:S(2)}) collective-permute-start(f32[3,64,512]{2,1,0:T(8,128)S(1)} %get-tuple-element.82.refs_9_), channel_id=1, source_target_pairs={{0,1},{1,0},{2,3},{3,2},{4,5},{5,4},{6,7},{7,6},{8,9},{9,8},{10,11... | collective-permute-start | bytes 1179656 | tf_op jit(solution)/shard_map/ppermute | solution.py:300
  20.1 9.9 %collective-permute-start.4 = (f32[3,64,768]{2,1,0:T(8,128)S(1)}, f32[3,64,768]{2,1,0:T(8,128)S(1)}, u32[]{:S(2)}, u32[]{:S(2)}) collective-permute-start(f32[3,64,768]{2,1,0:T(8,128)S(1)} %get-tuple-element.83.refs_9_), channel_id=1, source_target_pairs={{0,1},{1,0},{2,3},{3,2},{4,5},{5,4},{6,7},{7,6},{8,9},{9,8},{10,11... | collective-permute-start | bytes 1769480 | tf_op jit(solution)/shard_map/ppermute | solution.py:300
  28.2 3.9 %collective-permute-start.5 = (f32[3,64,768]{2,1,0:T(8,128)S(1)}, f32[3,64,768]{2,1,0:T(8,128)S(1)}, u32[]{:S(2)}, u32[]{:S(2)}) collective-permute-start(f32[3,64,768]{2,1,0:T(8,128)S(1)} %get-tuple-element.94.refs_9_), channel_id=1, source_target_pairs={{0,1},{1,0},{2,3},{3,2},{4,5},{5,4},{6,7},{7,6},{8,9},{9,8},{10,11... | collective-permute-start | bytes 1769480 | tf_op jit(solution)/shard_map/ppermute | solution.py:300
  28.3 7.7 %collective-permute-start.6 = (bf16[3,64,512]{2,1,0:T(8,128)(2,1)S(1)}, bf16[3,64,512]{2,1,0:T(8,128)(2,1)S(1)}, u32[]{:S(2)}, u32[]{:S(2)}) collective-permute-start(bf16[3,64,512]{2,1,0:T(8,128)(2,1)S(1)} %get-tuple-element.97), channel_id=1, source_target_pairs={{0,2},{1,3},{2,0},{3,1},{4,6},{5,7},{6,4},{7,5},{8,10},{9,11},{10,... | collective-permute-start | bytes 589832 | tf_op jit(solution)/shard_map/ppermute | solution.py:304
  31.7 12.2 %collective-permute-start.8 = (bf16[3,64,768]{2,1,0:T(8,128)(2,1)S(1)}, bf16[3,64,768]{2,1,0:T(8,128)(2,1)S(1)}, u32[]{:S(2)}, u32[]{:S(2)}) collective-permute-start(bf16[3,64,768]{2,1,0:T(8,128)(2,1)S(1)} %get-tuple-element.108), channel_id=1, source_target_pairs={{0,2},{1,3},{2,0},{3,1},{4,6},{5,7},{6,4},{7,5},{8,10},{9,11},{10,... | collective-permute-start | bytes 884744 | tf_op jit(solution)/shard_map/ppermute | solution.py:304
  36.7 3.6 %collective-permute-start.7 = (bf16[3,64,512]{2,1,0:T(8,128)(2,1)S(1)}, bf16[3,64,512]{2,1,0:T(8,128)(2,1)S(1)}, u32[]{:S(2)}, u32[]{:S(2)}) collective-permute-start(bf16[3,64,512]{2,1,0:T(8,128)(2,1)S(1)} %activate.3.refs_1_), channel_id=1, source_target_pairs={{0,1},{1,0},{2,3},{3,2},{4,5},{5,4},{6,7},{7,6},{8,9},{9,8},{10,11... | collective-permute-start | bytes 589832 | tf_op jit(solution)/shard_map/ppermute | solution.py:300
  44.6 6.7 %collective-permute-start.9 = (bf16[3,64,768]{2,1,0:T(8,128)(2,1)S(1)}, bf16[3,64,768]{2,1,0:T(8,128)(2,1)S(1)}, u32[]{:S(2)}, u32[]{:S(2)}) collective-permute-start(bf16[3,64,768]{2,1,0:T(8,128)(2,1)S(1)} %activate.4.refs_1_), channel_id=1, source_target_pairs={{0,1},{1,0},{2,3},{3,2},{4,5},{5,4},{6,7},{7,6},{8,9},{9,8},{10,11... | collective-permute-start | bytes 884744 | tf_op jit(solution)/shard_map/ppermute | solution.py:300
  45.2 10.7 %collective-permute-start.10 = (bf16[3,64,768]{2,1,0:T(8,128)(2,1)S(1)}, bf16[3,64,768]{2,1,0:T(8,128)(2,1)S(1)}, u32[]{:S(2)}, u32[]{:S(2)}) collective-permute-start(bf16[3,64,768]{2,1,0:T(8,128)(2,1)S(1)} %get-tuple-element.117), channel_id=1, source_target_pairs={{0,2},{1,3},{2,0},{3,1},{4,6},{5,7},{6,4},{7,5},{8,10},{9,11},{10,... | collective-permute-start | bytes 884744 | tf_op jit(solution)/shard_map/ppermute | solution.py:304
  56.6 2.0 %collective-permute-start.11 = (bf16[3,64,768]{2,1,0:T(8,128)(2,1)S(1)}, bf16[3,64,768]{2,1,0:T(8,128)(2,1)S(1)}, u32[]{:S(2)}, u32[]{:S(2)}) collective-permute-start(bf16[3,64,768]{2,1,0:T(8,128)(2,1)S(1)} %activate.5.refs_1_), channel_id=1, source_target_pairs={{0,1},{1,0},{2,3},{3,2},{4,5},{5,4},{6,7},{7,6},{8,9},{9,8},{10,11... | collective-permute-start | bytes 884744 | tf_op jit(solution)/shard_map/ppermute | solution.py:300
  60.6 13.5 %collective-permute-start.12 = (bf16[2,16,1024]{2,1,0:T(8,128)(2,1)S(1)}, bf16[2,16,1024]{2,1,0:T(8,128)(2,1)S(1)}, u32[]{:S(2)}, u32[]{:S(2)}) collective-permute-start(bf16[2,16,1024]{2,1,0:T(8,128)(2,1)S(1)} %get-tuple-element.119), channel_id=1, source_target_pairs={{0,4},{4,0},{8,12},{12,8},{1,5},{5,1},{9,13},{13,9},{2,6},{6,2},{1... | collective-permute-start | bytes 196616 | tf_op jit(solution)/shard_map/ppermute | solution.py:297
  61.9 12.2 %collective-permute-start.13 = (bf16[2,16,1024]{2,1,0:T(8,128)(2,1)S(1)}, bf16[2,16,1024]{2,1,0:T(8,128)(2,1)S(1)}, u32[]{:S(2)}, u32[]{:S(2)}) collective-permute-start(bf16[2,16,1024]{2,1,0:T(8,128)(2,1)S(1)} %get-tuple-element.120), channel_id=1, source_target_pairs={{0,8},{4,12},{8,0},{12,4},{1,9},{5,13},{9,1},{13,5},{2,10},{6,14},... | collective-permute-start | bytes 196616 | tf_op jit(solution)/shard_map/ppermute | solution.py:297
  64.8 9.3 %collective-permute-start.14 = (bf16[2,16,1024]{2,1,0:T(8,128)(2,1)S(1)}, bf16[2,16,1024]{2,1,0:T(8,128)(2,1)S(1)}, u32[]{:S(2)}, u32[]{:S(2)}) collective-permute-start(bf16[2,16,1024]{2,1,0:T(8,128)(2,1)S(1)} %get-tuple-element.121), channel_id=1, source_target_pairs={{0,12},{4,8},{8,4},{12,0},{1,13},{5,9},{9,5},{13,1},{2,14},{6,10},... | collective-permute-start | bytes 196616 | tf_op jit(solution)/shard_map/ppermute | solution.py:297

commit v8 on v7

--- a/solution.py
+++ b/solution.py
@@ -15,6 +15,7 @@
 PIECES = [2, 3, 3]
 SPLIT = 4
 KEPT = ("kg", "ku", "kd")
+MASKS = ("mask_gate", "mask_up", "mask_down_t")
 F32 = jnp.float32
 BF16 = jnp.bfloat16
 
@@ -94,33 +95,22 @@
     return pl.ds(pl.multiple_of(start, BLK), size)
 
 
-def fetch(r, loads, sems):
+def fetch_kernel(r):
     copies = []
-
-    for which, first, targets in loads:
-        gate, up, down = (getattr(r, name) for name in targets)
-        size, width = down.shape
-        base = r.place[which] + first
-        for source, target in ((r.w_gate, gate), (r.w_up, up)):
-            for row in range(0, width, width // SPLIT):
-                rows = slice(row, row + width // SPLIT)
-                copies.append((source.at[rows, span(base, size)], target.at[rows, :]))
-        for row in range(0, size, BLK):
-            copies.append((r.w_down.at[span(base + row, BLK), :], down.at[row : row + BLK, :]))
-    copies = [pltpu.make_async_copy(a, b, sems.at[k]) for k, (a, b) in enumerate(copies)]
-    for copy in copies:
+    for source, target in ((r.w_gate, r.kg), (r.w_up, r.ku), (r.w_down, r.kd)):
+        height = source.shape[0] // SPLIT
+        for k in range(SPLIT):
+            rows = slice(k * height, (k + 1) * height)
+            copies.append((source.at[rows, :], target.at[rows, :]))
+    for k in MASKS:
+        copies.append((getattr(r, "hbm_" + k), getattr(r, k)))
+    copies = [pltpu.make_async_copy(a, b, r.sems.at[k]) for k, (a, b) in enumerate(copies)]
+    for copy in copies[-len(MASKS) :] + copies[: -len(MASKS)]:
         copy.start()
-    return copies
-
-
-def count_copies(sizes):
-    return sum(2 * SPLIT + size // BLK for size in sizes)
-
-
-def fetch_kernel(loads, r):
-    copies = fetch(r, loads, r.sems)
+    for copy in copies[-len(MASKS) :]:
+        copy.wait()
     spread(r)
-    for copy in copies:
+    for copy in copies[: -len(MASKS)]:
         copy.wait()
 
 
@@ -132,7 +122,7 @@
 
 
 def assemble_kernel(r):
-    blocks = [ref for name, ref in vars(r).items() if name.startswith("block")]
+    blocks = [ref for name, ref in sorted(vars(r).items()) if name.startswith("block")]
     tok = jnp.concatenate([block[0] for block in blocks], axis=0)
     cot = jnp.concatenate([block[1] for block in blocks], axis=0)
     r.cot[...] = cot
@@ -153,8 +143,7 @@
     return sum(value[b * rows : (b + 1) * rows, :] * m for b, m in enumerate(masks))
 
 
-def partial_kernel(which, start, tile, loads, r):
-    copies = fetch(r, loads, r.sems) if loads else []
+def partial_kernel(which, start, tile, r):
     pairs, _, size = r.tok_d.shape
     for first in range(0, r.send.shape[2], tile):
         at = span(r.place[which] + start + first, tile)
@@ -165,9 +154,9 @@
             bands = range(p * size // BLK, (p + 1) * size // BLK)
             for k, (left, right, mask, dims) in enumerate(
                 (
-                    (r.tok_d[p], r.kg[part, local], r.mg, (1, 0)),
-                    (r.tok_d[p], r.ku[part, local], r.mu, (1, 0)),
-                    (r.cot_d[p], r.kd[local, part], r.mdt, (1, 1)),
+                    (r.tok_d[p], r.kg[part, at], r.mg, (1, 0)),
+                    (r.tok_d[p], r.ku[part, at], r.mu, (1, 0)),
+                    (r.cot_d[p], r.kd[at, part], r.mdt, (1, 1)),
                 )
             ):
                 totals[k] += masked_sum(left, right, [mask[b, :, at] for b in bands], dims)
@@ -176,8 +165,6 @@
                 value = value + r.received[k, :, local]
                 r.own[k, :, local] = value
             r.send[k, :, local] = value.astype(r.send.dtype)
-    for copy in copies:
-        copy.wait()
 
 
 def act_kernel(r):
@@ -193,7 +180,7 @@
     r.act[2] = (back * silu).astype(BF16)
 
 
-def add_rows(r, i, block, local):
+def add_rows(r, i, block, at):
     width, tile = r.acc.shape[2], r.act_d.shape[3]
     size = min(DEPTH, width)
     for f in range(0, width, size):
@@ -202,10 +189,10 @@
         def masks(mask):
             return [mask[block + b][:, part] for b in range(tile // BLK)]
 
-        r.acc[0, :, part] += masked_sum(r.act_d[i, 0], r.kd[local, part], masks(r.md))
+        r.acc[0, :, part] += masked_sum(r.act_d[i, 0], r.kd[at, part], masks(r.md))
         r.acc[1, :, part] += masked_sum(
-            r.act_d[i, 1], r.kg[part, local], masks(r.mgt), (1, 1)
-        ) + masked_sum(r.act_d[i, 2], r.ku[part, local], masks(r.mut), (1, 1))
+            r.act_d[i, 1], r.kg[part, at], masks(r.mgt), (1, 1)
+        ) + masked_sum(r.act_d[i, 2], r.ku[part, at], masks(r.mut), (1, 1))
 
 
 class Outbox:
@@ -228,41 +215,41 @@
                 copy.wait()
 
 
-def back_kernel(which, start, do_rows, do_grads, r):
-    _, rows, size = r.act.shape
+def back_kernel(items, do_rows, do_grads, r):
     tile = r.act_d.shape[3]
-    base = r.place[which] + start
-    at = span(base, size)
+    spots = tile // BLK
     r.act_d[...] = jnp.zeros_like(r.act_d)
-    groups = 0
     if do_rows:
         r.acc[...] = r.sums[...] if hasattr(r, "sums") else jnp.zeros_like(r.acc)
     if do_grads:
         groups, height, _ = r.tok_t.shape
         by_cols, by_rows = Outbox(r.col_slots, r.col_sems), Outbox(r.row_slots, r.row_sems)
-    tiles = [slice(i * tile, (i + 1) * tile) for i in range(size // tile)]
-    block = lax.div(base, BLK)
-    spots = tile // BLK
-    for i, local in enumerate(tiles):
-        for k in range(3 if do_rows else 1):
-            diagonal(r.act_d.at[i, k], r.act[k, :, local])
-    for i in range(max(groups, len(tiles)) if do_grads else 0):
-        if i < groups:
-            band = slice(i * height, (i + 1) * height)
-            for out, k, mask in ((r.gg, 1, r.mg), (r.gu, 2, r.mu)):
-                right = r.masked_act.at[k - 1]
-                for j in range(height // BLK):
-                    keep = mask[i * (height // BLK) + j, :, at].astype(BF16)
-                    right[j * rows : (j + 1) * rows, :] = r.act[k] * keep
-                by_cols.put(dot(r.tok_t[i], right[...]), out.at[band, at])
-        if i < len(tiles):
-            for b in range(spots):
-                keep = r.md[block + i * spots + b].astype(BF16)
-                r.masked_cot[b * rows : (b + 1) * rows, :] = r.cot[...] * keep
-            value = dot(r.act_d[i, 0].T, r.masked_cot[...])
-            by_rows.put(value, r.gd.at[span(base + i * tile, tile), :])
-    for i, local in enumerate(tiles if do_rows else []):
-        add_rows(r, i, block + i * spots, local)
+    for act, which, start in items:
+        act = getattr(r, act)
+        _, rows, size = act.shape
+        base = r.place[which] + start
+        at, block = span(base, size), lax.div(base, BLK)
+        tiles = [slice(i * tile, (i + 1) * tile) for i in range(size // tile)]
+        for i, local in enumerate(tiles):
+            for k in range(3 if do_rows else 1):
+                diagonal(r.act_d.at[i, k], act[k, :, local])
+        for i in range(max(groups, len(tiles)) if do_grads else 0):
+            if i < groups:
+                band = slice(i * height, (i + 1) * height)
+                for out, k, mask in ((r.gg, 1, r.mg), (r.gu, 2, r.mu)):
+                    right = r.masked_act.at[k - 1]
+                    for j in range(height // BLK):
+                        keep = mask[i * (height // BLK) + j, :, at].astype(BF16)
+                        right[j * rows : (j + 1) * rows, :] = act[k] * keep
+                    by_cols.put(dot(r.tok_t[i], right[...]), out.at[band, at])
+            if i < len(tiles):
+                for b in range(spots):
+                    keep = r.md[block + i * spots + b].astype(BF16)
+                    r.masked_cot[b * rows : (b + 1) * rows, :] = r.cot[...] * keep
+                value = dot(r.act_d[i, 0].T, r.masked_cot[...])
+                by_rows.put(value, r.gd.at[span(base + i * tile, tile), :])
+        for i in range(len(tiles) if do_rows else 0):
+            add_rows(r, i, block + i * spots, span(base + i * tile, tile))
     if do_rows:
         if hasattr(r, "new_sums"):
             r.new_sums[...] = r.acc[...]
@@ -315,9 +302,6 @@
     weights = {"w_gate": (w_gate, ANY), "w_up": (w_up, ANY), "w_down": (w_down, ANY)}
     weights = {k: (hbm(w), spec) for k, (w, spec) in weights.items()}
 
-    def kept_shapes(p):
-        return [shape(width, split[p]), shape(width, split[p]), shape(split[p], width)]
-
     block = jnp.stack([tokens, grad_out])
     if direct:
         blocks = [block] + [trade(block, s) for s in range(1, n_grid)]
@@ -326,39 +310,23 @@
 
     across_shape = shape(width // BLK, 1, units, kind=F32)
     along_shape = shape(units // BLK, 1, width, kind=F32)
-    masks = {"mask_gate": mask_gate, "mask_up": mask_up, "mask_down_t": mask_down.T}
-    kept = {}
-
-    def loading(pieces):
-        loads, outs = [], {}
-        for which, p in pieces:
-            names = [f"{k}_{which}_{p}" for k in KEPT]
-            loads.append((which, starts[p], names))
-            outs.update({k: pinned(s) for k, s in zip(names, kept_shapes(p))})
-        count = count_copies([split[p] for _, p in pieces])
-        return loads, outs, {"sems": pltpu.SemaphoreType.DMA((count,))} if pieces else {}
-
-    def keep(got, pieces):
-        for which, p in pieces:
-            kept[which, p] = {k: got[f"{k}_{which}_{p}"] for k in KEPT}
-
-    first = [(1, p) for p in range(min(n, 2))]
-    loads, outs, scratch = loading(first)
-    got = call(
-        functools.partial(fetch_kernel, loads),
+    masks = dict(zip(MASKS, (mask_gate, mask_up, mask_down.T)))
+    values = call(
+        fetch_kernel,
         "fetch",
         place,
-        {**weights, **{k: (hbm(m), whole(m)) for k, m in masks.items()}},
+        {**weights, **{"hbm_" + k: (hbm(m), ANY) for k, m in masks.items()}},
         {
             **{k: pinned(across_shape) for k in ("mg", "mu", "mdt")},
             **{k: pinned(along_shape) for k in ("mgt", "mut", "md")},
-            **outs,
+            **{k: pinned(shape(*w.shape)) for k, w in zip(KEPT, (w_gate, w_up, w_down))},
         },
-        scratch=scratch,
+        scratch={
+            **{k: pltpu.VMEM(m.shape, m.dtype) for k, m in masks.items()},
+            "sems": pltpu.SemaphoreType.DMA((3 * SPLIT + len(masks),)),
+        },
         vmem=grant(4),
     )
-    values = {k: got[k] for k in ("mg", "mu", "mdt", "mgt", "mut", "md")}
-    keep(got, first)
 
     pair = min(DEPTH, width) // BLK
     pair_shape = shape(width // (pair * BLK), pair * rows, pair * BLK)
@@ -368,7 +336,7 @@
         place,
         {
             "after": (values["mg"], ANY),
-            **{f"block{k}": (b, whole(b)) for k, b in enumerate(blocks)},
+            **{f"block{k}": (b, whole(b)) for k, b in reversed(list(enumerate(blocks)))},
         },
         {
             "cot": pinned(shape(rows, width)),
@@ -382,28 +350,17 @@
     def held(*names):
         return {k: pinned(values[k]) for k in names}
 
-    def partials(which, p, pieces, after=None, received=None):
+    def partials(which, p, after=None, received=None):
         trio = (3, rows, split[p])
-        ins = held("tok_d", "cot_d", "mg", "mu", "mdt")
-        ins.update({k: pinned(v) for k, v in kept[which, p].items()})
+        ins = held("tok_d", "cot_d", "mg", "mu", "mdt", *KEPT)
         outs = {"send": pinned(shape(*trio, kind=F32))}
         if after is not None:
             ins["after"] = (after, ANY)
         if received is not None:
             ins["received"] = pinned(received)
             outs = {"own": pinned(shape(*trio, kind=F32)), "send": pinned(shape(*trio))}
-        loads, fetched, scratch = loading(pieces)
-        got = call(
-            functools.partial(partial_kernel, which, starts[p], tile, loads),
-            "partials",
-            place,
-            {**ins, **(weights if loads else {})},
-            {**outs, **fetched},
-            scratch=scratch,
-            vmem=grant(2),
-        )
-        keep(got, pieces)
-        return got
+        kernel = functools.partial(partial_kernel, which, starts[p], tile)
+        return call(kernel, "partials", place, ins, outs, vmem=grant(2))
 
     def activate(own, others, after):
         ins = {"own": pinned(own), "after": (after, ANY)}
@@ -411,14 +368,15 @@
         outs = {"act": pinned(shape(*own.shape))}
         return call(act_kernel, "activate", place, ins, outs, vmem=grant(2))["act"]
 
-    def back(which, p, act, do_rows, do_grads, state, last=False):
-        ins = {"act": pinned(act), **held("md")}
+    def back(pieces, do_rows, do_grads, state, last=False):
+        items = [(f"act{k}", which, starts[p]) for k, (which, p, _) in enumerate(pieces)]
+        ins = {f"act{k}": pinned(act) for k, (_, _, act) in enumerate(pieces)}
+        ins.update(held("md"))
         outs, aliases = {}, {}
-        spots, size = tile // BLK, split[p]
+        spots, size = tile // BLK, split[pieces[0][1]]
         scratch = {"act_d": pltpu.VMEM((size // tile, 3, spots * rows, tile), BF16)}
         if do_rows:
-            ins.update({k: pinned(v) for k, v in kept[which, p].items()})
-            ins.update(held("mgt", "mut"))
+            ins.update(held("mgt", "mut", *KEPT))
             scratch["acc"] = pltpu.VMEM((2, rows, width), F32)
             if "sums" in state:
                 ins["sums"] = pinned(state["sums"])
@@ -447,7 +405,7 @@
             if "rows0" in state:
                 ins["after"] = (state["rows0"], ANY)
         got = call(
-            functools.partial(back_kernel, which, starts[p], do_rows, do_grads),
+            functools.partial(back_kernel, items, do_rows, do_grads),
             "_".join(["back"] + ["rows"] * do_rows + ["grads"] * do_grads),
             place,
             ins,
@@ -461,11 +419,10 @@
     sent, sums, theirs, after = [], [], [], None
     for p in range(n + 1):
         if p < n:
-            after = partials(1, p, [(0, p)], after)["send"]
+            after = partials(1, p, after)["send"]
             sent.append(swap(after))
         if p > 0:
-            ahead = [(1, p + 1)] if p + 1 < n else []
-            got = partials(0, p - 1, ahead, after, sent[p - 1])
+            got = partials(0, p - 1, after, sent[p - 1])
             after = got["own"]
             sums.append(after)
             theirs.append(across(got["send"]))
@@ -475,11 +432,10 @@
         last = p == n - 1
         act = activate(sums[p], theirs[p], state.get("sums", after))
         act_other = swap(act)
-        state = back(0, p, act, True, not last, state)
-        state = back(1, p, act_other, True, not last, state, last)
+        state = back([(0, p, act)], True, not last, state)
+        state = back([(1, p, act_other)], True, not last, state, last)
         if last:
-            state = back(0, p, act, False, True, state)
-            state = back(1, p, act_other, False, True, state)
+            state = back([(0, p, act), (1, p, act_other)], False, True, state)
 
     if direct:
         both = state["rows0"].astype(F32)

time: 75.1 us -> 68.8 us (0.916)
  Pallas kernels: 54.7 us -> 48.6 us
    pallas_call x19 -> x18, Pallas kernels: 54.7 us -> 48.6 us  [call(): pl.pallas_call(body, out_shape=[shape for shape, _ in outs.values()], gri...]
where the time goes in v8:
time: 68.8 us; the launch traced here: 68.6 us
  Pallas kernels  48.6 us (71%)
  starting transfers between devices  15.4 us (22%)
  waiting for transfers between devices  2.24 us (3%)
  other arithmetic  0.9 us (1%)
  between operations  0.88 us (1%)
    pallas_call x18, Pallas kernels, call(): pl.pallas_call(body, out_shape=[shape for shape, _ in outs.values()], gri...  48.6 us
    ppermute x6, starting transfers between devices, trade(): return lax.ppermute(array, 'grid', [(i, i ^ s) for i in range(n_grid)])  10.1 us
    ppermute x3, starting transfers between devices, across(): lax.ppermute(array, 'dp', [(i, (i // 2 + s) % pairs * 2 + i % 2) for i in...  3.85 us
    ppermute x3, waiting for transfers between devices, across(): lax.ppermute(array, 'dp', [(i, (i // 2 + s) % pairs * 2 + i % 2) for i in...  2.21 us
    ppermute x6, starting transfers between devices, swap(): return lax.ppermute(array, 'dp', [(i, i ^ 1) for i in range(n_dp)])  1.41 us
  transfers between devices with their start and end apart: 15, of which 1 were waited for; matrix products, arithmetic and copies ran while one was open for 0% of the time, Pallas kernels for 63%

profile of v8, /device:TPU:0, one launch (start us, length us, event | category | flops | bytes accessed | tf_op | source)
XLA Modules:
  0.0 68.6 jit_solution(18424339310532146363)
XLA Ops:
  0.6 0.8 %pad_maximum_fusion.refs_5_ = bf16[2,16,1024]{2,1,0:T(8,128)(2,1)S(1)} fusion(bf16[1,16,1024]{2,1,0:T(8,128)(2,1)} %bitcast.9, bf16[1,16,1024]{2,1,0:T(8,128)(2,1)} %bitcast.10), kind=kLoop, calls=%fused_computation.1 | loop fusion | flops 32768 | bytes 131072 | tf_op jit(solution)/shard_map/stack | solution.py:305
  1.4 3.1 %collective-permute-start.2 = (bf16[2,16,1024]{2,1,0:T(8,128)(2,1)S(1)}, bf16[2,16,1024]{2,1,0:T(8,128)(2,1)S(1)}, u32[]{:S(2)}, u32[]{:S(2)}) collective-permute-start(bf16[2,16,1024]{2,1,0:T(8,128)(2,1)S(1)} %pad_maximum_fusion.refs_5_), channel_id=1, source_target_pairs={{0,4},{4,0},{8,12},{12,8},{1,5},{5,1},{9,13},{13,9},{2,6},{6,2},{1... | collective-permute-start | bytes 196616 | tf_op jit(solution)/shard_map/ppermute | solution.py:284
  4.5 2.6 %collective-permute-start.1 = (bf16[2,16,1024]{2,1,0:T(8,128)(2,1)S(1)}, bf16[2,16,1024]{2,1,0:T(8,128)(2,1)S(1)}, u32[]{:S(2)}, u32[]{:S(2)}) collective-permute-start(bf16[2,16,1024]{2,1,0:T(8,128)(2,1)S(1)} %pad_maximum_fusion.refs_5_), channel_id=1, source_target_pairs={{0,8},{4,12},{8,0},{12,4},{1,9},{5,13},{9,1},{13,5},{2,10},{6,14},... | collective-permute-start | bytes 196616 | tf_op jit(solution)/shard_map/ppermute | solution.py:284
  7.1 0.0 collective-permute-start
  7.1 0.1 pad_add_fusion.refs_0_
  7.2 8.9 %fetch.1 = (f32[8,1,4096]{2,1,0:T(1,128)S(1)}, f32[8,1,4096]{2,1,0:T(1,128)S(1)}, f32[8,1,4096]{2,1,0:T(1,128)S(1)}, f32[32,1,1024]{2,1,0:T(1,128)S(1)}, f32[32,...) custom-call(s32[2]{0:T(128)S(1)} %pad_add_fusion.refs_0_, ...), custom_call_target="tpu_custom_call" | custom-call | flops 1 | bytes 1 | tf_op jit(solution)/shard_map/fetch/pallas_call | solution.py:44
  16.1 0.0 collective-permute-done.2.refs_4_
  16.1 0.0 collective-permute-done.1.refs_3_
  16.1 0.0 collective-permute-done.refs_2_
  16.1 0.7 %assemble.1 = (bf16[64,1024]{1,0:T(8,128)(2,1)S(1)}, bf16[4,128,256]{2,1,0:T(8,128)(2,1)S(1)}, bf16[4,128,256]{2,1,0:T(8,128)(2,1)S(1)}, bf16[4,256,128]{2,1,0:T(8,128)(2,1)S(1)}) custom-call(s32[2]{0:T(128)S(1)} %pad_add_fusion.refs_0_, f32[8,1,4096]{2,1,0:T(1,128)S(1)} %get-tuple-element.47.refs_1_.refs_3_.refs_10_.refs_11_.refs_6_, ...), custom_call_target="tpu_custom_call" | custom-call | flops 1 | bytes 1 | tf_op jit(solution)/shard_map/assemble/pallas_call | solution.py:44
  16.9 1.3 %partials.6.refs_9_ = f32[3,64,512]{2,1,0:T(8,128)S(1)} custom-call(s32[2]{0:T(128)S(1)} %pad_add_fusion.refs_0_, bf16[4,128,256]{2,1,0:T(8,128)(2,1)S(1)} %get-tuple-element.48.refs_1_, bf16[4,128,256]{2,1,0:T(8,128)(2,1)S(1)} %get-tuple-element.49.refs_2_, f32[8,1,4096]{2,1,0:T(1,128)S(1)} %get-tuple-element.47.refs_1_.refs_3_.refs_10_.refs_11_.refs_6_, ...), custom_call_target="tpu_custom_call" | custom-call | flops 1 | bytes 1 | tf_op jit(solution)/shard_map/partials/pallas_call | solution.py:44
  18.2 0.1 collective-permute-start.3
  18.3 1.7 %partials.7.refs_9_ = f32[3,64,768]{2,1,0:T(8,128)S(1)} custom-call(s32[2]{0:T(128)S(1)} %pad_add_fusion.refs_0_, bf16[4,128,256]{2,1,0:T(8,128)(2,1)S(1)} %get-tuple-element.48.refs_1_, bf16[4,128,256]{2,1,0:T(8,128)(2,1)S(1)} %get-tuple-element.49.refs_2_, f32[8,1,4096]{2,1,0:T(1,128)S(1)} %get-tuple-element.47.refs_1_.refs_3_.refs_10_.refs_11_.refs_6_, ...), custom_call_target="tpu_custom_call" | custom-call | flops 1 | bytes 1 | tf_op jit(solution)/shard_map/partials/pallas_call | solution.py:44
  19.9 0.6 collective-permute-start.4
  20.5 0.0 collective-permute-done.3.refs_10_
  20.5 1.3 %partials.8 = (f32[3,64,512]{2,1,0:T(8,128)S(1)}, bf16[3,64,512]{2,1,0:T(8,128)(2,1)S(1)}) custom-call(s32[2]{0:T(128)S(1)} %pad_add_fusion.refs_0_, bf16[4,128,256]{2,1,0:T(8,128)(2,1)S(1)} %get-tuple-element.48.refs_1_, bf16[4,128,256]{2,1,0:T(8,128)(2,1)S(1)} %get-tuple-element.49.refs_2_, ...), custom_call_target="tpu_custom_call" | custom-call | flops 1 | bytes 1 | tf_op jit(solution)/shard_map/partials/pallas_call | solution.py:44
  21.8 1.7 %partials.9.refs_9_ = f32[3,64,768]{2,1,0:T(8,128)S(1)} custom-call(s32[2]{0:T(128)S(1)} %pad_add_fusion.refs_0_, bf16[4,128,256]{2,1,0:T(8,128)(2,1)S(1)} %get-tuple-element.48.refs_1_, bf16[4,128,256]{2,1,0:T(8,128)(2,1)S(1)} %get-tuple-element.49.refs_2_, f32[8,1,4096]{2,1,0:T(1,128)S(1)} %get-tuple-element.47.refs_1_.refs_3_.refs_10_.refs_11_.refs_6_, ...), custom_call_target="tpu_custom_call" | custom-call | flops 1 | bytes 1 | tf_op jit(solution)/shard_map/partials/pallas_call | solution.py:44
  23.5 0.1 collective-permute-start.5
  23.6 1.8 %collective-permute-start.6 = (bf16[3,64,512]{2,1,0:T(8,128)(2,1)S(1)}, bf16[3,64,512]{2,1,0:T(8,128)(2,1)S(1)}, u32[]{:S(2)}, u32[]{:S(2)}) collective-permute-start(bf16[3,64,512]{2,1,0:T(8,128)(2,1)S(1)} %get-tuple-element.58), channel_id=1, source_target_pairs={{0,2},{1,3},{2,0},{3,1},{4,6},{5,7},{6,4},{7,5},{8,10},{9,11},{10,... | collective-permute-start | bytes 589832 | tf_op jit(solution)/shard_map/ppermute | solution.py:291
  25.4 0.0 collective-permute-done.4.refs_10_
  25.4 1.7 %partials.10 = (f32[3,64,768]{2,1,0:T(8,128)S(1)}, bf16[3,64,768]{2,1,0:T(8,128)(2,1)S(1)}) custom-call(s32[2]{0:T(128)S(1)} %pad_add_fusion.refs_0_, bf16[4,128,256]{2,1,0:T(8,128)(2,1)S(1)} %get-tuple-element.48.refs_1_, bf16[4,128,256]{2,1,0:T(8,128)(2,1)S(1)} %get-tuple-element.49.refs_2_, ...), custom_call_target="tpu_custom_call" | custom-call | flops 1 | bytes 1 | tf_op jit(solution)/shard_map/partials/pallas_call | solution.py:44
  27.1 0.4 collective-permute-start.8
  27.4 0.0 collective-permute-done.5.refs_10_
  27.4 1.7 %partials.11 = (f32[3,64,768]{2,1,0:T(8,128)S(1)}, bf16[3,64,768]{2,1,0:T(8,128)(2,1)S(1)}) custom-call(s32[2]{0:T(128)S(1)} %pad_add_fusion.refs_0_, bf16[4,128,256]{2,1,0:T(8,128)(2,1)S(1)} %get-tuple-element.48.refs_1_, bf16[4,128,256]{2,1,0:T(8,128)(2,1)S(1)} %get-tuple-element.49.refs_2_, ...), custom_call_target="tpu_custom_call" | custom-call | flops 1 | bytes 1 | tf_op jit(solution)/shard_map/partials/pallas_call | solution.py:44
  29.1 2.2 %collective-permute-done.6.refs_3_ = bf16[3,64,512]{2,1,0:T(8,128)(2,1)S(1)} collective-permute-done((bf16[3,64,512]{2,1,0:T(8,128)(2,1)S(1)}, bf16[3,64,512]{2,1,0:T(8,128)(2,1)S(1)}, u32[]{:S(2)}, u32[]{:S(2)}) %collective-permute-start.6) | collective-permute-done | bytes 196640 | tf_op jit(solution)/shard_map/ppermute | solution.py:291
  31.3 0.6 activate.3.refs_1_
  32.0 0.1 collective-permute-start.7
  32.1 3.5 %back_rows_grads.4 = (f32[2,64,1024]{2,1,0:T(8,128)S(1)}, f32[1024,4096]{1,0:T(8,128)}, f32[1024,4096]{1,0:T(8,128)}, f32[4096,1024]{1,0:T(8,128)}) custom-call(s32[2]{0:T(128)S(1)} %pad_add_fusion.refs_0_, bf16[3,64,512]{2,1,0:T(8,128)(2,1)S(1)} %activate.3.refs_1_, f32[32,1,1024]{2,1,0:T(1,128)S(1)} %get-tuple-element.59.refs_2_.refs_3_, ...), custom_call_target="tpu_custom_call" | custom-call | flops 1 | bytes 1 | tf_op jit(solution)/shard_map/back_rows_grads/pallas_call | solution.py:44
  35.6 0.0 collective-permute-done.7.refs_1_
  35.6 3.5 %back_rows_grads.5 = (f32[2,64,1024]{2,1,0:T(8,128)S(1)}, f32[1024,4096]{1,0:T(8,128)}, f32[1024,4096]{1,0:T(8,128)}, f32[4096,1024]{1,0:T(8,128)}) custom-call(s32[2]{0:T(128)S(1)} %pad_add_fusion.refs_0_, bf16[3,64,512]{2,1,0:T(8,128)(2,1)S(1)} %collective-permute-done.7.refs_1_, ...), custom_call_target="tpu_custom_call", output_to_operand_aliasing={{1}: (13, {}), {2}: (14, {}), {3}: (15, {})} | custom-call | flops 1 | bytes 1 | tf_op jit(solution)/shard_map/back_rows_grads/pallas_call | solution.py:44
  39.2 0.0 collective-permute-done.8.refs_3_
  39.2 0.7 %activate.4.refs_1_ = bf16[3,64,768]{2,1,0:T(8,128)(2,1)S(1)} custom-call(s32[2]{0:T(128)S(1)} %pad_add_fusion.refs_0_, f32[3,64,768]{2,1,0:T(8,128)S(1)} %get-tuple-element.56.refs_9_.refs_1_, f32[2,64,1024]{2,1,0:T(8,128)S(1)} %get-tuple-element.68.refs_2_.refs_8_, bf16[3,64,768]{2,1,0:T(8,128)(2,1)S(1)} %collective-permute-done.8.refs_3_), custom_call_target="tpu_custom_call" | custom-call | flops 1 | bytes 1 | tf_op jit(solution)/shard_map/activate/pallas_call | solution.py:44
  39.9 0.6 collective-permute-start.9
  40.4 1.7 %collective-permute-start.10 = (bf16[3,64,768]{2,1,0:T(8,128)(2,1)S(1)}, bf16[3,64,768]{2,1,0:T(8,128)(2,1)S(1)}, u32[]{:S(2)}, u32[]{:S(2)}) collective-permute-start(bf16[3,64,768]{2,1,0:T(8,128)(2,1)S(1)} %get-tuple-element.78), channel_id=1, source_target_pairs={{0,2},{1,3},{2,0},{3,1},{4,6},{5,7},{6,4},{7,5},{8,10},{9,11},{10,... | collective-permute-start | bytes 884744 | tf_op jit(solution)/shard_map/ppermute | solution.py:291
  42.1 4.5 %back_rows_grads.6 = (f32[2,64,1024]{2,1,0:T(8,128)S(1)}, f32[1024,4096]{1,0:T(8,128)}, f32[1024,4096]{1,0:T(8,128)}, f32[4096,1024]{1,0:T(8,128)}) custom-call(s32[2]{0:T(128)S(1)} %pad_add_fusion.refs_0_, bf16[3,64,768]{2,1,0:T(8,128)(2,1)S(1)} %activate.4.refs_1_, ...), custom_call_target="tpu_custom_call", output_to_operand_aliasing={{1}: (13, {}), {2}: (14, {}), {3}: (15, {})} | custom-call | flops 1 | bytes 1 | tf_op jit(solution)/shard_map/back_rows_grads/pallas_call | solution.py:44
  46.7 0.0 collective-permute-done.9.refs_1_
  46.7 4.5 %back_rows_grads.7 = (f32[2,64,1024]{2,1,0:T(8,128)S(1)}, f32[1024,4096]{1,0:T(8,128)}, f32[1024,4096]{1,0:T(8,128)}, f32[4096,1024]{1,0:T(8,128)}) custom-call(s32[2]{0:T(128)S(1)} %pad_add_fusion.refs_0_, bf16[3,64,768]{2,1,0:T(8,128)(2,1)S(1)} %collective-permute-done.9.refs_1_, ...), custom_call_target="tpu_custom_call", output_to_operand_aliasing={{1}: (13, {}), {2}: (14, {}), {3}: (15, {})} | custom-call | flops 1 | bytes 1 | tf_op jit(solution)/shard_map/back_rows_grads/pallas_call | solution.py:44
  51.2 0.0 collective-permute-done.10.refs_3_
  51.2 0.7 %activate.5.refs_1_ = bf16[3,64,768]{2,1,0:T(8,128)(2,1)S(1)} custom-call(s32[2]{0:T(128)S(1)} %pad_add_fusion.refs_0_, f32[3,64,768]{2,1,0:T(8,128)S(1)} %get-tuple-element.57.refs_2_.refs_1_, f32[2,64,1024]{2,1,0:T(8,128)S(1)} %get-tuple-element.77.refs_2_.refs_8_, bf16[3,64,768]{2,1,0:T(8,128)(2,1)S(1)} %collective-permute-done.10.refs_3_), custom_call_target="tpu_custom_call" | custom-call | flops 1 | bytes 1 | tf_op jit(solution)/shard_map/activate/pallas_call | solution.py:44
  51.9 0.1 collective-permute-start.11
  52.0 2.0 %back_rows.2.refs_8_ = f32[2,64,1024]{2,1,0:T(8,128)S(1)} custom-call(s32[2]{0:T(128)S(1)} %pad_add_fusion.refs_0_, bf16[3,64,768]{2,1,0:T(8,128)(2,1)S(1)} %activate.5.refs_1_, f32[32,1,1024]{2,1,0:T(1,128)S(1)} %get-tuple-element.59.refs_2_.refs_3_, f32[32,1,1024]{2,1,0:T(1,128)S(1)} %get-tuple-element.60.refs_3_, ...), custom_call_target="tpu_custom_call" | custom-call | flops 1 | bytes 1 | tf_op jit(solution)/shard_map/back_rows/pallas_call | solution.py:44
  54.0 0.0 collective-permute-done.11.refs_1_.refs_2_
  54.0 2.0 %back_rows.3 = (bf16[2,16,1024]{2,1,0:T(8,128)(2,1)S(1)}, bf16[2,16,1024]{2,1,0:T(8,128)(2,1)S(1)}, bf16[2,16,1024]{2,1,0:T(8,128)(2,1)S(1)}, bf16[2,16,1024]{2,1,0:T(8,128)(2,1)S(1)}) custom-call(s32[2]{0:T(128)S(1)} %pad_add_fusion.refs_0_, bf16[3,64,768]{2,1,0:T(8,128)(2,1)S(1)} %collective-permute-done.11.refs_1_.refs_2_, ...), custom_call_target="tpu_custom_call" | custom-call | flops 1 | bytes 1 | tf_op jit(solution)/shard_map/back_rows/pallas_call | solution.py:44
  56.1 0.8 %collective-permute-start.12 = (bf16[2,16,1024]{2,1,0:T(8,128)(2,1)S(1)}, bf16[2,16,1024]{2,1,0:T(8,128)(2,1)S(1)}, u32[]{:S(2)}, u32[]{:S(2)}) collective-permute-start(bf16[2,16,1024]{2,1,0:T(8,128)(2,1)S(1)} %get-tuple-element.80), channel_id=1, source_target_pairs={{0,4},{4,0},{8,12},{12,8},{1,5},{5,1},{9,13},{13,9},{2,6},{6,2},{1... | collective-permute-start | bytes 196616 | tf_op jit(solution)/shard_map/ppermute | solution.py:284
  56.8 3.5 %collective-permute-start.13 = (bf16[2,16,1024]{2,1,0:T(8,128)(2,1)S(1)}, bf16[2,16,1024]{2,1,0:T(8,128)(2,1)S(1)}, u32[]{:S(2)}, u32[]{:S(2)}) collective-permute-start(bf16[2,16,1024]{2,1,0:T(8,128)(2,1)S(1)} %get-tuple-element.81), channel_id=1, source_target_pairs={{0,8},{4,12},{8,0},{12,4},{1,9},{5,13},{9,1},{13,5},{2,10},{6,14},... | collective-permute-start | bytes 196616 | tf_op jit(solution)/shard_map/ppermute | solution.py:284
  60.3 0.2 collective-permute-start.14
  60.5 7.4 %back_grads.1 = (f32[1024,4096]{1,0:T(8,128)}, f32[1024,4096]{1,0:T(8,128)}, f32[4096,1024]{1,0:T(8,128)}) custom-call(s32[2]{0:T(128)S(1)} %pad_add_fusion.refs_0_, bf16[3,64,768]{2,1,0:T(8,128)(2,1)S(1)} %activate.5.refs_1_, ...), custom_call_target="tpu_custom_call", output_to_operand_aliasing={{0}: (8, {}), {1}: (9, {}), {2}: (10, {})} | custom-call | flops 1 | bytes 1 | tf_op jit(solution)/shard_map/back_grads/pallas_call | solution.py:44
  67.9 0.0 collective-permute-done.12
  67.9 0.0 collective-permute-done.13
  67.9 0.0 collective-permute-done.14
  68.0 0.6 slice_bitcast_fusion
  (1 shorter events, 0.0 us)
Async XLA Ops:
  1.4 14.7 %collective-permute-start.2 = (bf16[2,16,1024]{2,1,0:T(8,128)(2,1)S(1)}, bf16[2,16,1024]{2,1,0:T(8,128)(2,1)S(1)}, u32[]{:S(2)}, u32[]{:S(2)}) collective-permute-start(bf16[2,16,1024]{2,1,0:T(8,128)(2,1)S(1)} %pad_maximum_fusion.refs_5_), channel_id=1, source_target_pairs={{0,4},{4,0},{8,12},{12,8},{1,5},{5,1},{9,13},{13,9},{2,6},{6,2},{1... | collective-permute-start | bytes 196616 | tf_op jit(solution)/shard_map/ppermute | solution.py:284
  4.5 11.6 %collective-permute-start.1 = (bf16[2,16,1024]{2,1,0:T(8,128)(2,1)S(1)}, bf16[2,16,1024]{2,1,0:T(8,128)(2,1)S(1)}, u32[]{:S(2)}, u32[]{:S(2)}) collective-permute-start(bf16[2,16,1024]{2,1,0:T(8,128)(2,1)S(1)} %pad_maximum_fusion.refs_5_), channel_id=1, source_target_pairs={{0,8},{4,12},{8,0},{12,4},{1,9},{5,13},{9,1},{13,5},{2,10},{6,14},... | collective-permute-start | bytes 196616 | tf_op jit(solution)/shard_map/ppermute | solution.py:284
  7.1 9.1 %collective-permute-start = (bf16[2,16,1024]{2,1,0:T(8,128)(2,1)S(1)}, bf16[2,16,1024]{2,1,0:T(8,128)(2,1)S(1)}, u32[]{:S(2)}, u32[]{:S(2)}) collective-permute-start(bf16[2,16,1024]{2,1,0:T(8,128)(2,1)S(1)} %pad_maximum_fusion.refs_5_), channel_id=1, source_target_pairs={{0,12},{4,8},{8,4},{12,0},{1,13},{5,9},{9,5},{13,1},{2,14},{6,10},... | collective-permute-start | bytes 196616 | tf_op jit(solution)/shard_map/ppermute | solution.py:284
  18.2 2.3 %collective-permute-start.3 = (f32[3,64,512]{2,1,0:T(8,128)S(1)}, f32[3,64,512]{2,1,0:T(8,128)S(1)}, u32[]{:S(2)}, u32[]{:S(2)}) collective-permute-start(f32[3,64,512]{2,1,0:T(8,128)S(1)} %partials.6.refs_9_), channel_id=1, source_target_pairs={{0,1},{1,0},{2,3},{3,2},{4,5},{5,4},{6,7},{7,6},{8,9},{9,8},{10,11... | collective-permute-start | bytes 1179656 | tf_op jit(solution)/shard_map/ppermute | solution.py:287
  19.9 5.4 %collective-permute-start.4 = (f32[3,64,768]{2,1,0:T(8,128)S(1)}, f32[3,64,768]{2,1,0:T(8,128)S(1)}, u32[]{:S(2)}, u32[]{:S(2)}) collective-permute-start(f32[3,64,768]{2,1,0:T(8,128)S(1)} %partials.7.refs_9_), channel_id=1, source_target_pairs={{0,1},{1,0},{2,3},{3,2},{4,5},{5,4},{6,7},{7,6},{8,9},{9,8},{10,11... | collective-permute-start | bytes 1769480 | tf_op jit(solution)/shard_map/ppermute | solution.py:287
  23.5 3.9 %collective-permute-start.5 = (f32[3,64,768]{2,1,0:T(8,128)S(1)}, f32[3,64,768]{2,1,0:T(8,128)S(1)}, u32[]{:S(2)}, u32[]{:S(2)}) collective-permute-start(f32[3,64,768]{2,1,0:T(8,128)S(1)} %partials.9.refs_9_), channel_id=1, source_target_pairs={{0,1},{1,0},{2,3},{3,2},{4,5},{5,4},{6,7},{7,6},{8,9},{9,8},{10,11... | collective-permute-start | bytes 1769480 | tf_op jit(solution)/shard_map/ppermute | solution.py:287
  23.6 7.8 %collective-permute-start.6 = (bf16[3,64,512]{2,1,0:T(8,128)(2,1)S(1)}, bf16[3,64,512]{2,1,0:T(8,128)(2,1)S(1)}, u32[]{:S(2)}, u32[]{:S(2)}) collective-permute-start(bf16[3,64,512]{2,1,0:T(8,128)(2,1)S(1)} %get-tuple-element.58), channel_id=1, source_target_pairs={{0,2},{1,3},{2,0},{3,1},{4,6},{5,7},{6,4},{7,5},{8,10},{9,11},{10,... | collective-permute-start | bytes 589832 | tf_op jit(solution)/shard_map/ppermute | solution.py:291
  27.1 12.1 %collective-permute-start.8 = (bf16[3,64,768]{2,1,0:T(8,128)(2,1)S(1)}, bf16[3,64,768]{2,1,0:T(8,128)(2,1)S(1)}, u32[]{:S(2)}, u32[]{:S(2)}) collective-permute-start(bf16[3,64,768]{2,1,0:T(8,128)(2,1)S(1)} %get-tuple-element.69), channel_id=1, source_target_pairs={{0,2},{1,3},{2,0},{3,1},{4,6},{5,7},{6,4},{7,5},{8,10},{9,11},{10,... | collective-permute-start | bytes 884744 | tf_op jit(solution)/shard_map/ppermute | solution.py:291
  32.0 3.6 %collective-permute-start.7 = (bf16[3,64,512]{2,1,0:T(8,128)(2,1)S(1)}, bf16[3,64,512]{2,1,0:T(8,128)(2,1)S(1)}, u32[]{:S(2)}, u32[]{:S(2)}) collective-permute-start(bf16[3,64,512]{2,1,0:T(8,128)(2,1)S(1)} %activate.3.refs_1_), channel_id=1, source_target_pairs={{0,1},{1,0},{2,3},{3,2},{4,5},{5,4},{6,7},{7,6},{8,9},{9,8},{10,11... | collective-permute-start | bytes 589832 | tf_op jit(solution)/shard_map/ppermute | solution.py:287
  39.9 6.8 %collective-permute-start.9 = (bf16[3,64,768]{2,1,0:T(8,128)(2,1)S(1)}, bf16[3,64,768]{2,1,0:T(8,128)(2,1)S(1)}, u32[]{:S(2)}, u32[]{:S(2)}) collective-permute-start(bf16[3,64,768]{2,1,0:T(8,128)(2,1)S(1)} %activate.4.refs_1_), channel_id=1, source_target_pairs={{0,1},{1,0},{2,3},{3,2},{4,5},{5,4},{6,7},{7,6},{8,9},{9,8},{10,11... | collective-permute-start | bytes 884744 | tf_op jit(solution)/shard_map/ppermute | solution.py:287
  40.4 10.8 %collective-permute-start.10 = (bf16[3,64,768]{2,1,0:T(8,128)(2,1)S(1)}, bf16[3,64,768]{2,1,0:T(8,128)(2,1)S(1)}, u32[]{:S(2)}, u32[]{:S(2)}) collective-permute-start(bf16[3,64,768]{2,1,0:T(8,128)(2,1)S(1)} %get-tuple-element.78), channel_id=1, source_target_pairs={{0,2},{1,3},{2,0},{3,1},{4,6},{5,7},{6,4},{7,5},{8,10},{9,11},{10,... | collective-permute-start | bytes 884744 | tf_op jit(solution)/shard_map/ppermute | solution.py:291
  51.9 2.1 %collective-permute-start.11 = (bf16[3,64,768]{2,1,0:T(8,128)(2,1)S(1)}, bf16[3,64,768]{2,1,0:T(8,128)(2,1)S(1)}, u32[]{:S(2)}, u32[]{:S(2)}) collective-permute-start(bf16[3,64,768]{2,1,0:T(8,128)(2,1)S(1)} %activate.5.refs_1_), channel_id=1, source_target_pairs={{0,1},{1,0},{2,3},{3,2},{4,5},{5,4},{6,7},{7,6},{8,9},{9,8},{10,11... | collective-permute-start | bytes 884744 | tf_op jit(solution)/shard_map/ppermute | solution.py:287
  56.1 11.8 %collective-permute-start.12 = (bf16[2,16,1024]{2,1,0:T(8,128)(2,1)S(1)}, bf16[2,16,1024]{2,1,0:T(8,128)(2,1)S(1)}, u32[]{:S(2)}, u32[]{:S(2)}) collective-permute-start(bf16[2,16,1024]{2,1,0:T(8,128)(2,1)S(1)} %get-tuple-element.80), channel_id=1, source_target_pairs={{0,4},{4,0},{8,12},{12,8},{1,5},{5,1},{9,13},{13,9},{2,6},{6,2},{1... | collective-permute-start | bytes 196616 | tf_op jit(solution)/shard_map/ppermute | solution.py:284
  56.8 11.1 %collective-permute-start.13 = (bf16[2,16,1024]{2,1,0:T(8,128)(2,1)S(1)}, bf16[2,16,1024]{2,1,0:T(8,128)(2,1)S(1)}, u32[]{:S(2)}, u32[]{:S(2)}) collective-permute-start(bf16[2,16,1024]{2,1,0:T(8,128)(2,1)S(1)} %get-tuple-element.81), channel_id=1, source_target_pairs={{0,8},{4,12},{8,0},{12,4},{1,9},{5,13},{9,1},{13,5},{2,10},{6,14},... | collective-permute-start | bytes 196616 | tf_op jit(solution)/shard_map/ppermute | solution.py:284
  60.3 7.6 %collective-permute-start.14 = (bf16[2,16,1024]{2,1,0:T(8,128)(2,1)S(1)}, bf16[2,16,1024]{2,1,0:T(8,128)(2,1)S(1)}, u32[]{:S(2)}, u32[]{:S(2)}) collective-permute-start(bf16[2,16,1024]{2,1,0:T(8,128)(2,1)S(1)} %get-tuple-element.82), channel_id=1, source_target_pairs={{0,12},{4,8},{8,4},{12,0},{1,13},{5,9},{9,5},{13,1},{2,14},{6,10},... | collective-permute-start | bytes 196616 | tf_op jit(solution)/shard_map/ppermute | solution.py:284

commit v9 on v8

--- a/solution.py
+++ b/solution.py
@@ -33,9 +33,9 @@
     return (pltpu.with_memory_space_constraint(array, pltpu.VMEM), spec)
 
 
-def call(kernel, name, scalars, ins, outs, scratch=None, aliases=None, vmem=2):
+def call(kernel, name, ins, outs, scratch=None, aliases=None, vmem=2):
     scratch = scratch or {}
-    names = ["place", *ins, *outs, *scratch]
+    names = [*ins, *outs, *scratch]
     in_names, out_names = list(ins), list(outs)
 
     def body(*refs):
@@ -44,20 +44,16 @@
     results = pl.pallas_call(
         body,
         out_shape=[shape for shape, _ in outs.values()],
-        grid_spec=pltpu.PrefetchScalarGridSpec(
-            num_scalar_prefetch=1,
-            grid=(1,),
-            in_specs=[spec for _, spec in ins.values()],
-            out_specs=[spec for _, spec in outs.values()],
-            scratch_shapes=list(scratch.values()),
-        ),
+        in_specs=[spec for _, spec in ins.values()],
+        out_specs=[spec for _, spec in outs.values()],
+        scratch_shapes=list(scratch.values()),
         input_output_aliases={
-            1 + in_names.index(i): out_names.index(o) for i, o in (aliases or {}).items()
+            in_names.index(i): out_names.index(o) for i, o in (aliases or {}).items()
         },
         compiler_params=pltpu.CompilerParams(vmem_limit_bytes=vmem * MIB),
         cost_estimate=pl.CostEstimate(flops=1, bytes_accessed=1, transcendentals=0),
         name=name,
-    )(scalars, *[array for array, _ in ins.values()])
+    )(*[array for array, _ in ins.values()])
     return dict(zip(out_names, results))
 
 
@@ -89,6 +85,11 @@
         value = dot(entries, features, (0, 0))
         for b in range(along):
             by_features[b] = value[b : b + 1, :]
+
+
+def first_unit(which, half):
+    core = lax.rem(lax.axis_index("dp"), 2)
+    return (core if which == 0 else 1 - core) * half
 
 
 def span(start, size):
@@ -143,10 +144,11 @@
     return sum(value[b * rows : (b + 1) * rows, :] * m for b, m in enumerate(masks))
 
 
-def partial_kernel(which, start, tile, r):
+def partial_kernel(which, start, half, tile, r):
     pairs, _, size = r.tok_d.shape
+    base = first_unit(which, half) + start
     for first in range(0, r.send.shape[2], tile):
-        at = span(r.place[which] + start + first, tile)
+        at = span(base + first, tile)
         local = slice(first, first + tile)
         totals = [0.0, 0.0, 0.0]
         for p in range(pairs):
@@ -215,7 +217,7 @@
                 copy.wait()
 
 
-def back_kernel(items, do_rows, do_grads, r):
+def back_kernel(items, half, do_rows, do_grads, r):
     tile = r.act_d.shape[3]
     spots = tile // BLK
     r.act_d[...] = jnp.zeros_like(r.act_d)
@@ -227,7 +229,7 @@
     for act, which, start in items:
         act = getattr(r, act)
         _, rows, size = act.shape
-        base = r.place[which] + start
+        base = first_unit(which, half) + start
         at, block = span(base, size), lax.div(base, BLK)
         tiles = [slice(i * tile, (i + 1) * tile) for i in range(size // tile)]
         for i, local in enumerate(tiles):
@@ -277,9 +279,6 @@
     direct = n_grid == 4
     grant = lambda mib: mib if rows <= 64 else 32
 
-    core = lax.axis_index("dp") % 2
-    place = jnp.stack([core * half, (1 - core) * half]).astype(jnp.int32)
-
     def trade(array, s):
         return lax.ppermute(array, "grid", [(i, i ^ s) for i in range(n_grid)])
 
@@ -314,7 +313,6 @@
     values = call(
         fetch_kernel,
         "fetch",
-        place,
         {**weights, **{"hbm_" + k: (hbm(m), ANY) for k, m in masks.items()}},
         {
             **{k: pinned(across_shape) for k in ("mg", "mu", "mdt")},
@@ -333,7 +331,6 @@
     values |= call(
         assemble_kernel,
         "assemble",
-        place,
         {
             "after": (values["mg"], ANY),
             **{f"block{k}": (b, whole(b)) for k, b in reversed(list(enumerate(blocks)))},
@@ -359,14 +356,14 @@
         if received is not None:
             ins["received"] = pinned(received)
             outs = {"own": pinned(shape(*trio, kind=F32)), "send": pinned(shape(*trio))}
-        kernel = functools.partial(partial_kernel, which, starts[p], tile)
-        return call(kernel, "partials", place, ins, outs, vmem=grant(2))
+        kernel = functools.partial(partial_kernel, which, starts[p], half, tile)
+        return call(kernel, "partials", ins, outs, vmem=grant(2))
 
     def activate(own, others, after):
         ins = {"own": pinned(own), "after": (after, ANY)}
         ins.update({f"other{k}": pinned(a) for k, a in enumerate(others)})
         outs = {"act": pinned(shape(*own.shape))}
-        return call(act_kernel, "activate", place, ins, outs, vmem=grant(2))["act"]
+        return call(act_kernel, "activate", ins, outs, vmem=grant(2))["act"]
 
     def back(pieces, do_rows, do_grads, state, last=False):
         items = [(f"act{k}", which, starts[p]) for k, (which, p, _) in enumerate(pieces)]
@@ -405,9 +402,8 @@
             if "rows0" in state:
                 ins["after"] = (state["rows0"], ANY)
         got = call(
-            functools.partial(back_kernel, items, do_rows, do_grads),
+            functools.partial(back_kernel, items, half, do_rows, do_grads),
             "_".join(["back"] + ["rows"] * do_rows + ["grads"] * do_grads),
-            place,
             ins,
             outs,
             scratch=scratch,

time: 68.8 us -> 60.3 us (0.88)
  Pallas kernels: 48.6 us -> 38.8 us
  waiting for transfers between devices: 2.24 us -> 3.56 us
    pallas_call x18, Pallas kernels: 48.6 us -> 38.8 us  [call(): pl.pallas_call(body, out_shape=[shape for shape, _ in outs.values()], in_...]
    ppermute x3, waiting for transfers between devices: 2.21 us -> 3.39 us  [across(): lax.ppermute(array, 'dp', [(i, (i // 2 + s) % pairs * 2 + i % 2) for i in...]
  transfers between devices with their start and end apart: 15 -> 15, of which waited for: 1 -> 2; matrix products, arithmetic and copies ran while one was open for 0% -> 0% of each run, Pallas kernels for 63% -> 60%
where the time goes in v9:
time: 60.3 us; the launch traced here: 60.1 us
  Pallas kernels  38.8 us (64%)
  starting transfers between devices  15.5 us (26%)
  waiting for transfers between devices  3.56 us (6%)
  between operations  0.89 us (1%)
  other arithmetic  0.82 us (1%)
  local copies, waits for them, and re-layouts  0.63 us (1%)
    pallas_call x18, Pallas kernels, call(): pl.pallas_call(body, out_shape=[shape for shape, _ in outs.values()], in_...  38.8 us
    ppermute x6, starting transfers between devices, trade(): return lax.ppermute(array, 'grid', [(i, i ^ s) for i in range(n_grid)])  10.1 us
    ppermute x3, starting transfers between devices, across(): lax.ppermute(array, 'dp', [(i, (i // 2 + s) % pairs * 2 + i % 2) for i in...  3.82 us
    ppermute x3, waiting for transfers between devices, across(): lax.ppermute(array, 'dp', [(i, (i // 2 + s) % pairs * 2 + i % 2) for i in...  3.39 us
    ppermute x6, starting transfers between devices, swap(): return lax.ppermute(array, 'dp', [(i, i ^ 1) for i in range(n_dp)])  1.52 us
  transfers between devices with their start and end apart: 15, of which 2 were waited for; matrix products, arithmetic and copies ran while one was open for 0% of the time, Pallas kernels for 60%

profile of v9, /device:TPU:0, one launch (start us, length us, event | category | flops | bytes accessed | tf_op | source)
XLA Modules:
  0.0 60.1 jit_solution(3891253558467056971)
XLA Ops:
  0.6 0.8 %pad_maximum_fusion.refs_4_ = bf16[2,16,1024]{2,1,0:T(8,128)(2,1)S(1)} fusion(bf16[1,16,1024]{2,1,0:T(8,128)(2,1)} %bitcast.7, bf16[1,16,1024]{2,1,0:T(8,128)(2,1)} %bitcast.8), kind=kLoop, calls=%fused_computation.1 | loop fusion | flops 32768 | bytes 131072 | tf_op jit(solution)/shard_map/stack | solution.py:304
  1.4 3.1 %collective-permute-start.2 = (bf16[2,16,1024]{2,1,0:T(8,128)(2,1)S(1)}, bf16[2,16,1024]{2,1,0:T(8,128)(2,1)S(1)}, u32[]{:S(2)}, u32[]{:S(2)}) collective-permute-start(bf16[2,16,1024]{2,1,0:T(8,128)(2,1)S(1)} %pad_maximum_fusion.refs_4_), channel_id=1, source_target_pairs={{0,4},{4,0},{8,12},{12,8},{1,5},{5,1},{9,13},{13,9},{2,6},{6,2},{1... | collective-permute-start | bytes 196616 | tf_op jit(solution)/shard_map/ppermute | solution.py:283
  4.5 2.6 %collective-permute-start.1 = (bf16[2,16,1024]{2,1,0:T(8,128)(2,1)S(1)}, bf16[2,16,1024]{2,1,0:T(8,128)(2,1)S(1)}, u32[]{:S(2)}, u32[]{:S(2)}) collective-permute-start(bf16[2,16,1024]{2,1,0:T(8,128)(2,1)S(1)} %pad_maximum_fusion.refs_4_), channel_id=1, source_target_pairs={{0,8},{4,12},{8,0},{12,4},{1,9},{5,13},{9,1},{13,5},{2,10},{6,14},... | collective-permute-start | bytes 196616 | tf_op jit(solution)/shard_map/ppermute | solution.py:283
  7.1 0.0 collective-permute-start
  7.1 8.4 %fetch.1 = (f32[8,1,4096]{2,1,0:T(1,128)S(1)}, f32[8,1,4096]{2,1,0:T(1,128)S(1)}, f32[8,1,4096]{2,1,0:T(1,128)S(1)}, f32[32,1,1024]{2,1,0:T(1,128)S(1)}, f32[32,...) custom-call(bf16[1024,4096]{1,0:T(8,128)(2,1)} %refs_0_.1, ...), custom_call_target="tpu_custom_call" | custom-call | flops 1 | bytes 1 | tf_op jit(solution)/shard_map/fetch/pallas_call | solution.py:44
  15.5 0.0 collective-permute-done.2.refs_3_
  15.5 0.0 collective-permute-done.1.refs_2_
  15.5 0.0 collective-permute-done.refs_1_
  15.5 0.2 assemble.1
  15.7 0.8 %partials.6.refs_8_ = f32[3,64,512]{2,1,0:T(8,128)S(1)} custom-call(bf16[4,128,256]{2,1,0:T(8,128)(2,1)S(1)} %get-tuple-element.48.refs_0_, bf16[4,128,256]{2,1,0:T(8,128)(2,1)S(1)} %get-tuple-element.49.refs_1_, f32[8,1,4096]{2,1,0:T(1,128)S(1)} %get-tuple-element.47.refs_0_.refs_2_.refs_9_.refs_10_.refs_5_, ...), custom_call_target="tpu_custom_call" | custom-call | flops 1 | bytes 1 | tf_op jit(solution)/shard_map/partials/pallas_call | solution.py:44
  16.5 0.1 collective-permute-start.3
  16.6 1.1 %partials.7.refs_8_ = f32[3,64,768]{2,1,0:T(8,128)S(1)} custom-call(bf16[4,128,256]{2,1,0:T(8,128)(2,1)S(1)} %get-tuple-element.48.refs_0_, bf16[4,128,256]{2,1,0:T(8,128)(2,1)S(1)} %get-tuple-element.49.refs_1_, f32[8,1,4096]{2,1,0:T(1,128)S(1)} %get-tuple-element.47.refs_0_.refs_2_.refs_9_.refs_10_.refs_5_, ...), custom_call_target="tpu_custom_call" | custom-call | flops 1 | bytes 1 | tf_op jit(solution)/shard_map/partials/pallas_call | solution.py:44
  17.7 0.5 collective-permute-start.4
  18.2 0.0 collective-permute-done.3.refs_9_
  18.3 0.8 %partials.8 = (f32[3,64,512]{2,1,0:T(8,128)S(1)}, bf16[3,64,512]{2,1,0:T(8,128)(2,1)S(1)}) custom-call(bf16[4,128,256]{2,1,0:T(8,128)(2,1)S(1)} %get-tuple-element.48.refs_0_, bf16[4,128,256]{2,1,0:T(8,128)(2,1)S(1)} %get-tuple-element.49.refs_1_, f32[8,1,4096]{2,1,0:T(1,128)S(1)} %get-tuple-element.47.refs_0_.refs_2_.refs_9_.refs_10_.refs_5_, ...), custom_call_target="tpu_custom_call" | custom-call | flops 1 | bytes 1 | tf_op jit(solution)/shard_map/partials/pallas_call | solution.py:44
  19.1 1.1 %partials.9.refs_8_ = f32[3,64,768]{2,1,0:T(8,128)S(1)} custom-call(bf16[4,128,256]{2,1,0:T(8,128)(2,1)S(1)} %get-tuple-element.48.refs_0_, bf16[4,128,256]{2,1,0:T(8,128)(2,1)S(1)} %get-tuple-element.49.refs_1_, f32[8,1,4096]{2,1,0:T(1,128)S(1)} %get-tuple-element.47.refs_0_.refs_2_.refs_9_.refs_10_.refs_5_, ...), custom_call_target="tpu_custom_call" | custom-call | flops 1 | bytes 1 | tf_op jit(solution)/shard_map/partials/pallas_call | solution.py:44
  20.2 0.2 collective-permute-start.5
  20.4 1.7 %collective-permute-start.6 = (bf16[3,64,512]{2,1,0:T(8,128)(2,1)S(1)}, bf16[3,64,512]{2,1,0:T(8,128)(2,1)S(1)}, u32[]{:S(2)}, u32[]{:S(2)}) collective-permute-start(bf16[3,64,512]{2,1,0:T(8,128)(2,1)S(1)} %get-tuple-element.58), channel_id=1, source_target_pairs={{0,2},{1,3},{2,0},{3,1},{4,6},{5,7},{6,4},{7,5},{8,10},{9,11},{10,... | collective-permute-start | bytes 589832 | tf_op jit(solution)/shard_map/ppermute | solution.py:290
  22.1 0.0 collective-permute-done.4.refs_9_
  22.1 1.1 %partials.10 = (f32[3,64,768]{2,1,0:T(8,128)S(1)}, bf16[3,64,768]{2,1,0:T(8,128)(2,1)S(1)}) custom-call(bf16[4,128,256]{2,1,0:T(8,128)(2,1)S(1)} %get-tuple-element.48.refs_0_, bf16[4,128,256]{2,1,0:T(8,128)(2,1)S(1)} %get-tuple-element.49.refs_1_, f32[8,1,4096]{2,1,0:T(1,128)S(1)} %get-tuple-element.47.refs_0_.refs_2_.refs_9_.refs_10_.refs_5_, ...), custom_call_target="tpu_custom_call" | custom-call | flops 1 | bytes 1 | tf_op jit(solution)/shard_map/partials/pallas_call | solution.py:44
  23.3 0.4 collective-permute-start.8
  23.6 0.0 collective-permute-done.5.refs_9_
  23.6 1.1 %partials.11 = (f32[3,64,768]{2,1,0:T(8,128)S(1)}, bf16[3,64,768]{2,1,0:T(8,128)(2,1)S(1)}) custom-call(bf16[4,128,256]{2,1,0:T(8,128)(2,1)S(1)} %get-tuple-element.48.refs_0_, bf16[4,128,256]{2,1,0:T(8,128)(2,1)S(1)} %get-tuple-element.49.refs_1_, f32[8,1,4096]{2,1,0:T(1,128)S(1)} %get-tuple-element.47.refs_0_.refs_2_.refs_9_.refs_10_.refs_5_, ...), custom_call_target="tpu_custom_call" | custom-call | flops 1 | bytes 1 | tf_op jit(solution)/shard_map/partials/pallas_call | solution.py:44
  24.8 3.4 %collective-permute-done.6.refs_2_ = bf16[3,64,512]{2,1,0:T(8,128)(2,1)S(1)} collective-permute-done((bf16[3,64,512]{2,1,0:T(8,128)(2,1)S(1)}, bf16[3,64,512]{2,1,0:T(8,128)(2,1)S(1)}, u32[]{:S(2)}, u32[]{:S(2)}) %collective-permute-start.6) | collective-permute-done | bytes 196640 | tf_op jit(solution)/shard_map/ppermute | solution.py:290
  28.2 0.1 activate.3.refs_0_
  28.2 0.1 collective-permute-start.7
  28.3 3.0 %back_rows_grads.4 = (f32[2,64,1024]{2,1,0:T(8,128)S(1)}, f32[1024,4096]{1,0:T(8,128)}, f32[1024,4096]{1,0:T(8,128)}, f32[4096,1024]{1,0:T(8,128)}) custom-call(bf16[3,64,512]{2,1,0:T(8,128)(2,1)S(1)} %activate.3.refs_0_, f32[32,1,1024]{2,1,0:T(1,128)S(1)} %get-tuple-element.59.refs_1_.refs_2_, f32[32,1,1024]{2,1,0:T(1,128)S(1)} %get-tuple-element.60.refs_2_, ...), custom_call_target="tpu_custom_call" | custom-call | flops 1 | bytes 1 | tf_op jit(solution)/shard_map/back_rows_grads/pallas_call | solution.py:44
  31.3 0.0 collective-permute-done.7.refs_0_
  31.3 3.0 %back_rows_grads.5 = (f32[2,64,1024]{2,1,0:T(8,128)S(1)}, f32[1024,4096]{1,0:T(8,128)}, f32[1024,4096]{1,0:T(8,128)}, f32[4096,1024]{1,0:T(8,128)}) custom-call(bf16[3,64,512]{2,1,0:T(8,128)(2,1)S(1)} %collective-permute-done.7.refs_0_, ...), custom_call_target="tpu_custom_call", output_to_operand_aliasing={{1}: (12, {}), {2}: (13, {}), {3}: (14, {})} | custom-call | flops 1 | bytes 1 | tf_op jit(solution)/shard_map/back_rows_grads/pallas_call | solution.py:44
  34.4 0.0 collective-permute-done.8.refs_2_
  34.4 0.1 activate.4.refs_0_
  34.5 0.6 collective-permute-start.9
  35.1 1.7 %collective-permute-start.10 = (bf16[3,64,768]{2,1,0:T(8,128)(2,1)S(1)}, bf16[3,64,768]{2,1,0:T(8,128)(2,1)S(1)}, u32[]{:S(2)}, u32[]{:S(2)}) collective-permute-start(bf16[3,64,768]{2,1,0:T(8,128)(2,1)S(1)} %get-tuple-element.78), channel_id=1, source_target_pairs={{0,2},{1,3},{2,0},{3,1},{4,6},{5,7},{6,4},{7,5},{8,10},{9,11},{10,... | collective-permute-start | bytes 884744 | tf_op jit(solution)/shard_map/ppermute | solution.py:290
  36.8 4.0 %back_rows_grads.6 = (f32[2,64,1024]{2,1,0:T(8,128)S(1)}, f32[1024,4096]{1,0:T(8,128)}, f32[1024,4096]{1,0:T(8,128)}, f32[4096,1024]{1,0:T(8,128)}) custom-call(bf16[3,64,768]{2,1,0:T(8,128)(2,1)S(1)} %activate.4.refs_0_, f32[32,1,1024]{2,1,0:T(1,128)S(1)} %get-tuple-element.59.refs_1_.refs_2_, ...), custom_call_target="tpu_custom_call", output_to_operand_aliasing={{1}: (12, {}), {2}: (13, {}), {3}: (14, {})} | custom-call | flops 1 | bytes 1 | tf_op jit(solution)/shard_map/back_rows_grads/pallas_call | solution.py:44
  40.8 0.0 collective-permute-done.9.refs_0_
  40.8 4.0 %back_rows_grads.7 = (f32[2,64,1024]{2,1,0:T(8,128)S(1)}, f32[1024,4096]{1,0:T(8,128)}, f32[1024,4096]{1,0:T(8,128)}, f32[4096,1024]{1,0:T(8,128)}) custom-call(bf16[3,64,768]{2,1,0:T(8,128)(2,1)S(1)} %collective-permute-done.9.refs_0_, ...), custom_call_target="tpu_custom_call", output_to_operand_aliasing={{1}: (12, {}), {2}: (13, {}), {3}: (14, {})} | custom-call | flops 1 | bytes 1 | tf_op jit(solution)/shard_map/back_rows_grads/pallas_call | solution.py:44
  44.8 0.0 collective-permute-done.10.refs_2_
  44.8 0.1 activate.5.refs_0_
  45.0 0.1 collective-permute-start.11
  45.1 1.5 %back_rows.2.refs_7_ = f32[2,64,1024]{2,1,0:T(8,128)S(1)} custom-call(bf16[3,64,768]{2,1,0:T(8,128)(2,1)S(1)} %activate.5.refs_0_, f32[32,1,1024]{2,1,0:T(1,128)S(1)} %get-tuple-element.59.refs_1_.refs_2_, f32[32,1,1024]{2,1,0:T(1,128)S(1)} %get-tuple-element.60.refs_2_, f32[32,1,1024]{2,1,0:T(1,128)S(1)} %get-tuple-element.61.refs_3_, ...), custom_call_target="tpu_custom_call" | custom-call | flops 1 | bytes 1 | tf_op jit(solution)/shard_map/back_rows/pallas_call | solution.py:44
  46.5 0.1 collective-permute-done.11.refs_0_.refs_1_
  46.6 1.5 %back_rows.3 = (bf16[2,16,1024]{2,1,0:T(8,128)(2,1)S(1)}, bf16[2,16,1024]{2,1,0:T(8,128)(2,1)S(1)}, bf16[2,16,1024]{2,1,0:T(8,128)(2,1)S(1)}, bf16[2,16,1024]{2,1,0:T(8,128)(2,1)S(1)}) custom-call(bf16[3,64,768]{2,1,0:T(8,128)(2,1)S(1)} %collective-permute-done.11.refs_0_.refs_1_, f32[32,1,1024]{2,1,0:T(1,128)S(1)} %get-tuple-element.59.refs_1_.refs_2_, ...), custom_call_target="tpu_custom_call" | custom-call | flops 1 | bytes 1 | tf_op jit(solution)/shard_map/back_rows/pallas_call | solution.py:44
  48.1 0.7 %collective-permute-start.12 = (bf16[2,16,1024]{2,1,0:T(8,128)(2,1)S(1)}, bf16[2,16,1024]{2,1,0:T(8,128)(2,1)S(1)}, u32[]{:S(2)}, u32[]{:S(2)}) collective-permute-start(bf16[2,16,1024]{2,1,0:T(8,128)(2,1)S(1)} %get-tuple-element.80), channel_id=1, source_target_pairs={{0,4},{4,0},{8,12},{12,8},{1,5},{5,1},{9,13},{13,9},{2,6},{6,2},{1... | collective-permute-start | bytes 196616 | tf_op jit(solution)/shard_map/ppermute | solution.py:283
  48.9 3.5 %collective-permute-start.13 = (bf16[2,16,1024]{2,1,0:T(8,128)(2,1)S(1)}, bf16[2,16,1024]{2,1,0:T(8,128)(2,1)S(1)}, u32[]{:S(2)}, u32[]{:S(2)}) collective-permute-start(bf16[2,16,1024]{2,1,0:T(8,128)(2,1)S(1)} %get-tuple-element.81), channel_id=1, source_target_pairs={{0,8},{4,12},{8,0},{12,4},{1,9},{5,13},{9,1},{13,5},{2,10},{6,14},... | collective-permute-start | bytes 196616 | tf_op jit(solution)/shard_map/ppermute | solution.py:283
  52.3 0.2 collective-permute-start.14
  52.6 6.8 %back_grads.1 = (f32[1024,4096]{1,0:T(8,128)}, f32[1024,4096]{1,0:T(8,128)}, f32[4096,1024]{1,0:T(8,128)}) custom-call(bf16[3,64,768]{2,1,0:T(8,128)(2,1)S(1)} %activate.5.refs_0_, bf16[3,64,768]{2,1,0:T(8,128)(2,1)S(1)} %collective-permute-done.11.refs_0_.refs_1_, ...), custom_call_target="tpu_custom_call", output_to_operand_aliasing={{0}: (7, {}), {1}: (8, {}), {2}: (9, {})} | custom-call | flops 1 | bytes 1 | tf_op jit(solution)/shard_map/back_grads/pallas_call | solution.py:44
  59.4 0.0 collective-permute-done.12
  59.4 0.0 collective-permute-done.13
  59.4 0.0 collective-permute-done.14
  59.5 0.6 %slice_bitcast_fusion = (bf16[16,1024]{1,0:T(8,128)(2,1)}, bf16[16,1024]{1,0:T(8,128)(2,1)}) fusion(bf16[2,16,1024]{2,1,0:T(8,128)(2,1)S(1)} %add_convert_fusion), kind=kLoop, calls=%fused_computation.2 | loop fusion | bytes 131072 | tf_op jit(solution)/shard_map/squeeze | solution.py:443
  (1 shorter events, 0.0 us)
Async XLA Ops:
  1.4 14.1 %collective-permute-start.2 = (bf16[2,16,1024]{2,1,0:T(8,128)(2,1)S(1)}, bf16[2,16,1024]{2,1,0:T(8,128)(2,1)S(1)}, u32[]{:S(2)}, u32[]{:S(2)}) collective-permute-start(bf16[2,16,1024]{2,1,0:T(8,128)(2,1)S(1)} %pad_maximum_fusion.refs_4_), channel_id=1, source_target_pairs={{0,4},{4,0},{8,12},{12,8},{1,5},{5,1},{9,13},{13,9},{2,6},{6,2},{1... | collective-permute-start | bytes 196616 | tf_op jit(solution)/shard_map/ppermute | solution.py:283
  4.5 11.0 %collective-permute-start.1 = (bf16[2,16,1024]{2,1,0:T(8,128)(2,1)S(1)}, bf16[2,16,1024]{2,1,0:T(8,128)(2,1)S(1)}, u32[]{:S(2)}, u32[]{:S(2)}) collective-permute-start(bf16[2,16,1024]{2,1,0:T(8,128)(2,1)S(1)} %pad_maximum_fusion.refs_4_), channel_id=1, source_target_pairs={{0,8},{4,12},{8,0},{12,4},{1,9},{5,13},{9,1},{13,5},{2,10},{6,14},... | collective-permute-start | bytes 196616 | tf_op jit(solution)/shard_map/ppermute | solution.py:283
  7.1 8.4 %collective-permute-start = (bf16[2,16,1024]{2,1,0:T(8,128)(2,1)S(1)}, bf16[2,16,1024]{2,1,0:T(8,128)(2,1)S(1)}, u32[]{:S(2)}, u32[]{:S(2)}) collective-permute-start(bf16[2,16,1024]{2,1,0:T(8,128)(2,1)S(1)} %pad_maximum_fusion.refs_4_), channel_id=1, source_target_pairs={{0,12},{4,8},{8,4},{12,0},{1,13},{5,9},{9,5},{13,1},{2,14},{6,10},... | collective-permute-start | bytes 196616 | tf_op jit(solution)/shard_map/ppermute | solution.py:283
  16.5 1.8 %collective-permute-start.3 = (f32[3,64,512]{2,1,0:T(8,128)S(1)}, f32[3,64,512]{2,1,0:T(8,128)S(1)}, u32[]{:S(2)}, u32[]{:S(2)}) collective-permute-start(f32[3,64,512]{2,1,0:T(8,128)S(1)} %partials.6.refs_8_), channel_id=1, source_target_pairs={{0,1},{1,0},{2,3},{3,2},{4,5},{5,4},{6,7},{7,6},{8,9},{9,8},{10,11... | collective-permute-start | bytes 1179656 | tf_op jit(solution)/shard_map/ppermute | solution.py:286
  17.7 4.4 %collective-permute-start.4 = (f32[3,64,768]{2,1,0:T(8,128)S(1)}, f32[3,64,768]{2,1,0:T(8,128)S(1)}, u32[]{:S(2)}, u32[]{:S(2)}) collective-permute-start(f32[3,64,768]{2,1,0:T(8,128)S(1)} %partials.7.refs_8_), channel_id=1, source_target_pairs={{0,1},{1,0},{2,3},{3,2},{4,5},{5,4},{6,7},{7,6},{8,9},{9,8},{10,11... | collective-permute-start | bytes 1769480 | tf_op jit(solution)/shard_map/ppermute | solution.py:286
  20.2 3.4 %collective-permute-start.5 = (f32[3,64,768]{2,1,0:T(8,128)S(1)}, f32[3,64,768]{2,1,0:T(8,128)S(1)}, u32[]{:S(2)}, u32[]{:S(2)}) collective-permute-start(f32[3,64,768]{2,1,0:T(8,128)S(1)} %partials.9.refs_8_), channel_id=1, source_target_pairs={{0,1},{1,0},{2,3},{3,2},{4,5},{5,4},{6,7},{7,6},{8,9},{9,8},{10,11... | collective-permute-start | bytes 1769480 | tf_op jit(solution)/shard_map/ppermute | solution.py:286
  20.4 7.7 %collective-permute-start.6 = (bf16[3,64,512]{2,1,0:T(8,128)(2,1)S(1)}, bf16[3,64,512]{2,1,0:T(8,128)(2,1)S(1)}, u32[]{:S(2)}, u32[]{:S(2)}) collective-permute-start(bf16[3,64,512]{2,1,0:T(8,128)(2,1)S(1)} %get-tuple-element.58), channel_id=1, source_target_pairs={{0,2},{1,3},{2,0},{3,1},{4,6},{5,7},{6,4},{7,5},{8,10},{9,11},{10,... | collective-permute-start | bytes 589832 | tf_op jit(solution)/shard_map/ppermute | solution.py:290
  23.3 11.1 %collective-permute-start.8 = (bf16[3,64,768]{2,1,0:T(8,128)(2,1)S(1)}, bf16[3,64,768]{2,1,0:T(8,128)(2,1)S(1)}, u32[]{:S(2)}, u32[]{:S(2)}) collective-permute-start(bf16[3,64,768]{2,1,0:T(8,128)(2,1)S(1)} %get-tuple-element.69), channel_id=1, source_target_pairs={{0,2},{1,3},{2,0},{3,1},{4,6},{5,7},{6,4},{7,5},{8,10},{9,11},{10,... | collective-permute-start | bytes 884744 | tf_op jit(solution)/shard_map/ppermute | solution.py:290
  28.2 3.1 %collective-permute-start.7 = (bf16[3,64,512]{2,1,0:T(8,128)(2,1)S(1)}, bf16[3,64,512]{2,1,0:T(8,128)(2,1)S(1)}, u32[]{:S(2)}, u32[]{:S(2)}) collective-permute-start(bf16[3,64,512]{2,1,0:T(8,128)(2,1)S(1)} %activate.3.refs_0_), channel_id=1, source_target_pairs={{0,1},{1,0},{2,3},{3,2},{4,5},{5,4},{6,7},{7,6},{8,9},{9,8},{10,11... | collective-permute-start | bytes 589832 | tf_op jit(solution)/shard_map/ppermute | solution.py:286
  34.5 6.3 %collective-permute-start.9 = (bf16[3,64,768]{2,1,0:T(8,128)(2,1)S(1)}, bf16[3,64,768]{2,1,0:T(8,128)(2,1)S(1)}, u32[]{:S(2)}, u32[]{:S(2)}) collective-permute-start(bf16[3,64,768]{2,1,0:T(8,128)(2,1)S(1)} %activate.4.refs_0_), channel_id=1, source_target_pairs={{0,1},{1,0},{2,3},{3,2},{4,5},{5,4},{6,7},{7,6},{8,9},{9,8},{10,11... | collective-permute-start | bytes 884744 | tf_op jit(solution)/shard_map/ppermute | solution.py:286
  35.1 9.7 %collective-permute-start.10 = (bf16[3,64,768]{2,1,0:T(8,128)(2,1)S(1)}, bf16[3,64,768]{2,1,0:T(8,128)(2,1)S(1)}, u32[]{:S(2)}, u32[]{:S(2)}) collective-permute-start(bf16[3,64,768]{2,1,0:T(8,128)(2,1)S(1)} %get-tuple-element.78), channel_id=1, source_target_pairs={{0,2},{1,3},{2,0},{3,1},{4,6},{5,7},{6,4},{7,5},{8,10},{9,11},{10,... | collective-permute-start | bytes 884744 | tf_op jit(solution)/shard_map/ppermute | solution.py:290
  45.0 1.6 %collective-permute-start.11 = (bf16[3,64,768]{2,1,0:T(8,128)(2,1)S(1)}, bf16[3,64,768]{2,1,0:T(8,128)(2,1)S(1)}, u32[]{:S(2)}, u32[]{:S(2)}) collective-permute-start(bf16[3,64,768]{2,1,0:T(8,128)(2,1)S(1)} %activate.5.refs_0_), channel_id=1, source_target_pairs={{0,1},{1,0},{2,3},{3,2},{4,5},{5,4},{6,7},{7,6},{8,9},{9,8},{10,11... | collective-permute-start | bytes 884744 | tf_op jit(solution)/shard_map/ppermute | solution.py:286
  48.1 11.3 %collective-permute-start.12 = (bf16[2,16,1024]{2,1,0:T(8,128)(2,1)S(1)}, bf16[2,16,1024]{2,1,0:T(8,128)(2,1)S(1)}, u32[]{:S(2)}, u32[]{:S(2)}) collective-permute-start(bf16[2,16,1024]{2,1,0:T(8,128)(2,1)S(1)} %get-tuple-element.80), channel_id=1, source_target_pairs={{0,4},{4,0},{8,12},{12,8},{1,5},{5,1},{9,13},{13,9},{2,6},{6,2},{1... | collective-permute-start | bytes 196616 | tf_op jit(solution)/shard_map/ppermute | solution.py:283
  48.9 10.6 %collective-permute-start.13 = (bf16[2,16,1024]{2,1,0:T(8,128)(2,1)S(1)}, bf16[2,16,1024]{2,1,0:T(8,128)(2,1)S(1)}, u32[]{:S(2)}, u32[]{:S(2)}) collective-permute-start(bf16[2,16,1024]{2,1,0:T(8,128)(2,1)S(1)} %get-tuple-element.81), channel_id=1, source_target_pairs={{0,8},{4,12},{8,0},{12,4},{1,9},{5,13},{9,1},{13,5},{2,10},{6,14},... | collective-permute-start | bytes 196616 | tf_op jit(solution)/shard_map/ppermute | solution.py:283
  52.3 7.1 %collective-permute-start.14 = (bf16[2,16,1024]{2,1,0:T(8,128)(2,1)S(1)}, bf16[2,16,1024]{2,1,0:T(8,128)(2,1)S(1)}, u32[]{:S(2)}, u32[]{:S(2)}) collective-permute-start(bf16[2,16,1024]{2,1,0:T(8,128)(2,1)S(1)} %get-tuple-element.82), channel_id=1, source_target_pairs={{0,12},{4,8},{8,4},{12,0},{1,13},{5,9},{9,5},{13,1},{2,14},{6,10},... | collective-permute-start | bytes 196616 | tf_op jit(solution)/shard_map/ppermute | solution.py:283

commit v10 on v9

--- a/solution.py
+++ b/solution.py
@@ -96,22 +96,33 @@
     return pl.ds(pl.multiple_of(start, BLK), size)
 
 
-def fetch_kernel(r):
-    copies = []
-    for source, target in ((r.w_gate, r.kg), (r.w_up, r.ku), (r.w_down, r.kd)):
-        height = source.shape[0] // SPLIT
-        for k in range(SPLIT):
-            rows = slice(k * height, (k + 1) * height)
-            copies.append((source.at[rows, :], target.at[rows, :]))
-    for k in MASKS:
-        copies.append((getattr(r, "hbm_" + k), getattr(r, k)))
-    copies = [pltpu.make_async_copy(a, b, r.sems.at[k]) for k, (a, b) in enumerate(copies)]
-    for copy in copies[-len(MASKS) :] + copies[: -len(MASKS)]:
+def copy_all(pairs, sems, first=0):
+    copies = [pltpu.make_async_copy(a, b, sems.at[first + k]) for k, (a, b) in enumerate(pairs)]
+    for copy in copies:
         copy.start()
-    for copy in copies[-len(MASKS) :]:
+    return copies
+
+
+def in_bands(source, target):
+    height = source.shape[0] // SPLIT
+    bands = [slice(k * height, (k + 1) * height) for k in range(SPLIT)]
+    return [(source.at[band, :], target.at[band, :]) for band in bands]
+
+
+def first_kernel(r):
+    small = [(getattr(r, "hbm_" + k), getattr(r, k)) for k in MASKS]
+    small += [(r.tokens, r.block.at[0]), (r.grad_out, r.block.at[1])]
+    small = copy_all(small, r.sems)
+    large = copy_all(in_bands(r.w_down, r.kd), r.sems, len(small))
+    for copy in small:
         copy.wait()
     spread(r)
-    for copy in copies[: -len(MASKS)]:
+    for copy in large:
+        copy.wait()
+
+
+def fetch_kernel(r):
+    for copy in copy_all(in_bands(r.w_gate, r.kg) + in_bands(r.w_up, r.ku), r.sems):
         copy.wait()
 
 
@@ -220,7 +231,6 @@
 def back_kernel(items, half, do_rows, do_grads, r):
     tile = r.act_d.shape[3]
     spots = tile // BLK
-    r.act_d[...] = jnp.zeros_like(r.act_d)
     if do_rows:
         r.acc[...] = r.sums[...] if hasattr(r, "sums") else jnp.zeros_like(r.acc)
     if do_grads:
@@ -232,19 +242,20 @@
         base = first_unit(which, half) + start
         at, block = span(base, size), lax.div(base, BLK)
         tiles = [slice(i * tile, (i + 1) * tile) for i in range(size // tile)]
+        for i in range(groups if do_grads else 0):
+            band = slice(i * height, (i + 1) * height)
+            for out, k, mask in ((r.gg, 1, r.mg), (r.gu, 2, r.mu)):
+                right = r.masked_act.at[k - 1]
+                for j in range(height // BLK):
+                    keep = mask[i * (height // BLK) + j, :, at].astype(BF16)
+                    right[j * rows : (j + 1) * rows, :] = act[k] * keep
+                by_cols.put(dot(r.tok_t[i], right[...]), out.at[band, at])
+        if act is r.act0:
+            r.act_d[...] = jnp.zeros_like(r.act_d)
         for i, local in enumerate(tiles):
             for k in range(3 if do_rows else 1):
                 diagonal(r.act_d.at[i, k], act[k, :, local])
-        for i in range(max(groups, len(tiles)) if do_grads else 0):
-            if i < groups:
-                band = slice(i * height, (i + 1) * height)
-                for out, k, mask in ((r.gg, 1, r.mg), (r.gu, 2, r.mu)):
-                    right = r.masked_act.at[k - 1]
-                    for j in range(height // BLK):
-                        keep = mask[i * (height // BLK) + j, :, at].astype(BF16)
-                        right[j * rows : (j + 1) * rows, :] = act[k] * keep
-                    by_cols.put(dot(r.tok_t[i], right[...]), out.at[band, at])
-            if i < len(tiles):
+            if do_grads:
                 for b in range(spots):
                     keep = r.md[block + i * spots + b].astype(BF16)
                     r.masked_cot[b * rows : (b + 1) * rows, :] = r.cot[...] * keep
@@ -301,29 +312,42 @@
     weights = {"w_gate": (w_gate, ANY), "w_up": (w_up, ANY), "w_down": (w_down, ANY)}
     weights = {k: (hbm(w), spec) for k, (w, spec) in weights.items()}
 
-    block = jnp.stack([tokens, grad_out])
+    across_shape = shape(width // BLK, 1, units, kind=F32)
+    along_shape = shape(units // BLK, 1, width, kind=F32)
+    masks = dict(zip(MASKS, (mask_gate, mask_up, mask_down.T)))
+    values = call(
+        first_kernel,
+        "first",
+        {
+            "w_down": weights["w_down"],
+            **{"hbm_" + k: (hbm(m), ANY) for k, m in masks.items()},
+            "tokens": (hbm(tokens), ANY),
+            "grad_out": (hbm(grad_out), ANY),
+        },
+        {
+            "block": pinned(shape(2, *tokens.shape)),
+            **{k: pinned(across_shape) for k in ("mg", "mu", "mdt")},
+            **{k: pinned(along_shape) for k in ("mgt", "mut", "md")},
+            "kd": pinned(shape(*w_down.shape)),
+        },
+        scratch={
+            **{k: pltpu.VMEM(m.shape, m.dtype) for k, m in masks.items()},
+            "sems": pltpu.SemaphoreType.DMA((SPLIT + len(masks) + 2,)),
+        },
+        vmem=grant(4),
+    )
+    block = values["block"]
     if direct:
         blocks = [block] + [trade(block, s) for s in range(1, n_grid)]
     else:
         blocks = [lax.all_gather(block, "grid", axis=1, tiled=True)]
-
-    across_shape = shape(width // BLK, 1, units, kind=F32)
-    along_shape = shape(units // BLK, 1, width, kind=F32)
-    masks = dict(zip(MASKS, (mask_gate, mask_up, mask_down.T)))
-    values = call(
+    values |= call(
         fetch_kernel,
         "fetch",
-        {**weights, **{"hbm_" + k: (hbm(m), ANY) for k, m in masks.items()}},
-        {
-            **{k: pinned(across_shape) for k in ("mg", "mu", "mdt")},
-            **{k: pinned(along_shape) for k in ("mgt", "mut", "md")},
-            **{k: pinned(shape(*w.shape)) for k, w in zip(KEPT, (w_gate, w_up, w_down))},
-        },
-        scratch={
-            **{k: pltpu.VMEM(m.shape, m.dtype) for k, m in masks.items()},
-            "sems": pltpu.SemaphoreType.DMA((3 * SPLIT + len(masks),)),
-        },
-        vmem=grant(4),
+        {"w_gate": weights["w_gate"], "w_up": weights["w_up"], "after": (values["mg"], ANY)},
+        {"kg": pinned(shape(*w_gate.shape)), "ku": pinned(shape(*w_up.shape))},
+        scratch={"sems": pltpu.SemaphoreType.DMA((2 * SPLIT,))},
+        vmem=grant(2),
     )
 
     pair = min(DEPTH, width) // BLK
@@ -332,7 +356,7 @@
         assemble_kernel,
         "assemble",
         {
-            "after": (values["mg"], ANY),
+            "after": (values["kg"], ANY),
             **{f"block{k}": (b, whole(b)) for k, b in reversed(list(enumerate(blocks)))},
         },
         {
@@ -413,12 +437,12 @@
         return {**state, **{k.replace("new_", ""): v for k, v in got.items()}}
 
     sent, sums, theirs, after = [], [], [], None
-    for p in range(n + 1):
-        if p < n:
+    for which, p in [(1, p) for p in range(n)] + [(0, p) for p in range(n)]:
+        if which == 1:
             after = partials(1, p, after)["send"]
             sent.append(swap(after))
-        if p > 0:
-            got = partials(0, p - 1, after, sent[p - 1])
+        else:
+            got = partials(0, p, after, sent[p])
             after = got["own"]
             sums.append(after)
             theirs.append(across(got["send"]))
@@ -428,10 +452,10 @@
         last = p == n - 1
         act = activate(sums[p], theirs[p], state.get("sums", after))
         act_other = swap(act)
-        state = back([(0, p, act)], True, not last, state)
+        state = back([(0, p, act)], True, True, state)
         state = back([(1, p, act_other)], True, not last, state, last)
         if last:
-            state = back([(0, p, act), (1, p, act_other)], False, True, state)
+            state = back([(1, p, act_other)], False, True, state)
 
     if direct:
         both = state["rows0"].astype(F32)

time: 60.3 us -> 62.9 us (1.043)
  waiting for transfers between devices: 3.56 us -> 6.21 us
  Pallas kernels: 38.8 us -> 39.7 us
  other arithmetic: 0.82 us -> 0.04 us
    ppermute x6, waiting for transfers between devices: 0.02 us -> 1.98 us  [trade(): return lax.ppermute(array, 'grid', [(i, i ^ s) for i in range(n_grid)])]
    pallas_call x18 -> x19, Pallas kernels: 38.8 us -> 39.7 us  [call(): pl.pallas_call(body, out_shape=[shape for shape, _ in outs.values()], in_...]
    another operation x1 -> x0, other arithmetic: 0.78 us -> none  [shards(): block = jnp.stack([tokens, grad_out])]
    ppermute x6, waiting for transfers between devices: 0.15 us -> 0.81 us  [swap(): return lax.ppermute(array, 'dp', [(i, i ^ 1) for i in range(n_dp)])]
  transfers between devices with their start and end apart: 15 -> 15, of which waited for: 2 -> 4; matrix products, arithmetic and copies ran while one was open for 0% -> 0% of each run, Pallas kernels for 60% -> 51%
where the time goes in v10:
time: 62.9 us; the launch traced here: 62.7 us
  Pallas kernels  39.7 us (63%)
  starting transfers between devices  15.3 us (24%)
  waiting for transfers between devices  6.21 us (10%)
  between operations  0.89 us (1%)
  local copies, waits for them, and re-layouts  0.63 us (1%)
    pallas_call x19, Pallas kernels, call(): pl.pallas_call(body, out_shape=[shape for shape, _ in outs.values()], in_...  39.7 us
    ppermute x6, starting transfers between devices, trade(): return lax.ppermute(array, 'grid', [(i, i ^ s) for i in range(n_grid)])  10.1 us
    ppermute x3, starting transfers between devices, across(): lax.ppermute(array, 'dp', [(i, (i // 2 + s) % pairs * 2 + i % 2) for i in...  3.76 us
    ppermute x3, waiting for transfers between devices, across(): lax.ppermute(array, 'dp', [(i, (i // 2 + s) % pairs * 2 + i % 2) for i in...  3.42 us
    ppermute x6, waiting for transfers between devices, trade(): return lax.ppermute(array, 'grid', [(i, i ^ s) for i in range(n_grid)])  1.98 us
    ppermute x6, starting transfers between devices, swap(): return lax.ppermute(array, 'dp', [(i, i ^ 1) for i in range(n_dp)])  1.42 us
  transfers between devices with their start and end apart: 15, of which 4 were waited for; matrix products, arithmetic and copies ran while one was open for 0% of the time, Pallas kernels for 51%

profile of v10, /device:TPU:0, one launch (start us, length us, event | category | flops | bytes accessed | tf_op | source)
XLA Modules:
  0.0 62.7 jit_solution(1905507944809514971)
XLA Ops:
  0.6 3.6 %first.1 = (bf16[2,16,1024]{2,1,0:T(8,128)(2,1)S(1)}, f32[8,1,4096]{2,1,0:T(1,128)S(1)}, f32[8,1,4096]{2,1,0:T(1,128)S(1)}, f32[8,1,4096]{2,1,0:T(1,128)S(1)}, f...) custom-call(bf16[4096,1024]{1,0:T(8,128)(2,1)} %refs_0_.2, ...), custom_call_target="tpu_custom_call" | custom-call | flops 1 | bytes 1 | tf_op jit(solution)/shard_map/first/pallas_call | solution.py:44
  4.3 3.1 %collective-permute-start.2 = (bf16[2,16,1024]{2,1,0:T(8,128)(2,1)S(1)}, bf16[2,16,1024]{2,1,0:T(8,128)(2,1)S(1)}, u32[]{:S(2)}, u32[]{:S(2)}) collective-permute-start(bf16[2,16,1024]{2,1,0:T(8,128)(2,1)S(1)} %get-tuple-element.54.refs_4_), channel_id=1, source_target_pairs={{0,4},{4,0},{8,12},{12,8},{1,5},{5,1},{9,13},{13,9},{2,6},{6,2},{1... | collective-permute-start | bytes 196616 | tf_op jit(solution)/shard_map/ppermute | solution.py:294
  7.4 2.6 %collective-permute-start.1 = (bf16[2,16,1024]{2,1,0:T(8,128)(2,1)S(1)}, bf16[2,16,1024]{2,1,0:T(8,128)(2,1)S(1)}, u32[]{:S(2)}, u32[]{:S(2)}) collective-permute-start(bf16[2,16,1024]{2,1,0:T(8,128)(2,1)S(1)} %get-tuple-element.54.refs_4_), channel_id=1, source_target_pairs={{0,8},{4,12},{8,0},{12,4},{1,9},{5,13},{9,1},{13,5},{2,10},{6,14},... | collective-permute-start | bytes 196616 | tf_op jit(solution)/shard_map/ppermute | solution.py:294
  9.9 0.0 collective-permute-start
  9.9 5.9 %fetch.1 = (bf16[1024,4096]{1,0:T(8,128)(2,1)S(1)}, bf16[1024,4096]{1,0:T(8,128)(2,1)S(1)}) custom-call(bf16[1024,4096]{1,0:T(8,128)(2,1)} %refs_0_.3, bf16[1024,4096]{1,0:T(8,128)(2,1)} %refs_1_.3, f32[8,1,4096]{2,1,0:T(1,128)S(1)} %get-tuple-element.52.refs_2_.refs_9_.refs_10_.refs_4_), custom_call_target="tpu_custom_call" | custom-call | flops 1 | bytes 1 | tf_op jit(solution)/shard_map/fetch/pallas_call | solution.py:44
  15.9 0.0 collective-permute-done.2.refs_3_
  15.9 0.0 collective-permute-done.1.refs_2_
  15.9 0.1 collective-permute-done.refs_1_
  16.0 0.2 assemble.1
  16.2 0.8 %partials.6.refs_8_ = f32[3,64,512]{2,1,0:T(8,128)S(1)} custom-call(bf16[4,128,256]{2,1,0:T(8,128)(2,1)S(1)} %get-tuple-element.55.refs_0_, bf16[4,128,256]{2,1,0:T(8,128)(2,1)S(1)} %get-tuple-element.56.refs_1_, f32[8,1,4096]{2,1,0:T(1,128)S(1)} %get-tuple-element.52.refs_2_.refs_9_.refs_10_.refs_4_, ...), custom_call_target="tpu_custom_call" | custom-call | flops 1 | bytes 1 | tf_op jit(solution)/shard_map/partials/pallas_call | solution.py:44
  17.0 1.1 %partials.7.refs_8_ = f32[3,64,768]{2,1,0:T(8,128)S(1)} custom-call(bf16[4,128,256]{2,1,0:T(8,128)(2,1)S(1)} %get-tuple-element.55.refs_0_, bf16[4,128,256]{2,1,0:T(8,128)(2,1)S(1)} %get-tuple-element.56.refs_1_, f32[8,1,4096]{2,1,0:T(1,128)S(1)} %get-tuple-element.52.refs_2_.refs_9_.refs_10_.refs_4_, ...), custom_call_target="tpu_custom_call" | custom-call | flops 1 | bytes 1 | tf_op jit(solution)/shard_map/partials/pallas_call | solution.py:44
  18.1 0.1 collective-permute-start.4
  18.2 0.5 collective-permute-start.3
  18.7 1.1 %partials.8.refs_8_ = f32[3,64,768]{2,1,0:T(8,128)S(1)} custom-call(bf16[4,128,256]{2,1,0:T(8,128)(2,1)S(1)} %get-tuple-element.55.refs_0_, bf16[4,128,256]{2,1,0:T(8,128)(2,1)S(1)} %get-tuple-element.56.refs_1_, f32[8,1,4096]{2,1,0:T(1,128)S(1)} %get-tuple-element.52.refs_2_.refs_9_.refs_10_.refs_4_, ...), custom_call_target="tpu_custom_call" | custom-call | flops 1 | bytes 1 | tf_op jit(solution)/shard_map/partials/pallas_call | solution.py:44
  19.8 0.1 collective-permute-start.5
  19.9 0.8 %collective-permute-done.3.refs_9_ = f32[3,64,512]{2,1,0:T(8,128)S(1)} collective-permute-done((f32[3,64,512]{2,1,0:T(8,128)S(1)}, f32[3,64,512]{2,1,0:T(8,128)S(1)}, u32[]{:S(2)}, u32[]{:S(2)}) %collective-permute-start.3) | collective-permute-done | bytes 393248 | tf_op jit(solution)/shard_map/ppermute | solution.py:297
  20.7 0.8 %partials.9 = (f32[3,64,512]{2,1,0:T(8,128)S(1)}, bf16[3,64,512]{2,1,0:T(8,128)(2,1)S(1)}) custom-call(bf16[4,128,256]{2,1,0:T(8,128)(2,1)S(1)} %get-tuple-element.55.refs_0_, bf16[4,128,256]{2,1,0:T(8,128)(2,1)S(1)} %get-tuple-element.56.refs_1_, f32[8,1,4096]{2,1,0:T(1,128)S(1)} %get-tuple-element.52.refs_2_.refs_9_.refs_10_.refs_4_, ...), custom_call_target="tpu_custom_call" | custom-call | flops 1 | bytes 1 | tf_op jit(solution)/shard_map/partials/pallas_call | solution.py:44
  21.5 1.7 %collective-permute-start.6 = (bf16[3,64,512]{2,1,0:T(8,128)(2,1)S(1)}, bf16[3,64,512]{2,1,0:T(8,128)(2,1)S(1)}, u32[]{:S(2)}, u32[]{:S(2)}) collective-permute-start(bf16[3,64,512]{2,1,0:T(8,128)(2,1)S(1)} %get-tuple-element.64), channel_id=1, source_target_pairs={{0,2},{1,3},{2,0},{3,1},{4,6},{5,7},{6,4},{7,5},{8,10},{9,11},{10,... | collective-permute-start | bytes 589832 | tf_op jit(solution)/shard_map/ppermute | solution.py:301
  23.2 0.0 collective-permute-done.4.refs_9_
  23.2 1.1 %partials.10 = (f32[3,64,768]{2,1,0:T(8,128)S(1)}, bf16[3,64,768]{2,1,0:T(8,128)(2,1)S(1)}) custom-call(bf16[4,128,256]{2,1,0:T(8,128)(2,1)S(1)} %get-tuple-element.55.refs_0_, bf16[4,128,256]{2,1,0:T(8,128)(2,1)S(1)} %get-tuple-element.56.refs_1_, f32[8,1,4096]{2,1,0:T(1,128)S(1)} %get-tuple-element.52.refs_2_.refs_9_.refs_10_.refs_4_, ...), custom_call_target="tpu_custom_call" | custom-call | flops 1 | bytes 1 | tf_op jit(solution)/shard_map/partials/pallas_call | solution.py:44
  24.3 0.5 collective-permute-start.8
  24.8 0.0 collective-permute-done.5.refs_9_
  24.8 1.1 %partials.11 = (f32[3,64,768]{2,1,0:T(8,128)S(1)}, bf16[3,64,768]{2,1,0:T(8,128)(2,1)S(1)}) custom-call(bf16[4,128,256]{2,1,0:T(8,128)(2,1)S(1)} %get-tuple-element.55.refs_0_, bf16[4,128,256]{2,1,0:T(8,128)(2,1)S(1)} %get-tuple-element.56.refs_1_, f32[8,1,4096]{2,1,0:T(1,128)S(1)} %get-tuple-element.52.refs_2_.refs_9_.refs_10_.refs_4_, ...), custom_call_target="tpu_custom_call" | custom-call | flops 1 | bytes 1 | tf_op jit(solution)/shard_map/partials/pallas_call | solution.py:44
  25.9 3.4 %collective-permute-done.6.refs_2_ = bf16[3,64,512]{2,1,0:T(8,128)(2,1)S(1)} collective-permute-done((bf16[3,64,512]{2,1,0:T(8,128)(2,1)S(1)}, bf16[3,64,512]{2,1,0:T(8,128)(2,1)S(1)}, u32[]{:S(2)}, u32[]{:S(2)}) %collective-permute-start.6) | collective-permute-done | bytes 196640 | tf_op jit(solution)/shard_map/ppermute | solution.py:301
  29.3 0.1 activate.3.refs_0_
  29.4 0.1 collective-permute-start.7
  29.5 3.0 %back_rows_grads.5 = (f32[2,64,1024]{2,1,0:T(8,128)S(1)}, f32[1024,4096]{1,0:T(8,128)}, f32[1024,4096]{1,0:T(8,128)}, f32[4096,1024]{1,0:T(8,128)}) custom-call(bf16[3,64,512]{2,1,0:T(8,128)(2,1)S(1)} %activate.3.refs_0_, f32[32,1,1024]{2,1,0:T(1,128)S(1)} %get-tuple-element.65.refs_1_, f32[32,1,1024]{2,1,0:T(1,128)S(1)} %get-tuple-element.66.refs_2_, ...), custom_call_target="tpu_custom_call" | custom-call | flops 1 | bytes 1 | tf_op jit(solution)/shard_map/back_rows_grads/pallas_call | solution.py:44
  32.6 0.0 collective-permute-done.7.refs_0_
  32.6 3.0 %back_rows_grads.6 = (f32[2,64,1024]{2,1,0:T(8,128)S(1)}, f32[1024,4096]{1,0:T(8,128)}, f32[1024,4096]{1,0:T(8,128)}, f32[4096,1024]{1,0:T(8,128)}) custom-call(bf16[3,64,512]{2,1,0:T(8,128)(2,1)S(1)} %collective-permute-done.7.refs_0_, f32[32,1,1024]{2,1,0:T(1,128)S(1)} %get-tuple-element.65.refs_1_, ...), custom_call_target="tpu_custom_call", output_to_operand_aliasing={{1}: (12, {}), {2}: (13, {}), {3}: (14, {})} | custom-call | flops 1 | bytes 1 | tf_op jit(solution)/shard_map/back_rows_grads/pallas_call | solution.py:44
  35.6 0.0 collective-permute-done.8.refs_2_
  35.6 0.1 activate.4.refs_0_
  35.8 0.6 collective-permute-start.9
  36.3 1.6 %collective-permute-start.10 = (bf16[3,64,768]{2,1,0:T(8,128)(2,1)S(1)}, bf16[3,64,768]{2,1,0:T(8,128)(2,1)S(1)}, u32[]{:S(2)}, u32[]{:S(2)}) collective-permute-start(bf16[3,64,768]{2,1,0:T(8,128)(2,1)S(1)} %get-tuple-element.84), channel_id=1, source_target_pairs={{0,2},{1,3},{2,0},{3,1},{4,6},{5,7},{6,4},{7,5},{8,10},{9,11},{10,... | collective-permute-start | bytes 884744 | tf_op jit(solution)/shard_map/ppermute | solution.py:301
  37.9 4.0 %back_rows_grads.7 = (f32[2,64,1024]{2,1,0:T(8,128)S(1)}, f32[1024,4096]{1,0:T(8,128)}, f32[1024,4096]{1,0:T(8,128)}, f32[4096,1024]{1,0:T(8,128)}) custom-call(bf16[3,64,768]{2,1,0:T(8,128)(2,1)S(1)} %activate.4.refs_0_, f32[32,1,1024]{2,1,0:T(1,128)S(1)} %get-tuple-element.65.refs_1_, ...), custom_call_target="tpu_custom_call", output_to_operand_aliasing={{1}: (12, {}), {2}: (13, {}), {3}: (14, {})} | custom-call | flops 1 | bytes 1 | tf_op jit(solution)/shard_map/back_rows_grads/pallas_call | solution.py:44
  41.9 0.0 collective-permute-done.9.refs_0_
  41.9 4.0 %back_rows_grads.8 = (f32[2,64,1024]{2,1,0:T(8,128)S(1)}, f32[1024,4096]{1,0:T(8,128)}, f32[1024,4096]{1,0:T(8,128)}, f32[4096,1024]{1,0:T(8,128)}) custom-call(bf16[3,64,768]{2,1,0:T(8,128)(2,1)S(1)} %collective-permute-done.9.refs_0_, f32[32,1,1024]{2,1,0:T(1,128)S(1)} %get-tuple-element.65.refs_1_, ...), custom_call_target="tpu_custom_call", output_to_operand_aliasing={{1}: (12, {}), {2}: (13, {}), {3}: (14, {})} | custom-call | flops 1 | bytes 1 | tf_op jit(solution)/shard_map/back_rows_grads/pallas_call | solution.py:44
  46.0 0.0 collective-permute-done.10.refs_2_
  46.0 0.1 activate.5.refs_0_
  46.1 0.1 collective-permute-start.11
  46.2 4.0 %back_rows_grads.9 = (f32[2,64,1024]{2,1,0:T(8,128)S(1)}, f32[1024,4096]{1,0:T(8,128)}, f32[1024,4096]{1,0:T(8,128)}, f32[4096,1024]{1,0:T(8,128)}) custom-call(bf16[3,64,768]{2,1,0:T(8,128)(2,1)S(1)} %activate.5.refs_0_, f32[32,1,1024]{2,1,0:T(1,128)S(1)} %get-tuple-element.65.refs_1_, ...), custom_call_target="tpu_custom_call", output_to_operand_aliasing={{1}: (12, {}), {2}: (13, {}), {3}: (14, {})} | custom-call | flops 1 | bytes 1 | tf_op jit(solution)/shard_map/back_rows_grads/pallas_call | solution.py:44
  50.2 0.0 collective-permute-done.11.refs_0_
  50.2 1.5 %back_rows.1 = (bf16[2,16,1024]{2,1,0:T(8,128)(2,1)S(1)}, bf16[2,16,1024]{2,1,0:T(8,128)(2,1)S(1)}, bf16[2,16,1024]{2,1,0:T(8,128)(2,1)S(1)}, bf16[2,16,1024]{2,1,0:T(8,128)(2,1)S(1)}) custom-call(bf16[3,64,768]{2,1,0:T(8,128)(2,1)S(1)} %collective-permute-done.11.refs_0_, f32[32,1,1024]{2,1,0:T(1,128)S(1)} %get-tuple-element.65.refs_1_, ...), custom_call_target="tpu_custom_call" | custom-call | flops 1 | bytes 1 | tf_op jit(solution)/shard_map/back_rows/pallas_call | solution.py:44
  51.7 0.7 %collective-permute-start.12 = (bf16[2,16,1024]{2,1,0:T(8,128)(2,1)S(1)}, bf16[2,16,1024]{2,1,0:T(8,128)(2,1)S(1)}, u32[]{:S(2)}, u32[]{:S(2)}) collective-permute-start(bf16[2,16,1024]{2,1,0:T(8,128)(2,1)S(1)} %get-tuple-element.90), channel_id=1, source_target_pairs={{0,4},{4,0},{8,12},{12,8},{1,5},{5,1},{9,13},{13,9},{2,6},{6,2},{1... | collective-permute-start | bytes 196616 | tf_op jit(solution)/shard_map/ppermute | solution.py:294
  52.5 3.5 %collective-permute-start.13 = (bf16[2,16,1024]{2,1,0:T(8,128)(2,1)S(1)}, bf16[2,16,1024]{2,1,0:T(8,128)(2,1)S(1)}, u32[]{:S(2)}, u32[]{:S(2)}) collective-permute-start(bf16[2,16,1024]{2,1,0:T(8,128)(2,1)S(1)} %get-tuple-element.91), channel_id=1, source_target_pairs={{0,8},{4,12},{8,0},{12,4},{1,9},{5,13},{9,1},{13,5},{2,10},{6,14},... | collective-permute-start | bytes 196616 | tf_op jit(solution)/shard_map/ppermute | solution.py:294
  55.9 0.2 collective-permute-start.14
  56.2 4.0 %back_grads.1 = (f32[1024,4096]{1,0:T(8,128)}, f32[1024,4096]{1,0:T(8,128)}, f32[4096,1024]{1,0:T(8,128)}) custom-call(bf16[3,64,768]{2,1,0:T(8,128)(2,1)S(1)} %collective-permute-done.11.refs_0_, f32[32,1,1024]{2,1,0:T(1,128)S(1)} %get-tuple-element.65.refs_1_, ...), custom_call_target="tpu_custom_call", output_to_operand_aliasing={{0}: (6, {}), {1}: (7, {}), {2}: (8, {})} | custom-call | flops 1 | bytes 1 | tf_op jit(solution)/shard_map/back_grads/pallas_call | solution.py:44
  60.2 0.0 collective-permute-done.12
  60.2 0.0 collective-permute-done.13
  60.2 1.8 %collective-permute-done.14 = bf16[2,16,1024]{2,1,0:T(8,128)(2,1)S(1)} collective-permute-done((bf16[2,16,1024]{2,1,0:T(8,128)(2,1)S(1)}, bf16[2,16,1024]{2,1,0:T(8,128)(2,1)S(1)}, u32[]{:S(2)}, u32[]{:S(2)}) %collective-permute-start.14) | collective-permute-done | bytes 65568 | tf_op jit(solution)/shard_map/ppermute | solution.py:294
  62.1 0.6 %slice_bitcast_fusion = (bf16[16,1024]{1,0:T(8,128)(2,1)}, bf16[16,1024]{1,0:T(8,128)(2,1)}) fusion(bf16[2,16,1024]{2,1,0:T(8,128)(2,1)S(1)} %add_convert_fusion), kind=kLoop, calls=%fused_computation.1 | loop fusion | bytes 131072 | tf_op jit(solution)/shard_map/squeeze | solution.py:467
  (1 shorter events, 0.0 us)
Async XLA Ops:
  4.3 11.6 %collective-permute-start.2 = (bf16[2,16,1024]{2,1,0:T(8,128)(2,1)S(1)}, bf16[2,16,1024]{2,1,0:T(8,128)(2,1)S(1)}, u32[]{:S(2)}, u32[]{:S(2)}) collective-permute-start(bf16[2,16,1024]{2,1,0:T(8,128)(2,1)S(1)} %get-tuple-element.54.refs_4_), channel_id=1, source_target_pairs={{0,4},{4,0},{8,12},{12,8},{1,5},{5,1},{9,13},{13,9},{2,6},{6,2},{1... | collective-permute-start | bytes 196616 | tf_op jit(solution)/shard_map/ppermute | solution.py:294
  7.4 8.5 %collective-permute-start.1 = (bf16[2,16,1024]{2,1,0:T(8,128)(2,1)S(1)}, bf16[2,16,1024]{2,1,0:T(8,128)(2,1)S(1)}, u32[]{:S(2)}, u32[]{:S(2)}) collective-permute-start(bf16[2,16,1024]{2,1,0:T(8,128)(2,1)S(1)} %get-tuple-element.54.refs_4_), channel_id=1, source_target_pairs={{0,8},{4,12},{8,0},{12,4},{1,9},{5,13},{9,1},{13,5},{2,10},{6,14},... | collective-permute-start | bytes 196616 | tf_op jit(solution)/shard_map/ppermute | solution.py:294
  9.9 6.1 %collective-permute-start = (bf16[2,16,1024]{2,1,0:T(8,128)(2,1)S(1)}, bf16[2,16,1024]{2,1,0:T(8,128)(2,1)S(1)}, u32[]{:S(2)}, u32[]{:S(2)}) collective-permute-start(bf16[2,16,1024]{2,1,0:T(8,128)(2,1)S(1)} %get-tuple-element.54.refs_4_), channel_id=1, source_target_pairs={{0,12},{4,8},{8,4},{12,0},{1,13},{5,9},{9,5},{13,1},{2,14},{6,10},... | collective-permute-start | bytes 196616 | tf_op jit(solution)/shard_map/ppermute | solution.py:294
  18.1 5.1 %collective-permute-start.4 = (f32[3,64,768]{2,1,0:T(8,128)S(1)}, f32[3,64,768]{2,1,0:T(8,128)S(1)}, u32[]{:S(2)}, u32[]{:S(2)}) collective-permute-start(f32[3,64,768]{2,1,0:T(8,128)S(1)} %partials.7.refs_8_), channel_id=1, source_target_pairs={{0,1},{1,0},{2,3},{3,2},{4,5},{5,4},{6,7},{7,6},{8,9},{9,8},{10,11... | collective-permute-start | bytes 1769480 | tf_op jit(solution)/shard_map/ppermute | solution.py:297
  18.2 2.6 %collective-permute-start.3 = (f32[3,64,512]{2,1,0:T(8,128)S(1)}, f32[3,64,512]{2,1,0:T(8,128)S(1)}, u32[]{:S(2)}, u32[]{:S(2)}) collective-permute-start(f32[3,64,512]{2,1,0:T(8,128)S(1)} %partials.6.refs_8_), channel_id=1, source_target_pairs={{0,1},{1,0},{2,3},{3,2},{4,5},{5,4},{6,7},{7,6},{8,9},{9,8},{10,11... | collective-permute-start | bytes 1179656 | tf_op jit(solution)/shard_map/ppermute | solution.py:297
  19.8 5.0 %collective-permute-start.5 = (f32[3,64,768]{2,1,0:T(8,128)S(1)}, f32[3,64,768]{2,1,0:T(8,128)S(1)}, u32[]{:S(2)}, u32[]{:S(2)}) collective-permute-start(f32[3,64,768]{2,1,0:T(8,128)S(1)} %partials.8.refs_8_), channel_id=1, source_target_pairs={{0,1},{1,0},{2,3},{3,2},{4,5},{5,4},{6,7},{7,6},{8,9},{9,8},{10,11... | collective-permute-start | bytes 1769480 | tf_op jit(solution)/shard_map/ppermute | solution.py:297
  21.5 7.8 %collective-permute-start.6 = (bf16[3,64,512]{2,1,0:T(8,128)(2,1)S(1)}, bf16[3,64,512]{2,1,0:T(8,128)(2,1)S(1)}, u32[]{:S(2)}, u32[]{:S(2)}) collective-permute-start(bf16[3,64,512]{2,1,0:T(8,128)(2,1)S(1)} %get-tuple-element.64), channel_id=1, source_target_pairs={{0,2},{1,3},{2,0},{3,1},{4,6},{5,7},{6,4},{7,5},{8,10},{9,11},{10,... | collective-permute-start | bytes 589832 | tf_op jit(solution)/shard_map/ppermute | solution.py:301
  24.3 11.3 %collective-permute-start.8 = (bf16[3,64,768]{2,1,0:T(8,128)(2,1)S(1)}, bf16[3,64,768]{2,1,0:T(8,128)(2,1)S(1)}, u32[]{:S(2)}, u32[]{:S(2)}) collective-permute-start(bf16[3,64,768]{2,1,0:T(8,128)(2,1)S(1)} %get-tuple-element.75), channel_id=1, source_target_pairs={{0,2},{1,3},{2,0},{3,1},{4,6},{5,7},{6,4},{7,5},{8,10},{9,11},{10,... | collective-permute-start | bytes 884744 | tf_op jit(solution)/shard_map/ppermute | solution.py:301
  29.4 3.1 %collective-permute-start.7 = (bf16[3,64,512]{2,1,0:T(8,128)(2,1)S(1)}, bf16[3,64,512]{2,1,0:T(8,128)(2,1)S(1)}, u32[]{:S(2)}, u32[]{:S(2)}) collective-permute-start(bf16[3,64,512]{2,1,0:T(8,128)(2,1)S(1)} %activate.3.refs_0_), channel_id=1, source_target_pairs={{0,1},{1,0},{2,3},{3,2},{4,5},{5,4},{6,7},{7,6},{8,9},{9,8},{10,11... | collective-permute-start | bytes 589832 | tf_op jit(solution)/shard_map/ppermute | solution.py:297
  35.8 6.2 %collective-permute-start.9 = (bf16[3,64,768]{2,1,0:T(8,128)(2,1)S(1)}, bf16[3,64,768]{2,1,0:T(8,128)(2,1)S(1)}, u32[]{:S(2)}, u32[]{:S(2)}) collective-permute-start(bf16[3,64,768]{2,1,0:T(8,128)(2,1)S(1)} %activate.4.refs_0_), channel_id=1, source_target_pairs={{0,1},{1,0},{2,3},{3,2},{4,5},{5,4},{6,7},{7,6},{8,9},{9,8},{10,11... | collective-permute-start | bytes 884744 | tf_op jit(solution)/shard_map/ppermute | solution.py:297
  36.3 9.7 %collective-permute-start.10 = (bf16[3,64,768]{2,1,0:T(8,128)(2,1)S(1)}, bf16[3,64,768]{2,1,0:T(8,128)(2,1)S(1)}, u32[]{:S(2)}, u32[]{:S(2)}) collective-permute-start(bf16[3,64,768]{2,1,0:T(8,128)(2,1)S(1)} %get-tuple-element.84), channel_id=1, source_target_pairs={{0,2},{1,3},{2,0},{3,1},{4,6},{5,7},{6,4},{7,5},{8,10},{9,11},{10,... | collective-permute-start | bytes 884744 | tf_op jit(solution)/shard_map/ppermute | solution.py:301
  46.1 4.1 %collective-permute-start.11 = (bf16[3,64,768]{2,1,0:T(8,128)(2,1)S(1)}, bf16[3,64,768]{2,1,0:T(8,128)(2,1)S(1)}, u32[]{:S(2)}, u32[]{:S(2)}) collective-permute-start(bf16[3,64,768]{2,1,0:T(8,128)(2,1)S(1)} %activate.5.refs_0_), channel_id=1, source_target_pairs={{0,1},{1,0},{2,3},{3,2},{4,5},{5,4},{6,7},{7,6},{8,9},{9,8},{10,11... | collective-permute-start | bytes 884744 | tf_op jit(solution)/shard_map/ppermute | solution.py:297
  51.7 8.5 %collective-permute-start.12 = (bf16[2,16,1024]{2,1,0:T(8,128)(2,1)S(1)}, bf16[2,16,1024]{2,1,0:T(8,128)(2,1)S(1)}, u32[]{:S(2)}, u32[]{:S(2)}) collective-permute-start(bf16[2,16,1024]{2,1,0:T(8,128)(2,1)S(1)} %get-tuple-element.90), channel_id=1, source_target_pairs={{0,4},{4,0},{8,12},{12,8},{1,5},{5,1},{9,13},{13,9},{2,6},{6,2},{1... | collective-permute-start | bytes 196616 | tf_op jit(solution)/shard_map/ppermute | solution.py:294
  52.5 7.8 %collective-permute-start.13 = (bf16[2,16,1024]{2,1,0:T(8,128)(2,1)S(1)}, bf16[2,16,1024]{2,1,0:T(8,128)(2,1)S(1)}, u32[]{:S(2)}, u32[]{:S(2)}) collective-permute-start(bf16[2,16,1024]{2,1,0:T(8,128)(2,1)S(1)} %get-tuple-element.91), channel_id=1, source_target_pairs={{0,8},{4,12},{8,0},{12,4},{1,9},{5,13},{9,1},{13,5},{2,10},{6,14},... | collective-permute-start | bytes 196616 | tf_op jit(solution)/shard_map/ppermute | solution.py:294
  55.9 6.1 %collective-permute-start.14 = (bf16[2,16,1024]{2,1,0:T(8,128)(2,1)S(1)}, bf16[2,16,1024]{2,1,0:T(8,128)(2,1)S(1)}, u32[]{:S(2)}, u32[]{:S(2)}) collective-permute-start(bf16[2,16,1024]{2,1,0:T(8,128)(2,1)S(1)} %get-tuple-element.92), channel_id=1, source_target_pairs={{0,12},{4,8},{8,4},{12,0},{1,13},{5,9},{9,5},{13,1},{2,14},{6,10},... | collective-permute-start | bytes 196616 | tf_op jit(solution)/shard_map/ppermute | solution.py:294

commit v11 on v9

--- a/solution.py
+++ b/solution.py
@@ -220,7 +220,6 @@
 def back_kernel(items, half, do_rows, do_grads, r):
     tile = r.act_d.shape[3]
     spots = tile // BLK
-    r.act_d[...] = jnp.zeros_like(r.act_d)
     if do_rows:
         r.acc[...] = r.sums[...] if hasattr(r, "sums") else jnp.zeros_like(r.acc)
     if do_grads:
@@ -232,19 +231,20 @@
         base = first_unit(which, half) + start
         at, block = span(base, size), lax.div(base, BLK)
         tiles = [slice(i * tile, (i + 1) * tile) for i in range(size // tile)]
+        for i in range(groups if do_grads else 0):
+            band = slice(i * height, (i + 1) * height)
+            for out, k, mask in ((r.gg, 1, r.mg), (r.gu, 2, r.mu)):
+                right = r.masked_act.at[k - 1]
+                for j in range(height // BLK):
+                    keep = mask[i * (height // BLK) + j, :, at].astype(BF16)
+                    right[j * rows : (j + 1) * rows, :] = act[k] * keep
+                by_cols.put(dot(r.tok_t[i], right[...]), out.at[band, at])
+        if act is r.act0:
+            r.act_d[...] = jnp.zeros_like(r.act_d)
         for i, local in enumerate(tiles):
             for k in range(3 if do_rows else 1):
                 diagonal(r.act_d.at[i, k], act[k, :, local])
-        for i in range(max(groups, len(tiles)) if do_grads else 0):
-            if i < groups:
-                band = slice(i * height, (i + 1) * height)
-                for out, k, mask in ((r.gg, 1, r.mg), (r.gu, 2, r.mu)):
-                    right = r.masked_act.at[k - 1]
-                    for j in range(height // BLK):
-                        keep = mask[i * (height // BLK) + j, :, at].astype(BF16)
-                        right[j * rows : (j + 1) * rows, :] = act[k] * keep
-                    by_cols.put(dot(r.tok_t[i], right[...]), out.at[band, at])
-            if i < len(tiles):
+            if do_grads:
                 for b in range(spots):
                     keep = r.md[block + i * spots + b].astype(BF16)
                     r.masked_cot[b * rows : (b + 1) * rows, :] = r.cot[...] * keep
@@ -428,10 +428,13 @@
         last = p == n - 1
         act = activate(sums[p], theirs[p], state.get("sums", after))
         act_other = swap(act)
-        state = back([(0, p, act)], True, not last, state)
-        state = back([(1, p, act_other)], True, not last, state, last)
+        both_halves = [(0, p, act), (1, p, act_other)]
         if last:
-            state = back([(0, p, act), (1, p, act_other)], False, True, state)
+            state = back(both_halves[:1], True, False, state)
+            state = back(both_halves[1:], True, False, state, last)
+            state = back(both_halves, False, True, state)
+        else:
+            state = back(both_halves, True, True, state)
 
     if direct:
         both = state["rows0"].astype(F32)

time: 60.3 us -> 61 us (1.012)
  waiting for transfers between devices: 3.56 us -> 4.91 us
    ppermute x6, waiting for transfers between devices: 0.15 us -> 1.51 us  [swap(): return lax.ppermute(array, 'dp', [(i, i ^ 1) for i in range(n_dp)])]
    pallas_call x18 -> x16, Pallas kernels: 38.8 us -> 38.4 us  [call(): pl.pallas_call(body, out_shape=[shape for shape, _ in outs.values()], in_...]
  transfers between devices with their start and end apart: 15 -> 15, of which waited for: 2 -> 2; matrix products, arithmetic and copies ran while one was open for 0% -> 0% of each run, Pallas kernels for 60% -> 59%
where the time goes in v11:
time: 61 us; the launch traced here: 60.8 us
  Pallas kernels  38.4 us (63%)
  starting transfers between devices  15.2 us (25%)
  waiting for transfers between devices  4.91 us (8%)
  between operations  0.85 us (1%)
  other arithmetic  0.82 us (1%)
  local copies, waits for them, and re-layouts  0.63 us (1%)
    pallas_call x16, Pallas kernels, call(): pl.pallas_call(body, out_shape=[shape for shape, _ in outs.values()], in_...  38.4 us
    ppermute x6, starting transfers between devices, trade(): return lax.ppermute(array, 'grid', [(i, i ^ s) for i in range(n_grid)])  10.1 us
    ppermute x3, starting transfers between devices, across(): lax.ppermute(array, 'dp', [(i, (i // 2 + s) % pairs * 2 + i % 2) for i in...  3.84 us
    ppermute x3, waiting for transfers between devices, across(): lax.ppermute(array, 'dp', [(i, (i // 2 + s) % pairs * 2 + i % 2) for i in...  3.39 us
    ppermute x6, waiting for transfers between devices, swap(): return lax.ppermute(array, 'dp', [(i, i ^ 1) for i in range(n_dp)])  1.51 us
    ppermute x6, starting transfers between devices, swap(): return lax.ppermute(array, 'dp', [(i, i ^ 1) for i in range(n_dp)])  1.24 us
  transfers between devices with their start and end apart: 15, of which 2 were waited for; matrix products, arithmetic and copies ran while one was open for 0% of the time, Pallas kernels for 59%

profile of v11, /device:TPU:0, one launch (start us, length us, event | category | flops | bytes accessed | tf_op | source)
XLA Modules:
  0.0 60.8 jit_solution(7245031190482780293)
XLA Ops:
  0.6 0.8 %pad_maximum_fusion.refs_4_ = bf16[2,16,1024]{2,1,0:T(8,128)(2,1)S(1)} fusion(bf16[1,16,1024]{2,1,0:T(8,128)(2,1)} %bitcast.7, bf16[1,16,1024]{2,1,0:T(8,128)(2,1)} %bitcast.8), kind=kLoop, calls=%fused_computation.1 | loop fusion | flops 32768 | bytes 131072 | tf_op jit(solution)/shard_map/stack | solution.py:304
  1.4 3.1 %collective-permute-start.2 = (bf16[2,16,1024]{2,1,0:T(8,128)(2,1)S(1)}, bf16[2,16,1024]{2,1,0:T(8,128)(2,1)S(1)}, u32[]{:S(2)}, u32[]{:S(2)}) collective-permute-start(bf16[2,16,1024]{2,1,0:T(8,128)(2,1)S(1)} %pad_maximum_fusion.refs_4_), channel_id=1, source_target_pairs={{0,4},{4,0},{8,12},{12,8},{1,5},{5,1},{9,13},{13,9},{2,6},{6,2},{1... | collective-permute-start | bytes 196616 | tf_op jit(solution)/shard_map/ppermute | solution.py:283
  4.5 2.6 %collective-permute-start.1 = (bf16[2,16,1024]{2,1,0:T(8,128)(2,1)S(1)}, bf16[2,16,1024]{2,1,0:T(8,128)(2,1)S(1)}, u32[]{:S(2)}, u32[]{:S(2)}) collective-permute-start(bf16[2,16,1024]{2,1,0:T(8,128)(2,1)S(1)} %pad_maximum_fusion.refs_4_), channel_id=1, source_target_pairs={{0,8},{4,12},{8,0},{12,4},{1,9},{5,13},{9,1},{13,5},{2,10},{6,14},... | collective-permute-start | bytes 196616 | tf_op jit(solution)/shard_map/ppermute | solution.py:283
  7.1 0.0 collective-permute-start
  7.1 8.4 %fetch.1 = (f32[8,1,4096]{2,1,0:T(1,128)S(1)}, f32[8,1,4096]{2,1,0:T(1,128)S(1)}, f32[8,1,4096]{2,1,0:T(1,128)S(1)}, f32[32,1,1024]{2,1,0:T(1,128)S(1)}, f32[32,...) custom-call(bf16[1024,4096]{1,0:T(8,128)(2,1)} %refs_0_.1, ...), custom_call_target="tpu_custom_call" | custom-call | flops 1 | bytes 1 | tf_op jit(solution)/shard_map/fetch/pallas_call | solution.py:44
  15.5 0.0 collective-permute-done.2.refs_3_
  15.5 0.0 collective-permute-done.1.refs_2_
  15.5 0.0 collective-permute-done.refs_1_
  15.5 0.2 assemble.1
  15.7 0.8 %partials.6.refs_8_ = f32[3,64,512]{2,1,0:T(8,128)S(1)} custom-call(bf16[4,128,256]{2,1,0:T(8,128)(2,1)S(1)} %get-tuple-element.40.refs_0_, bf16[4,128,256]{2,1,0:T(8,128)(2,1)S(1)} %get-tuple-element.41.refs_1_, f32[8,1,4096]{2,1,0:T(1,128)S(1)} %get-tuple-element.39.refs_0_.refs_2_.refs_10_.refs_11_.refs_5_, ...), custom_call_target="tpu_custom_call" | custom-call | flops 1 | bytes 1 | tf_op jit(solution)/shard_map/partials/pallas_call | solution.py:44
  16.5 0.1 collective-permute-start.3
  16.6 1.1 %partials.7.refs_8_ = f32[3,64,768]{2,1,0:T(8,128)S(1)} custom-call(bf16[4,128,256]{2,1,0:T(8,128)(2,1)S(1)} %get-tuple-element.40.refs_0_, bf16[4,128,256]{2,1,0:T(8,128)(2,1)S(1)} %get-tuple-element.41.refs_1_, f32[8,1,4096]{2,1,0:T(1,128)S(1)} %get-tuple-element.39.refs_0_.refs_2_.refs_10_.refs_11_.refs_5_, ...), custom_call_target="tpu_custom_call" | custom-call | flops 1 | bytes 1 | tf_op jit(solution)/shard_map/partials/pallas_call | solution.py:44
  17.7 0.5 collective-permute-start.4
  18.2 0.0 collective-permute-done.3.refs_9_
  18.3 0.8 %partials.8 = (f32[3,64,512]{2,1,0:T(8,128)S(1)}, bf16[3,64,512]{2,1,0:T(8,128)(2,1)S(1)}) custom-call(bf16[4,128,256]{2,1,0:T(8,128)(2,1)S(1)} %get-tuple-element.40.refs_0_, bf16[4,128,256]{2,1,0:T(8,128)(2,1)S(1)} %get-tuple-element.41.refs_1_, f32[8,1,4096]{2,1,0:T(1,128)S(1)} %get-tuple-element.39.refs_0_.refs_2_.refs_10_.refs_11_.refs_5_, ...), custom_call_target="tpu_custom_call" | custom-call | flops 1 | bytes 1 | tf_op jit(solution)/shard_map/partials/pallas_call | solution.py:44
  19.1 1.1 %partials.9.refs_8_ = f32[3,64,768]{2,1,0:T(8,128)S(1)} custom-call(bf16[4,128,256]{2,1,0:T(8,128)(2,1)S(1)} %get-tuple-element.40.refs_0_, bf16[4,128,256]{2,1,0:T(8,128)(2,1)S(1)} %get-tuple-element.41.refs_1_, f32[8,1,4096]{2,1,0:T(1,128)S(1)} %get-tuple-element.39.refs_0_.refs_2_.refs_10_.refs_11_.refs_5_, ...), custom_call_target="tpu_custom_call" | custom-call | flops 1 | bytes 1 | tf_op jit(solution)/shard_map/partials/pallas_call | solution.py:44
  20.2 0.2 collective-permute-start.5
  20.4 1.7 %collective-permute-start.6 = (bf16[3,64,512]{2,1,0:T(8,128)(2,1)S(1)}, bf16[3,64,512]{2,1,0:T(8,128)(2,1)S(1)}, u32[]{:S(2)}, u32[]{:S(2)}) collective-permute-start(bf16[3,64,512]{2,1,0:T(8,128)(2,1)S(1)} %get-tuple-element.50), channel_id=1, source_target_pairs={{0,2},{1,3},{2,0},{3,1},{4,6},{5,7},{6,4},{7,5},{8,10},{9,11},{10,... | collective-permute-start | bytes 589832 | tf_op jit(solution)/shard_map/ppermute | solution.py:290
  22.1 0.0 collective-permute-done.4.refs_9_
  22.1 1.1 %partials.10 = (f32[3,64,768]{2,1,0:T(8,128)S(1)}, bf16[3,64,768]{2,1,0:T(8,128)(2,1)S(1)}) custom-call(bf16[4,128,256]{2,1,0:T(8,128)(2,1)S(1)} %get-tuple-element.40.refs_0_, bf16[4,128,256]{2,1,0:T(8,128)(2,1)S(1)} %get-tuple-element.41.refs_1_, f32[8,1,4096]{2,1,0:T(1,128)S(1)} %get-tuple-element.39.refs_0_.refs_2_.refs_10_.refs_11_.refs_5_, ...), custom_call_target="tpu_custom_call" | custom-call | flops 1 | bytes 1 | tf_op jit(solution)/shard_map/partials/pallas_call | solution.py:44
  23.3 0.4 collective-permute-start.8
  23.6 0.0 collective-permute-done.5.refs_9_
  23.6 1.1 %partials.11 = (f32[3,64,768]{2,1,0:T(8,128)S(1)}, bf16[3,64,768]{2,1,0:T(8,128)(2,1)S(1)}) custom-call(bf16[4,128,256]{2,1,0:T(8,128)(2,1)S(1)} %get-tuple-element.40.refs_0_, bf16[4,128,256]{2,1,0:T(8,128)(2,1)S(1)} %get-tuple-element.41.refs_1_, f32[8,1,4096]{2,1,0:T(1,128)S(1)} %get-tuple-element.39.refs_0_.refs_2_.refs_10_.refs_11_.refs_5_, ...), custom_call_target="tpu_custom_call" | custom-call | flops 1 | bytes 1 | tf_op jit(solution)/shard_map/partials/pallas_call | solution.py:44
  24.8 3.4 %collective-permute-done.6.refs_2_ = bf16[3,64,512]{2,1,0:T(8,128)(2,1)S(1)} collective-permute-done((bf16[3,64,512]{2,1,0:T(8,128)(2,1)S(1)}, bf16[3,64,512]{2,1,0:T(8,128)(2,1)S(1)}, u32[]{:S(2)}, u32[]{:S(2)}) %collective-permute-start.6) | collective-permute-done | bytes 196640 | tf_op jit(solution)/shard_map/ppermute | solution.py:290
  28.2 0.1 activate.3.refs_0_
  28.2 0.1 collective-permute-start.7
  28.3 1.4 %collective-permute-done.7.refs_1_ = bf16[3,64,512]{2,1,0:T(8,128)(2,1)S(1)} collective-permute-done((bf16[3,64,512]{2,1,0:T(8,128)(2,1)S(1)}, bf16[3,64,512]{2,1,0:T(8,128)(2,1)S(1)}, u32[]{:S(2)}, u32[]{:S(2)}) %collective-permute-start.7) | collective-permute-done | bytes 196640 | tf_op jit(solution)/shard_map/ppermute | solution.py:286
  29.8 5.5 %back_rows_grads.2 = (f32[2,64,1024]{2,1,0:T(8,128)S(1)}, f32[1024,4096]{1,0:T(8,128)}, f32[1024,4096]{1,0:T(8,128)}, f32[4096,1024]{1,0:T(8,128)}) custom-call(bf16[3,64,512]{2,1,0:T(8,128)(2,1)S(1)} %activate.3.refs_0_, bf16[3,64,512]{2,1,0:T(8,128)(2,1)S(1)} %collective-permute-done.7.refs_1_, f32[32,1,1024]{2,1,0:T(1,128)S(1)} %get-tuple-element.51.refs_2_.refs_1_, ...), custom_call_target="tpu_custom_call" | custom-call | flops 1 | bytes 1 | tf_op jit(solution)/shard_map/back_rows_grads/pallas_call | solution.py:44
  35.3 0.0 collective-permute-done.8.refs_2_
  35.3 0.1 activate.4.refs_0_
  35.4 0.2 collective-permute-start.9
  35.6 1.7 %collective-permute-start.10 = (bf16[3,64,768]{2,1,0:T(8,128)(2,1)S(1)}, bf16[3,64,768]{2,1,0:T(8,128)(2,1)S(1)}, u32[]{:S(2)}, u32[]{:S(2)}) collective-permute-start(bf16[3,64,768]{2,1,0:T(8,128)(2,1)S(1)} %get-tuple-element.62), channel_id=1, source_target_pairs={{0,2},{1,3},{2,0},{3,1},{4,6},{5,7},{6,4},{7,5},{8,10},{9,11},{10,... | collective-permute-start | bytes 884744 | tf_op jit(solution)/shard_map/ppermute | solution.py:290
  37.4 0.0 collective-permute-done.9.refs_1_
  37.4 8.1 %back_rows_grads.3 = (f32[2,64,1024]{2,1,0:T(8,128)S(1)}, f32[1024,4096]{1,0:T(8,128)}, f32[1024,4096]{1,0:T(8,128)}, f32[4096,1024]{1,0:T(8,128)}) custom-call(bf16[3,64,768]{2,1,0:T(8,128)(2,1)S(1)} %activate.4.refs_0_, bf16[3,64,768]{2,1,0:T(8,128)(2,1)S(1)} %collective-permute-done.9.refs_1_, ...), custom_call_target="tpu_custom_call", output_to_operand_aliasing={{1}: (13, {}), {2}: (14, {}), {3}: (15, {})} | custom-call | flops 1 | bytes 1 | tf_op jit(solution)/shard_map/back_rows_grads/pallas_call | solution.py:44
  45.5 0.0 collective-permute-done.10.refs_2_
  45.5 0.1 activate.5.refs_0_
  45.6 0.2 collective-permute-start.11
  45.8 1.5 %back_rows.2.refs_7_ = f32[2,64,1024]{2,1,0:T(8,128)S(1)} custom-call(bf16[3,64,768]{2,1,0:T(8,128)(2,1)S(1)} %activate.5.refs_0_, f32[32,1,1024]{2,1,0:T(1,128)S(1)} %get-tuple-element.51.refs_2_.refs_1_, f32[32,1,1024]{2,1,0:T(1,128)S(1)} %get-tuple-element.52.refs_3_.refs_2_, f32[32,1,1024]{2,1,0:T(1,128)S(1)} %get-tuple-element.53.refs_4_.refs_3_, ...), custom_call_target="tpu_custom_call" | custom-call | flops 1 | bytes 1 | tf_op jit(solution)/shard_map/back_rows/pallas_call | solution.py:44
  47.2 0.0 collective-permute-done.11.refs_0_.refs_1_
  47.3 1.5 %back_rows.3 = (bf16[2,16,1024]{2,1,0:T(8,128)(2,1)S(1)}, bf16[2,16,1024]{2,1,0:T(8,128)(2,1)S(1)}, bf16[2,16,1024]{2,1,0:T(8,128)(2,1)S(1)}, bf16[2,16,1024]{2,1,0:T(8,128)(2,1)S(1)}) custom-call(bf16[3,64,768]{2,1,0:T(8,128)(2,1)S(1)} %collective-permute-done.11.refs_0_.refs_1_, f32[32,1,1024]{2,1,0:T(1,128)S(1)} %get-tuple-element.51.refs_2_.refs_1_, ...), custom_call_target="tpu_custom_call" | custom-call | flops 1 | bytes 1 | tf_op jit(solution)/shard_map/back_rows/pallas_call | solution.py:44
  48.7 0.7 %collective-permute-start.12 = (bf16[2,16,1024]{2,1,0:T(8,128)(2,1)S(1)}, bf16[2,16,1024]{2,1,0:T(8,128)(2,1)S(1)}, u32[]{:S(2)}, u32[]{:S(2)}) collective-permute-start(bf16[2,16,1024]{2,1,0:T(8,128)(2,1)S(1)} %get-tuple-element.64), channel_id=1, source_target_pairs={{0,4},{4,0},{8,12},{12,8},{1,5},{5,1},{9,13},{13,9},{2,6},{6,2},{1... | collective-permute-start | bytes 196616 | tf_op jit(solution)/shard_map/ppermute | solution.py:283
  49.5 3.5 %collective-permute-start.13 = (bf16[2,16,1024]{2,1,0:T(8,128)(2,1)S(1)}, bf16[2,16,1024]{2,1,0:T(8,128)(2,1)S(1)}, u32[]{:S(2)}, u32[]{:S(2)}) collective-permute-start(bf16[2,16,1024]{2,1,0:T(8,128)(2,1)S(1)} %get-tuple-element.65), channel_id=1, source_target_pairs={{0,8},{4,12},{8,0},{12,4},{1,9},{5,13},{9,1},{13,5},{2,10},{6,14},... | collective-permute-start | bytes 196616 | tf_op jit(solution)/shard_map/ppermute | solution.py:283
  53.0 0.2 collective-permute-start.14
  53.2 6.9 %back_grads.1 = (f32[1024,4096]{1,0:T(8,128)}, f32[1024,4096]{1,0:T(8,128)}, f32[4096,1024]{1,0:T(8,128)}) custom-call(bf16[3,64,768]{2,1,0:T(8,128)(2,1)S(1)} %activate.5.refs_0_, bf16[3,64,768]{2,1,0:T(8,128)(2,1)S(1)} %collective-permute-done.11.refs_0_.refs_1_, ...), custom_call_target="tpu_custom_call", output_to_operand_aliasing={{0}: (7, {}), {1}: (8, {}), {2}: (9, {})} | custom-call | flops 1 | bytes 1 | tf_op jit(solution)/shard_map/back_grads/pallas_call | solution.py:44
  60.1 0.0 collective-permute-done.12
  60.1 0.0 collective-permute-done.13
  60.1 0.0 collective-permute-done.14
  60.1 0.6 %slice_bitcast_fusion = (bf16[16,1024]{1,0:T(8,128)(2,1)}, bf16[16,1024]{1,0:T(8,128)(2,1)}) fusion(bf16[2,16,1024]{2,1,0:T(8,128)(2,1)S(1)} %add_convert_fusion), kind=kLoop, calls=%fused_computation.2 | loop fusion | bytes 131072 | tf_op jit(solution)/shard_map/squeeze | solution.py:446
  (1 shorter events, 0.0 us)
Async XLA Ops:
  1.4 14.1 %collective-permute-start.2 = (bf16[2,16,1024]{2,1,0:T(8,128)(2,1)S(1)}, bf16[2,16,1024]{2,1,0:T(8,128)(2,1)S(1)}, u32[]{:S(2)}, u32[]{:S(2)}) collective-permute-start(bf16[2,16,1024]{2,1,0:T(8,128)(2,1)S(1)} %pad_maximum_fusion.refs_4_), channel_id=1, source_target_pairs={{0,4},{4,0},{8,12},{12,8},{1,5},{5,1},{9,13},{13,9},{2,6},{6,2},{1... | collective-permute-start | bytes 196616 | tf_op jit(solution)/shard_map/ppermute | solution.py:283
  4.5 11.0 %collective-permute-start.1 = (bf16[2,16,1024]{2,1,0:T(8,128)(2,1)S(1)}, bf16[2,16,1024]{2,1,0:T(8,128)(2,1)S(1)}, u32[]{:S(2)}, u32[]{:S(2)}) collective-permute-start(bf16[2,16,1024]{2,1,0:T(8,128)(2,1)S(1)} %pad_maximum_fusion.refs_4_), channel_id=1, source_target_pairs={{0,8},{4,12},{8,0},{12,4},{1,9},{5,13},{9,1},{13,5},{2,10},{6,14},... | collective-permute-start | bytes 196616 | tf_op jit(solution)/shard_map/ppermute | solution.py:283
  7.1 8.4 %collective-permute-start = (bf16[2,16,1024]{2,1,0:T(8,128)(2,1)S(1)}, bf16[2,16,1024]{2,1,0:T(8,128)(2,1)S(1)}, u32[]{:S(2)}, u32[]{:S(2)}) collective-permute-start(bf16[2,16,1024]{2,1,0:T(8,128)(2,1)S(1)} %pad_maximum_fusion.refs_4_), channel_id=1, source_target_pairs={{0,12},{4,8},{8,4},{12,0},{1,13},{5,9},{9,5},{13,1},{2,14},{6,10},... | collective-permute-start | bytes 196616 | tf_op jit(solution)/shard_map/ppermute | solution.py:283
  16.5 1.8 %collective-permute-start.3 = (f32[3,64,512]{2,1,0:T(8,128)S(1)}, f32[3,64,512]{2,1,0:T(8,128)S(1)}, u32[]{:S(2)}, u32[]{:S(2)}) collective-permute-start(f32[3,64,512]{2,1,0:T(8,128)S(1)} %partials.6.refs_8_), channel_id=1, source_target_pairs={{0,1},{1,0},{2,3},{3,2},{4,5},{5,4},{6,7},{7,6},{8,9},{9,8},{10,11... | collective-permute-start | bytes 1179656 | tf_op jit(solution)/shard_map/ppermute | solution.py:286
  17.7 4.4 %collective-permute-start.4 = (f32[3,64,768]{2,1,0:T(8,128)S(1)}, f32[3,64,768]{2,1,0:T(8,128)S(1)}, u32[]{:S(2)}, u32[]{:S(2)}) collective-permute-start(f32[3,64,768]{2,1,0:T(8,128)S(1)} %partials.7.refs_8_), channel_id=1, source_target_pairs={{0,1},{1,0},{2,3},{3,2},{4,5},{5,4},{6,7},{7,6},{8,9},{9,8},{10,11... | collective-permute-start | bytes 1769480 | tf_op jit(solution)/shard_map/ppermute | solution.py:286
  20.2 3.4 %collective-permute-start.5 = (f32[3,64,768]{2,1,0:T(8,128)S(1)}, f32[3,64,768]{2,1,0:T(8,128)S(1)}, u32[]{:S(2)}, u32[]{:S(2)}) collective-permute-start(f32[3,64,768]{2,1,0:T(8,128)S(1)} %partials.9.refs_8_), channel_id=1, source_target_pairs={{0,1},{1,0},{2,3},{3,2},{4,5},{5,4},{6,7},{7,6},{8,9},{9,8},{10,11... | collective-permute-start | bytes 1769480 | tf_op jit(solution)/shard_map/ppermute | solution.py:286
  20.4 7.7 %collective-permute-start.6 = (bf16[3,64,512]{2,1,0:T(8,128)(2,1)S(1)}, bf16[3,64,512]{2,1,0:T(8,128)(2,1)S(1)}, u32[]{:S(2)}, u32[]{:S(2)}) collective-permute-start(bf16[3,64,512]{2,1,0:T(8,128)(2,1)S(1)} %get-tuple-element.50), channel_id=1, source_target_pairs={{0,2},{1,3},{2,0},{3,1},{4,6},{5,7},{6,4},{7,5},{8,10},{9,11},{10,... | collective-permute-start | bytes 589832 | tf_op jit(solution)/shard_map/ppermute | solution.py:290
  23.3 12.0 %collective-permute-start.8 = (bf16[3,64,768]{2,1,0:T(8,128)(2,1)S(1)}, bf16[3,64,768]{2,1,0:T(8,128)(2,1)S(1)}, u32[]{:S(2)}, u32[]{:S(2)}) collective-permute-start(bf16[3,64,768]{2,1,0:T(8,128)(2,1)S(1)} %get-tuple-element.57), channel_id=1, source_target_pairs={{0,2},{1,3},{2,0},{3,1},{4,6},{5,7},{6,4},{7,5},{8,10},{9,11},{10,... | collective-permute-start | bytes 884744 | tf_op jit(solution)/shard_map/ppermute | solution.py:290
  28.2 1.5 %collective-permute-start.7 = (bf16[3,64,512]{2,1,0:T(8,128)(2,1)S(1)}, bf16[3,64,512]{2,1,0:T(8,128)(2,1)S(1)}, u32[]{:S(2)}, u32[]{:S(2)}) collective-permute-start(bf16[3,64,512]{2,1,0:T(8,128)(2,1)S(1)} %activate.3.refs_0_), channel_id=1, source_target_pairs={{0,1},{1,0},{2,3},{3,2},{4,5},{5,4},{6,7},{7,6},{8,9},{9,8},{10,11... | collective-permute-start | bytes 589832 | tf_op jit(solution)/shard_map/ppermute | solution.py:286
  35.4 1.9 %collective-permute-start.9 = (bf16[3,64,768]{2,1,0:T(8,128)(2,1)S(1)}, bf16[3,64,768]{2,1,0:T(8,128)(2,1)S(1)}, u32[]{:S(2)}, u32[]{:S(2)}) collective-permute-start(bf16[3,64,768]{2,1,0:T(8,128)(2,1)S(1)} %activate.4.refs_0_), channel_id=1, source_target_pairs={{0,1},{1,0},{2,3},{3,2},{4,5},{5,4},{6,7},{7,6},{8,9},{9,8},{10,11... | collective-permute-start | bytes 884744 | tf_op jit(solution)/shard_map/ppermute | solution.py:286
  35.6 9.8 %collective-permute-start.10 = (bf16[3,64,768]{2,1,0:T(8,128)(2,1)S(1)}, bf16[3,64,768]{2,1,0:T(8,128)(2,1)S(1)}, u32[]{:S(2)}, u32[]{:S(2)}) collective-permute-start(bf16[3,64,768]{2,1,0:T(8,128)(2,1)S(1)} %get-tuple-element.62), channel_id=1, source_target_pairs={{0,2},{1,3},{2,0},{3,1},{4,6},{5,7},{6,4},{7,5},{8,10},{9,11},{10,... | collective-permute-start | bytes 884744 | tf_op jit(solution)/shard_map/ppermute | solution.py:290
  45.6 1.6 %collective-permute-start.11 = (bf16[3,64,768]{2,1,0:T(8,128)(2,1)S(1)}, bf16[3,64,768]{2,1,0:T(8,128)(2,1)S(1)}, u32[]{:S(2)}, u32[]{:S(2)}) collective-permute-start(bf16[3,64,768]{2,1,0:T(8,128)(2,1)S(1)} %activate.5.refs_0_), channel_id=1, source_target_pairs={{0,1},{1,0},{2,3},{3,2},{4,5},{5,4},{6,7},{7,6},{8,9},{9,8},{10,11... | collective-permute-start | bytes 884744 | tf_op jit(solution)/shard_map/ppermute | solution.py:286
  48.7 11.3 %collective-permute-start.12 = (bf16[2,16,1024]{2,1,0:T(8,128)(2,1)S(1)}, bf16[2,16,1024]{2,1,0:T(8,128)(2,1)S(1)}, u32[]{:S(2)}, u32[]{:S(2)}) collective-permute-start(bf16[2,16,1024]{2,1,0:T(8,128)(2,1)S(1)} %get-tuple-element.64), channel_id=1, source_target_pairs={{0,4},{4,0},{8,12},{12,8},{1,5},{5,1},{9,13},{13,9},{2,6},{6,2},{1... | collective-permute-start | bytes 196616 | tf_op jit(solution)/shard_map/ppermute | solution.py:283
  49.5 10.6 %collective-permute-start.13 = (bf16[2,16,1024]{2,1,0:T(8,128)(2,1)S(1)}, bf16[2,16,1024]{2,1,0:T(8,128)(2,1)S(1)}, u32[]{:S(2)}, u32[]{:S(2)}) collective-permute-start(bf16[2,16,1024]{2,1,0:T(8,128)(2,1)S(1)} %get-tuple-element.65), channel_id=1, source_target_pairs={{0,8},{4,12},{8,0},{12,4},{1,9},{5,13},{9,1},{13,5},{2,10},{6,14},... | collective-permute-start | bytes 196616 | tf_op jit(solution)/shard_map/ppermute | solution.py:283
  53.0 7.1 %collective-permute-start.14 = (bf16[2,16,1024]{2,1,0:T(8,128)(2,1)S(1)}, bf16[2,16,1024]{2,1,0:T(8,128)(2,1)S(1)}, u32[]{:S(2)}, u32[]{:S(2)}) collective-permute-start(bf16[2,16,1024]{2,1,0:T(8,128)(2,1)S(1)} %get-tuple-element.66), channel_id=1, source_target_pairs={{0,12},{4,8},{8,4},{12,0},{1,13},{5,9},{9,5},{13,1},{2,14},{6,10},... | collective-permute-start | bytes 196616 | tf_op jit(solution)/shard_map/ppermute | solution.py:283

commit v12 on v9

--- a/solution.py
+++ b/solution.py
@@ -98,11 +98,6 @@
 
 def fetch_kernel(r):
     copies = []
-    for source, target in ((r.w_gate, r.kg), (r.w_up, r.ku), (r.w_down, r.kd)):
-        height = source.shape[0] // SPLIT
-        for k in range(SPLIT):
-            rows = slice(k * height, (k + 1) * height)
-            copies.append((source.at[rows, :], target.at[rows, :]))
     for k in MASKS:
         copies.append((getattr(r, "hbm_" + k), getattr(r, k)))
     copies = [pltpu.make_async_copy(a, b, r.sems.at[k]) for k, (a, b) in enumerate(copies)]
@@ -317,7 +312,6 @@
         {
             **{k: pinned(across_shape) for k in ("mg", "mu", "mdt")},
             **{k: pinned(along_shape) for k in ("mgt", "mut", "md")},
-            **{k: pinned(shape(*w.shape)) for k, w in zip(KEPT, (w_gate, w_up, w_down))},
         },
         scratch={
             **{k: pltpu.VMEM(m.shape, m.dtype) for k, m in masks.items()},
@@ -326,6 +320,7 @@
         vmem=grant(4),
     )
 
+    values.update(kg=w_gate, ku=w_up, kd=w_down)
     pair = min(DEPTH, width) // BLK
     pair_shape = shape(width // (pair * BLK), pair * rows, pair * BLK)
     values |= call(

time: 60.3 us -> 57.9 us (0.960)
  Pallas kernels: 38.8 us -> 31.7 us
  waiting for transfers between devices: 3.56 us -> 8.23 us
    pallas_call x18, Pallas kernels: 38.8 us -> 31.7 us  [call(): pl.pallas_call(body, out_shape=[shape for shape, _ in outs.values()], in_...]
    ppermute x6, waiting for transfers between devices: 0.02 us -> 4.69 us  [trade(): return lax.ppermute(array, 'grid', [(i, i ^ s) for i in range(n_grid)])]
  transfers between devices with their start and end apart: 15 -> 15, of which waited for: 2 -> 4; matrix products, arithmetic and copies ran while one was open for 0% -> 0% of each run, Pallas kernels for 60% -> 50%
where the time goes in v12:
time: 57.9 us; the launch traced here: 57.8 us
  Pallas kernels  31.7 us (55%)
  starting transfers between devices  15.2 us (26%)
  waiting for transfers between devices  8.23 us (14%)
  other arithmetic  0.97 us (2%)
  between operations  0.96 us (2%)
  local copies, waits for them, and re-layouts  0.66 us (1%)
    pallas_call x18, Pallas kernels, call(): pl.pallas_call(body, out_shape=[shape for shape, _ in outs.values()], in_...  31.7 us
    ppermute x6, starting transfers between devices, trade(): return lax.ppermute(array, 'grid', [(i, i ^ s) for i in range(n_grid)])  10.1 us
    ppermute x6, waiting for transfers between devices, trade(): return lax.ppermute(array, 'grid', [(i, i ^ s) for i in range(n_grid)])  4.69 us
    ppermute x3, starting transfers between devices, across(): lax.ppermute(array, 'dp', [(i, (i // 2 + s) % pairs * 2 + i % 2) for i in...  3.6 us
    ppermute x3, waiting for transfers between devices, across(): lax.ppermute(array, 'dp', [(i, (i // 2 + s) % pairs * 2 + i % 2) for i in...  3.39 us
    ppermute x6, starting transfers between devices, swap(): return lax.ppermute(array, 'dp', [(i, i ^ 1) for i in range(n_dp)])  1.52 us
  transfers between devices with their start and end apart: 15, of which 4 were waited for; matrix products, arithmetic and copies ran while one was open for 0% of the time, Pallas kernels for 50%

profile of v12, /device:TPU:0, one launch (start us, length us, event | category | flops | bytes accessed | tf_op | source)
XLA Modules:
  0.0 57.8 jit_solution(7748848400219080896)
XLA Ops:
  0.6 0.0 copy-start
  0.6 0.0 slice-start.2
  0.7 0.0 slice-start
  0.7 0.9 %pad_maximum_fusion.refs_4_ = bf16[2,16,1024]{2,1,0:T(8,128)(2,1)S(1)} fusion(bf16[1,16,1024]{2,1,0:T(8,128)(2,1)} %bitcast.11, bf16[1,16,1024]{2,1,0:T(8,128)(2,1)} %bitcast.12), kind=kLoop, calls=%fused_computation.1 | loop fusion | flops 32768 | bytes 131072 | tf_op jit(solution)/shard_map/stack | solution.py:299
  1.6 3.1 %collective-permute-start.2 = (bf16[2,16,1024]{2,1,0:T(8,128)(2,1)S(1)}, bf16[2,16,1024]{2,1,0:T(8,128)(2,1)S(1)}, u32[]{:S(2)}, u32[]{:S(2)}) collective-permute-start(bf16[2,16,1024]{2,1,0:T(8,128)(2,1)S(1)} %pad_maximum_fusion.refs_4_), channel_id=1, source_target_pairs={{0,4},{4,0},{8,12},{12,8},{1,5},{5,1},{9,13},{13,9},{2,6},{6,2},{1... | collective-permute-start | bytes 196616 | tf_op jit(solution)/shard_map/ppermute | solution.py:278
  4.7 2.6 %collective-permute-start.1 = (bf16[2,16,1024]{2,1,0:T(8,128)(2,1)S(1)}, bf16[2,16,1024]{2,1,0:T(8,128)(2,1)S(1)}, u32[]{:S(2)}, u32[]{:S(2)}) collective-permute-start(bf16[2,16,1024]{2,1,0:T(8,128)(2,1)S(1)} %pad_maximum_fusion.refs_4_), channel_id=1, source_target_pairs={{0,8},{4,12},{8,0},{12,4},{1,9},{5,13},{9,1},{13,5},{2,10},{6,14},... | collective-permute-start | bytes 196616 | tf_op jit(solution)/shard_map/ppermute | solution.py:278
  7.3 0.0 collective-permute-start
  7.3 0.0 slice-start.1
  7.3 0.0 slice-start.3
  7.3 1.4 %fetch.1 = (f32[8,1,4096]{2,1,0:T(1,128)S(1)}, f32[8,1,4096]{2,1,0:T(1,128)S(1)}, f32[8,1,4096]{2,1,0:T(1,128)S(1)}, f32[32,1,1024]{2,1,0:T(1,128)S(1)}, f32[32,...) custom-call(bf16[1024,4096]{1,0:T(8,128)(2,1)} %refs_4_.13, bf16[1024,4096]{1,0:T(8,128)(2,1)} %refs_5_.23, ...), custom_call_target="tpu_custom_call" | custom-call | flops 1 | bytes 1 | tf_op jit(solution)/shard_map/fetch/pallas_call | solution.py:44
  8.7 0.0 collective-permute-done.2.refs_3_
  8.7 3.3 %collective-permute-done.1.refs_2_ = bf16[2,16,1024]{2,1,0:T(8,128)(2,1)S(1)} collective-permute-done((bf16[2,16,1024]{2,1,0:T(8,128)(2,1)S(1)}, bf16[2,16,1024]{2,1,0:T(8,128)(2,1)S(1)}, u32[]{:S(2)}, u32[]{:S(2)}) %collective-permute-start.1) | collective-permute-done | bytes 65568 | tf_op jit(solution)/shard_map/ppermute | solution.py:278
  11.9 1.4 %collective-permute-done.refs_1_ = bf16[2,16,1024]{2,1,0:T(8,128)(2,1)S(1)} collective-permute-done((bf16[2,16,1024]{2,1,0:T(8,128)(2,1)S(1)}, bf16[2,16,1024]{2,1,0:T(8,128)(2,1)S(1)}, u32[]{:S(2)}, u32[]{:S(2)}) %collective-permute-start) | collective-permute-done | bytes 65568 | tf_op jit(solution)/shard_map/ppermute | solution.py:278
  13.3 0.2 assemble.1
  13.5 0.0 copy-done
  13.5 0.0 slice-done.2
  13.6 0.0 slice-done
  13.6 0.0 slice-done.1
  13.6 0.0 slice-done.3
  13.6 0.8 %partials.6.refs_8_ = f32[3,64,512]{2,1,0:T(8,128)S(1)} custom-call(bf16[4,128,256]{2,1,0:T(8,128)(2,1)S(1)} %get-tuple-element.45.refs_0_, bf16[4,128,256]{2,1,0:T(8,128)(2,1)S(1)} %get-tuple-element.46.refs_1_, f32[8,1,4096]{2,1,0:T(1,128)S(1)} %get-tuple-element.44.refs_0_.refs_2_.refs_9_.refs_10_.refs_5_, ...), custom_call_target="tpu_custom_call" | custom-call | flops 1 | bytes 1 | tf_op jit(solution)/shard_map/partials/pallas_call | solution.py:44
  14.4 0.1 collective-permute-start.3
  14.5 1.1 %partials.7.refs_8_ = f32[3,64,768]{2,1,0:T(8,128)S(1)} custom-call(bf16[4,128,256]{2,1,0:T(8,128)(2,1)S(1)} %get-tuple-element.45.refs_0_, bf16[4,128,256]{2,1,0:T(8,128)(2,1)S(1)} %get-tuple-element.46.refs_1_, f32[8,1,4096]{2,1,0:T(1,128)S(1)} %get-tuple-element.44.refs_0_.refs_2_.refs_9_.refs_10_.refs_5_, ...), custom_call_target="tpu_custom_call" | custom-call | flops 1 | bytes 1 | tf_op jit(solution)/shard_map/partials/pallas_call | solution.py:44
  15.6 0.5 collective-permute-start.4
  16.1 0.0 collective-permute-done.3.refs_9_
  16.2 0.8 %partials.8 = (f32[3,64,512]{2,1,0:T(8,128)S(1)}, bf16[3,64,512]{2,1,0:T(8,128)(2,1)S(1)}) custom-call(bf16[4,128,256]{2,1,0:T(8,128)(2,1)S(1)} %get-tuple-element.45.refs_0_, bf16[4,128,256]{2,1,0:T(8,128)(2,1)S(1)} %get-tuple-element.46.refs_1_, f32[8,1,4096]{2,1,0:T(1,128)S(1)} %get-tuple-element.44.refs_0_.refs_2_.refs_9_.refs_10_.refs_5_, ...), custom_call_target="tpu_custom_call" | custom-call | flops 1 | bytes 1 | tf_op jit(solution)/shard_map/partials/pallas_call | solution.py:44
  17.0 1.1 %partials.9.refs_8_ = f32[3,64,768]{2,1,0:T(8,128)S(1)} custom-call(bf16[4,128,256]{2,1,0:T(8,128)(2,1)S(1)} %get-tuple-element.45.refs_0_, bf16[4,128,256]{2,1,0:T(8,128)(2,1)S(1)} %get-tuple-element.46.refs_1_, f32[8,1,4096]{2,1,0:T(1,128)S(1)} %get-tuple-element.44.refs_0_.refs_2_.refs_9_.refs_10_.refs_5_, ...), custom_call_target="tpu_custom_call" | custom-call | flops 1 | bytes 1 | tf_op jit(solution)/shard_map/partials/pallas_call | solution.py:44
  18.1 0.2 collective-permute-start.5
  18.3 1.5 %collective-permute-start.6 = (bf16[3,64,512]{2,1,0:T(8,128)(2,1)S(1)}, bf16[3,64,512]{2,1,0:T(8,128)(2,1)S(1)}, u32[]{:S(2)}, u32[]{:S(2)}) collective-permute-start(bf16[3,64,512]{2,1,0:T(8,128)(2,1)S(1)} %get-tuple-element.52), channel_id=1, source_target_pairs={{0,2},{1,3},{2,0},{3,1},{4,6},{5,7},{6,4},{7,5},{8,10},{9,11},{10,... | collective-permute-start | bytes 589832 | tf_op jit(solution)/shard_map/ppermute | solution.py:285
  19.8 0.0 collective-permute-done.4.refs_9_
  19.8 1.1 %partials.10 = (f32[3,64,768]{2,1,0:T(8,128)S(1)}, bf16[3,64,768]{2,1,0:T(8,128)(2,1)S(1)}) custom-call(bf16[4,128,256]{2,1,0:T(8,128)(2,1)S(1)} %get-tuple-element.45.refs_0_, bf16[4,128,256]{2,1,0:T(8,128)(2,1)S(1)} %get-tuple-element.46.refs_1_, f32[8,1,4096]{2,1,0:T(1,128)S(1)} %get-tuple-element.44.refs_0_.refs_2_.refs_9_.refs_10_.refs_5_, ...), custom_call_target="tpu_custom_call" | custom-call | flops 1 | bytes 1 | tf_op jit(solution)/shard_map/partials/pallas_call | solution.py:44
  20.9 0.6 %collective-permute-start.8 = (bf16[3,64,768]{2,1,0:T(8,128)(2,1)S(1)}, bf16[3,64,768]{2,1,0:T(8,128)(2,1)S(1)}, u32[]{:S(2)}, u32[]{:S(2)}) collective-permute-start(bf16[3,64,768]{2,1,0:T(8,128)(2,1)S(1)} %get-tuple-element.63), channel_id=1, source_target_pairs={{0,2},{1,3},{2,0},{3,1},{4,6},{5,7},{6,4},{7,5},{8,10},{9,11},{10,... | collective-permute-start | bytes 884744 | tf_op jit(solution)/shard_map/ppermute | solution.py:285
  21.5 0.0 collective-permute-done.5.refs_9_
  21.5 1.1 %partials.11 = (f32[3,64,768]{2,1,0:T(8,128)S(1)}, bf16[3,64,768]{2,1,0:T(8,128)(2,1)S(1)}) custom-call(bf16[4,128,256]{2,1,0:T(8,128)(2,1)S(1)} %get-tuple-element.45.refs_0_, bf16[4,128,256]{2,1,0:T(8,128)(2,1)S(1)} %get-tuple-element.46.refs_1_, f32[8,1,4096]{2,1,0:T(1,128)S(1)} %get-tuple-element.44.refs_0_.refs_2_.refs_9_.refs_10_.refs_5_, ...), custom_call_target="tpu_custom_call" | custom-call | flops 1 | bytes 1 | tf_op jit(solution)/shard_map/partials/pallas_call | solution.py:44
  22.6 3.4 %collective-permute-done.6.refs_2_ = bf16[3,64,512]{2,1,0:T(8,128)(2,1)S(1)} collective-permute-done((bf16[3,64,512]{2,1,0:T(8,128)(2,1)S(1)}, bf16[3,64,512]{2,1,0:T(8,128)(2,1)S(1)}, u32[]{:S(2)}, u32[]{:S(2)}) %collective-permute-start.6) | collective-permute-done | bytes 196640 | tf_op jit(solution)/shard_map/ppermute | solution.py:285
  26.0 0.1 activate.3.refs_0_
  26.1 0.1 collective-permute-start.7
  26.2 3.0 %back_rows_grads.4 = (f32[2,64,1024]{2,1,0:T(8,128)S(1)}, f32[1024,4096]{1,0:T(8,128)}, f32[1024,4096]{1,0:T(8,128)}, f32[4096,1024]{1,0:T(8,128)}) custom-call(bf16[3,64,512]{2,1,0:T(8,128)(2,1)S(1)} %activate.3.refs_0_, f32[32,1,1024]{2,1,0:T(1,128)S(1)} %get-tuple-element.53.refs_1_.refs_2_, f32[32,1,1024]{2,1,0:T(1,128)S(1)} %get-tuple-element.54.refs_2_, ...), custom_call_target="tpu_custom_call" | custom-call | flops 1 | bytes 1 | tf_op jit(solution)/shard_map/back_rows_grads/pallas_call | solution.py:44
  29.2 0.0 collective-permute-done.7.refs_0_
  29.2 3.0 %back_rows_grads.5 = (f32[2,64,1024]{2,1,0:T(8,128)S(1)}, f32[1024,4096]{1,0:T(8,128)}, f32[1024,4096]{1,0:T(8,128)}, f32[4096,1024]{1,0:T(8,128)}) custom-call(bf16[3,64,512]{2,1,0:T(8,128)(2,1)S(1)} %collective-permute-done.7.refs_0_, ...), custom_call_target="tpu_custom_call", output_to_operand_aliasing={{1}: (12, {}), {2}: (13, {}), {3}: (14, {})} | custom-call | flops 1 | bytes 1 | tf_op jit(solution)/shard_map/back_rows_grads/pallas_call | solution.py:44
  32.3 0.0 collective-permute-done.8.refs_2_
  32.3 0.1 activate.4.refs_0_
  32.4 0.6 collective-permute-start.9
  33.0 1.5 %collective-permute-start.10 = (bf16[3,64,768]{2,1,0:T(8,128)(2,1)S(1)}, bf16[3,64,768]{2,1,0:T(8,128)(2,1)S(1)}, u32[]{:S(2)}, u32[]{:S(2)}) collective-permute-start(bf16[3,64,768]{2,1,0:T(8,128)(2,1)S(1)} %get-tuple-element.72), channel_id=1, source_target_pairs={{0,2},{1,3},{2,0},{3,1},{4,6},{5,7},{6,4},{7,5},{8,10},{9,11},{10,... | collective-permute-start | bytes 884744 | tf_op jit(solution)/shard_map/ppermute | solution.py:285
  34.5 4.0 %back_rows_grads.6 = (f32[2,64,1024]{2,1,0:T(8,128)S(1)}, f32[1024,4096]{1,0:T(8,128)}, f32[1024,4096]{1,0:T(8,128)}, f32[4096,1024]{1,0:T(8,128)}) custom-call(bf16[3,64,768]{2,1,0:T(8,128)(2,1)S(1)} %activate.4.refs_0_, f32[32,1,1024]{2,1,0:T(1,128)S(1)} %get-tuple-element.53.refs_1_.refs_2_, ...), custom_call_target="tpu_custom_call", output_to_operand_aliasing={{1}: (12, {}), {2}: (13, {}), {3}: (14, {})} | custom-call | flops 1 | bytes 1 | tf_op jit(solution)/shard_map/back_rows_grads/pallas_call | solution.py:44
  38.5 0.0 collective-permute-done.9.refs_0_
  38.5 4.0 %back_rows_grads.7 = (f32[2,64,1024]{2,1,0:T(8,128)S(1)}, f32[1024,4096]{1,0:T(8,128)}, f32[1024,4096]{1,0:T(8,128)}, f32[4096,1024]{1,0:T(8,128)}) custom-call(bf16[3,64,768]{2,1,0:T(8,128)(2,1)S(1)} %collective-permute-done.9.refs_0_, ...), custom_call_target="tpu_custom_call", output_to_operand_aliasing={{1}: (12, {}), {2}: (13, {}), {3}: (14, {})} | custom-call | flops 1 | bytes 1 | tf_op jit(solution)/shard_map/back_rows_grads/pallas_call | solution.py:44
  42.5 0.0 collective-permute-done.10.refs_2_
  42.5 0.1 activate.5.refs_0_
  42.7 0.1 collective-permute-start.11
  42.7 1.5 %back_rows.2.refs_7_ = f32[2,64,1024]{2,1,0:T(8,128)S(1)} custom-call(bf16[3,64,768]{2,1,0:T(8,128)(2,1)S(1)} %activate.5.refs_0_, f32[32,1,1024]{2,1,0:T(1,128)S(1)} %get-tuple-element.53.refs_1_.refs_2_, f32[32,1,1024]{2,1,0:T(1,128)S(1)} %get-tuple-element.54.refs_2_, f32[32,1,1024]{2,1,0:T(1,128)S(1)} %get-tuple-element.55.refs_3_, ...), custom_call_target="tpu_custom_call" | custom-call | flops 1 | bytes 1 | tf_op jit(solution)/shard_map/back_rows/pallas_call | solution.py:44
  44.2 0.1 collective-permute-done.11.refs_0_.refs_1_
  44.3 1.5 %back_rows.3 = (bf16[2,16,1024]{2,1,0:T(8,128)(2,1)S(1)}, bf16[2,16,1024]{2,1,0:T(8,128)(2,1)S(1)}, bf16[2,16,1024]{2,1,0:T(8,128)(2,1)S(1)}, bf16[2,16,1024]{2,1,0:T(8,128)(2,1)S(1)}) custom-call(bf16[3,64,768]{2,1,0:T(8,128)(2,1)S(1)} %collective-permute-done.11.refs_0_.refs_1_, f32[32,1,1024]{2,1,0:T(1,128)S(1)} %get-tuple-element.53.refs_1_.refs_2_, ...), custom_call_target="tpu_custom_call" | custom-call | flops 1 | bytes 1 | tf_op jit(solution)/shard_map/back_rows/pallas_call | solution.py:44
  45.8 0.1 collective-permute-start.12
  45.9 2.3 %collective-permute-start.13 = (bf16[2,16,1024]{2,1,0:T(8,128)(2,1)S(1)}, bf16[2,16,1024]{2,1,0:T(8,128)(2,1)S(1)}, u32[]{:S(2)}, u32[]{:S(2)}) collective-permute-start(bf16[2,16,1024]{2,1,0:T(8,128)(2,1)S(1)} %get-tuple-element.75), channel_id=1, source_target_pairs={{0,8},{4,12},{8,0},{12,4},{1,9},{5,13},{9,1},{13,5},{2,10},{6,14},... | collective-permute-start | bytes 196616 | tf_op jit(solution)/shard_map/ppermute | solution.py:278
  48.2 2.0 %collective-permute-start.14 = (bf16[2,16,1024]{2,1,0:T(8,128)(2,1)S(1)}, bf16[2,16,1024]{2,1,0:T(8,128)(2,1)S(1)}, u32[]{:S(2)}, u32[]{:S(2)}) collective-permute-start(bf16[2,16,1024]{2,1,0:T(8,128)(2,1)S(1)} %get-tuple-element.76), channel_id=1, source_target_pairs={{0,12},{4,8},{8,4},{12,0},{1,13},{5,9},{9,5},{13,1},{2,14},{6,10},... | collective-permute-start | bytes 196616 | tf_op jit(solution)/shard_map/ppermute | solution.py:278
  50.2 6.8 %back_grads.1 = (f32[1024,4096]{1,0:T(8,128)}, f32[1024,4096]{1,0:T(8,128)}, f32[4096,1024]{1,0:T(8,128)}) custom-call(bf16[3,64,768]{2,1,0:T(8,128)(2,1)S(1)} %activate.5.refs_0_, bf16[3,64,768]{2,1,0:T(8,128)(2,1)S(1)} %collective-permute-done.11.refs_0_.refs_1_, ...), custom_call_target="tpu_custom_call", output_to_operand_aliasing={{0}: (7, {}), {1}: (8, {}), {2}: (9, {})} | custom-call | flops 1 | bytes 1 | tf_op jit(solution)/shard_map/back_grads/pallas_call | solution.py:44
  57.1 0.0 collective-permute-done.12
  57.1 0.0 collective-permute-done.13
  57.1 0.0 collective-permute-done.14
  57.2 0.6 %slice_bitcast_fusion = (bf16[16,1024]{1,0:T(8,128)(2,1)}, bf16[16,1024]{1,0:T(8,128)(2,1)}) fusion(bf16[2,16,1024]{2,1,0:T(8,128)(2,1)S(1)} %add_convert_fusion), kind=kLoop, calls=%fused_computation.2 | loop fusion | bytes 131072 | tf_op jit(solution)/shard_map/squeeze | solution.py:438
  (3 shorter events, 0.0 us)
Async XLA Ops:
  0.6 12.9 %copy-start = (bf16[4096,1024]{1,0:T(8,128)(2,1)S(1)}, bf16[4096,1024]{1,0:T(8,128)(2,1)}, u32[]{:S(2)}) copy-start(bf16[4096,1024]{1,0:T(8,128)(2,1)} %refs_6_.23) | copy-start | bytes 25165828
  0.6 12.9 %slice-start.2 = ((s8[8388608]{0:T(1024)(128)(4,1)}), s8[4194304]{0:T(1024)(128)(4,1)S(1)}, s32[]{:S(2)}) async-start(s8[8388608]{0:T(1024)(128)(4,1)} %bitcast.9), calls=%async_computation.2 | async-start | bytes 8388608
  0.7 12.9 %slice-start = ((s8[8388608]{0:T(1024)(128)(4,1)}), s8[4194304]{0:T(1024)(128)(4,1)S(1)}, s32[]{:S(2)}) async-start(s8[8388608]{0:T(1024)(128)(4,1)} %bitcast.7), calls=%async_computation | async-start | bytes 8388608
  1.6 7.1 %collective-permute-start.2 = (bf16[2,16,1024]{2,1,0:T(8,128)(2,1)S(1)}, bf16[2,16,1024]{2,1,0:T(8,128)(2,1)S(1)}, u32[]{:S(2)}, u32[]{:S(2)}) collective-permute-start(bf16[2,16,1024]{2,1,0:T(8,128)(2,1)S(1)} %pad_maximum_fusion.refs_4_), channel_id=1, source_target_pairs={{0,4},{4,0},{8,12},{12,8},{1,5},{5,1},{9,13},{13,9},{2,6},{6,2},{1... | collective-permute-start | bytes 196616 | tf_op jit(solution)/shard_map/ppermute | solution.py:278
  4.7 7.3 %collective-permute-start.1 = (bf16[2,16,1024]{2,1,0:T(8,128)(2,1)S(1)}, bf16[2,16,1024]{2,1,0:T(8,128)(2,1)S(1)}, u32[]{:S(2)}, u32[]{:S(2)}) collective-permute-start(bf16[2,16,1024]{2,1,0:T(8,128)(2,1)S(1)} %pad_maximum_fusion.refs_4_), channel_id=1, source_target_pairs={{0,8},{4,12},{8,0},{12,4},{1,9},{5,13},{9,1},{13,5},{2,10},{6,14},... | collective-permute-start | bytes 196616 | tf_op jit(solution)/shard_map/ppermute | solution.py:278
  7.3 6.1 %collective-permute-start = (bf16[2,16,1024]{2,1,0:T(8,128)(2,1)S(1)}, bf16[2,16,1024]{2,1,0:T(8,128)(2,1)S(1)}, u32[]{:S(2)}, u32[]{:S(2)}) collective-permute-start(bf16[2,16,1024]{2,1,0:T(8,128)(2,1)S(1)} %pad_maximum_fusion.refs_4_), channel_id=1, source_target_pairs={{0,12},{4,8},{8,4},{12,0},{1,13},{5,9},{9,5},{13,1},{2,14},{6,10},... | collective-permute-start | bytes 196616 | tf_op jit(solution)/shard_map/ppermute | solution.py:278
  7.3 6.3 %slice-start.1 = ((s8[8388608]{0:T(1024)(128)(4,1)}), s8[4194304]{0:T(1024)(128)(4,1)S(1)}, s32[]{:S(2)}) async-start(s8[8388608]{0:T(1024)(128)(4,1)} %bitcast.7), calls=%async_computation.1 | async-start | bytes 8388608
  7.3 6.3 %slice-start.3 = ((s8[8388608]{0:T(1024)(128)(4,1)}), s8[4194304]{0:T(1024)(128)(4,1)S(1)}, s32[]{:S(2)}) async-start(s8[8388608]{0:T(1024)(128)(4,1)} %bitcast.9), calls=%async_computation.3 | async-start | bytes 8388608
  14.4 1.8 %collective-permute-start.3 = (f32[3,64,512]{2,1,0:T(8,128)S(1)}, f32[3,64,512]{2,1,0:T(8,128)S(1)}, u32[]{:S(2)}, u32[]{:S(2)}) collective-permute-start(f32[3,64,512]{2,1,0:T(8,128)S(1)} %partials.6.refs_8_), channel_id=1, source_target_pairs={{0,1},{1,0},{2,3},{3,2},{4,5},{5,4},{6,7},{7,6},{8,9},{9,8},{10,11... | collective-permute-start | bytes 1179656 | tf_op jit(solution)/shard_map/ppermute | solution.py:281
  15.6 4.2 %collective-permute-start.4 = (f32[3,64,768]{2,1,0:T(8,128)S(1)}, f32[3,64,768]{2,1,0:T(8,128)S(1)}, u32[]{:S(2)}, u32[]{:S(2)}) collective-permute-start(f32[3,64,768]{2,1,0:T(8,128)S(1)} %partials.7.refs_8_), channel_id=1, source_target_pairs={{0,1},{1,0},{2,3},{3,2},{4,5},{5,4},{6,7},{7,6},{8,9},{9,8},{10,11... | collective-permute-start | bytes 1769480 | tf_op jit(solution)/shard_map/ppermute | solution.py:281
  18.1 3.4 %collective-permute-start.5 = (f32[3,64,768]{2,1,0:T(8,128)S(1)}, f32[3,64,768]{2,1,0:T(8,128)S(1)}, u32[]{:S(2)}, u32[]{:S(2)}) collective-permute-start(f32[3,64,768]{2,1,0:T(8,128)S(1)} %partials.9.refs_8_), channel_id=1, source_target_pairs={{0,1},{1,0},{2,3},{3,2},{4,5},{5,4},{6,7},{7,6},{8,9},{9,8},{10,11... | collective-permute-start | bytes 1769480 | tf_op jit(solution)/shard_map/ppermute | solution.py:281
  18.3 7.7 %collective-permute-start.6 = (bf16[3,64,512]{2,1,0:T(8,128)(2,1)S(1)}, bf16[3,64,512]{2,1,0:T(8,128)(2,1)S(1)}, u32[]{:S(2)}, u32[]{:S(2)}) collective-permute-start(bf16[3,64,512]{2,1,0:T(8,128)(2,1)S(1)} %get-tuple-element.52), channel_id=1, source_target_pairs={{0,2},{1,3},{2,0},{3,1},{4,6},{5,7},{6,4},{7,5},{8,10},{9,11},{10,... | collective-permute-start | bytes 589832 | tf_op jit(solution)/shard_map/ppermute | solution.py:285
  20.9 11.3 %collective-permute-start.8 = (bf16[3,64,768]{2,1,0:T(8,128)(2,1)S(1)}, bf16[3,64,768]{2,1,0:T(8,128)(2,1)S(1)}, u32[]{:S(2)}, u32[]{:S(2)}) collective-permute-start(bf16[3,64,768]{2,1,0:T(8,128)(2,1)S(1)} %get-tuple-element.63), channel_id=1, source_target_pairs={{0,2},{1,3},{2,0},{3,1},{4,6},{5,7},{6,4},{7,5},{8,10},{9,11},{10,... | collective-permute-start | bytes 884744 | tf_op jit(solution)/shard_map/ppermute | solution.py:285
  26.1 3.1 %collective-permute-start.7 = (bf16[3,64,512]{2,1,0:T(8,128)(2,1)S(1)}, bf16[3,64,512]{2,1,0:T(8,128)(2,1)S(1)}, u32[]{:S(2)}, u32[]{:S(2)}) collective-permute-start(bf16[3,64,512]{2,1,0:T(8,128)(2,1)S(1)} %activate.3.refs_0_), channel_id=1, source_target_pairs={{0,1},{1,0},{2,3},{3,2},{4,5},{5,4},{6,7},{7,6},{8,9},{9,8},{10,11... | collective-permute-start | bytes 589832 | tf_op jit(solution)/shard_map/ppermute | solution.py:281
  32.4 6.1 %collective-permute-start.9 = (bf16[3,64,768]{2,1,0:T(8,128)(2,1)S(1)}, bf16[3,64,768]{2,1,0:T(8,128)(2,1)S(1)}, u32[]{:S(2)}, u32[]{:S(2)}) collective-permute-start(bf16[3,64,768]{2,1,0:T(8,128)(2,1)S(1)} %activate.4.refs_0_), channel_id=1, source_target_pairs={{0,1},{1,0},{2,3},{3,2},{4,5},{5,4},{6,7},{7,6},{8,9},{9,8},{10,11... | collective-permute-start | bytes 884744 | tf_op jit(solution)/shard_map/ppermute | solution.py:281
  33.0 9.5 %collective-permute-start.10 = (bf16[3,64,768]{2,1,0:T(8,128)(2,1)S(1)}, bf16[3,64,768]{2,1,0:T(8,128)(2,1)S(1)}, u32[]{:S(2)}, u32[]{:S(2)}) collective-permute-start(bf16[3,64,768]{2,1,0:T(8,128)(2,1)S(1)} %get-tuple-element.72), channel_id=1, source_target_pairs={{0,2},{1,3},{2,0},{3,1},{4,6},{5,7},{6,4},{7,5},{8,10},{9,11},{10,... | collective-permute-start | bytes 884744 | tf_op jit(solution)/shard_map/ppermute | solution.py:285
  42.7 1.6 %collective-permute-start.11 = (bf16[3,64,768]{2,1,0:T(8,128)(2,1)S(1)}, bf16[3,64,768]{2,1,0:T(8,128)(2,1)S(1)}, u32[]{:S(2)}, u32[]{:S(2)}) collective-permute-start(bf16[3,64,768]{2,1,0:T(8,128)(2,1)S(1)} %activate.5.refs_0_), channel_id=1, source_target_pairs={{0,1},{1,0},{2,3},{3,2},{4,5},{5,4},{6,7},{7,6},{8,9},{9,8},{10,11... | collective-permute-start | bytes 884744 | tf_op jit(solution)/shard_map/ppermute | solution.py:281
  45.8 11.3 %collective-permute-start.12 = (bf16[2,16,1024]{2,1,0:T(8,128)(2,1)S(1)}, bf16[2,16,1024]{2,1,0:T(8,128)(2,1)S(1)}, u32[]{:S(2)}, u32[]{:S(2)}) collective-permute-start(bf16[2,16,1024]{2,1,0:T(8,128)(2,1)S(1)} %get-tuple-element.74), channel_id=1, source_target_pairs={{0,4},{4,0},{8,12},{12,8},{1,5},{5,1},{9,13},{13,9},{2,6},{6,2},{1... | collective-permute-start | bytes 196616 | tf_op jit(solution)/shard_map/ppermute | solution.py:278
  45.9 11.2 %collective-permute-start.13 = (bf16[2,16,1024]{2,1,0:T(8,128)(2,1)S(1)}, bf16[2,16,1024]{2,1,0:T(8,128)(2,1)S(1)}, u32[]{:S(2)}, u32[]{:S(2)}) collective-permute-start(bf16[2,16,1024]{2,1,0:T(8,128)(2,1)S(1)} %get-tuple-element.75), channel_id=1, source_target_pairs={{0,8},{4,12},{8,0},{12,4},{1,9},{5,13},{9,1},{13,5},{2,10},{6,14},... | collective-permute-start | bytes 196616 | tf_op jit(solution)/shard_map/ppermute | solution.py:278
  48.2 8.9 %collective-permute-start.14 = (bf16[2,16,1024]{2,1,0:T(8,128)(2,1)S(1)}, bf16[2,16,1024]{2,1,0:T(8,128)(2,1)S(1)}, u32[]{:S(2)}, u32[]{:S(2)}) collective-permute-start(bf16[2,16,1024]{2,1,0:T(8,128)(2,1)S(1)} %get-tuple-element.76), channel_id=1, source_target_pairs={{0,12},{4,8},{8,4},{12,0},{1,13},{5,9},{9,5},{13,1},{2,14},{6,10},... | collective-permute-start | bytes 196616 | tf_op jit(solution)/shard_map/ppermute | solution.py:278

commit v13 on v12

--- a/solution.py
+++ b/solution.py
@@ -12,7 +12,7 @@
 MIB = 1024 * 1024
 DEPTH = 256
 ANY = pl.BlockSpec(memory_space=pl.ANY)
-PIECES = [2, 3, 3]
+PIECES = [1, 3, 4]
 SPLIT = 4
 KEPT = ("kg", "ku", "kd")
 MASKS = ("mask_gate", "mask_up", "mask_down_t")
@@ -298,7 +298,8 @@
 
     block = jnp.stack([tokens, grad_out])
     if direct:
-        blocks = [block] + [trade(block, s) for s in range(1, n_grid)]
+        blocks = [block, trade(block, 1), trade(block, 2)]
+        blocks.append(trade(blocks[2], 1))
     else:
         blocks = [lax.all_gather(block, "grid", axis=1, tiled=True)]
 
@@ -386,6 +387,8 @@
             scratch["masked_act"] = pltpu.VMEM((2, pair * rows, size), BF16)
             scratch["masked_cot"] = pltpu.VMEM((spots * rows, width), BF16)
             by_cols, by_rows = 2 * width // (pair * BLK), size // tile
+            if by_rows > 3:
+                by_cols = by_cols * 5 // 8
             scratch["col_slots"] = pltpu.VMEM((by_cols, pair * BLK, size), F32)
             scratch["row_slots"] = pltpu.VMEM((by_rows, tile, width), F32)
             scratch["col_sems"] = pltpu.SemaphoreType.DMA((by_cols,))

time: 57.9 us -> 66 us (1.14)
  waiting for transfers between devices: 8.23 us -> 13.7 us
  starting transfers between devices: 15.2 us -> 16.7 us
  Pallas kernels: 31.7 us -> 32.5 us
    ppermute x3, waiting for transfers between devices: 3.39 us -> 7.76 us  [across(): lax.ppermute(array, 'dp', [(i, (i // 2 + s) % pairs * 2 + i % 2) for i in...]
    ppermute x6, waiting for transfers between devices: 0.15 us -> 2.93 us  [swap(): return lax.ppermute(array, 'dp', [(i, i ^ 1) for i in range(n_dp)])]
    ppermute x6, waiting for transfers between devices: 4.69 us -> 2.99 us  [trade(): return lax.ppermute(array, 'grid', [(i, i ^ s) for i in range(n_grid)])]
    ppermute x6, starting transfers between devices: 10.1 us -> 11.7 us  [trade(): return lax.ppermute(array, 'grid', [(i, i ^ s) for i in range(n_grid)])]
    pallas_call x18, Pallas kernels: 31.7 us -> 32.5 us  [call(): pl.pallas_call(body, out_shape=[shape for shape, _ in outs.values()], in_...]
  transfers between devices with their start and end apart: 15 -> 15, of which waited for: 4 -> 5; matrix products, arithmetic and copies ran while one was open for 0% -> 0% of each run, Pallas kernels for 50% -> 42%
where the time goes in v13:
time: 66 us; the launch traced here: 65.8 us
  Pallas kernels  32.5 us (49%)
  starting transfers between devices  16.7 us (25%)
  waiting for transfers between devices  13.7 us (21%)
  local copies, waits for them, and re-layouts  1.04 us (2%)
  other arithmetic  0.97 us (1%)
  between operations  0.93 us (1%)
    pallas_call x18, Pallas kernels, call(): pl.pallas_call(body, out_shape=[shape for shape, _ in outs.values()], in_...  32.5 us
    ppermute x6, starting transfers between devices, trade(): return lax.ppermute(array, 'grid', [(i, i ^ s) for i in range(n_grid)])  11.7 us
    ppermute x3, waiting for transfers between devices, across(): lax.ppermute(array, 'dp', [(i, (i // 2 + s) % pairs * 2 + i % 2) for i in...  7.76 us
    ppermute x3, starting transfers between devices, across(): lax.ppermute(array, 'dp', [(i, (i // 2 + s) % pairs * 2 + i % 2) for i in...  3.66 us
    ppermute x6, waiting for transfers between devices, trade(): return lax.ppermute(array, 'grid', [(i, i ^ s) for i in range(n_grid)])  2.99 us
    ppermute x6, waiting for transfers between devices, swap(): return lax.ppermute(array, 'dp', [(i, i ^ 1) for i in range(n_dp)])  2.93 us
    ppermute x6, starting transfers between devices, swap(): return lax.ppermute(array, 'dp', [(i, i ^ 1) for i in range(n_dp)])  1.35 us
  transfers between devices with their start and end apart: 15, of which 5 were waited for; matrix products, arithmetic and copies ran while one was open for 0% of the time, Pallas kernels for 42%

profile of v13, /device:TPU:0, one launch (start us, length us, event | category | flops | bytes accessed | tf_op | source)
XLA Modules:
  0.0 65.8 jit_solution(9361305868241433758)
XLA Ops:
  0.6 0.0 copy-start
  0.6 0.0 slice-start.2
  0.7 0.0 slice-start
  0.7 0.9 %pad_maximum_fusion.refs_4_ = bf16[2,16,1024]{2,1,0:T(8,128)(2,1)S(1)} fusion(bf16[1,16,1024]{2,1,0:T(8,128)(2,1)} %bitcast.11, bf16[1,16,1024]{2,1,0:T(8,128)(2,1)} %bitcast.12), kind=kLoop, calls=%fused_computation.1 | loop fusion | flops 32768 | bytes 131072 | tf_op jit(solution)/shard_map/stack | solution.py:299
  1.6 4.1 %collective-permute-start = (bf16[2,16,1024]{2,1,0:T(8,128)(2,1)S(1)}, bf16[2,16,1024]{2,1,0:T(8,128)(2,1)S(1)}, u32[]{:S(2)}, u32[]{:S(2)}) collective-permute-start(bf16[2,16,1024]{2,1,0:T(8,128)(2,1)S(1)} %pad_maximum_fusion.refs_4_), channel_id=1, source_target_pairs={{0,8},{4,12},{8,0},{12,4},{1,9},{5,13},{9,1},{13,5},{2,10},{6,14},... | collective-permute-start | bytes 196616 | tf_op jit(solution)/shard_map/ppermute | solution.py:278
  5.7 1.6 %collective-permute-start.2 = (bf16[2,16,1024]{2,1,0:T(8,128)(2,1)S(1)}, bf16[2,16,1024]{2,1,0:T(8,128)(2,1)S(1)}, u32[]{:S(2)}, u32[]{:S(2)}) collective-permute-start(bf16[2,16,1024]{2,1,0:T(8,128)(2,1)S(1)} %pad_maximum_fusion.refs_4_), channel_id=1, source_target_pairs={{0,4},{4,0},{8,12},{12,8},{1,5},{5,1},{9,13},{13,9},{2,6},{6,2},{1... | collective-permute-start | bytes 196616 | tf_op jit(solution)/shard_map/ppermute | solution.py:278
  7.3 1.5 %collective-permute-done.refs_2_ = bf16[2,16,1024]{2,1,0:T(8,128)(2,1)S(1)} collective-permute-done((bf16[2,16,1024]{2,1,0:T(8,128)(2,1)S(1)}, bf16[2,16,1024]{2,1,0:T(8,128)(2,1)S(1)}, u32[]{:S(2)}, u32[]{:S(2)}) %collective-permute-start) | collective-permute-done | bytes 65568 | tf_op jit(solution)/shard_map/ppermute | solution.py:278
  8.7 1.4 %collective-permute-start.1 = (bf16[2,16,1024]{2,1,0:T(8,128)(2,1)S(1)}, bf16[2,16,1024]{2,1,0:T(8,128)(2,1)S(1)}, u32[]{:S(2)}, u32[]{:S(2)}) collective-permute-start(bf16[2,16,1024]{2,1,0:T(8,128)(2,1)S(1)} %collective-permute-done.refs_2_), channel_id=1, source_target_pairs={{0,4},{4,0},{8,12},{12,8},{1,5},{5,1},{9,13},{13,9},{2,6},{6,2},{1... | collective-permute-start | bytes 196616 | tf_op jit(solution)/shard_map/ppermute | solution.py:278
  10.1 0.0 slice-start.1
  10.1 0.0 slice-start.3
  10.1 1.4 %fetch.1 = (f32[8,1,4096]{2,1,0:T(1,128)S(1)}, f32[8,1,4096]{2,1,0:T(1,128)S(1)}, f32[8,1,4096]{2,1,0:T(1,128)S(1)}, f32[32,1,1024]{2,1,0:T(1,128)S(1)}, f32[32,...) custom-call(bf16[1024,4096]{1,0:T(8,128)(2,1)} %refs_4_.13, bf16[1024,4096]{1,0:T(8,128)(2,1)} %refs_5_.23, ...), custom_call_target="tpu_custom_call" | custom-call | flops 1 | bytes 1 | tf_op jit(solution)/shard_map/fetch/pallas_call | solution.py:44
  11.5 0.0 collective-permute-done.2.refs_3_
  11.5 1.5 %collective-permute-done.1.refs_1_ = bf16[2,16,1024]{2,1,0:T(8,128)(2,1)S(1)} collective-permute-done((bf16[2,16,1024]{2,1,0:T(8,128)(2,1)S(1)}, bf16[2,16,1024]{2,1,0:T(8,128)(2,1)S(1)}, u32[]{:S(2)}, u32[]{:S(2)}) %collective-permute-start.1) | collective-permute-done | bytes 65568 | tf_op jit(solution)/shard_map/ppermute | solution.py:278
  13.0 0.2 assemble.1
  13.2 0.0 copy-done
  13.2 0.0 slice-done.2
  13.2 0.0 slice-done
  13.2 0.0 slice-done.1
  13.2 0.4 slice-done.3
  13.6 0.4 partials.6.refs_8_
  14.1 0.1 collective-permute-start.3
  14.2 1.1 %partials.7.refs_8_ = f32[3,64,768]{2,1,0:T(8,128)S(1)} custom-call(bf16[4,128,256]{2,1,0:T(8,128)(2,1)S(1)} %get-tuple-element.45.refs_0_, bf16[4,128,256]{2,1,0:T(8,128)(2,1)S(1)} %get-tuple-element.46.refs_1_, f32[8,1,4096]{2,1,0:T(1,128)S(1)} %get-tuple-element.44.refs_0_.refs_2_.refs_9_.refs_10_.refs_5_, ...), custom_call_target="tpu_custom_call" | custom-call | flops 1 | bytes 1 | tf_op jit(solution)/shard_map/partials/pallas_call | solution.py:44
  15.3 0.3 collective-permute-done.3.refs_9_
  15.6 0.4 partials.8
  16.0 1.4 %partials.9.refs_8_ = f32[3,64,1024]{2,1,0:T(8,128)S(1)} custom-call(bf16[4,128,256]{2,1,0:T(8,128)(2,1)S(1)} %get-tuple-element.45.refs_0_, bf16[4,128,256]{2,1,0:T(8,128)(2,1)S(1)} %get-tuple-element.46.refs_1_, f32[8,1,4096]{2,1,0:T(1,128)S(1)} %get-tuple-element.44.refs_0_.refs_2_.refs_9_.refs_10_.refs_5_, ...), custom_call_target="tpu_custom_call" | custom-call | flops 1 | bytes 1 | tf_op jit(solution)/shard_map/partials/pallas_call | solution.py:44
  17.5 0.3 collective-permute-start.5
  17.8 0.3 collective-permute-start.4
  18.1 2.6 %collective-permute-done.4.refs_9_ = f32[3,64,768]{2,1,0:T(8,128)S(1)} collective-permute-done((f32[3,64,768]{2,1,0:T(8,128)S(1)}, f32[3,64,768]{2,1,0:T(8,128)S(1)}, u32[]{:S(2)}, u32[]{:S(2)}) %collective-permute-start.4) | collective-permute-done | bytes 589856 | tf_op jit(solution)/shard_map/ppermute | solution.py:281
  20.7 1.1 %partials.10 = (f32[3,64,768]{2,1,0:T(8,128)S(1)}, bf16[3,64,768]{2,1,0:T(8,128)(2,1)S(1)}) custom-call(bf16[4,128,256]{2,1,0:T(8,128)(2,1)S(1)} %get-tuple-element.45.refs_0_, bf16[4,128,256]{2,1,0:T(8,128)(2,1)S(1)} %get-tuple-element.46.refs_1_, f32[8,1,4096]{2,1,0:T(1,128)S(1)} %get-tuple-element.44.refs_0_.refs_2_.refs_9_.refs_10_.refs_5_, ...), custom_call_target="tpu_custom_call" | custom-call | flops 1 | bytes 1 | tf_op jit(solution)/shard_map/partials/pallas_call | solution.py:44
  21.8 1.6 %collective-permute-start.8 = (bf16[3,64,768]{2,1,0:T(8,128)(2,1)S(1)}, bf16[3,64,768]{2,1,0:T(8,128)(2,1)S(1)}, u32[]{:S(2)}, u32[]{:S(2)}) collective-permute-start(bf16[3,64,768]{2,1,0:T(8,128)(2,1)S(1)} %get-tuple-element.63), channel_id=1, source_target_pairs={{0,2},{1,3},{2,0},{3,1},{4,6},{5,7},{6,4},{7,5},{8,10},{9,11},{10,... | collective-permute-start | bytes 884744 | tf_op jit(solution)/shard_map/ppermute | solution.py:285
  23.4 0.5 collective-permute-start.6
  23.9 0.0 collective-permute-done.5.refs_9_
  23.9 1.4 %partials.11 = (f32[3,64,1024]{2,1,0:T(8,128)S(1)}, bf16[3,64,1024]{2,1,0:T(8,128)(2,1)S(1)}) custom-call(bf16[4,128,256]{2,1,0:T(8,128)(2,1)S(1)} %get-tuple-element.45.refs_0_, bf16[4,128,256]{2,1,0:T(8,128)(2,1)S(1)} %get-tuple-element.46.refs_1_, f32[8,1,4096]{2,1,0:T(1,128)S(1)} %get-tuple-element.44.refs_0_.refs_2_.refs_9_.refs_10_.refs_5_, ...), custom_call_target="tpu_custom_call" | custom-call | flops 1 | bytes 1 | tf_op jit(solution)/shard_map/partials/pallas_call | solution.py:44
  25.3 7.8 %collective-permute-done.6.refs_2_ = bf16[3,64,256]{2,1,0:T(8,128)(2,1)S(1)} collective-permute-done((bf16[3,64,256]{2,1,0:T(8,128)(2,1)S(1)}, bf16[3,64,256]{2,1,0:T(8,128)(2,1)S(1)}, u32[]{:S(2)}, u32[]{:S(2)}) %collective-permute-start.6) | collective-permute-done | bytes 98336 | tf_op jit(solution)/shard_map/ppermute | solution.py:285
  33.2 0.1 collective-permute-start.7
  33.2 1.6 %collective-permute-start.10 = (bf16[3,64,1024]{2,1,0:T(8,128)(2,1)S(1)}, bf16[3,64,1024]{2,1,0:T(8,128)(2,1)S(1)}, u32[]{:S(2)}, u32[]{:S(2)}) collective-permute-start(bf16[3,64,1024]{2,1,0:T(8,128)(2,1)S(1)} %get-tuple-element.72), channel_id=1, source_target_pairs={{0,2},{1,3},{2,0},{3,1},{4,6},{5,7},{6,4},{7,5},{8,10},{9,11},{10,... | collective-permute-start | bytes 1179656 | tf_op jit(solution)/shard_map/ppermute | solution.py:285
  34.8 2.0 %back_rows_grads.4 = (f32[2,64,1024]{2,1,0:T(8,128)S(1)}, f32[1024,4096]{1,0:T(8,128)}, f32[1024,4096]{1,0:T(8,128)}, f32[4096,1024]{1,0:T(8,128)}) custom-call(bf16[3,64,256]{2,1,0:T(8,128)(2,1)S(1)} %activate.3.refs_0_, f32[32,1,1024]{2,1,0:T(1,128)S(1)} %get-tuple-element.53.refs_1_.refs_2_, f32[32,1,1024]{2,1,0:T(1,128)S(1)} %get-tuple-element.54.refs_2_, ...), custom_call_target="tpu_custom_call" | custom-call | flops 1 | bytes 1 | tf_op jit(solution)/shard_map/back_rows_grads/pallas_call | solution.py:44
  36.8 0.0 collective-permute-done.7.refs_0_
  36.8 2.0 %back_rows_grads.5 = (f32[2,64,1024]{2,1,0:T(8,128)S(1)}, f32[1024,4096]{1,0:T(8,128)}, f32[1024,4096]{1,0:T(8,128)}, f32[4096,1024]{1,0:T(8,128)}) custom-call(bf16[3,64,256]{2,1,0:T(8,128)(2,1)S(1)} %collective-permute-done.7.refs_0_, ...), custom_call_target="tpu_custom_call", output_to_operand_aliasing={{1}: (12, {}), {2}: (13, {}), {3}: (14, {})} | custom-call | flops 1 | bytes 1 | tf_op jit(solution)/shard_map/back_rows_grads/pallas_call | solution.py:44
  38.8 0.0 collective-permute-done.8.refs_2_
  38.8 0.1 activate.4.refs_0_
  39.0 0.2 collective-permute-start.9
  39.2 4.0 %back_rows_grads.6 = (f32[2,64,1024]{2,1,0:T(8,128)S(1)}, f32[1024,4096]{1,0:T(8,128)}, f32[1024,4096]{1,0:T(8,128)}, f32[4096,1024]{1,0:T(8,128)}) custom-call(bf16[3,64,768]{2,1,0:T(8,128)(2,1)S(1)} %activate.4.refs_0_, f32[32,1,1024]{2,1,0:T(1,128)S(1)} %get-tuple-element.53.refs_1_.refs_2_, ...), custom_call_target="tpu_custom_call", output_to_operand_aliasing={{1}: (12, {}), {2}: (13, {}), {3}: (14, {})} | custom-call | flops 1 | bytes 1 | tf_op jit(solution)/shard_map/back_rows_grads/pallas_call | solution.py:44
  43.2 0.0 collective-permute-done.9.refs_0_
  43.2 4.0 %back_rows_grads.7 = (f32[2,64,1024]{2,1,0:T(8,128)S(1)}, f32[1024,4096]{1,0:T(8,128)}, f32[1024,4096]{1,0:T(8,128)}, f32[4096,1024]{1,0:T(8,128)}) custom-call(bf16[3,64,768]{2,1,0:T(8,128)(2,1)S(1)} %collective-permute-done.9.refs_0_, ...), custom_call_target="tpu_custom_call", output_to_operand_aliasing={{1}: (12, {}), {2}: (13, {}), {3}: (14, {})} | custom-call | flops 1 | bytes 1 | tf_op jit(solution)/shard_map/back_rows_grads/pallas_call | solution.py:44
  47.3 0.0 collective-permute-done.10.refs_2_
  47.3 0.2 activate.5.refs_0_
  47.5 0.4 collective-permute-start.11
  47.9 1.9 %back_rows.2.refs_7_ = f32[2,64,1024]{2,1,0:T(8,128)S(1)} custom-call(bf16[3,64,1024]{2,1,0:T(8,128)(2,1)S(1)} %activate.5.refs_0_, f32[32,1,1024]{2,1,0:T(1,128)S(1)} %get-tuple-element.53.refs_1_.refs_2_, f32[32,1,1024]{2,1,0:T(1,128)S(1)} %get-tuple-element.54.refs_2_, f32[32,1,1024]{2,1,0:T(1,128)S(1)} %get-tuple-element.55.refs_3_, ...), custom_call_target="tpu_custom_call" | custom-call | flops 1 | bytes 1 | tf_op jit(solution)/shard_map/back_rows/pallas_call | solution.py:44
  49.8 0.0 collective-permute-done.11.refs_0_.refs_1_
  49.8 1.9 %back_rows.3 = (bf16[2,16,1024]{2,1,0:T(8,128)(2,1)S(1)}, bf16[2,16,1024]{2,1,0:T(8,128)(2,1)S(1)}, bf16[2,16,1024]{2,1,0:T(8,128)(2,1)S(1)}, bf16[2,16,1024]{2,1,0:T(8,128)(2,1)S(1)}) custom-call(bf16[3,64,1024]{2,1,0:T(8,128)(2,1)S(1)} %collective-permute-done.11.refs_0_.refs_1_, f32[32,1,1024]{2,1,0:T(1,128)S(1)} %get-tuple-element.53.refs_1_.refs_2_, ...), custom_call_target="tpu_custom_call" | custom-call | flops 1 | bytes 1 | tf_op jit(solution)/shard_map/back_rows/pallas_call | solution.py:44
  51.7 1.1 %collective-permute-start.12 = (bf16[2,16,1024]{2,1,0:T(8,128)(2,1)S(1)}, bf16[2,16,1024]{2,1,0:T(8,128)(2,1)S(1)}, u32[]{:S(2)}, u32[]{:S(2)}) collective-permute-start(bf16[2,16,1024]{2,1,0:T(8,128)(2,1)S(1)} %get-tuple-element.74), channel_id=1, source_target_pairs={{0,4},{4,0},{8,12},{12,8},{1,5},{5,1},{9,13},{13,9},{2,6},{6,2},{1... | collective-permute-start | bytes 196616 | tf_op jit(solution)/shard_map/ppermute | solution.py:278
  52.8 3.2 %collective-permute-start.13 = (bf16[2,16,1024]{2,1,0:T(8,128)(2,1)S(1)}, bf16[2,16,1024]{2,1,0:T(8,128)(2,1)S(1)}, u32[]{:S(2)}, u32[]{:S(2)}) collective-permute-start(bf16[2,16,1024]{2,1,0:T(8,128)(2,1)S(1)} %get-tuple-element.75), channel_id=1, source_target_pairs={{0,8},{4,12},{8,0},{12,4},{1,9},{5,13},{9,1},{13,5},{2,10},{6,14},... | collective-permute-start | bytes 196616 | tf_op jit(solution)/shard_map/ppermute | solution.py:278
  56.0 0.4 collective-permute-start.14
  56.4 8.7 %back_grads.1 = (f32[1024,4096]{1,0:T(8,128)}, f32[1024,4096]{1,0:T(8,128)}, f32[4096,1024]{1,0:T(8,128)}) custom-call(bf16[3,64,1024]{2,1,0:T(8,128)(2,1)S(1)} %activate.5.refs_0_, bf16[3,64,1024]{2,1,0:T(8,128)(2,1)S(1)} %collective-permute-done.11.refs_0_.refs_1_, ...), custom_call_target="tpu_custom_call", output_to_operand_aliasing={{0}: (7, {}), {1}: (8, {}), {2}: (9, {})} | custom-call | flops 1 | bytes 1 | tf_op jit(solution)/shard_map/back_grads/pallas_call | solution.py:44
  65.1 0.0 collective-permute-done.12
  65.1 0.0 collective-permute-done.13
  65.1 0.0 collective-permute-done.14
  65.2 0.6 slice_bitcast_fusion
  (4 shorter events, 0.1 us)
Async XLA Ops:
  0.6 12.6 %copy-start = (bf16[4096,1024]{1,0:T(8,128)(2,1)S(1)}, bf16[4096,1024]{1,0:T(8,128)(2,1)}, u32[]{:S(2)}) copy-start(bf16[4096,1024]{1,0:T(8,128)(2,1)} %refs_6_.23) | copy-start | bytes 25165828
  0.6 12.6 %slice-start.2 = ((s8[8388608]{0:T(1024)(128)(4,1)}), s8[4194304]{0:T(1024)(128)(4,1)S(1)}, s32[]{:S(2)}) async-start(s8[8388608]{0:T(1024)(128)(4,1)} %bitcast.9), calls=%async_computation.2 | async-start | bytes 8388608
  0.7 12.6 %slice-start = ((s8[8388608]{0:T(1024)(128)(4,1)}), s8[4194304]{0:T(1024)(128)(4,1)S(1)}, s32[]{:S(2)}) async-start(s8[8388608]{0:T(1024)(128)(4,1)} %bitcast.7), calls=%async_computation | async-start | bytes 8388608
  1.6 7.1 %collective-permute-start = (bf16[2,16,1024]{2,1,0:T(8,128)(2,1)S(1)}, bf16[2,16,1024]{2,1,0:T(8,128)(2,1)S(1)}, u32[]{:S(2)}, u32[]{:S(2)}) collective-permute-start(bf16[2,16,1024]{2,1,0:T(8,128)(2,1)S(1)} %pad_maximum_fusion.refs_4_), channel_id=1, source_target_pairs={{0,8},{4,12},{8,0},{12,4},{1,9},{5,13},{9,1},{13,5},{2,10},{6,14},... | collective-permute-start | bytes 196616 | tf_op jit(solution)/shard_map/ppermute | solution.py:278
  5.7 5.8 %collective-permute-start.2 = (bf16[2,16,1024]{2,1,0:T(8,128)(2,1)S(1)}, bf16[2,16,1024]{2,1,0:T(8,128)(2,1)S(1)}, u32[]{:S(2)}, u32[]{:S(2)}) collective-permute-start(bf16[2,16,1024]{2,1,0:T(8,128)(2,1)S(1)} %pad_maximum_fusion.refs_4_), channel_id=1, source_target_pairs={{0,4},{4,0},{8,12},{12,8},{1,5},{5,1},{9,13},{13,9},{2,6},{6,2},{1... | collective-permute-start | bytes 196616 | tf_op jit(solution)/shard_map/ppermute | solution.py:278
  8.7 4.3 %collective-permute-start.1 = (bf16[2,16,1024]{2,1,0:T(8,128)(2,1)S(1)}, bf16[2,16,1024]{2,1,0:T(8,128)(2,1)S(1)}, u32[]{:S(2)}, u32[]{:S(2)}) collective-permute-start(bf16[2,16,1024]{2,1,0:T(8,128)(2,1)S(1)} %collective-permute-done.refs_2_), channel_id=1, source_target_pairs={{0,4},{4,0},{8,12},{12,8},{1,5},{5,1},{9,13},{13,9},{2,6},{6,2},{1... | collective-permute-start | bytes 196616 | tf_op jit(solution)/shard_map/ppermute | solution.py:278
  10.1 3.1 %slice-start.1 = ((s8[8388608]{0:T(1024)(128)(4,1)}), s8[4194304]{0:T(1024)(128)(4,1)S(1)}, s32[]{:S(2)}) async-start(s8[8388608]{0:T(1024)(128)(4,1)} %bitcast.7), calls=%async_computation.1 | async-start | bytes 8388608
  10.1 3.5 %slice-start.3 = ((s8[8388608]{0:T(1024)(128)(4,1)}), s8[4194304]{0:T(1024)(128)(4,1)S(1)}, s32[]{:S(2)}) async-start(s8[8388608]{0:T(1024)(128)(4,1)} %bitcast.9), calls=%async_computation.3 | async-start | bytes 8388608
  14.1 1.5 %collective-permute-start.3 = (f32[3,64,256]{2,1,0:T(8,128)S(1)}, f32[3,64,256]{2,1,0:T(8,128)S(1)}, u32[]{:S(2)}, u32[]{:S(2)}) collective-permute-start(f32[3,64,256]{2,1,0:T(8,128)S(1)} %partials.6.refs_8_), channel_id=1, source_target_pairs={{0,1},{1,0},{2,3},{3,2},{4,5},{5,4},{6,7},{7,6},{8,9},{9,8},{10,11... | collective-permute-start | bytes 589832 | tf_op jit(solution)/shard_map/ppermute | solution.py:281
  17.5 6.4 %collective-permute-start.5 = (f32[3,64,1024]{2,1,0:T(8,128)S(1)}, f32[3,64,1024]{2,1,0:T(8,128)S(1)}, u32[]{:S(2)}, u32[]{:S(2)}) collective-permute-start(f32[3,64,1024]{2,1,0:T(8,128)S(1)} %partials.9.refs_8_), channel_id=1, source_target_pairs={{0,1},{1,0},{2,3},{3,2},{4,5},{5,4},{6,7},{7,6},{8,9},{9,8},{10,11... | collective-permute-start | bytes 2359304 | tf_op jit(solution)/shard_map/ppermute | solution.py:281
  17.8 2.9 %collective-permute-start.4 = (f32[3,64,768]{2,1,0:T(8,128)S(1)}, f32[3,64,768]{2,1,0:T(8,128)S(1)}, u32[]{:S(2)}, u32[]{:S(2)}) collective-permute-start(f32[3,64,768]{2,1,0:T(8,128)S(1)} %partials.7.refs_8_), channel_id=1, source_target_pairs={{0,1},{1,0},{2,3},{3,2},{4,5},{5,4},{6,7},{7,6},{8,9},{9,8},{10,11... | collective-permute-start | bytes 1769480 | tf_op jit(solution)/shard_map/ppermute | solution.py:281
  21.8 17.0 %collective-permute-start.8 = (bf16[3,64,768]{2,1,0:T(8,128)(2,1)S(1)}, bf16[3,64,768]{2,1,0:T(8,128)(2,1)S(1)}, u32[]{:S(2)}, u32[]{:S(2)}) collective-permute-start(bf16[3,64,768]{2,1,0:T(8,128)(2,1)S(1)} %get-tuple-element.63), channel_id=1, source_target_pairs={{0,2},{1,3},{2,0},{3,1},{4,6},{5,7},{6,4},{7,5},{8,10},{9,11},{10,... | collective-permute-start | bytes 884744 | tf_op jit(solution)/shard_map/ppermute | solution.py:285
  23.4 9.7 %collective-permute-start.6 = (bf16[3,64,256]{2,1,0:T(8,128)(2,1)S(1)}, bf16[3,64,256]{2,1,0:T(8,128)(2,1)S(1)}, u32[]{:S(2)}, u32[]{:S(2)}) collective-permute-start(bf16[3,64,256]{2,1,0:T(8,128)(2,1)S(1)} %get-tuple-element.52), channel_id=1, source_target_pairs={{0,2},{1,3},{2,0},{3,1},{4,6},{5,7},{6,4},{7,5},{8,10},{9,11},{10,... | collective-permute-start | bytes 294920 | tf_op jit(solution)/shard_map/ppermute | solution.py:285
  33.2 3.7 %collective-permute-start.7 = (bf16[3,64,256]{2,1,0:T(8,128)(2,1)S(1)}, bf16[3,64,256]{2,1,0:T(8,128)(2,1)S(1)}, u32[]{:S(2)}, u32[]{:S(2)}) collective-permute-start(bf16[3,64,256]{2,1,0:T(8,128)(2,1)S(1)} %activate.3.refs_0_), channel_id=1, source_target_pairs={{0,1},{1,0},{2,3},{3,2},{4,5},{5,4},{6,7},{7,6},{8,9},{9,8},{10,11... | collective-permute-start | bytes 294920 | tf_op jit(solution)/shard_map/ppermute | solution.py:281
  33.2 14.0 %collective-permute-start.10 = (bf16[3,64,1024]{2,1,0:T(8,128)(2,1)S(1)}, bf16[3,64,1024]{2,1,0:T(8,128)(2,1)S(1)}, u32[]{:S(2)}, u32[]{:S(2)}) collective-permute-start(bf16[3,64,1024]{2,1,0:T(8,128)(2,1)S(1)} %get-tuple-element.72), channel_id=1, source_target_pairs={{0,2},{1,3},{2,0},{3,1},{4,6},{5,7},{6,4},{7,5},{8,10},{9,11},{10,... | collective-permute-start | bytes 1179656 | tf_op jit(solution)/shard_map/ppermute | solution.py:285
  39.0 4.2 %collective-permute-start.9 = (bf16[3,64,768]{2,1,0:T(8,128)(2,1)S(1)}, bf16[3,64,768]{2,1,0:T(8,128)(2,1)S(1)}, u32[]{:S(2)}, u32[]{:S(2)}) collective-permute-start(bf16[3,64,768]{2,1,0:T(8,128)(2,1)S(1)} %activate.4.refs_0_), channel_id=1, source_target_pairs={{0,1},{1,0},{2,3},{3,2},{4,5},{5,4},{6,7},{7,6},{8,9},{9,8},{10,11... | collective-permute-start | bytes 884744 | tf_op jit(solution)/shard_map/ppermute | solution.py:281
  47.5 2.3 %collective-permute-start.11 = (bf16[3,64,1024]{2,1,0:T(8,128)(2,1)S(1)}, bf16[3,64,1024]{2,1,0:T(8,128)(2,1)S(1)}, u32[]{:S(2)}, u32[]{:S(2)}) collective-permute-start(bf16[3,64,1024]{2,1,0:T(8,128)(2,1)S(1)} %activate.5.refs_0_), channel_id=1, source_target_pairs={{0,1},{1,0},{2,3},{3,2},{4,5},{5,4},{6,7},{7,6},{8,9},{9,8},{10,11... | collective-permute-start | bytes 1179656 | tf_op jit(solution)/shard_map/ppermute | solution.py:281
  51.7 13.4 %collective-permute-start.12 = (bf16[2,16,1024]{2,1,0:T(8,128)(2,1)S(1)}, bf16[2,16,1024]{2,1,0:T(8,128)(2,1)S(1)}, u32[]{:S(2)}, u32[]{:S(2)}) collective-permute-start(bf16[2,16,1024]{2,1,0:T(8,128)(2,1)S(1)} %get-tuple-element.74), channel_id=1, source_target_pairs={{0,4},{4,0},{8,12},{12,8},{1,5},{5,1},{9,13},{13,9},{2,6},{6,2},{1... | collective-permute-start | bytes 196616 | tf_op jit(solution)/shard_map/ppermute | solution.py:278
  52.8 12.4 %collective-permute-start.13 = (bf16[2,16,1024]{2,1,0:T(8,128)(2,1)S(1)}, bf16[2,16,1024]{2,1,0:T(8,128)(2,1)S(1)}, u32[]{:S(2)}, u32[]{:S(2)}) collective-permute-start(bf16[2,16,1024]{2,1,0:T(8,128)(2,1)S(1)} %get-tuple-element.75), channel_id=1, source_target_pairs={{0,8},{4,12},{8,0},{12,4},{1,9},{5,13},{9,1},{13,5},{2,10},{6,14},... | collective-permute-start | bytes 196616 | tf_op jit(solution)/shard_map/ppermute | solution.py:278
  56.0 9.2 %collective-permute-start.14 = (bf16[2,16,1024]{2,1,0:T(8,128)(2,1)S(1)}, bf16[2,16,1024]{2,1,0:T(8,128)(2,1)S(1)}, u32[]{:S(2)}, u32[]{:S(2)}) collective-permute-start(bf16[2,16,1024]{2,1,0:T(8,128)(2,1)S(1)} %get-tuple-element.76), channel_id=1, source_target_pairs={{0,12},{4,8},{8,4},{12,0},{1,13},{5,9},{9,5},{13,1},{2,14},{6,10},... | collective-permute-start | bytes 196616 | tf_op jit(solution)/shard_map/ppermute | solution.py:278

commit v14 on v11

--- a/solution.py
+++ b/solution.py
@@ -12,7 +12,7 @@
 MIB = 1024 * 1024
 DEPTH = 256
 ANY = pl.BlockSpec(memory_space=pl.ANY)
-PIECES = [2, 3, 3]
+PIECES = [2,3,3]
 SPLIT = 4
 KEPT = ("kg", "ku", "kd")
 MASKS = ("mask_gate", "mask_up", "mask_down_t")
@@ -98,11 +98,6 @@
 
 def fetch_kernel(r):
     copies = []
-    for source, target in ((r.w_gate, r.kg), (r.w_up, r.ku), (r.w_down, r.kd)):
-        height = source.shape[0] // SPLIT
-        for k in range(SPLIT):
-            rows = slice(k * height, (k + 1) * height)
-            copies.append((source.at[rows, :], target.at[rows, :]))
     for k in MASKS:
         copies.append((getattr(r, "hbm_" + k), getattr(r, k)))
     copies = [pltpu.make_async_copy(a, b, r.sems.at[k]) for k, (a, b) in enumerate(copies)]
@@ -183,7 +178,7 @@
 
 
 def add_rows(r, i, block, at):
-    width, tile = r.acc.shape[2], r.act_d.shape[3]
+    width, tile = r.acc.shape[2], r.act_d.shape[4]
     size = min(DEPTH, width)
     for f in range(0, width, size):
         part = slice(f, f + size)
@@ -191,10 +186,10 @@
         def masks(mask):
             return [mask[block + b][:, part] for b in range(tile // BLK)]
 
-        r.acc[0, :, part] += masked_sum(r.act_d[i, 0], r.kd[at, part], masks(r.md))
+        r.acc[0, :, part] += masked_sum(r.act_d[*i, 0], r.kd[at, part], masks(r.md))
         r.acc[1, :, part] += masked_sum(
-            r.act_d[i, 1], r.kg[part, at], masks(r.mgt), (1, 1)
-        ) + masked_sum(r.act_d[i, 2], r.ku[part, at], masks(r.mut), (1, 1))
+            r.act_d[*i, 1], r.kg[part, at], masks(r.mgt), (1, 1)
+        ) + masked_sum(r.act_d[*i, 2], r.ku[part, at], masks(r.mut), (1, 1))
 
 
 class Outbox:
@@ -218,14 +213,15 @@
 
 
 def back_kernel(items, half, do_rows, do_grads, r):
-    tile = r.act_d.shape[3]
+    tile = r.act_d.shape[4]
     spots = tile // BLK
     if do_rows:
         r.acc[...] = r.sums[...] if hasattr(r, "sums") else jnp.zeros_like(r.acc)
     if do_grads:
         groups, height, _ = r.tok_t.shape
         by_cols, by_rows = Outbox(r.col_slots, r.col_sems), Outbox(r.row_slots, r.row_sems)
-    for act, which, start in items:
+    waiting = []
+    for n, (act, which, start) in enumerate(items):
         act = getattr(r, act)
         _, rows, size = act.shape
         base = first_unit(which, half) + start
@@ -239,19 +235,21 @@
                     keep = mask[i * (height // BLK) + j, :, at].astype(BF16)
                     right[j * rows : (j + 1) * rows, :] = act[k] * keep
                 by_cols.put(dot(r.tok_t[i], right[...]), out.at[band, at])
-        if act is r.act0:
+        if n == 0:
             r.act_d[...] = jnp.zeros_like(r.act_d)
         for i, local in enumerate(tiles):
             for k in range(3 if do_rows else 1):
-                diagonal(r.act_d.at[i, k], act[k, :, local])
+                diagonal(r.act_d.at[n, i, k], act[k, :, local])
             if do_grads:
                 for b in range(spots):
                     keep = r.md[block + i * spots + b].astype(BF16)
                     r.masked_cot[b * rows : (b + 1) * rows, :] = r.cot[...] * keep
-                value = dot(r.act_d[i, 0].T, r.masked_cot[...])
+                value = dot(r.act_d[n, i, 0].T, r.masked_cot[...])
                 by_rows.put(value, r.gd.at[span(base + i * tile, tile), :])
-        for i in range(len(tiles) if do_rows else 0):
-            add_rows(r, i, block + i * spots, span(base + i * tile, tile))
+        if do_rows:
+            waiting += [(n, i, block + i * spots, base + i * tile) for i in range(len(tiles))]
+    for n, i, block, start in waiting:
+        add_rows(r, (n, i), block, span(start, tile))
     if do_rows:
         if hasattr(r, "new_sums"):
             r.new_sums[...] = r.acc[...]
@@ -317,7 +315,6 @@
         {
             **{k: pinned(across_shape) for k in ("mg", "mu", "mdt")},
             **{k: pinned(along_shape) for k in ("mgt", "mut", "md")},
-            **{k: pinned(shape(*w.shape)) for k, w in zip(KEPT, (w_gate, w_up, w_down))},
         },
         scratch={
             **{k: pltpu.VMEM(m.shape, m.dtype) for k, m in masks.items()},
@@ -326,6 +323,7 @@
         vmem=grant(4),
     )
 
+    values.update(kg=w_gate, ku=w_up, kd=w_down)
     pair = min(DEPTH, width) // BLK
     pair_shape = shape(width // (pair * BLK), pair * rows, pair * BLK)
     values |= call(
@@ -371,7 +369,7 @@
         ins.update(held("md"))
         outs, aliases = {}, {}
         spots, size = tile // BLK, split[pieces[0][1]]
-        scratch = {"act_d": pltpu.VMEM((size // tile, 3, spots * rows, tile), BF16)}
+        scratch = {"act_d": pltpu.VMEM((len(pieces), size // tile, 3, spots * rows, tile), BF16)}
         if do_rows:
             ins.update(held("mgt", "mut", *KEPT))
             scratch["acc"] = pltpu.VMEM((2, rows, width), F32)
@@ -428,13 +426,13 @@
         last = p == n - 1
         act = activate(sums[p], theirs[p], state.get("sums", after))
         act_other = swap(act)
-        both_halves = [(0, p, act), (1, p, act_other)]
+        if 0 < p < n - 1:
+            state = back([(0, p, act), (1, p, act_other)], True, True, state)
+            continue
+        state = back([(0, p, act)], True, not last, state)
+        state = back([(1, p, act_other)], True, not last, state, last)
         if last:
-            state = back(both_halves[:1], True, False, state)
-            state = back(both_halves[1:], True, False, state, last)
-            state = back(both_halves, False, True, state)
-        else:
-            state = back(both_halves, True, True, state)
+            state = back([(0, p, act), (1, p, act_other)], False, True, state)
 
     if direct:
         both = state["rows0"].astype(F32)

time: 61 us -> 58.2 us (0.954)
  Pallas kernels: 38.4 us -> 32 us
  waiting for transfers between devices: 4.91 us -> 8.18 us
    pallas_call x16 -> x17, Pallas kernels: 38.4 us -> 32 us  [call(): pl.pallas_call(body, out_shape=[shape for shape, _ in outs.values()], in_...]
    ppermute x6, waiting for transfers between devices: 0.02 us -> 4.69 us  [trade(): return lax.ppermute(array, 'grid', [(i, i ^ s) for i in range(n_grid)])]
    ppermute x6, waiting for transfers between devices: 1.51 us -> 0.11 us  [swap(): return lax.ppermute(array, 'dp', [(i, i ^ 1) for i in range(n_dp)])]
  transfers between devices with their start and end apart: 15 -> 15, of which waited for: 2 -> 4; matrix products, arithmetic and copies ran while one was open for 0% -> 0% of each run, Pallas kernels for 59% -> 50%
where the time goes in v14:
time: 58.2 us; the launch traced here: 58 us
  Pallas kernels  32 us (55%)
  starting transfers between devices  15.3 us (26%)
  waiting for transfers between devices  8.18 us (14%)
  other arithmetic  0.97 us (2%)
  between operations  0.94 us (2%)
  local copies, waits for them, and re-layouts  0.66 us (1%)
    pallas_call x17, Pallas kernels, call(): pl.pallas_call(body, out_shape=[shape for shape, _ in outs.values()], in_...  32 us
    ppermute x6, starting transfers between devices, trade(): return lax.ppermute(array, 'grid', [(i, i ^ s) for i in range(n_grid)])  10.1 us
    ppermute x6, waiting for transfers between devices, trade(): return lax.ppermute(array, 'grid', [(i, i ^ s) for i in range(n_grid)])  4.69 us
    ppermute x3, starting transfers between devices, across(): lax.ppermute(array, 'dp', [(i, (i // 2 + s) % pairs * 2 + i % 2) for i in...  3.6 us
    ppermute x3, waiting for transfers between devices, across(): lax.ppermute(array, 'dp', [(i, (i // 2 + s) % pairs * 2 + i % 2) for i in...  3.39 us
    ppermute x6, starting transfers between devices, swap(): return lax.ppermute(array, 'dp', [(i, i ^ 1) for i in range(n_dp)])  1.58 us
  transfers between devices with their start and end apart: 15, of which 4 were waited for; matrix products, arithmetic and copies ran while one was open for 0% of the time, Pallas kernels for 50%

profile of v14, /device:TPU:0, one launch (start us, length us, event | category | flops | bytes accessed | tf_op | source)
XLA Modules:
  0.0 58.0 jit_solution(12087157814965046793)
XLA Ops:
  0.6 0.0 copy-start
  0.6 0.0 slice-start.2
  0.7 0.0 slice-start
  0.7 0.9 %pad_maximum_fusion.refs_4_ = bf16[2,16,1024]{2,1,0:T(8,128)(2,1)S(1)} fusion(bf16[1,16,1024]{2,1,0:T(8,128)(2,1)} %bitcast.11, bf16[1,16,1024]{2,1,0:T(8,128)(2,1)} %bitcast.12), kind=kLoop, calls=%fused_computation.1 | loop fusion | flops 32768 | bytes 131072 | tf_op jit(solution)/shard_map/stack | solution.py:302
  1.6 3.1 %collective-permute-start.2 = (bf16[2,16,1024]{2,1,0:T(8,128)(2,1)S(1)}, bf16[2,16,1024]{2,1,0:T(8,128)(2,1)S(1)}, u32[]{:S(2)}, u32[]{:S(2)}) collective-permute-start(bf16[2,16,1024]{2,1,0:T(8,128)(2,1)S(1)} %pad_maximum_fusion.refs_4_), channel_id=1, source_target_pairs={{0,4},{4,0},{8,12},{12,8},{1,5},{5,1},{9,13},{13,9},{2,6},{6,2},{1... | collective-permute-start | bytes 196616 | tf_op jit(solution)/shard_map/ppermute | solution.py:281
  4.7 2.6 %collective-permute-start.1 = (bf16[2,16,1024]{2,1,0:T(8,128)(2,1)S(1)}, bf16[2,16,1024]{2,1,0:T(8,128)(2,1)S(1)}, u32[]{:S(2)}, u32[]{:S(2)}) collective-permute-start(bf16[2,16,1024]{2,1,0:T(8,128)(2,1)S(1)} %pad_maximum_fusion.refs_4_), channel_id=1, source_target_pairs={{0,8},{4,12},{8,0},{12,4},{1,9},{5,13},{9,1},{13,5},{2,10},{6,14},... | collective-permute-start | bytes 196616 | tf_op jit(solution)/shard_map/ppermute | solution.py:281
  7.3 0.0 collective-permute-start
  7.3 0.0 slice-start.1
  7.3 0.0 slice-start.3
  7.3 1.4 %fetch.1 = (f32[8,1,4096]{2,1,0:T(1,128)S(1)}, f32[8,1,4096]{2,1,0:T(1,128)S(1)}, f32[8,1,4096]{2,1,0:T(1,128)S(1)}, f32[32,1,1024]{2,1,0:T(1,128)S(1)}, f32[32,...) custom-call(bf16[1024,4096]{1,0:T(8,128)(2,1)} %refs_4_.9, bf16[1024,4096]{1,0:T(8,128)(2,1)} %refs_5_.21, ...), custom_call_target="tpu_custom_call" | custom-call | flops 1 | bytes 1 | tf_op jit(solution)/shard_map/fetch/pallas_call | solution.py:44
  8.7 0.0 collective-permute-done.2.refs_3_
  8.7 3.3 %collective-permute-done.1.refs_2_ = bf16[2,16,1024]{2,1,0:T(8,128)(2,1)S(1)} collective-permute-done((bf16[2,16,1024]{2,1,0:T(8,128)(2,1)S(1)}, bf16[2,16,1024]{2,1,0:T(8,128)(2,1)S(1)}, u32[]{:S(2)}, u32[]{:S(2)}) %collective-permute-start.1) | collective-permute-done | bytes 65568 | tf_op jit(solution)/shard_map/ppermute | solution.py:281
  11.9 1.4 %collective-permute-done.refs_1_ = bf16[2,16,1024]{2,1,0:T(8,128)(2,1)S(1)} collective-permute-done((bf16[2,16,1024]{2,1,0:T(8,128)(2,1)S(1)}, bf16[2,16,1024]{2,1,0:T(8,128)(2,1)S(1)}, u32[]{:S(2)}, u32[]{:S(2)}) %collective-permute-start) | collective-permute-done | bytes 65568 | tf_op jit(solution)/shard_map/ppermute | solution.py:281
  13.3 0.2 assemble.1
  13.5 0.0 copy-done
  13.5 0.0 slice-done.2
  13.6 0.0 slice-done
  13.6 0.0 slice-done.1
  13.6 0.0 slice-done.3
  13.6 0.8 %partials.6.refs_8_ = f32[3,64,512]{2,1,0:T(8,128)S(1)} custom-call(bf16[4,128,256]{2,1,0:T(8,128)(2,1)S(1)} %get-tuple-element.41.refs_0_, bf16[4,128,256]{2,1,0:T(8,128)(2,1)S(1)} %get-tuple-element.42.refs_1_, f32[8,1,4096]{2,1,0:T(1,128)S(1)} %get-tuple-element.40.refs_0_.refs_2_.refs_9_.refs_10_.refs_11_.refs_5_, ...), custom_call_target="tpu_custom_call" | custom-call | flops 1 | bytes 1 | tf_op jit(solution)/shard_map/partials/pallas_call | solution.py:44
  14.4 0.1 collective-permute-start.3
  14.5 1.1 %partials.7.refs_8_ = f32[3,64,768]{2,1,0:T(8,128)S(1)} custom-call(bf16[4,128,256]{2,1,0:T(8,128)(2,1)S(1)} %get-tuple-element.41.refs_0_, bf16[4,128,256]{2,1,0:T(8,128)(2,1)S(1)} %get-tuple-element.42.refs_1_, f32[8,1,4096]{2,1,0:T(1,128)S(1)} %get-tuple-element.40.refs_0_.refs_2_.refs_9_.refs_10_.refs_11_.refs_5_, ...), custom_call_target="tpu_custom_call" | custom-call | flops 1 | bytes 1 | tf_op jit(solution)/shard_map/partials/pallas_call | solution.py:44
  15.6 0.5 collective-permute-start.4
  16.1 0.0 collective-permute-done.3.refs_9_
  16.2 0.8 %partials.8 = (f32[3,64,512]{2,1,0:T(8,128)S(1)}, bf16[3,64,512]{2,1,0:T(8,128)(2,1)S(1)}) custom-call(bf16[4,128,256]{2,1,0:T(8,128)(2,1)S(1)} %get-tuple-element.41.refs_0_, bf16[4,128,256]{2,1,0:T(8,128)(2,1)S(1)} %get-tuple-element.42.refs_1_, f32[8,1,4096]{2,1,0:T(1,128)S(1)} %get-tuple-element.40.refs_0_.refs_2_.refs_9_.refs_10_.refs_11_.refs_5_, ...), custom_call_target="tpu_custom_call" | custom-call | flops 1 | bytes 1 | tf_op jit(solution)/shard_map/partials/pallas_call | solution.py:44
  17.0 1.1 %partials.9.refs_8_ = f32[3,64,768]{2,1,0:T(8,128)S(1)} custom-call(bf16[4,128,256]{2,1,0:T(8,128)(2,1)S(1)} %get-tuple-element.41.refs_0_, bf16[4,128,256]{2,1,0:T(8,128)(2,1)S(1)} %get-tuple-element.42.refs_1_, f32[8,1,4096]{2,1,0:T(1,128)S(1)} %get-tuple-element.40.refs_0_.refs_2_.refs_9_.refs_10_.refs_11_.refs_5_, ...), custom_call_target="tpu_custom_call" | custom-call | flops 1 | bytes 1 | tf_op jit(solution)/shard_map/partials/pallas_call | solution.py:44
  18.1 0.2 collective-permute-start.5
  18.3 1.5 %collective-permute-start.6 = (bf16[3,64,512]{2,1,0:T(8,128)(2,1)S(1)}, bf16[3,64,512]{2,1,0:T(8,128)(2,1)S(1)}, u32[]{:S(2)}, u32[]{:S(2)}) collective-permute-start(bf16[3,64,512]{2,1,0:T(8,128)(2,1)S(1)} %get-tuple-element.48), channel_id=1, source_target_pairs={{0,2},{1,3},{2,0},{3,1},{4,6},{5,7},{6,4},{7,5},{8,10},{9,11},{10,... | collective-permute-start | bytes 589832 | tf_op jit(solution)/shard_map/ppermute | solution.py:288
  19.8 0.0 collective-permute-done.4.refs_9_
  19.8 1.1 %partials.10 = (f32[3,64,768]{2,1,0:T(8,128)S(1)}, bf16[3,64,768]{2,1,0:T(8,128)(2,1)S(1)}) custom-call(bf16[4,128,256]{2,1,0:T(8,128)(2,1)S(1)} %get-tuple-element.41.refs_0_, bf16[4,128,256]{2,1,0:T(8,128)(2,1)S(1)} %get-tuple-element.42.refs_1_, f32[8,1,4096]{2,1,0:T(1,128)S(1)} %get-tuple-element.40.refs_0_.refs_2_.refs_9_.refs_10_.refs_11_.refs_5_, ...), custom_call_target="tpu_custom_call" | custom-call | flops 1 | bytes 1 | tf_op jit(solution)/shard_map/partials/pallas_call | solution.py:44
  20.9 0.6 %collective-permute-start.8 = (bf16[3,64,768]{2,1,0:T(8,128)(2,1)S(1)}, bf16[3,64,768]{2,1,0:T(8,128)(2,1)S(1)}, u32[]{:S(2)}, u32[]{:S(2)}) collective-permute-start(bf16[3,64,768]{2,1,0:T(8,128)(2,1)S(1)} %get-tuple-element.59), channel_id=1, source_target_pairs={{0,2},{1,3},{2,0},{3,1},{4,6},{5,7},{6,4},{7,5},{8,10},{9,11},{10,... | collective-permute-start | bytes 884744 | tf_op jit(solution)/shard_map/ppermute | solution.py:288
  21.5 0.0 collective-permute-done.5.refs_9_
  21.5 1.1 %partials.11 = (f32[3,64,768]{2,1,0:T(8,128)S(1)}, bf16[3,64,768]{2,1,0:T(8,128)(2,1)S(1)}) custom-call(bf16[4,128,256]{2,1,0:T(8,128)(2,1)S(1)} %get-tuple-element.41.refs_0_, bf16[4,128,256]{2,1,0:T(8,128)(2,1)S(1)} %get-tuple-element.42.refs_1_, f32[8,1,4096]{2,1,0:T(1,128)S(1)} %get-tuple-element.40.refs_0_.refs_2_.refs_9_.refs_10_.refs_11_.refs_5_, ...), custom_call_target="tpu_custom_call" | custom-call | flops 1 | bytes 1 | tf_op jit(solution)/shard_map/partials/pallas_call | solution.py:44
  22.6 3.4 %collective-permute-done.6.refs_2_ = bf16[3,64,512]{2,1,0:T(8,128)(2,1)S(1)} collective-permute-done((bf16[3,64,512]{2,1,0:T(8,128)(2,1)S(1)}, bf16[3,64,512]{2,1,0:T(8,128)(2,1)S(1)}, u32[]{:S(2)}, u32[]{:S(2)}) %collective-permute-start.6) | collective-permute-done | bytes 196640 | tf_op jit(solution)/shard_map/ppermute | solution.py:288
  26.0 0.1 activate.3.refs_0_
  26.1 0.1 collective-permute-start.7
  26.2 3.0 %back_rows_grads.3 = (f32[2,64,1024]{2,1,0:T(8,128)S(1)}, f32[1024,4096]{1,0:T(8,128)}, f32[1024,4096]{1,0:T(8,128)}, f32[4096,1024]{1,0:T(8,128)}) custom-call(bf16[3,64,512]{2,1,0:T(8,128)(2,1)S(1)} %activate.3.refs_0_, f32[32,1,1024]{2,1,0:T(1,128)S(1)} %get-tuple-element.49.refs_1_.refs_2_, f32[32,1,1024]{2,1,0:T(1,128)S(1)} %get-tuple-element.50.refs_2_.refs_3_, ...), custom_call_target="tpu_custom_call" | custom-call | flops 1 | bytes 1 | tf_op jit(solution)/shard_map/back_rows_grads/pallas_call | solution.py:44
  29.2 0.0 collective-permute-done.7.refs_0_
  29.2 3.0 %back_rows_grads.4 = (f32[2,64,1024]{2,1,0:T(8,128)S(1)}, f32[1024,4096]{1,0:T(8,128)}, f32[1024,4096]{1,0:T(8,128)}, f32[4096,1024]{1,0:T(8,128)}) custom-call(bf16[3,64,512]{2,1,0:T(8,128)(2,1)S(1)} %collective-permute-done.7.refs_0_, ...), custom_call_target="tpu_custom_call", output_to_operand_aliasing={{1}: (12, {}), {2}: (13, {}), {3}: (14, {})} | custom-call | flops 1 | bytes 1 | tf_op jit(solution)/shard_map/back_rows_grads/pallas_call | solution.py:44
  32.3 0.0 collective-permute-done.8.refs_2_
  32.3 0.1 activate.4.refs_0_
  32.4 0.6 collective-permute-start.9
  33.0 1.5 %collective-permute-start.10 = (bf16[3,64,768]{2,1,0:T(8,128)(2,1)S(1)}, bf16[3,64,768]{2,1,0:T(8,128)(2,1)S(1)}, u32[]{:S(2)}, u32[]{:S(2)}) collective-permute-start(bf16[3,64,768]{2,1,0:T(8,128)(2,1)S(1)} %get-tuple-element.64), channel_id=1, source_target_pairs={{0,2},{1,3},{2,0},{3,1},{4,6},{5,7},{6,4},{7,5},{8,10},{9,11},{10,... | collective-permute-start | bytes 884744 | tf_op jit(solution)/shard_map/ppermute | solution.py:288
  34.5 0.0 collective-permute-done.9.refs_1_
  34.5 8.2 %back_rows_grads.5 = (f32[2,64,1024]{2,1,0:T(8,128)S(1)}, f32[1024,4096]{1,0:T(8,128)}, f32[1024,4096]{1,0:T(8,128)}, f32[4096,1024]{1,0:T(8,128)}) custom-call(bf16[3,64,768]{2,1,0:T(8,128)(2,1)S(1)} %activate.4.refs_0_, bf16[3,64,768]{2,1,0:T(8,128)(2,1)S(1)} %collective-permute-done.9.refs_1_, ...), custom_call_target="tpu_custom_call", output_to_operand_aliasing={{1}: (13, {}), {2}: (14, {}), {3}: (15, {})} | custom-call | flops 1 | bytes 1 | tf_op jit(solution)/shard_map/back_rows_grads/pallas_call | solution.py:44
  42.7 0.0 collective-permute-done.10.refs_2_
  42.7 0.1 activate.5.refs_0_
  42.9 0.1 collective-permute-start.11
  43.0 1.5 %back_rows.2.refs_7_ = f32[2,64,1024]{2,1,0:T(8,128)S(1)} custom-call(bf16[3,64,768]{2,1,0:T(8,128)(2,1)S(1)} %activate.5.refs_0_, f32[32,1,1024]{2,1,0:T(1,128)S(1)} %get-tuple-element.49.refs_1_.refs_2_, f32[32,1,1024]{2,1,0:T(1,128)S(1)} %get-tuple-element.50.refs_2_.refs_3_, f32[32,1,1024]{2,1,0:T(1,128)S(1)} %get-tuple-element.51.refs_3_.refs_4_, ...), custom_call_target="tpu_custom_call" | custom-call | flops 1 | bytes 1 | tf_op jit(solution)/shard_map/back_rows/pallas_call | solution.py:44
  44.5 0.1 collective-permute-done.11.refs_0_.refs_1_
  44.5 1.5 %back_rows.3 = (bf16[2,16,1024]{2,1,0:T(8,128)(2,1)S(1)}, bf16[2,16,1024]{2,1,0:T(8,128)(2,1)S(1)}, bf16[2,16,1024]{2,1,0:T(8,128)(2,1)S(1)}, bf16[2,16,1024]{2,1,0:T(8,128)(2,1)S(1)}) custom-call(bf16[3,64,768]{2,1,0:T(8,128)(2,1)S(1)} %collective-permute-done.11.refs_0_.refs_1_, f32[32,1,1024]{2,1,0:T(1,128)S(1)} %get-tuple-element.49.refs_1_.refs_2_, ...), custom_call_target="tpu_custom_call" | custom-call | flops 1 | bytes 1 | tf_op jit(solution)/shard_map/back_rows/pallas_call | solution.py:44
  46.0 0.1 collective-permute-start.12
  46.1 2.3 %collective-permute-start.13 = (bf16[2,16,1024]{2,1,0:T(8,128)(2,1)S(1)}, bf16[2,16,1024]{2,1,0:T(8,128)(2,1)S(1)}, u32[]{:S(2)}, u32[]{:S(2)}) collective-permute-start(bf16[2,16,1024]{2,1,0:T(8,128)(2,1)S(1)} %get-tuple-element.67), channel_id=1, source_target_pairs={{0,8},{4,12},{8,0},{12,4},{1,9},{5,13},{9,1},{13,5},{2,10},{6,14},... | collective-permute-start | bytes 196616 | tf_op jit(solution)/shard_map/ppermute | solution.py:281
  48.4 2.1 %collective-permute-start.14 = (bf16[2,16,1024]{2,1,0:T(8,128)(2,1)S(1)}, bf16[2,16,1024]{2,1,0:T(8,128)(2,1)S(1)}, u32[]{:S(2)}, u32[]{:S(2)}) collective-permute-start(bf16[2,16,1024]{2,1,0:T(8,128)(2,1)S(1)} %get-tuple-element.68), channel_id=1, source_target_pairs={{0,12},{4,8},{8,4},{12,0},{1,13},{5,9},{9,5},{13,1},{2,14},{6,10},... | collective-permute-start | bytes 196616 | tf_op jit(solution)/shard_map/ppermute | solution.py:281
  50.5 6.9 %back_grads.1 = (f32[1024,4096]{1,0:T(8,128)}, f32[1024,4096]{1,0:T(8,128)}, f32[4096,1024]{1,0:T(8,128)}) custom-call(bf16[3,64,768]{2,1,0:T(8,128)(2,1)S(1)} %activate.5.refs_0_, bf16[3,64,768]{2,1,0:T(8,128)(2,1)S(1)} %collective-permute-done.11.refs_0_.refs_1_, ...), custom_call_target="tpu_custom_call", output_to_operand_aliasing={{0}: (7, {}), {1}: (8, {}), {2}: (9, {})} | custom-call | flops 1 | bytes 1 | tf_op jit(solution)/shard_map/back_grads/pallas_call | solution.py:44
  57.3 0.0 collective-permute-done.12
  57.3 0.0 collective-permute-done.13
  57.3 0.0 collective-permute-done.14
  57.4 0.6 %slice_bitcast_fusion = (bf16[16,1024]{1,0:T(8,128)(2,1)}, bf16[16,1024]{1,0:T(8,128)(2,1)}) fusion(bf16[2,16,1024]{2,1,0:T(8,128)(2,1)S(1)} %add_convert_fusion), kind=kLoop, calls=%fused_computation.2 | loop fusion | bytes 131072 | tf_op jit(solution)/shard_map/squeeze | solution.py:444
  (3 shorter events, 0.0 us)
Async XLA Ops:
  0.6 12.9 %copy-start = (bf16[4096,1024]{1,0:T(8,128)(2,1)S(1)}, bf16[4096,1024]{1,0:T(8,128)(2,1)}, u32[]{:S(2)}) copy-start(bf16[4096,1024]{1,0:T(8,128)(2,1)} %refs_6_.21) | copy-start | bytes 25165828
  0.6 12.9 %slice-start.2 = ((s8[8388608]{0:T(1024)(128)(4,1)}), s8[4194304]{0:T(1024)(128)(4,1)S(1)}, s32[]{:S(2)}) async-start(s8[8388608]{0:T(1024)(128)(4,1)} %bitcast.9), calls=%async_computation.2 | async-start | bytes 8388608
  0.7 12.9 %slice-start = ((s8[8388608]{0:T(1024)(128)(4,1)}), s8[4194304]{0:T(1024)(128)(4,1)S(1)}, s32[]{:S(2)}) async-start(s8[8388608]{0:T(1024)(128)(4,1)} %bitcast.7), calls=%async_computation | async-start | bytes 8388608
  1.6 7.1 %collective-permute-start.2 = (bf16[2,16,1024]{2,1,0:T(8,128)(2,1)S(1)}, bf16[2,16,1024]{2,1,0:T(8,128)(2,1)S(1)}, u32[]{:S(2)}, u32[]{:S(2)}) collective-permute-start(bf16[2,16,1024]{2,1,0:T(8,128)(2,1)S(1)} %pad_maximum_fusion.refs_4_), channel_id=1, source_target_pairs={{0,4},{4,0},{8,12},{12,8},{1,5},{5,1},{9,13},{13,9},{2,6},{6,2},{1... | collective-permute-start | bytes 196616 | tf_op jit(solution)/shard_map/ppermute | solution.py:281
  4.7 7.3 %collective-permute-start.1 = (bf16[2,16,1024]{2,1,0:T(8,128)(2,1)S(1)}, bf16[2,16,1024]{2,1,0:T(8,128)(2,1)S(1)}, u32[]{:S(2)}, u32[]{:S(2)}) collective-permute-start(bf16[2,16,1024]{2,1,0:T(8,128)(2,1)S(1)} %pad_maximum_fusion.refs_4_), channel_id=1, source_target_pairs={{0,8},{4,12},{8,0},{12,4},{1,9},{5,13},{9,1},{13,5},{2,10},{6,14},... | collective-permute-start | bytes 196616 | tf_op jit(solution)/shard_map/ppermute | solution.py:281
  7.3 6.1 %collective-permute-start = (bf16[2,16,1024]{2,1,0:T(8,128)(2,1)S(1)}, bf16[2,16,1024]{2,1,0:T(8,128)(2,1)S(1)}, u32[]{:S(2)}, u32[]{:S(2)}) collective-permute-start(bf16[2,16,1024]{2,1,0:T(8,128)(2,1)S(1)} %pad_maximum_fusion.refs_4_), channel_id=1, source_target_pairs={{0,12},{4,8},{8,4},{12,0},{1,13},{5,9},{9,5},{13,1},{2,14},{6,10},... | collective-permute-start | bytes 196616 | tf_op jit(solution)/shard_map/ppermute | solution.py:281
  7.3 6.3 %slice-start.1 = ((s8[8388608]{0:T(1024)(128)(4,1)}), s8[4194304]{0:T(1024)(128)(4,1)S(1)}, s32[]{:S(2)}) async-start(s8[8388608]{0:T(1024)(128)(4,1)} %bitcast.7), calls=%async_computation.1 | async-start | bytes 8388608
  7.3 6.3 %slice-start.3 = ((s8[8388608]{0:T(1024)(128)(4,1)}), s8[4194304]{0:T(1024)(128)(4,1)S(1)}, s32[]{:S(2)}) async-start(s8[8388608]{0:T(1024)(128)(4,1)} %bitcast.9), calls=%async_computation.3 | async-start | bytes 8388608
  14.4 1.8 %collective-permute-start.3 = (f32[3,64,512]{2,1,0:T(8,128)S(1)}, f32[3,64,512]{2,1,0:T(8,128)S(1)}, u32[]{:S(2)}, u32[]{:S(2)}) collective-permute-start(f32[3,64,512]{2,1,0:T(8,128)S(1)} %partials.6.refs_8_), channel_id=1, source_target_pairs={{0,1},{1,0},{2,3},{3,2},{4,5},{5,4},{6,7},{7,6},{8,9},{9,8},{10,11... | collective-permute-start | bytes 1179656 | tf_op jit(solution)/shard_map/ppermute | solution.py:284
  15.6 4.2 %collective-permute-start.4 = (f32[3,64,768]{2,1,0:T(8,128)S(1)}, f32[3,64,768]{2,1,0:T(8,128)S(1)}, u32[]{:S(2)}, u32[]{:S(2)}) collective-permute-start(f32[3,64,768]{2,1,0:T(8,128)S(1)} %partials.7.refs_8_), channel_id=1, source_target_pairs={{0,1},{1,0},{2,3},{3,2},{4,5},{5,4},{6,7},{7,6},{8,9},{9,8},{10,11... | collective-permute-start | bytes 1769480 | tf_op jit(solution)/shard_map/ppermute | solution.py:284
  18.1 3.4 %collective-permute-start.5 = (f32[3,64,768]{2,1,0:T(8,128)S(1)}, f32[3,64,768]{2,1,0:T(8,128)S(1)}, u32[]{:S(2)}, u32[]{:S(2)}) collective-permute-start(f32[3,64,768]{2,1,0:T(8,128)S(1)} %partials.9.refs_8_), channel_id=1, source_target_pairs={{0,1},{1,0},{2,3},{3,2},{4,5},{5,4},{6,7},{7,6},{8,9},{9,8},{10,11... | collective-permute-start | bytes 1769480 | tf_op jit(solution)/shard_map/ppermute | solution.py:284
  18.3 7.7 %collective-permute-start.6 = (bf16[3,64,512]{2,1,0:T(8,128)(2,1)S(1)}, bf16[3,64,512]{2,1,0:T(8,128)(2,1)S(1)}, u32[]{:S(2)}, u32[]{:S(2)}) collective-permute-start(bf16[3,64,512]{2,1,0:T(8,128)(2,1)S(1)} %get-tuple-element.48), channel_id=1, source_target_pairs={{0,2},{1,3},{2,0},{3,1},{4,6},{5,7},{6,4},{7,5},{8,10},{9,11},{10,... | collective-permute-start | bytes 589832 | tf_op jit(solution)/shard_map/ppermute | solution.py:288
  20.9 11.4 %collective-permute-start.8 = (bf16[3,64,768]{2,1,0:T(8,128)(2,1)S(1)}, bf16[3,64,768]{2,1,0:T(8,128)(2,1)S(1)}, u32[]{:S(2)}, u32[]{:S(2)}) collective-permute-start(bf16[3,64,768]{2,1,0:T(8,128)(2,1)S(1)} %get-tuple-element.59), channel_id=1, source_target_pairs={{0,2},{1,3},{2,0},{3,1},{4,6},{5,7},{6,4},{7,5},{8,10},{9,11},{10,... | collective-permute-start | bytes 884744 | tf_op jit(solution)/shard_map/ppermute | solution.py:288
  26.1 3.1 %collective-permute-start.7 = (bf16[3,64,512]{2,1,0:T(8,128)(2,1)S(1)}, bf16[3,64,512]{2,1,0:T(8,128)(2,1)S(1)}, u32[]{:S(2)}, u32[]{:S(2)}) collective-permute-start(bf16[3,64,512]{2,1,0:T(8,128)(2,1)S(1)} %activate.3.refs_0_), channel_id=1, source_target_pairs={{0,1},{1,0},{2,3},{3,2},{4,5},{5,4},{6,7},{7,6},{8,9},{9,8},{10,11... | collective-permute-start | bytes 589832 | tf_op jit(solution)/shard_map/ppermute | solution.py:284
  32.4 2.1 %collective-permute-start.9 = (bf16[3,64,768]{2,1,0:T(8,128)(2,1)S(1)}, bf16[3,64,768]{2,1,0:T(8,128)(2,1)S(1)}, u32[]{:S(2)}, u32[]{:S(2)}) collective-permute-start(bf16[3,64,768]{2,1,0:T(8,128)(2,1)S(1)} %activate.4.refs_0_), channel_id=1, source_target_pairs={{0,1},{1,0},{2,3},{3,2},{4,5},{5,4},{6,7},{7,6},{8,9},{9,8},{10,11... | collective-permute-start | bytes 884744 | tf_op jit(solution)/shard_map/ppermute | solution.py:284
  33.0 9.7 %collective-permute-start.10 = (bf16[3,64,768]{2,1,0:T(8,128)(2,1)S(1)}, bf16[3,64,768]{2,1,0:T(8,128)(2,1)S(1)}, u32[]{:S(2)}, u32[]{:S(2)}) collective-permute-start(bf16[3,64,768]{2,1,0:T(8,128)(2,1)S(1)} %get-tuple-element.64), channel_id=1, source_target_pairs={{0,2},{1,3},{2,0},{3,1},{4,6},{5,7},{6,4},{7,5},{8,10},{9,11},{10,... | collective-permute-start | bytes 884744 | tf_op jit(solution)/shard_map/ppermute | solution.py:288
  42.9 1.6 %collective-permute-start.11 = (bf16[3,64,768]{2,1,0:T(8,128)(2,1)S(1)}, bf16[3,64,768]{2,1,0:T(8,128)(2,1)S(1)}, u32[]{:S(2)}, u32[]{:S(2)}) collective-permute-start(bf16[3,64,768]{2,1,0:T(8,128)(2,1)S(1)} %activate.5.refs_0_), channel_id=1, source_target_pairs={{0,1},{1,0},{2,3},{3,2},{4,5},{5,4},{6,7},{7,6},{8,9},{9,8},{10,11... | collective-permute-start | bytes 884744 | tf_op jit(solution)/shard_map/ppermute | solution.py:284
  46.0 11.3 %collective-permute-start.12 = (bf16[2,16,1024]{2,1,0:T(8,128)(2,1)S(1)}, bf16[2,16,1024]{2,1,0:T(8,128)(2,1)S(1)}, u32[]{:S(2)}, u32[]{:S(2)}) collective-permute-start(bf16[2,16,1024]{2,1,0:T(8,128)(2,1)S(1)} %get-tuple-element.66), channel_id=1, source_target_pairs={{0,4},{4,0},{8,12},{12,8},{1,5},{5,1},{9,13},{13,9},{2,6},{6,2},{1... | collective-permute-start | bytes 196616 | tf_op jit(solution)/shard_map/ppermute | solution.py:281
  46.1 11.3 %collective-permute-start.13 = (bf16[2,16,1024]{2,1,0:T(8,128)(2,1)S(1)}, bf16[2,16,1024]{2,1,0:T(8,128)(2,1)S(1)}, u32[]{:S(2)}, u32[]{:S(2)}) collective-permute-start(bf16[2,16,1024]{2,1,0:T(8,128)(2,1)S(1)} %get-tuple-element.67), channel_id=1, source_target_pairs={{0,8},{4,12},{8,0},{12,4},{1,9},{5,13},{9,1},{13,5},{2,10},{6,14},... | collective-permute-start | bytes 196616 | tf_op jit(solution)/shard_map/ppermute | solution.py:281
  48.4 8.9 %collective-permute-start.14 = (bf16[2,16,1024]{2,1,0:T(8,128)(2,1)S(1)}, bf16[2,16,1024]{2,1,0:T(8,128)(2,1)S(1)}, u32[]{:S(2)}, u32[]{:S(2)}) collective-permute-start(bf16[2,16,1024]{2,1,0:T(8,128)(2,1)S(1)} %get-tuple-element.68), channel_id=1, source_target_pairs={{0,12},{4,8},{8,4},{12,0},{1,13},{5,9},{9,5},{13,1},{2,14},{6,10},... | collective-permute-start | bytes 196616 | tf_op jit(solution)/shard_map/ppermute | solution.py:281
